TPU v7x, 512 devices: a whole 4x4x16 slice. The times are simulated.
512 devices in a mesh: dp: 8 (over x, core), expert: 64 (over y, z).
Axes of the slice: x: 4, y: 4, z: 16, core: 2. Of those that a mesh axis runs over, the one named last changes fastest.
Arguments:
- tokens: bfloat16 [8, 8192, 2048], P('dp', 'expert'), may hold values from -6 to 6
- expert_ids: int32 [8, 8192, 8], P('dp', 'expert'), may hold values from 0 to 127, all different within a row; in each aligned block of 128 rows (0 to 127, 128 to 255, ..., all dimensions but the last counted through in order) at most 10 rows name the same one
- route_weights: int32 [8, 8192, 8], P('dp', 'expert'), may hold values from 1 to 8
- gate_weight: bfloat16 [64, 2048, 384], P('expert', 'dp'), may hold values from -0.125 to 0.125
- up_weight: bfloat16 [64, 2048, 384], P('expert', 'dp'), may hold values from -0.125 to 0.125
- cotangent: bfloat16 [8, 64, 640, 384], P('dp', 'expert'), may hold values from -6 to 6
Outputs:
- hidden: bfloat16 [8, 64, 640, 384], P('dp', 'expert')
- token_grads: float32 [8, 8192, 2048], P('dp', 'expert')
- gate_grads: float32 [64, 2048, 384], P('expert', 'dp')
- up_grads: float32 [64, 2048, 384], P('expert', 'dp')
Inputs may be any that keep to these rules, and one draw needn't show every extreme that they name: `expert_ids`: each token names 8 different experts; among the 128 tokens of one device no expert is named by more than 10 tokens, a bound that some block reaches.
All inputs are finite; a program needn't handle non-finite values.
Results may differ from a plain program's by a relative error of at most 0.015.
Values may be sent and summed in bfloat16 or wider, within the bound.
No kernel may reach another device: no remote copies, remote signals or barrier semaphores. Data moves between devices by JAX's collectives and lax.ppermute only.
A program may use at most 64 MiB of HBM per device.

v0:
```python
import jax
import jax.numpy as jnp
from jax import lax
from jax.sharding import PartitionSpec as P


def local_slots(expert_ids, route_weights, experts, capacity):
    labels = jnp.arange(2 * experts, dtype=jnp.int32)
    chosen = expert_ids[0]
    hit_counts = jnp.sum((chosen[:, :, None] == labels).astype(jnp.int32), axis=1)
    before = jnp.cumsum(hit_counts, axis=0) - hit_counts
    ranked = jnp.take_along_axis(before, chosen, axis=1)
    slot_ids = chosen * capacity + ranked
    columns = jnp.arange(experts * capacity, dtype=jnp.int32)
    matching = slot_ids[:, :, None] == columns
    select = jnp.any(matching, axis=1).astype(jnp.bfloat16)
    scales = route_weights[0].astype(jnp.float32) / 8.0
    slot_weight = jnp.sum(jnp.where(matching, scales[:, :, None], 0.0), axis=(0, 1))
    return (select, slot_weight)


def shards(tokens, expert_ids, route_weights, gate_weight, up_weight, cotangent):
    experts = lax.axis_size("expert")
    slot_count = cotangent.shape[2]
    capacity = slot_count // experts
    model_width = tokens.shape[2]
    hidden_units = gate_weight.shape[2]
    select, slot_weight = local_slots(expert_ids, route_weights, experts, capacity)
    outgoing = jnp.dot(select.T, tokens[0], preferred_element_type=jnp.float32).astype(jnp.bfloat16)
    outgoing = outgoing.reshape(experts, capacity, model_width)
    arrived, arrived_weight = (
        lax.all_to_all(outgoing, "expert", split_axis=0, concat_axis=0, tiled=True),
        lax.all_to_all(
            slot_weight.reshape(experts, capacity).astype(jnp.bfloat16),
            "expert",
            split_axis=0,
            concat_axis=0,
            tiled=True,
        ).astype(jnp.float32),
    )
    slot_rows = arrived.reshape(slot_count, model_width)
    weight_col = arrived_weight.reshape(slot_count, 1)
    stacked = jnp.concatenate((gate_weight, up_weight), axis=0)
    full_weights = lax.all_gather(stacked, "dp", axis=1, tiled=True)
    gate_pre = jnp.dot(slot_rows, full_weights[0], preferred_element_type=jnp.float32)
    up_pre = jnp.dot(slot_rows, full_weights[1], preferred_element_type=jnp.float32)
    hidden = (jax.nn.silu(gate_pre) * up_pre * weight_col).astype(jnp.bfloat16)
    sigmoid_gate = jax.nn.sigmoid(gate_pre)
    activation = gate_pre * sigmoid_gate
    act_slope = sigmoid_gate * (1.0 + gate_pre * (1.0 - sigmoid_gate))
    scaled = cotangent[0, 0].astype(jnp.float32) * weight_col
    grad_gate = (scaled * up_pre * act_slope).astype(jnp.bfloat16)
    grad_up = (scaled * activation).astype(jnp.bfloat16)
    grad_rows = jnp.dot(grad_gate, full_weights[0].T, preferred_element_type=jnp.float32)
    grad_rows = grad_rows + jnp.dot(grad_up, full_weights[1].T, preferred_element_type=jnp.float32)
    grad_pre = jnp.concatenate((grad_gate, grad_up), axis=1)
    weight_grads = lax.psum_scatter(
        lax.dot_general(
            slot_rows, grad_pre, (((0,), (0,)), ((), ())), preferred_element_type=jnp.float32
        ).astype(jnp.bfloat16),
        "dp",
        scatter_dimension=0,
        tiled=True,
    ).astype(jnp.float32)
    outgoing_grads = grad_rows.astype(jnp.bfloat16).reshape(experts, capacity, model_width)
    returned = lax.all_to_all(outgoing_grads, "expert", split_axis=0, concat_axis=0, tiled=True)
    token_grads = jnp.dot(
        select, returned.reshape(slot_count, model_width), preferred_element_type=jnp.float32
    )
    gate_grads = weight_grads[:, :hidden_units]
    up_grads = weight_grads[:, hidden_units:]
    return (hidden[None, None], token_grads[None], gate_grads[None], up_grads[None])


def solution(mesh):
    in_specs = (
        P("dp", "expert", None),
        P("dp", "expert", None),
        P("dp", "expert", None),
        P("expert", "dp", None),
        P("expert", "dp", None),
        P("dp", "expert", None, None),
    )
    out_specs = (
        P("dp", "expert", None, None),
        P("dp", "expert", None),
        P("expert", "dp", None),
        P("expert", "dp", None),
    )
    return jax.shard_map(shards, mesh=mesh, in_specs=in_specs, out_specs=out_specs, check_vma=False)
```

profile of v0, /device:TPU:6, one launch (start us, length us, event | category | flops | bytes accessed | tf_op | source)
XLA Modules:
  0.0 468.8 jit_solution(1424427655558972724)
XLA Ops:
  7.2 0.0 copy-start
  7.2 0.8 fusion.17
  7.9 0.8 copy.26
  8.7 0.7 multiply_bitcast_fusion
  9.4 0.1 copy.27
  9.5 0.1 reshape.115
  9.6 0.1 copy.28
  9.7 0.2 convert_reduce_fusion
  9.9 0.2 reduce_window_sum.11
  10.1 6.8 %gather_fusion = s32[1024]{0:T(1024)S(1)} fusion(s32[128,128]{1,0:T(8,128)S(1)} %sub.6, s32[1024]{0:T(1024)S(1)} %reshape.115), kind=kCustom, calls=%fused_computation | custom fusion | bytes 16384 | tf_op jit(solution)/shard_map/jit(take_along_axis)/gather | solution.py:12
  16.9 0.1 reshape.118
  17.0 0.4 select_reduce_fusion
  17.4 0.8 convert_element_type.79
  18.2 18.7 %all-to-all-start.1 = ((bf16[64,1,10]{2,1,0:T(2,128)(2,1)}), bf16[64,1,10]{2,1,0:T(2,128)(2,1)S(1)}, u32[]{:S(2)}, u32[]{:S(2)}) async-start(bf16[64,1,10]{2,1,0:T(2,128)(2,1)} %convert_element_type.79), calls=%async_computation.1 | async-start | bytes 65536 | tf_op jit(solution)/shard_map/all_to_all | solution.py:33
  36.9 0.9 fusion
  37.8 0.0 copy-done
  37.8 0.9 convolution_convert_fusion.1
  38.7 2.8 reshape.109
  41.5 0.0 copy-start.9
  41.5 0.0 copy-start.10
  41.5 0.0 copy-start.5
  41.5 9.8 %all-to-all-done.1 = bf16[64,1,10]{2,1,0:T(2,128)(2,1)S(1)} async-done(((bf16[64,1,10]{2,1,0:T(2,128)(2,1)}), bf16[64,1,10]{2,1,0:T(2,128)(2,1)S(1)}, u32[]{:S(2)}, u32[]{:S(2)}) %all-to-all-start.1) | async-done | bytes 1312 | tf_op jit(solution)/shard_map/all_to_all | solution.py:33
  51.3 5.7 %all-to-all-start = ((bf16[64,10,2048]{2,1,0:T(8,128)(2,1)}), bf16[64,10,2048]{2,1,0:T(8,128)(2,1)}, u32[]{:S(2)}, u32[]{:S(2)}) async-start(bf16[64,10,2048]{2,1,0:T(8,128)(2,1)} %reshape.109), calls=%async_computation | async-start | bytes 8388608 | tf_op jit(solution)/shard_map/all_to_all | solution.py:32
  57.0 0.2 all-gather.2.cloned.1.call-start
  57.2 0.0 copy-done.9
  57.2 0.0 copy-done.10
  57.3 0.8 pad_maximum_fusion
  58.1 0.0 all-gather.2.cloned.1.call-update
  58.1 0.0 copy-done.5
  58.1 1.0 copy.30
  59.1 0.1 convert_reduce_fusion.1
  59.2 0.1 reshape.113
  59.3 185.2 %all-to-all-done = bf16[64,10,2048]{2,1,0:T(8,128)(2,1)} async-done(((bf16[64,10,2048]{2,1,0:T(8,128)(2,1)}), bf16[64,10,2048]{2,1,0:T(8,128)(2,1)}, u32[]{:S(2)}, u32[]{:S(2)}) %all-to-all-start) | async-done | bytes 2621472 | tf_op jit(solution)/shard_map/all_to_all | solution.py:32
  244.5 4.1 reshape.110
  248.6 0.0 copy-start.2
  248.6 0.0 all-gather.2.cloned.1.call-done
  248.6 0.0 copy-start.1
  248.6 0.0 copy-start.8
  248.7 3.8 fusion.2
  252.4 0.0 copy-done.2
  252.5 0.0 copy-done.1
  252.5 0.0 copy-done.8
  252.5 2.6 fusion.10
  255.0 0.0 copy-start.4
  255.0 0.0 copy-start.7
  255.0 1.6 fusion.1
  256.6 0.0 copy-done.4
  256.6 0.0 copy-done.7
  256.6 1.6 add_convert_fusion
  258.2 2.8 reshape.111
  261.0 0.0 copy-start.3
  261.0 7.7 %all-to-all-start.2 = ((bf16[64,10,2048]{2,1,0:T(8,128)(2,1)}), bf16[64,10,2048]{2,1,0:T(8,128)(2,1)}, u32[]{:S(2)}, u32[]{:S(2)}) async-start(bf16[64,10,2048]{2,1,0:T(8,128)(2,1)} %reshape.111), calls=%async_computation.2 | async-start | bytes 8388608 | tf_op jit(solution)/shard_map/all_to_all | solution.py:66
  268.7 0.0 reduce-scatter.2.cloned.1.call-start
  268.7 0.0 copy-done.3
  268.7 5.2 %convolution_convert_fusion = bf16[2048,768]{1,0:T(8,128)(2,1)} fusion(bf16[640,2048]{1,0:T(8,128)(2,1)S(1)} %copy-done.3, bf16[640,384]{0,1:T(8,128)(2,1)} %copy-done.7, bf16[640,384]{0,1:T(8,128)(2,1)} %copy-done.4), kind=kOutput, calls=%fused_computation.2 | convolution fusion | flops 2016804864 | bytes 6750208 | tf_op jit(solution)/shard_map/dot_general | solution.py:58
  274.0 0.0 reduce-scatter.2.cloned.1.call-update
  274.0 1.0 copy-done.6
  275.0 1.0 copy.31
  276.0 39.8 %reduce-scatter.2.cloned.1.call-done = bf16[256,768]{1,0:T(8,128)(2,1)} async-done(((bf16[2048,768]{1,0:T(8,128)(2,1)}), bf16[256,768]{1,0:T(8,128)(2,1)}) %reduce-scatter.2.cloned.1.call-update) | async-done | bytes 393232 | tf_op jit(solution)/shard_map/reduce_scatter | solution.py:57
  315.8 1.0 convert_element_type.76
  316.9 0.9 slice_bitcast_fusion.6
  317.8 138.6 %all-to-all-done.2 = bf16[64,10,2048]{2,1,0:T(8,128)(2,1)} async-done(((bf16[64,10,2048]{2,1,0:T(8,128)(2,1)}), bf16[64,10,2048]{2,1,0:T(8,128)(2,1)}, u32[]{:S(2)}, u32[]{:S(2)}) %all-to-all-start.2) | async-done | bytes 2621472 | tf_op jit(solution)/shard_map/all_to_all | solution.py:66
  456.4 4.1 reshape.112
  460.4 1.6 convolution_bitcast_fusion
  (3 shorter events, 0.0 us)
Async XLA Ops:
  7.2 30.6 %copy-start = (bf16[1,128,2048]{2,1,0:T(8,128)(2,1)S(1)}, bf16[1,128,2048]{2,1,0:T(8,128)(2,1)}, u32[]{:S(2)}) copy-start(bf16[1,128,2048]{2,1,0:T(8,128)(2,1)} %param.6) | copy-start | bytes 1572868
  18.2 33.1 %all-to-all-start.1 = ((bf16[64,1,10]{2,1,0:T(2,128)(2,1)}), bf16[64,1,10]{2,1,0:T(2,128)(2,1)S(1)}, u32[]{:S(2)}, u32[]{:S(2)}) async-start(bf16[64,1,10]{2,1,0:T(2,128)(2,1)} %convert_element_type.79), calls=%async_computation.1 | async-start | bytes 65536 | tf_op jit(solution)/shard_map/all_to_all | solution.py:33
  41.5 15.8 %copy-start.9 = (bf16[1,256,384]{2,1,0:T(8,128)(2,1)S(1)}, bf16[1,256,384]{2,1,0:T(8,128)(2,1)}, u32[]{:S(2)}) copy-start(bf16[1,256,384]{2,1,0:T(8,128)(2,1)} %param.10) | copy-start | bytes 589828
  41.5 15.8 %copy-start.10 = (bf16[1,256,384]{2,1,0:T(8,128)(2,1)S(1)}, bf16[1,256,384]{2,1,0:T(8,128)(2,1)}, u32[]{:S(2)}) copy-start(bf16[1,256,384]{2,1,0:T(8,128)(2,1)} %param.9) | copy-start | bytes 589828
  41.5 16.6 %copy-start.5 = (bf16[1,1,640,384]{3,2,1,0:T(8,128)(2,1)S(1)}, bf16[1,1,640,384]{3,2,1,0:T(8,128)(2,1)}, u32[]{:S(2)}) copy-start(bf16[1,1,640,384]{3,2,1,0:T(8,128)(2,1)} %param.11) | copy-start | bytes 1474564
  51.3 193.2 %all-to-all-start = ((bf16[64,10,2048]{2,1,0:T(8,128)(2,1)}), bf16[64,10,2048]{2,1,0:T(8,128)(2,1)}, u32[]{:S(2)}, u32[]{:S(2)}) async-start(bf16[64,10,2048]{2,1,0:T(8,128)(2,1)} %reshape.109), calls=%async_computation | async-start | bytes 8388608 | tf_op jit(solution)/shard_map/all_to_all | solution.py:32
  57.0 191.6 %all-gather.2.cloned.1.call-start = ((), (), s32[]{:S(2)}) async-start(), calls=%async_computation.4 | async-start | bytes 3538944 | tf_op jit(solution)/shard_map/all_gather | solution.py:44
  248.6 3.9 copy-start.2
  248.6 3.8 copy-start.1
  248.6 3.8 copy-start.8
  255.0 1.6 copy-start.4
  255.0 1.6 copy-start.7
  261.0 7.7 %copy-start.3 = (bf16[640,2048]{1,0:T(8,128)(2,1)S(1)}, bf16[640,2048]{1,0:T(8,128)(2,1)}, u32[]{:S(2)}) copy-start(bf16[640,2048]{1,0:T(8,128)(2,1)} %copy-done.2) | copy-start | bytes 7864324
  261.0 195.4 %all-to-all-start.2 = ((bf16[64,10,2048]{2,1,0:T(8,128)(2,1)}), bf16[64,10,2048]{2,1,0:T(8,128)(2,1)}, u32[]{:S(2)}, u32[]{:S(2)}) async-start(bf16[64,10,2048]{2,1,0:T(8,128)(2,1)} %reshape.111), calls=%async_computation.2 | async-start | bytes 8388608 | tf_op jit(solution)/shard_map/all_to_all | solution.py:66
  268.7 47.1 %reduce-scatter.2.cloned.1.call-start = ((), (), s32[]{:S(2)}) async-start(), calls=%async_computation.5 | async-start | bytes 3538944 | tf_op jit(solution)/shard_map/reduce_scatter | solution.py:57
  274.0 1.0 copy-start.6
Sparse Core Ops, SparseCore 0:
  60.5 35.0 all-gather.1
  274.1 41.6 reduce-scatter.1
where the time goes:
time: 469 us
  waiting for transfers between devices  373 us (80%)
  starting transfers between devices  32.4 us (7%)
  local copies, waits for them, and re-layouts  26.5 us (6%)
  matrix products  17.2 us (4%)
  between operations  14.3 us (3%)
  other arithmetic  5.01 us (1%)
    all_to_all x1, waiting for transfers between devices, shards(): lax.all_to_all(outgoing, 'expert', split_axis=0, concat_axis=0, tiled=True)  185 us
    all_to_all x1, waiting for transfers between devices, shards(): lax.all_to_all(outgoing_grads, 'expert', split_axis=0, concat_axis=0, til...  139 us
    reduce_scatter x1, waiting for transfers between devices, shards(): lax.psum_scatter(lax.dot_general(slot_rows, grad_pre, (((0,), (0,)), ((),...  39.8 us
    all_to_all x1, starting transfers between devices, shards(): lax.all_to_all(slot_weight.reshape(experts, capacity).astype(jnp.bfloat16...  18.7 us
    all_to_all x1, waiting for transfers between devices, shards(): lax.all_to_all(slot_weight.reshape(experts, capacity).astype(jnp.bfloat16...  9.81 us
  transfers between devices with their start and end apart: 5, of which 4 were waited for; matrix products, arithmetic and copies ran while one was open for 4% of the time, Pallas kernels for 0%

commit v1 on v0

v1 whole, which is shorter than its diff:
```python
import functools

import jax
import jax.numpy as jnp
from jax import lax
from jax.experimental import pallas as pl
from jax.experimental.pallas import tpu as pltpu
from jax.sharding import Mesh, PartitionSpec as P

N_Y = 4
N_Z = 16
FORWARD_SPLIT = (1024, 1024)
BACKWARD_SPLIT = (1024, 1024)
VMEM_BYTES = 48 * 1024 * 1024


def starts_of(widths):
    return [sum(widths[:i]) for i in range(len(widths))]


def routing_kernel(ids_ref, weights_ref, out_ref):
    rows, tokens = out_ref.shape
    row = lax.broadcasted_iota(jnp.int32, (rows, tokens), 0)
    kind = row % 8
    device = row // 8
    expert = jnp.where(kind < N_Y, kind * N_Z + device % N_Z, device)
    hits = jnp.zeros((rows, tokens), jnp.float32)
    eighths = jnp.zeros((rows, tokens), jnp.float32)
    for choice in range(ids_ref.shape[0]):
        named = ids_ref[choice : choice + 1, :] == expert
        hits = hits + jnp.where(named, 1.0, 0.0)
        eighths = eighths + jnp.where(named, weights_ref[choice : choice + 1, :].astype(jnp.float32), 0.0)
    earlier = lax.broadcasted_iota(jnp.int32, (tokens, tokens), 0)
    later = lax.broadcasted_iota(jnp.int32, (tokens, tokens), 1)
    triangle = jnp.where(earlier < later, 1.0, 0.0).astype(jnp.bfloat16)
    rank = jnp.dot(hits.astype(jnp.bfloat16), triangle, preferred_element_type=jnp.float32)
    rank = jnp.where(hits > 0.0, rank, -1.0)
    out_ref[...] = jnp.where(kind <= N_Y, rank, eighths).astype(jnp.bfloat16)


def slot_matrix(slot_ref, part, part_slots, part_tokens):
    columns = slice(part * part_tokens, (part + 1) * part_tokens)
    slot = lax.broadcasted_iota(jnp.int32, (part_slots, part_tokens), 0) + part * part_slots
    return jnp.concatenate(
        [jnp.where(slot_ref[y : y + 1, columns] == slot, 1.0, 0.0).astype(jnp.bfloat16) for y in range(N_Y)],
        axis=0,
    )


def pick_kernel(parts, slot_ref, tokens_ref, out_ref):
    part_slots = out_ref.shape[1] // parts
    part_tokens = tokens_ref.shape[0] // parts
    for part in range(parts):
        select = slot_matrix(slot_ref, part, part_slots, part_tokens)
        picked = jnp.dot(
            select,
            tokens_ref[part * part_tokens : (part + 1) * part_tokens, :],
            preferred_element_type=jnp.float32,
        ).astype(jnp.bfloat16)
        for y in range(N_Y):
            out_ref[y, part * part_slots : (part + 1) * part_slots, :] = picked[
                y * part_slots : (y + 1) * part_slots, :
            ]


def add_kernel(parts, slot_ref, grads_ref, out_ref):
    part_slots = grads_ref.shape[1] // parts
    part_tokens = out_ref.shape[0] // parts
    for part in range(parts):
        select = slot_matrix(slot_ref, part, part_slots, part_tokens)
        rows = jnp.concatenate(
            [grads_ref[y, part * part_slots : (part + 1) * part_slots, :] for y in range(N_Y)], axis=0
        )
        out_ref[part * part_tokens : (part + 1) * part_tokens, :] = lax.dot_general(
            select, rows, (((0,), (0,)), ((), ())), preferred_element_type=jnp.float32
        ).astype(jnp.bfloat16)


def call(kernel, out_shape, *operands):
    whole = pl.BlockSpec(memory_space=pltpu.VMEM)
    return pl.pallas_call(
        kernel,
        out_shape=out_shape,
        in_specs=[whole] * len(operands),
        out_specs=whole,
        compiler_params=pltpu.CompilerParams(vmem_limit_bytes=VMEM_BYTES),
    )(*operands)


def shards(tokens, expert_ids, route_weights, gate_weight, up_weight, cotangent):
    experts = N_Y * N_Z
    groups = lax.axis_size("dp")
    slot_count = cotangent.shape[2]
    capacity = slot_count // experts
    row_slots = N_Z * capacity
    block, model_width = tokens.shape[1], tokens.shape[2]
    hidden_units = gate_weight.shape[2]

    gathered = [
        lax.all_gather(tokens[0, :, start : start + width], "z", axis=0, tiled=True)
        for start, width in zip(starts_of(FORWARD_SPLIT), FORWARD_SPLIT)
    ]

    told = call(
        routing_kernel,
        jax.ShapeDtypeStruct((experts * 8, block), jnp.bfloat16),
        expert_ids[0].T,
        route_weights[0].T,
    )
    heard = lax.all_to_all(told.reshape(experts, 8, block), ("y", "z"), 0, 0, tiled=True)
    own_row = lax.dynamic_slice_in_dim(heard, lax.axis_index("y") * N_Z, N_Z, axis=0)
    rank = jnp.transpose(own_row[:, :N_Y], (1, 0, 2)).astype(jnp.int32)
    base = capacity * jnp.arange(N_Z, dtype=jnp.int32)[None, :, None]
    slot_of = jnp.where(rank >= 0, rank + base, -1).reshape(N_Y, N_Z * block)
    places = jnp.arange(capacity, dtype=jnp.int32).astype(jnp.bfloat16)
    weight_col = jnp.sum(
        jnp.where(heard[:, N_Y, None, :] == places[None, :, None], heard[:, N_Y + 1, None, :].astype(jnp.float32), 0.0),
        axis=2,
    ).reshape(slot_count, 1) / 8.0

    stacked = jnp.concatenate((gate_weight[0], up_weight[0]), axis=1)
    full_weights = lax.all_to_all(
        jnp.broadcast_to(stacked[None], (groups,) + stacked.shape), "dp", 0, 0, tiled=True
    ).reshape(model_width, 2 * hidden_units)

    pre = jnp.zeros((slot_count, 2 * hidden_units), jnp.float32)
    slot_rows = []
    for start, width, part in zip(starts_of(FORWARD_SPLIT), FORWARD_SPLIT, gathered):
        picked = call(
            functools.partial(pick_kernel, 2),
            jax.ShapeDtypeStruct((N_Y, row_slots, width), jnp.bfloat16),
            slot_of,
            part,
        )
        rows = lax.all_to_all(picked, "y", 0, 0, tiled=True).reshape(slot_count, width)
        slot_rows.append(rows)
        pre = pre + jnp.dot(rows, full_weights[start : start + width], preferred_element_type=jnp.float32)

    gate_pre, up_pre = pre[:, :hidden_units], pre[:, hidden_units:]
    sigmoid_gate = jax.nn.sigmoid(gate_pre)
    activation = gate_pre * sigmoid_gate
    hidden = (activation * up_pre * weight_col).astype(jnp.bfloat16)
    act_slope = sigmoid_gate * (1.0 + gate_pre * (1.0 - sigmoid_gate))
    scaled = cotangent[0, 0].astype(jnp.float32) * weight_col
    grad_gate = (scaled * up_pre * act_slope).astype(jnp.bfloat16)
    grad_up = (scaled * activation).astype(jnp.bfloat16)
    grad_pre = jnp.concatenate((grad_gate, grad_up), axis=1)

    token_grads = []
    for start, width in zip(starts_of(BACKWARD_SPLIT), BACKWARD_SPLIT):
        grad_rows = lax.dot_general(
            grad_pre,
            full_weights[start : start + width],
            (((1,), (1,)), ((), ())),
            preferred_element_type=jnp.float32,
        ).astype(jnp.bfloat16)
        returned = lax.all_to_all(grad_rows.reshape(N_Y, row_slots, width), "y", 0, 0, tiled=True)
        sums = call(
            functools.partial(add_kernel, 2),
            jax.ShapeDtypeStruct((N_Z * block, width), jnp.bfloat16),
            slot_of,
            returned,
        )
        token_grads.append(lax.psum_scatter(sums, "z", scatter_dimension=0, tiled=True).astype(jnp.float32))

    terms = [
        lax.dot_general(rows, grad_pre, (((0,), (0,)), ((), ())), preferred_element_type=jnp.float32).astype(
            jnp.bfloat16
        )
        for rows in slot_rows
    ]
    terms = jnp.concatenate(terms, axis=0).reshape(groups, model_width // groups, 2 * hidden_units)
    weight_grads = jnp.sum(lax.all_to_all(terms, "dp", 0, 0, tiled=True).astype(jnp.float32), axis=0)
    return (
        hidden[None, None],
        jnp.concatenate(token_grads, axis=1)[None],
        weight_grads[None, :, :hidden_units],
        weight_grads[None, :, hidden_units:],
    )


def solution(mesh):
    grid = Mesh(mesh.devices.reshape(mesh.shape["dp"], N_Y, N_Z), ("dp", "y", "z"))
    expert = ("y", "z")
    in_specs = (
        P("dp", expert, None),
        P("dp", expert, None),
        P("dp", expert, None),
        P(expert, "dp", None),
        P(expert, "dp", None),
        P("dp", expert, None, None),
    )
    out_specs = (
        P("dp", expert, None, None),
        P("dp", expert, None),
        P(expert, "dp", None),
        P(expert, "dp", None),
    )
    return jax.shard_map(shards, mesh=grid, in_specs=in_specs, out_specs=out_specs, check_vma=False)
```

time: 469 us -> 385 us (0.82)
  waiting for transfers between devices: 373 us -> 221 us
  blocking collectives: 0 us -> 70.9 us
  Pallas kernels: 0 us -> 11.1 us
  local copies, waits for them, and re-layouts: 26.5 us -> 15.9 us
    all_to_all x3 -> x4, waiting for transfers between devices: 334 us -> 22.2 us  [the longest x1 16.7 us: shards(): lax.all_to_all(told.reshape(experts, 8, block), ('y', 'z'), 0, 0, tiled=T...]
    all_gather x1 -> x2, waiting for transfers between devices: 0.02 us -> 112 us  [shards(): lax.all_gather(tokens[0, :, start:start + width], 'z', axis=0, tiled=True)]
    all_to_all x0 -> x3, blocking collectives: none -> 70.9 us  [the longest x1 41.4 us: shards(): lax.all_to_all(terms, 'dp', 0, 0, tiled=True).astype(jnp.float32)]
    reduce_scatter x1 -> x2, waiting for transfers between devices: 39.8 us -> 85.8 us  [shards(): lax.psum_scatter(sums, 'z', scatter_dimension=0, tiled=True)]
    reshape x4 -> x0, local copies, waits for them, and re-layouts: 13.7 us -> none  [the longest x1 4.08 us: shards(): slot_rows = arrived.reshape(slot_count, model_width)]
    pallas_call x0 -> x5, Pallas kernels: none -> 11.1 us  [call(): pl.pallas_call(kernel, out_shape=out_shape, in_specs=[whole] * len(operan...]
    gather x4 -> x0, local copies, waits for them, and re-layouts: 7.07 us -> none  [local_slots(): ranked = jnp.take_along_axis(before, chosen, axis=1)]
    unnamed x25, local copies, waits for them, and re-layouts: 3.83 us -> 9.5 us
  transfers between devices with their start and end apart: 5 -> 8, of which waited for: 4 -> 6; matrix products, arithmetic and copies ran while one was open for 4% -> 4% of each run, Pallas kernels for 0% -> 2%
where the time goes in v1:
time: 385 us; the launch traced here: 384 us
  waiting for transfers between devices  221 us (57%)
  blocking collectives  70.9 us (18%)
  starting transfers between devices  32.3 us (8%)
  local copies, waits for them, and re-layouts  15.9 us (4%)
  matrix products  15 us (4%)
  between operations  14 us (4%)
  Pallas kernels  11.1 us (3%)
  other arithmetic  4.58 us (1%)
    all_gather x2, waiting for transfers between devices, shards(): lax.all_gather(tokens[0, :, start:start + width], 'z', axis=0, tiled=True)  112 us
    reduce_scatter x2, waiting for transfers between devices, shards(): lax.psum_scatter(sums, 'z', scatter_dimension=0, tiled=True)  85.8 us
    all_to_all x1, blocking collectives, shards(): lax.all_to_all(terms, 'dp', 0, 0, tiled=True).astype(jnp.float32)  41.4 us
    all_to_all x2, blocking collectives, shards(): lax.all_to_all(grad_rows.reshape(N_Y, row_slots, width), 'y', 0, 0, tiled...  29.5 us
    all_to_all x1, starting transfers between devices, shards(): lax.all_to_all(told.reshape(experts, 8, block), ('y', 'z'), 0, 0, tiled=T...  18.7 us
    all_to_all x1, waiting for transfers between devices, shards(): lax.all_to_all(told.reshape(experts, 8, block), ('y', 'z'), 0, 0, tiled=T...  16.7 us
    pallas_call x5, Pallas kernels, call(): pl.pallas_call(kernel, out_shape=out_shape, in_specs=[whole] * len(operan...  11.1 us
    unnamed x25, local copies, waits for them, and re-layouts  9.5 us
  transfers between devices with their start and end apart: 8, of which 6 were waited for; matrix products, arithmetic and copies ran while one was open for 4% of the time, Pallas kernels for 2%

profile of v1, /device:TPU:6, one launch (start us, length us, event | category | flops | bytes accessed | tf_op | source)
XLA Modules:
  0.0 384.4 jit_solution(14285594287090431841)
XLA Ops:
  7.2 0.0 copy-start.5
  7.2 0.0 copy-start.4
  7.2 0.0 copy-start.10
  7.2 0.0 copy-start.11
  7.2 0.0 all-gather.5.cloned.1.call-start
  7.3 2.0 fusion.11
  9.2 0.0 all-gather.5.cloned.1.call-update
  9.2 0.0 all-gather.7.cloned.1.call-start
  9.3 0.7 all-gather.7.cloned.1.call-update
  10.0 0.0 copy-done.5
  10.0 0.0 copy-done.4
  10.0 1.2 shard_map.93
  11.2 18.7 %all-to-all-start = ((bf16[64,8,128]{2,1,0:T(8,128)(2,1)}), bf16[64,8,128]{2,1,0:T(8,128)(2,1)S(1)}, u32[]{:S(2)}, u32[]{:S(2)}) async-start(bf16[64,8,128]{2,1,0:T(8,128)(2,1)} %bitcast.4), calls=%async_computation | async-start | bytes 262144 | tf_op jit(solution)/shard_map/all_to_all | solution.py:110
  29.9 0.0 copy-done.10
  29.9 0.0 copy-done.11
  30.0 16.7 %all-to-all-done = bf16[64,8,128]{2,1,0:T(8,128)(2,1)S(1)} async-done(((bf16[64,8,128]{2,1,0:T(8,128)(2,1)}), bf16[64,8,128]{2,1,0:T(8,128)(2,1)S(1)}, u32[]{:S(2)}, u32[]{:S(2)}) %all-to-all-start) | async-done | bytes 131104 | tf_op jit(solution)/shard_map/all_to_all | solution.py:110
  46.7 1.9 broadcast_in_dim.45
  48.6 4.8 %all-to-all-start.2 = ((bf16[8,256,768]{2,1,0:T(8,128)(2,1)}), bf16[8,256,768]{2,1,0:T(8,128)(2,1)S(1)}, u32[]{:S(2)}, u32[]{:S(2)}) async-start(bf16[8,256,768]{2,1,0:T(8,128)(2,1)} %broadcast_in_dim.45), calls=%async_computation.2 | async-start | bytes 6291456 | tf_op jit(solution)/shard_map/all_to_all | solution.py:122
  53.4 0.1 fusion.9.slot_ref
  53.5 43.3 %all-gather.5.cloned.1.call-done = bf16[1,2048,1024]{2,1,0:T(8,128)(2,1)} async-done(((bf16[1,128,1024]{2,1,0:T(8,128)(2,1)}), bf16[1,2048,1024]{2,1,0:T(8,128)(2,1)}) %all-gather.5.cloned.1.call-update) | async-done | bytes 4194320 | tf_op jit(solution)/shard_map/all_gather | solution.py:100
  96.8 2.2 copy-done.3
  99.0 2.6 shard_map.94
  101.6 0.0 all-to-all-done.2
  101.6 4.3 %all-to-all-start.1 = ((bf16[4,160,1024]{2,1,0:T(8,128)(2,1)}), bf16[4,160,1024]{2,1,0:T(8,128)(2,1)}, u32[]{:S(2)}, u32[]{:S(2)}) async-start(bf16[4,160,1024]{2,1,0:T(8,128)(2,1)} %shard_map.94), calls=%async_computation.1 | async-start | bytes 2621440 | tf_op jit(solution)/shard_map/all_to_all | solution.py:135
  105.9 0.1 fusion.12
  106.0 68.5 %all-gather.7.cloned.1.call-done = bf16[1,2048,1024]{2,1,0:T(8,128)(2,1)} async-done(((bf16[1,128,1024]{2,1,0:T(8,128)(2,1)}), bf16[1,2048,1024]{2,1,0:T(8,128)(2,1)}) %all-gather.7.cloned.1.call-update) | async-done | bytes 4194320 | tf_op jit(solution)/shard_map/all_gather | solution.py:100
  174.5 2.2 copy-done.2
  176.7 2.6 shard_map.95
  179.4 0.0 all-to-all-done.1
  179.4 4.3 %all-to-all-start.3 = ((bf16[4,160,1024]{2,1,0:T(8,128)(2,1)}), bf16[4,160,1024]{2,1,0:T(8,128)(2,1)}, u32[]{:S(2)}, u32[]{:S(2)}) async-start(bf16[4,160,1024]{2,1,0:T(8,128)(2,1)} %shard_map.95), calls=%async_computation.3 | async-start | bytes 2621440 | tf_op jit(solution)/shard_map/all_to_all | solution.py:135
  183.7 0.0 reduce-scatter.3.cloned.1.call-start
  183.7 0.2 select_reduce_fusion
  184.0 0.1 copy.14
  184.1 0.1 div.14
  184.2 1.4 fusion.10
  185.6 1.2 copy-done.7
  186.7 3.9 %fusion.13 = f32[640,768]{1,0:T(8,128)} fusion(bf16[640,1024]{1,0:T(8,128)(2,1)} %bitcast.8, bf16[1024,768]{1,0:T(8,128)(2,1)S(1)} %bitcast.56), kind=kOutput, calls=%fused_computation.36 | convolution fusion | flops 1006632960 | bytes 4849664 | tf_op jit(solution)/shard_map/dot_general | solution.py:137
  190.6 5.4 %all-to-all-done.3 = bf16[4,160,1024]{2,1,0:T(8,128)(2,1)} async-done(((bf16[4,160,1024]{2,1,0:T(8,128)(2,1)}), bf16[4,160,1024]{2,1,0:T(8,128)(2,1)}, u32[]{:S(2)}, u32[]{:S(2)}) %all-to-all-start.3) | async-done | bytes 1310752 | tf_op jit(solution)/shard_map/all_to_all | solution.py:135
  196.1 0.0 copy-done.6
  196.1 3.2 convolution_add_fusion
  199.2 0.0 copy-done.9
  199.3 1.4 fusion.3
  200.7 1.2 convolution_convert_fusion.3
  201.9 14.7 %all_to_all.35.grads_ref = bf16[4,160,1024]{2,1,0:T(8,128)(2,1)S(1)} all-to-all(bf16[4,160,1024]{2,1,0:T(8,128)(2,1)S(1)} %bitcast.58), channel_id=1, replica_groups=mesh['dp'=8,'y'=4,'z'=16] {'y'}, dimensions={0} | all-to-all | bytes 2621440 | tf_op jit(solution)/shard_map/all_to_all | solution.py:157
  216.6 2.4 shard_map.96
  219.0 0.0 copy-start
  219.0 1.9 copy-done
  221.0 0.0 reduce-scatter.3.cloned.1.call-update
  221.0 0.0 reduce-scatter.5.cloned.1.call-start
  221.0 1.2 convolution_convert_fusion.2
  222.3 14.7 %all_to_all.36.grads_ref = bf16[4,160,1024]{2,1,0:T(8,128)(2,1)S(1)} all-to-all(bf16[4,160,1024]{2,1,0:T(8,128)(2,1)S(1)} %bitcast.59), channel_id=1, replica_groups=mesh['dp'=8,'y'=4,'z'=16] {'y'}, dimensions={0} | all-to-all | bytes 2621440 | tf_op jit(solution)/shard_map/all_to_all | solution.py:157
  237.0 2.4 shard_map.97
  239.4 0.0 copy-start.1
  239.4 2.0 copy-done.1
  241.4 0.0 reduce-scatter.5.cloned.1.call-update
  241.4 2.8 convolution_convert_fusion.1
  244.2 2.7 convolution_convert_fusion
  246.9 0.2 pad_maximum_fusion
  247.1 41.4 %all_to_all.37 = bf16[8,256,768]{2,1,0:T(8,128)(2,1)S(1)} all-to-all(bf16[8,256,768]{2,1,0:T(8,128)(2,1)S(1)} %bitcast.53), channel_id=1, replica_groups=mesh['dp'=8,'y'=4,'z'=16] {'dp'}, dimensions={0} | all-to-all | bytes 6291456 | tf_op jit(solution)/shard_map/all_to_all | solution.py:173
  288.5 0.4 convert_reduce_fusion
  289.0 0.9 slice_bitcast_fusion
  289.9 5.7 %reduce-scatter.3.cloned.1.call-done = bf16[128,1024]{1,0:T(8,128)(2,1)} async-done(((bf16[2048,1024]{1,0:T(8,128)(2,1)}), bf16[128,1024]{1,0:T(8,128)(2,1)}) %reduce-scatter.3.cloned.1.call-update) | async-done | bytes 262160 | tf_op jit(solution)/shard_map/reduce_scatter | solution.py:164
  295.6 80.1 %reduce-scatter.5.cloned.1.call-done = bf16[128,1024]{1,0:T(8,128)(2,1)} async-done(((bf16[2048,1024]{1,0:T(8,128)(2,1)}), bf16[128,1024]{1,0:T(8,128)(2,1)}) %reduce-scatter.5.cloned.1.call-update) | async-done | bytes 262160 | tf_op jit(solution)/shard_map/reduce_scatter | solution.py:164
  375.7 2.1 fusion.6
  (12 shorter events, 0.1 us)
Async XLA Ops:
  7.2 2.8 copy-start.5
  7.2 2.8 copy-start.4
  7.2 22.7 %copy-start.10 = (bf16[1,256,384]{2,1,0:T(8,128)(2,1)S(1)}, bf16[1,256,384]{2,1,0:T(8,128)(2,1)}, u32[]{:S(2)}) copy-start(bf16[1,256,384]{2,1,0:T(8,128)(2,1)} %param.10) | copy-start | bytes 589828
  7.2 22.7 %copy-start.11 = (bf16[1,256,384]{2,1,0:T(8,128)(2,1)S(1)}, bf16[1,256,384]{2,1,0:T(8,128)(2,1)}, u32[]{:S(2)}) copy-start(bf16[1,256,384]{2,1,0:T(8,128)(2,1)} %param.9) | copy-start | bytes 589828
  7.2 89.6 %all-gather.5.cloned.1.call-start = ((), (), s32[]{:S(2)}) async-start(), calls=%async_computation.11 | async-start | bytes 4456448 | tf_op jit(solution)/shard_map/all_gather | solution.py:100
  9.2 165.3 %all-gather.7.cloned.1.call-start = ((), (), s32[]{:S(2)}) async-start(), calls=%async_computation.12 | async-start | bytes 4456448 | tf_op jit(solution)/shard_map/all_gather | solution.py:100
  11.2 35.5 %all-to-all-start = ((bf16[64,8,128]{2,1,0:T(8,128)(2,1)}), bf16[64,8,128]{2,1,0:T(8,128)(2,1)S(1)}, u32[]{:S(2)}, u32[]{:S(2)}) async-start(bf16[64,8,128]{2,1,0:T(8,128)(2,1)} %bitcast.4), calls=%async_computation | async-start | bytes 262144 | tf_op jit(solution)/shard_map/all_to_all | solution.py:110
  48.6 53.0 %all-to-all-start.2 = ((bf16[8,256,768]{2,1,0:T(8,128)(2,1)}), bf16[8,256,768]{2,1,0:T(8,128)(2,1)S(1)}, u32[]{:S(2)}, u32[]{:S(2)}) async-start(bf16[8,256,768]{2,1,0:T(8,128)(2,1)} %broadcast_in_dim.45), calls=%async_computation.2 | async-start | bytes 6291456 | tf_op jit(solution)/shard_map/all_to_all | solution.py:122
  96.8 2.2 copy-start.3
  101.6 77.8 %all-to-all-start.1 = ((bf16[4,160,1024]{2,1,0:T(8,128)(2,1)}), bf16[4,160,1024]{2,1,0:T(8,128)(2,1)}, u32[]{:S(2)}, u32[]{:S(2)}) async-start(bf16[4,160,1024]{2,1,0:T(8,128)(2,1)} %shard_map.94), calls=%async_computation.1 | async-start | bytes 2621440 | tf_op jit(solution)/shard_map/all_to_all | solution.py:135
  174.5 2.2 copy-start.2
  179.4 16.7 %all-to-all-start.3 = ((bf16[4,160,1024]{2,1,0:T(8,128)(2,1)}), bf16[4,160,1024]{2,1,0:T(8,128)(2,1)}, u32[]{:S(2)}, u32[]{:S(2)}) async-start(bf16[4,160,1024]{2,1,0:T(8,128)(2,1)} %shard_map.95), calls=%async_computation.3 | async-start | bytes 2621440 | tf_op jit(solution)/shard_map/all_to_all | solution.py:135
  183.7 112.0 %reduce-scatter.3.cloned.1.call-start = ((), (), s32[]{:S(2)}) async-start(), calls=%async_computation.9 | async-start | bytes 4456448 | tf_op jit(solution)/shard_map/reduce_scatter | solution.py:164
  185.6 1.2 copy-start.7
  186.7 9.4 %copy-start.6 = (bf16[4,256,768]{2,1,0:T(8,128)(2,1)S(1)}, bf16[4,256,768]{2,1,0:T(8,128)(2,1)}, u32[]{:S(2)}) copy-start(bf16[4,256,768]{2,1,0:T(8,128)(2,1)} %get-tuple-element.4) | copy-start | bytes 4718596
  196.1 3.2 copy-start.9
  199.3 1.4 copy-start.8
  219.0 1.9 copy-start
  221.0 154.8 %reduce-scatter.5.cloned.1.call-start = ((), (), s32[]{:S(2)}) async-start(), calls=%async_computation.10 | async-start | bytes 4456448 | tf_op jit(solution)/shard_map/reduce_scatter | solution.py:164
  239.4 2.0 copy-start.1
Sparse Core Ops, SparseCore 0:
  10.7 86.0 all-gather.4
  99.5 75.0 all-gather.6
  221.1 74.4 reduce-scatter.2
  298.3 77.3 reduce-scatter.4

commit v2 on v0

v2 whole, which is shorter than its diff:
```python
import functools

import jax
import jax.numpy as jnp
import numpy as np
from jax import lax
from jax.experimental import pallas as pl
from jax.experimental.pallas import tpu as pltpu
from jax.sharding import Mesh, PartitionSpec as P

N_Y = 4
N_Z = 16
SLOTS = 10
REACH = 5
NEAR = (0, 1, -1, 2, -2, 3, -3, 4, -4, 5, -5)
FAR = (6, 7, 8, -7, -6)
NEAR_ROWS = 112
FAR_ROWS = 56
MESSAGE = (112, 64, 32)
VMEM_BYTES = 48 * 1024 * 1024
F32 = jnp.float32
BF16 = jnp.bfloat16


def call(kernel, out_shape, *operands, scalars=0, scratch=()):
    whole = pl.BlockSpec(memory_space=pltpu.VMEM)
    small = pl.BlockSpec(memory_space=pltpu.SMEM)
    return pl.pallas_call(
        kernel,
        out_shape=out_shape,
        in_specs=[small] * scalars + [whole] * (len(operands) - scalars),
        out_specs=jax.tree.map(lambda _: whole, out_shape),
        scratch_shapes=list(scratch),
        compiler_params=pltpu.CompilerParams(vmem_limit_bytes=VMEM_BYTES),
    )(*operands)


def array(shape, dtype=BF16):
    return jax.ShapeDtypeStruct(shape, dtype)


def iota(shape, dimension):
    return lax.broadcasted_iota(jnp.int32, shape, dimension)


def one_hot(condition):
    return jnp.where(condition, 1.0, 0.0).astype(BF16)


def dot(a, b, contract=(1, 0)):
    return lax.dot_general(a, b, (((contract[0],), (contract[1],)), ((), ())), preferred_element_type=F32)


def earlier_tokens(tokens):
    return one_hot(iota((tokens, tokens), 0) < iota((tokens, tokens), 1))


def routing_kernel(place_ref, heard_ref, source_ref, slot_ref, near_ref, far_ref, weight_ref, hits_ref):
    y, z = place_ref[0], place_ref[1]
    tokens = heard_ref.shape[2]
    top = heard_ref.shape[1] // 2
    triangle = earlier_tokens(tokens)

    hits_ref[...] = jnp.zeros_like(hits_ref)

    def look(row, offset, expert):
        ids = heard_ref[y * N_Z + lax.rem(z + offset + N_Z, N_Z)][:top].astype(jnp.int32)
        hits_ref[row : row + 1, :] = jnp.sum(jnp.where(ids == expert, 1.0, 0.0), axis=0, keepdims=True)

    for index, offset in enumerate(NEAR):
        for other in range(N_Y):
            look(8 * index + other, offset, other * N_Z + z)
    near_count = 8 * len(NEAR)
    for way, sign in enumerate((1, -1)):
        for place in range(SLOTS):
            step, other = place // N_Y, place % N_Y
            if step == 2 and sign < 0:
                other = other + 2
            expert = other * N_Z + lax.rem(z + sign * (step + 1) + N_Z, N_Z)
            look(near_count + 16 * way + place, -sign * REACH, expert)
    hits = hits_ref[...]
    rank = dot(hits.astype(BF16), triangle).astype(jnp.int32)
    row = iota((near_count, tokens), 0)
    base = (row & 7) * NEAR_ROWS + (row >> 3) * SLOTS
    near_ref[...] = jnp.where(hits[:near_count] > 0.0, base + rank[:near_count], -1)
    row = iota((32, tokens), 0) & 15
    far_ref[...] = jnp.where(hits[near_count:] > 0.0, row * SLOTS + rank[near_count:], -1)

    own = y * N_Z + z
    heard = heard_ref[...].astype(F32)
    named = heard[:, :top] == own.astype(F32)
    own_hits = jnp.sum(jnp.where(named, 1.0, 0.0), axis=1)
    own_weight = jnp.sum(jnp.where(named, heard[:, top:], 0.0), axis=1)
    own_rank = dot(own_hits.astype(BF16), triangle)
    rows = source_ref.shape[0]
    spread = one_hot(iota((rows, own_hits.shape[0]), 1) == source_ref[...])
    rank_of = dot(spread, own_rank.astype(BF16))
    weight_of = dot(spread, own_weight.astype(BF16))
    weight = jnp.where(rank_of == slot_ref[...].astype(F32), weight_of, 0.0)
    weight_ref[...] = jnp.sum(weight, axis=1, keepdims=True) * 0.125


def marked(position_ref, first, count, rows):
    row = iota((rows, position_ref.shape[1]), 0)
    mark = position_ref[first : first + 1, :] == row
    for index in range(1, count):
        mark = mark | (position_ref[first + index : first + index + 1, :] == row)
    return one_hot(mark)


def relative_kernel(row_ref, values_ref, out_ref):
    move = one_hot(iota((row_ref.shape[0], values_ref.shape[0]), 1) == row_ref[...])
    out_ref[...] = dot(move, values_ref[...]).astype(BF16)


def absolute_kernel(row_ref, near_ref, far_ref, out_ref):
    move = one_hot(iota((row_ref.shape[0], out_ref.shape[0]), 1) == row_ref[...])
    count = near_ref.shape[0]
    out = dot(move[:count], near_ref[...], (0, 0)) + dot(move[count:], far_ref[...], (0, 0))
    out_ref[...] = out.astype(BF16)


def far_message_kernel(way, far_ref, tokens_ref, out_ref):
    out_ref[...] = dot(marked(far_ref, 16 * way, SLOTS, out_ref.shape[0]), tokens_ref[...]).astype(BF16)


def near_pick_kernel(near_ref, *refs):
    out_ref = refs[-1]
    select = jnp.concatenate([marked(near_ref, 8 * i, N_Y, out_ref.shape[0]) for i in range(len(NEAR))], axis=1)
    tokens = jnp.concatenate([ref[...] for ref in refs[:-1]], axis=0)
    out_ref[...] = dot(select, tokens).astype(BF16)


def far_places():
    places = {}
    for hop in range(3):
        for way in range(2):
            source = FAR.index((REACH + 1 + hop) * (-1 if way == 0 else 1) if hop < 2 else 8)
            place = np.full((N_Y * FAR_ROWS, 1), -1, np.int32)
            for y in range(N_Y):
                if hop == 2 and y // 2 != way:
                    continue
                for slot in range(SLOTS):
                    row = y * SLOTS + slot if hop < 2 else 8 + (y % 2) * SLOTS + slot
                    place[y * FAR_ROWS + source * SLOTS + slot, 0] = row
            places[hop, way] = place
    return places


FAR_KEYS = tuple((hop, way) for hop in range(3) for way in range(2))


def far_pick_kernel(place_ref, *refs):
    out_ref = refs[-1]
    total = None
    for index, ref in enumerate(refs[:-1]):
        move = one_hot(iota((out_ref.shape[0], ref.shape[0]), 1) == place_ref[:, index : index + 1])
        part = dot(move, ref[...])
        total = part if total is None else total + part
    out_ref[...] = total.astype(BF16)


def far_part_kernel(place_ref, grads_ref, *out_refs):
    for index, ref in enumerate(out_refs):
        move = one_hot(iota((grads_ref.shape[0], ref.shape[0]), 1) == place_ref[:, index : index + 1])
        ref[...] = dot(move, grads_ref[...], (0, 0)).astype(BF16)


def expert_kernel(rows_ref, matrix_ref, weight_ref, cotangent_ref, hidden_ref, grad_ref, row_grads_ref):
    units = hidden_ref.shape[1]
    pre = dot(rows_ref[...], matrix_ref[...])
    gate_pre, up_pre = pre[:, :units], pre[:, units:]
    weight = weight_ref[...]
    sigmoid_gate = jax.nn.sigmoid(gate_pre)
    activation = gate_pre * sigmoid_gate
    hidden_ref[...] = (activation * up_pre * weight).astype(BF16)
    act_slope = sigmoid_gate * (1.0 + gate_pre * (1.0 - sigmoid_gate))
    scaled = cotangent_ref[...].astype(F32) * weight
    grad_ref[:, :units] = (scaled * up_pre * act_slope).astype(BF16)
    grad_ref[:, units:] = (scaled * activation).astype(BF16)
    row_grads_ref[...] = dot(grad_ref[...], matrix_ref[...], (1, 1)).astype(BF16)


def near_sum(index, near_ref, grads_ref):
    return dot(marked(near_ref, 8 * index, N_Y, grads_ref.shape[0]), grads_ref[...], (0, 0))


def first_sum_kernel(index, way, near_ref, far_ref, grads_ref, message_ref, out_ref):
    far = dot(marked(far_ref, 16 * way, SLOTS, message_ref.shape[0]), message_ref[...], (0, 0))
    out_ref[...] = (far + near_sum(index, near_ref, grads_ref)).astype(BF16)


def next_sum_kernel(index, near_ref, grads_ref, sum_ref, out_ref):
    out_ref[...] = (sum_ref[...].astype(F32) + near_sum(index, near_ref, grads_ref)).astype(BF16)


def last_sum_kernel(near_ref, grads_ref, up_ref, down_ref, out_ref):
    out_ref[...] = up_ref[...].astype(F32) + down_ref[...].astype(F32) + near_sum(0, near_ref, grads_ref)


def after(value, *others):
    return lax.optimization_barrier((value,) + others)[0]


def shards(tokens, expert_ids, route_weights, gate_weight, up_weight, cotangent):
    slot_count, units = cotangent.shape[2:]
    block, model_width = tokens.shape[1:]
    near_count, far_count = N_Y * NEAR_ROWS, N_Y * FAR_ROWS
    y, z = lax.axis_index("y"), lax.axis_index("z")

    def send(value, sign):
        return lax.ppermute(value, "z", [(i, (i + sign) % N_Z) for i in range(N_Z)])

    told = jnp.concatenate((expert_ids[0].T, route_weights[0].T), axis=0).astype(BF16)
    heard = lax.all_gather(told, ("y", "z"), axis=0)
    stacked = jnp.concatenate((gate_weight[0], up_weight[0]), axis=1)
    matrix = lax.all_gather(stacked, "dp", axis=0, tiled=True)

    group, offset, slot = np.full((3, near_count + far_count), -1, np.int32)
    for first, rows, sources in ((0, NEAR_ROWS, NEAR), (near_count, FAR_ROWS, FAR)):
        for other in range(N_Y):
            for index, source in enumerate(sources):
                at = first + other * rows + index * SLOTS
                group[at : at + SLOTS], offset[at : at + SLOTS] = other, source
                slot[at : at + SLOTS] = np.arange(SLOTS)
    source_of = jnp.where(group >= 0, group * N_Z + (z + offset + N_Z) % N_Z, -1).astype(jnp.int32)
    row_of = jnp.where(group >= 0, source_of * SLOTS + slot, -1).astype(jnp.int32)[:, None]
    near, far, weight = call(
        routing_kernel,
        (
            array((8 * len(NEAR), block), jnp.int32),
            array((32, block), jnp.int32),
            array((near_count + far_count, 1), F32),
        ),
        jnp.stack((y, z)).astype(jnp.int32),
        heard,
        source_of[:, None],
        jnp.asarray(slot)[:, None],
        scalars=1,
        scratch=(pltpu.VMEM((8 * len(NEAR) + 32, block), F32),),
    )
    cotangent_rows = call(
        relative_kernel, array((near_count + far_count, units)), row_of, cotangent[0, 0]
    )

    blocks = {0: tokens[0]}
    going = [tokens[0], tokens[0]]
    for hop in range(1, REACH + 1):
        going = [send(going[0], 1), send(going[1], -1)]
        blocks[-hop], blocks[hop] = going
    arrived = []
    going = [
        call(functools.partial(far_message_kernel, way), array((MESSAGE[0], model_width)), far, going[way])
        for way in range(2)
    ]
    for hop in range(3):
        going = [send(going[0], 1), send(going[1], -1)]
        arrived += going
        if hop == 0:
            going = [part[40:104] for part in going]
        elif hop == 1:
            going = [part[32:] for part in going]

    def exchange(rows):
        parts = rows.reshape(N_Y, rows.shape[0] // N_Y, model_width)
        return lax.all_to_all(parts, "y", 0, 0, tiled=True).reshape(rows.shape)

    near_rows = exchange(
        call(near_pick_kernel, array((near_count, model_width)), near, *[blocks[source] for source in NEAR])
    )
    places = far_places()
    place_of = jnp.asarray(np.concatenate([places[key] for key in FAR_KEYS], axis=1))
    far_rows = exchange(call(far_pick_kernel, array((far_count, model_width)), place_of, *arrived))

    def expert(rows, first):
        count = rows.shape[0]
        part = slice(first, first + count)
        return call(
            expert_kernel,
            (array((count, units)), array((count, 2 * units)), array((count, model_width))),
            rows,
            matrix,
            weight[part],
            cotangent_rows[part],
        )

    near_hidden, near_grads, near_back = expert(near_rows, 0)
    far_hidden, far_grads, far_back = expert(far_rows, near_count)

    far_back = exchange(far_back)
    near_back = exchange(after(near_back, far_back))
    parts = call(
        far_part_kernel,
        tuple(array((48 if hop < 2 else MESSAGE[2], model_width)) for hop, _ in FAR_KEYS),
        place_of,
        far_back,
    )
    going = list(parts[4:])
    for hop in (2, 1, 0):
        going = [send(going[0], -1), send(going[1], 1)]
        if hop == 2:
            going = [jnp.concatenate((parts[2 + way][:40], going[way][8:]), axis=0) for way in range(2)]
        elif hop == 1:
            blank = jnp.zeros((8, model_width), BF16)
            going = [jnp.concatenate((parts[way][:40], going[way], blank), axis=0) for way in range(2)]
    going = [
        call(
            functools.partial(first_sum_kernel, NEAR.index(REACH * (-1 if way == 0 else 1)), way),
            array((block, model_width)),
            near,
            far,
            near_back,
            going[way],
        )
        for way in range(2)
    ]
    for hop in range(REACH - 1, -1, -1):
        going = [send(going[0], -1), send(going[1], 1)]
        if hop:
            going = [
                call(
                    functools.partial(next_sum_kernel, NEAR.index(hop * (-1 if way == 0 else 1))),
                    array((block, model_width)),
                    near,
                    near_back,
                    going[way],
                )
                for way in range(2)
            ]
    token_grads = call(last_sum_kernel, array((block, model_width), F32), near, near_back, *going)

    far_rows, near_rows = after(far_rows, far_back), after(near_rows, far_back)
    terms = (dot(near_rows, near_grads, (0, 0)) + dot(far_rows, far_grads, (0, 0))).astype(BF16)
    weight_grads = lax.psum_scatter(terms, "dp", scatter_dimension=0, tiled=True).astype(F32)
    hidden = call(
        absolute_kernel,
        array((slot_count, units)),
        row_of,
        after(near_hidden, far_back),
        far_hidden,
    )
    return (
        hidden[None, None],
        token_grads[None],
        weight_grads[None, :, :units],
        weight_grads[None, :, units:],
    )


def solution(mesh):
    grid = Mesh(mesh.devices.reshape(mesh.shape["dp"], N_Y, N_Z), ("dp", "y", "z"))
    expert = ("y", "z")
    in_specs = (
        P("dp", expert, None),
        P("dp", expert, None),
        P("dp", expert, None),
        P(expert, "dp", None),
        P(expert, "dp", None),
        P("dp", expert, None, None),
    )
    out_specs = (
        P("dp", expert, None, None),
        P("dp", expert, None),
        P(expert, "dp", None),
        P(expert, "dp", None),
    )
    return jax.shard_map(shards, mesh=grid, in_specs=in_specs, out_specs=out_specs, check_vma=False)
```

time: 469 us -> 407 us (0.87)
  waiting for transfers between devices: 373 us -> 94.8 us
  starting transfers between devices: 32.4 us -> 141 us
  blocking collectives: 0 us -> 82.8 us
  Pallas kernels: 0 us -> 30.5 us
  matrix products: 17.2 us -> 5.66 us
    all_to_all x3 -> x4, waiting for transfers between devices: 334 us -> 8.47 us  [exchange(): return lax.all_to_all(parts, 'y', 0, 0, tiled=True).reshape(rows.shape)]
    ppermute x0 -> x32, starting transfers between devices: none -> 124 us  [send(): return lax.ppermute(value, 'z', [(i, (i + sign) % N_Z) for i in range(N_Z)])]
    ppermute x0 -> x32, waiting for transfers between devices: none -> 86.3 us  [send(): return lax.ppermute(value, 'z', [(i, (i + sign) % N_Z) for i in range(N_Z)])]
    all_gather x0 -> x1, blocking collectives: none -> 82.8 us  [shards(): heard = lax.all_gather(told, ('y', 'z'), axis=0)]
    reduce_scatter x1, waiting for transfers between devices: 39.8 us -> 0.01 us  [shards(): lax.psum_scatter(terms, 'dp', scatter_dimension=0, tiled=True).astype(F32)]
    pallas_call x0 -> x21, Pallas kernels: none -> 30.5 us  [call(): pl.pallas_call(kernel, out_shape=out_shape, in_specs=[small] * scalars +...]
    unnamed x25 -> x70, local copies, waits for them, and re-layouts: 3.83 us -> 23.2 us
    all_to_all x3 -> x4, starting transfers between devices: 32.1 us -> 16.4 us  [exchange(): return lax.all_to_all(parts, 'y', 0, 0, tiled=True).reshape(rows.shape)]
  transfers between devices with their start and end apart: 5 -> 38, of which waited for: 4 -> 21; matrix products, arithmetic and copies ran while one was open for 4% -> 2% of each run, Pallas kernels for 0% -> 8%
where the time goes in v2:
time: 407 us; the launch traced here: 404 us
  starting transfers between devices  141 us (35%)
  waiting for transfers between devices  94.8 us (23%)
  blocking collectives  82.8 us (20%)
  Pallas kernels  30.5 us (7%)
  local copies, waits for them, and re-layouts  28.4 us (7%)
  between operations  14.8 us (4%)
  matrix products  5.66 us (1%)
  other arithmetic  5.48 us (1%)
    ppermute x32, starting transfers between devices, send(): return lax.ppermute(value, 'z', [(i, (i + sign) % N_Z) for i in range(N_Z)])  124 us
    ppermute x32, waiting for transfers between devices, send(): return lax.ppermute(value, 'z', [(i, (i + sign) % N_Z) for i in range(N_Z)])  86.3 us
    all_gather x1, blocking collectives, shards(): heard = lax.all_gather(told, ('y', 'z'), axis=0)  82.8 us
    pallas_call x21, Pallas kernels, call(): pl.pallas_call(kernel, out_shape=out_shape, in_specs=[small] * scalars +...  30.5 us
    unnamed x70, local copies, waits for them, and re-layouts  23.2 us
    all_to_all x4, starting transfers between devices, exchange(): return lax.all_to_all(parts, 'y', 0, 0, tiled=True).reshape(rows.shape)  16.4 us
    all_to_all x4, waiting for transfers between devices, exchange(): return lax.all_to_all(parts, 'y', 0, 0, tiled=True).reshape(rows.shape)  8.47 us
  transfers between devices with their start and end apart: 38, of which 21 were waited for; matrix products, arithmetic and copies ran while one was open for 2% of the time, Pallas kernels for 8%

profile of v2, /device:TPU:6, one launch (start us, length us, event | category | flops | bytes accessed | tf_op | source)
XLA Modules:
  0.0 403.5 jit_solution(4984514017399711865)
XLA Ops:
  7.2 3.8 collective-permute-start.1
  11.0 9.5 %collective-permute-start = (bf16[128,2048]{1,0:T(8,128)(2,1)}, bf16[128,2048]{1,0:T(8,128)(2,1)S(1)}, u32[]{:S(2)}, u32[]{:S(2)}) collective-permute-start(bf16[128,2048]{1,0:T(8,128)(2,1)} %bitcast.54), channel_id=1, source_target_pairs={{0,15},{1,0},{2,1},{3,2},{4,3},{5,4},{6,5},{7,6},{8,7},{9,8},{10,9... | collective-permute-start | bytes 1572872 | tf_op jit(solution)/shard_map/ppermute | solution.py:212
  22.4 8.3 %collective-permute-done.1.refs_2_ = bf16[128,2048]{1,0:T(8,128)(2,1)S(1)} collective-permute-done((bf16[128,2048]{1,0:T(8,128)(2,1)}, bf16[128,2048]{1,0:T(8,128)(2,1)S(1)}, u32[]{:S(2)}, u32[]{:S(2)}) %collective-permute-start.1) | collective-permute-done | bytes 524320 | tf_op jit(solution)/shard_map/ppermute | solution.py:212
  30.7 1.9 collective-permute-start.3
  32.7 5.1 %collective-permute-start.2 = (bf16[128,2048]{1,0:T(8,128)(2,1)S(1)}, bf16[128,2048]{1,0:T(8,128)(2,1)S(1)}, u32[]{:S(2)}, u32[]{:S(2)}) collective-permute-start(bf16[128,2048]{1,0:T(8,128)(2,1)S(1)} %collective-permute-done.refs_1_), channel_id=1, source_target_pairs={{0,15},{1,0},{2,1},{3,2},{4,3},{5,4},{6,5},{7,6},{8,7},{9,8},{10,9... | collective-permute-start | bytes 1572872 | tf_op jit(solution)/shard_map/ppermute | solution.py:212
  38.6 8.3 %collective-permute-done.3.refs_4_ = bf16[128,2048]{1,0:T(8,128)(2,1)S(1)} collective-permute-done((bf16[128,2048]{1,0:T(8,128)(2,1)S(1)}, bf16[128,2048]{1,0:T(8,128)(2,1)S(1)}, u32[]{:S(2)}, u32[]{:S(2)}) %collective-permute-start.3) | collective-permute-done | bytes 524320 | tf_op jit(solution)/shard_map/ppermute | solution.py:212
  46.9 1.9 collective-permute-start.5
  49.7 5.1 %collective-permute-start.4 = (bf16[128,2048]{1,0:T(8,128)(2,1)S(1)}, bf16[128,2048]{1,0:T(8,128)(2,1)S(1)}, u32[]{:S(2)}, u32[]{:S(2)}) collective-permute-start(bf16[128,2048]{1,0:T(8,128)(2,1)S(1)} %collective-permute-done.2.refs_3_), channel_id=1, source_target_pairs={{0,15},{1,0},{2,1},{3,2},{4,3},{5,4},{6,5},{7,6},{8,7},{9,8},{10,9... | collective-permute-start | bytes 1572872 | tf_op jit(solution)/shard_map/ppermute | solution.py:212
  55.6 6.6 %collective-permute-done.5.refs_6_ = bf16[128,2048]{1,0:T(8,128)(2,1)S(1)} collective-permute-done((bf16[128,2048]{1,0:T(8,128)(2,1)S(1)}, bf16[128,2048]{1,0:T(8,128)(2,1)S(1)}, u32[]{:S(2)}, u32[]{:S(2)}) %collective-permute-start.5) | collective-permute-done | bytes 524320 | tf_op jit(solution)/shard_map/ppermute | solution.py:212
  62.2 1.9 collective-permute-start.7
  64.9 5.1 %collective-permute-start.6 = (bf16[128,2048]{1,0:T(8,128)(2,1)S(1)}, bf16[128,2048]{1,0:T(8,128)(2,1)S(1)}, u32[]{:S(2)}, u32[]{:S(2)}) collective-permute-start(bf16[128,2048]{1,0:T(8,128)(2,1)S(1)} %collective-permute-done.4.refs_5_), channel_id=1, source_target_pairs={{0,15},{1,0},{2,1},{3,2},{4,3},{5,4},{6,5},{7,6},{8,7},{9,8},{10,9... | collective-permute-start | bytes 1572872 | tf_op jit(solution)/shard_map/ppermute | solution.py:212
  70.9 5.7 %collective-permute-done.7.refs_8_ = bf16[128,2048]{1,0:T(8,128)(2,1)S(1)} collective-permute-done((bf16[128,2048]{1,0:T(8,128)(2,1)S(1)}, bf16[128,2048]{1,0:T(8,128)(2,1)S(1)}, u32[]{:S(2)}, u32[]{:S(2)}) %collective-permute-start.7) | collective-permute-done | bytes 524320 | tf_op jit(solution)/shard_map/ppermute | solution.py:212
  76.6 1.9 collective-permute-start.9
  78.6 5.6 %collective-permute-start.8 = (bf16[128,2048]{1,0:T(8,128)(2,1)S(1)}, bf16[128,2048]{1,0:T(8,128)(2,1)S(1)}, u32[]{:S(2)}, u32[]{:S(2)}) collective-permute-start(bf16[128,2048]{1,0:T(8,128)(2,1)S(1)} %collective-permute-done.6.refs_7_), channel_id=1, source_target_pairs={{0,15},{1,0},{2,1},{3,2},{4,3},{5,4},{6,5},{7,6},{8,7},{9,8},{10,9... | collective-permute-start | bytes 1572872 | tf_op jit(solution)/shard_map/ppermute | solution.py:212
  85.8 82.8 %all_gather.7.heard_ref = bf16[64,16,128]{2,1,0:T(8,128)(2,1)S(1)} all-gather(bf16[1,16,128]{2,1,0:T(8,128)(2,1)S(1)} %pad_maximum_fusion.3), channel_id=1, replica_groups=mesh['dp'=8,'y'=4,'z'=16] {'y','z'}, dimensions={0}, use_global_device_ids=true | all-gather | bytes 266240 | tf_op jit(solution)/shard_map/all_gather | solution.py:215
  171.2 1.9 collective-permute-start.10
  173.5 5.3 %collective-permute-start.11 = (bf16[112,2048]{1,0:T(8,128)(2,1)S(1)}, bf16[112,2048]{1,0:T(8,128)(2,1)S(1)}, u32[]{:S(2)}, u32[]{:S(2)}) collective-permute-start(bf16[112,2048]{1,0:T(8,128)(2,1)S(1)} %shard_map.152), channel_id=1, source_target_pairs={{0,15},{1,0},{2,1},{3,2},{4,3},{5,4},{6,5},{7,6},{8,7},{9,8},{10,9... | collective-permute-start | bytes 1376264 | tf_op jit(solution)/shard_map/ppermute | solution.py:212
  178.7 4.0 collective-permute-done.10.refs_0_
  182.8 1.9 collective-permute-start.12
  184.7 5.6 %collective-permute-start.13 = (bf16[64,2048]{1,0:T(8,128)(2,1)S(1)}, bf16[64,2048]{1,0:T(8,128)(2,1)S(1)}, u32[]{:S(2)}, u32[]{:S(2)}) collective-permute-start(bf16[64,2048]{1,0:T(8,128)(2,1)S(1)} %slice.66), channel_id=1, source_target_pairs={{0,15},{1,0},{2,1},{3,2},{4,3},{5,4},{6,5},{7,6},{8,7},{9,8},{10,9... | collective-permute-start | bytes 786440 | tf_op jit(solution)/shard_map/ppermute | solution.py:212
  190.3 1.9 collective-permute-done.12.refs_2_
  192.3 1.9 collective-permute-start.14
  194.2 5.6 %collective-permute-start.15 = (bf16[32,2048]{1,0:T(8,128)(2,1)S(1)}, bf16[32,2048]{1,0:T(8,128)(2,1)S(1)}, u32[]{:S(2)}, u32[]{:S(2)}) collective-permute-start(bf16[32,2048]{1,0:T(8,128)(2,1)S(1)} %slice.68), channel_id=1, source_target_pairs={{0,15},{1,0},{2,1},{3,2},{4,3},{5,4},{6,5},{7,6},{8,7},{9,8},{10,9... | collective-permute-start | bytes 393224 | tf_op jit(solution)/shard_map/ppermute | solution.py:212
  200.3 2.0 collective-permute-done.15.refs_5_
  202.3 2.6 shard_map.153
  204.9 3.8 all-to-all-start.1
  217.0 4.7 %shard_map.148 = bf16[448,2048]{1,0:T(8,128)(2,1)} custom-call(s32[88,128]{1,0:T(8,128)S(1)} %get-tuple-element.23.near_ref, bf16[128,2048]{1,0:T(8,128)(2,1)S(1)} %bitcast.55, bf16[128,2048]{1,0:T(8,128)(2,1)S(1)} %copy-done.7, bf16[128,2048]{1,0:T(8,128)(2,1)S(1)} %copy-done.5, bf16[128,2048]{1,0:T(8,128)(2,1)S(1)} %copy-done.11, ...), custom_call_target="tpu_custom_call" | custom-call | tf_op jit(solution)/shard_map/pallas_call | solution.py:28
  221.7 4.8 %all-to-all-start = ((bf16[4,112,2048]{2,1,0:T(8,128)(2,1)}), bf16[4,112,2048]{2,1,0:T(8,128)(2,1)S(1)}, u32[]{:S(2)}, u32[]{:S(2)}) async-start(bf16[4,112,2048]{2,1,0:T(8,128)(2,1)} %bitcast.57), calls=%async_computation | async-start | bytes 3670016 | tf_op jit(solution)/shard_map/all_to_all | solution.py:266
  231.2 1.9 copy-done
  233.0 2.3 shard_map.154
  237.7 3.9 all-to-all-done
  241.6 4.2 %all-to-all-start.2 = ((bf16[4,56,2048]{2,1,0:T(8,128)(2,1)}), bf16[4,56,2048]{2,1,0:T(8,128)(2,1)}, u32[]{:S(2)}, u32[]{:S(2)}) async-start(bf16[4,56,2048]{2,1,0:T(8,128)(2,1)} %bitcast.52), calls=%async_computation.2 | async-start | bytes 1835008 | tf_op jit(solution)/shard_map/all_to_all | solution.py:266
  248.0 5.6 %shard_map.150 = (bf16[448,384]{1,0:T(8,128)(2,1)S(1)}, bf16[448,768]{1,0:T(8,128)(2,1)S(1)}, bf16[448,2048]{1,0:T(8,128)(2,1)S(1)}) custom-call(bf16[448,2048]{1,0:T(8,128)(2,1)S(1)} %bitcast.49, bf16[2048,768]{1,0:T(8,128)(2,1)} %all-gather.2.cloned.1.call-done.matrix_ref, f32[448,1]{1,0:T(8,128)S(1)} %slice.48.weight_ref, ...), custom_call_target="tpu_custom_call" | custom-call | tf_op jit(solution)/shard_map/pallas_call | solution.py:28
  256.5 4.5 %all-to-all-done.2 = bf16[4,56,2048]{2,1,0:T(8,128)(2,1)} async-done(((bf16[4,56,2048]{2,1,0:T(8,128)(2,1)}), bf16[4,56,2048]{2,1,0:T(8,128)(2,1)}, u32[]{:S(2)}, u32[]{:S(2)}) %all-to-all-start.2) | async-done | bytes 917536 | tf_op jit(solution)/shard_map/all_to_all | solution.py:266
  261.1 3.0 fusion.3
  264.1 2.7 add_convert_fusion
  266.8 2.4 shard_map.156
  269.2 1.9 collective-permute-start.24
  271.1 3.6 all-to-all-start.3
  274.7 5.6 %collective-permute-start.16 = (bf16[32,2048]{1,0:T(8,128)(2,1)S(1)}, bf16[32,2048]{1,0:T(8,128)(2,1)S(1)}, u32[]{:S(2)}, u32[]{:S(2)}) collective-permute-start(bf16[32,2048]{1,0:T(8,128)(2,1)S(1)} %get-tuple-element.34), channel_id=1, source_target_pairs={{0,15},{1,0},{2,1},{3,2},{4,3},{5,4},{6,5},{7,6},{8,7},{9,8},{10,9... | collective-permute-start | bytes 393224 | tf_op jit(solution)/shard_map/ppermute | solution.py:212
  280.4 1.9 collective-permute-start.25
  282.3 1.9 collective-permute-done.16
  284.2 5.6 %collective-permute-start.17 = (bf16[64,2048]{1,0:T(8,128)(2,1)S(1)}, bf16[64,2048]{1,0:T(8,128)(2,1)S(1)}, u32[]{:S(2)}, u32[]{:S(2)}) collective-permute-start(bf16[64,2048]{1,0:T(8,128)(2,1)S(1)} %pad_maximum_fusion.1), channel_id=1, source_target_pairs={{0,15},{1,0},{2,1},{3,2},{4,3},{5,4},{6,5},{7,6},{8,7},{9,8},{10,9... | collective-permute-start | bytes 786440 | tf_op jit(solution)/shard_map/ppermute | solution.py:212
  290.0 2.7 collective-permute-done.25
  292.7 3.5 collective-permute-done.17
  297.2 5.6 %collective-permute-start.18 = (bf16[112,2048]{1,0:T(8,128)(2,1)S(1)}, bf16[112,2048]{1,0:T(8,128)(2,1)S(1)}, u32[]{:S(2)}, u32[]{:S(2)}) collective-permute-start(bf16[112,2048]{1,0:T(8,128)(2,1)S(1)} %get-tuple-element.47), channel_id=1, source_target_pairs={{0,15},{1,0},{2,1},{3,2},{4,3},{5,4},{6,5},{7,6},{8,7},{9,8},{10,9... | collective-permute-start | bytes 1376264 | tf_op jit(solution)/shard_map/ppermute | solution.py:212
  302.8 1.9 collective-permute-start.26
  304.7 7.4 %collective-permute-done.18.message_ref = bf16[112,2048]{1,0:T(8,128)(2,1)S(1)} collective-permute-done((bf16[112,2048]{1,0:T(8,128)(2,1)S(1)}, bf16[112,2048]{1,0:T(8,128)(2,1)S(1)}, u32[]{:S(2)}, u32[]{:S(2)}) %collective-permute-start.18) | collective-permute-done | bytes 458784 | tf_op jit(solution)/shard_map/ppermute | solution.py:212
  314.6 5.6 %collective-permute-start.19 = (bf16[128,2048]{1,0:T(8,128)(2,1)S(1)}, bf16[128,2048]{1,0:T(8,128)(2,1)S(1)}, u32[]{:S(2)}, u32[]{:S(2)}) collective-permute-start(bf16[128,2048]{1,0:T(8,128)(2,1)S(1)} %shard_map.157), channel_id=1, source_target_pairs={{0,15},{1,0},{2,1},{3,2},{4,3},{5,4},{6,5},{7,6},{8,7},{9,8},{10,9... | collective-permute-start | bytes 1572872 | tf_op jit(solution)/shard_map/ppermute | solution.py:212
  321.9 1.9 collective-permute-start.27
  323.8 7.9 %collective-permute-done.19.sum_ref = bf16[128,2048]{1,0:T(8,128)(2,1)S(1)} collective-permute-done((bf16[128,2048]{1,0:T(8,128)(2,1)S(1)}, bf16[128,2048]{1,0:T(8,128)(2,1)S(1)}, u32[]{:S(2)}, u32[]{:S(2)}) %collective-permute-start.19) | collective-permute-done | bytes 524320 | tf_op jit(solution)/shard_map/ppermute | solution.py:212
  332.2 5.6 %collective-permute-start.20 = (bf16[128,2048]{1,0:T(8,128)(2,1)S(1)}, bf16[128,2048]{1,0:T(8,128)(2,1)S(1)}, u32[]{:S(2)}, u32[]{:S(2)}) collective-permute-start(bf16[128,2048]{1,0:T(8,128)(2,1)S(1)} %shard_map.158), channel_id=1, source_target_pairs={{0,15},{1,0},{2,1},{3,2},{4,3},{5,4},{6,5},{7,6},{8,7},{9,8},{10,9... | collective-permute-start | bytes 1572872 | tf_op jit(solution)/shard_map/ppermute | solution.py:212
  338.4 1.9 collective-permute-start.28
  340.3 8.2 %collective-permute-done.20.sum_ref = bf16[128,2048]{1,0:T(8,128)(2,1)S(1)} collective-permute-done((bf16[128,2048]{1,0:T(8,128)(2,1)S(1)}, bf16[128,2048]{1,0:T(8,128)(2,1)S(1)}, u32[]{:S(2)}, u32[]{:S(2)}) %collective-permute-start.20) | collective-permute-done | bytes 524320 | tf_op jit(solution)/shard_map/ppermute | solution.py:212
  349.0 5.6 %collective-permute-start.21 = (bf16[128,2048]{1,0:T(8,128)(2,1)S(1)}, bf16[128,2048]{1,0:T(8,128)(2,1)S(1)}, u32[]{:S(2)}, u32[]{:S(2)}) collective-permute-start(bf16[128,2048]{1,0:T(8,128)(2,1)S(1)} %shard_map.159), channel_id=1, source_target_pairs={{0,15},{1,0},{2,1},{3,2},{4,3},{5,4},{6,5},{7,6},{8,7},{9,8},{10,9... | collective-permute-start | bytes 1572872 | tf_op jit(solution)/shard_map/ppermute | solution.py:212
  355.1 1.9 collective-permute-start.29
  357.1 4.2 %collective-permute-done.21.sum_ref = bf16[128,2048]{1,0:T(8,128)(2,1)S(1)} collective-permute-done((bf16[128,2048]{1,0:T(8,128)(2,1)S(1)}, bf16[128,2048]{1,0:T(8,128)(2,1)S(1)}, u32[]{:S(2)}, u32[]{:S(2)}) %collective-permute-start.21) | collective-permute-done | bytes 524320 | tf_op jit(solution)/shard_map/ppermute | solution.py:212
  361.8 5.6 %collective-permute-start.22 = (bf16[128,2048]{1,0:T(8,128)(2,1)S(1)}, bf16[128,2048]{1,0:T(8,128)(2,1)S(1)}, u32[]{:S(2)}, u32[]{:S(2)}) collective-permute-start(bf16[128,2048]{1,0:T(8,128)(2,1)S(1)} %shard_map.160), channel_id=1, source_target_pairs={{0,15},{1,0},{2,1},{3,2},{4,3},{5,4},{6,5},{7,6},{8,7},{9,8},{10,9... | collective-permute-start | bytes 1572872 | tf_op jit(solution)/shard_map/ppermute | solution.py:212
  368.0 2.1 collective-permute-start.30
  370.0 4.1 %collective-permute-done.22.sum_ref = bf16[128,2048]{1,0:T(8,128)(2,1)S(1)} collective-permute-done((bf16[128,2048]{1,0:T(8,128)(2,1)S(1)}, bf16[128,2048]{1,0:T(8,128)(2,1)S(1)}, u32[]{:S(2)}, u32[]{:S(2)}) %collective-permute-start.22) | collective-permute-done | bytes 524320 | tf_op jit(solution)/shard_map/ppermute | solution.py:212
  374.6 5.6 %collective-permute-start.23 = (bf16[128,2048]{1,0:T(8,128)(2,1)S(1)}, bf16[128,2048]{1,0:T(8,128)(2,1)S(1)}, u32[]{:S(2)}, u32[]{:S(2)}) collective-permute-start(bf16[128,2048]{1,0:T(8,128)(2,1)S(1)} %shard_map.161), channel_id=1, source_target_pairs={{0,15},{1,0},{2,1},{3,2},{4,3},{5,4},{6,5},{7,6},{8,7},{9,8},{10,9... | collective-permute-start | bytes 1572872 | tf_op jit(solution)/shard_map/ppermute | solution.py:212
  380.9 1.9 collective-permute-start.31
  384.4 2.4 collective-permute-done.23.up_ref
  386.9 6.3 %collective-permute-done.31.down_ref = bf16[128,2048]{1,0:T(8,128)(2,1)S(1)} collective-permute-done((bf16[128,2048]{1,0:T(8,128)(2,1)S(1)}, bf16[128,2048]{1,0:T(8,128)(2,1)S(1)}, u32[]{:S(2)}, u32[]{:S(2)}) %collective-permute-start.31) | collective-permute-done | bytes 524320 | tf_op jit(solution)/shard_map/ppermute | solution.py:212
  (136 shorter events, 46.0 us)
Async XLA Ops:
  7.2 224.0 %all-gather.2.cloned.1.call-start = ((), (), s32[]{:S(2)}) async-start(), calls=%async_computation.5 | async-start | bytes 3538944 | tf_op jit(solution)/shard_map/all_gather | solution.py:217
  7.2 23.5 %collective-permute-start.1 = (bf16[128,2048]{1,0:T(8,128)(2,1)}, bf16[128,2048]{1,0:T(8,128)(2,1)S(1)}, u32[]{:S(2)}, u32[]{:S(2)}) collective-permute-start(bf16[128,2048]{1,0:T(8,128)(2,1)} %bitcast.53), channel_id=1, source_target_pairs={{0,1},{1,2},{2,3},{3,4},{4,5},{5,6},{6,7},{7,8},{8,9},{9,10},{10,1... | collective-permute-start | bytes 1572872 | tf_op jit(solution)/shard_map/ppermute | solution.py:212
  11.0 21.6 %collective-permute-start = (bf16[128,2048]{1,0:T(8,128)(2,1)}, bf16[128,2048]{1,0:T(8,128)(2,1)S(1)}, u32[]{:S(2)}, u32[]{:S(2)}) collective-permute-start(bf16[128,2048]{1,0:T(8,128)(2,1)} %bitcast.54), channel_id=1, source_target_pairs={{0,15},{1,0},{2,1},{3,2},{4,3},{5,4},{6,5},{7,6},{8,7},{9,8},{10,9... | collective-permute-start | bytes 1572872 | tf_op jit(solution)/shard_map/ppermute | solution.py:212
  20.6 181.8 %copy-start.23 = (s32[224,6]{1,0:T(8,128)S(1)}, s32[224,6]{1,0:T(8,128)}, u32[]{:S(2)}) copy-start(s32[224,6]{1,0:T(8,128)} %constant.45.clone.place_ref) | copy-start | bytes 16132
  30.7 174.1 %copy-start.4 = (bf16[128,2048]{1,0:T(8,128)(2,1)}, bf16[128,2048]{1,0:T(8,128)(2,1)S(1)}, u32[]{:S(2)}) copy-start(bf16[128,2048]{1,0:T(8,128)(2,1)S(1)} %collective-permute-done.1.refs_2_) | copy-start | bytes 1572868
  30.7 16.2 %collective-permute-start.3 = (bf16[128,2048]{1,0:T(8,128)(2,1)S(1)}, bf16[128,2048]{1,0:T(8,128)(2,1)S(1)}, u32[]{:S(2)}, u32[]{:S(2)}) collective-permute-start(bf16[128,2048]{1,0:T(8,128)(2,1)S(1)} %collective-permute-done.1.refs_2_), channel_id=1, source_target_pairs={{0,1},{1,2},{2,3},{3,4},{4,5},{5,6},{6,7},{7,8},{8,9},{9,10},{10,1... | collective-permute-start | bytes 1572872 | tf_op jit(solution)/shard_map/ppermute | solution.py:212
  32.7 17.0 %collective-permute-start.2 = (bf16[128,2048]{1,0:T(8,128)(2,1)S(1)}, bf16[128,2048]{1,0:T(8,128)(2,1)S(1)}, u32[]{:S(2)}, u32[]{:S(2)}) collective-permute-start(bf16[128,2048]{1,0:T(8,128)(2,1)S(1)} %collective-permute-done.refs_1_), channel_id=1, source_target_pairs={{0,15},{1,0},{2,1},{3,2},{4,3},{5,4},{6,5},{7,6},{8,7},{9,8},{10,9... | collective-permute-start | bytes 1572872 | tf_op jit(solution)/shard_map/ppermute | solution.py:212
  46.9 15.3 %collective-permute-start.5 = (bf16[128,2048]{1,0:T(8,128)(2,1)S(1)}, bf16[128,2048]{1,0:T(8,128)(2,1)S(1)}, u32[]{:S(2)}, u32[]{:S(2)}) collective-permute-start(bf16[128,2048]{1,0:T(8,128)(2,1)S(1)} %collective-permute-done.3.refs_4_), channel_id=1, source_target_pairs={{0,1},{1,2},{2,3},{3,4},{4,5},{5,6},{6,7},{7,8},{8,9},{9,10},{10,1... | collective-permute-start | bytes 1572872 | tf_op jit(solution)/shard_map/ppermute | solution.py:212
  49.7 15.3 %collective-permute-start.4 = (bf16[128,2048]{1,0:T(8,128)(2,1)S(1)}, bf16[128,2048]{1,0:T(8,128)(2,1)S(1)}, u32[]{:S(2)}, u32[]{:S(2)}) collective-permute-start(bf16[128,2048]{1,0:T(8,128)(2,1)S(1)} %collective-permute-done.2.refs_3_), channel_id=1, source_target_pairs={{0,15},{1,0},{2,1},{3,2},{4,3},{5,4},{6,5},{7,6},{8,7},{9,8},{10,9... | collective-permute-start | bytes 1572872 | tf_op jit(solution)/shard_map/ppermute | solution.py:212
  62.2 14.4 %collective-permute-start.7 = (bf16[128,2048]{1,0:T(8,128)(2,1)S(1)}, bf16[128,2048]{1,0:T(8,128)(2,1)S(1)}, u32[]{:S(2)}, u32[]{:S(2)}) collective-permute-start(bf16[128,2048]{1,0:T(8,128)(2,1)S(1)} %collective-permute-done.5.refs_6_), channel_id=1, source_target_pairs={{0,1},{1,2},{2,3},{3,4},{4,5},{5,6},{6,7},{7,8},{8,9},{9,10},{10,1... | collective-permute-start | bytes 1572872 | tf_op jit(solution)/shard_map/ppermute | solution.py:212
  64.9 13.6 %collective-permute-start.6 = (bf16[128,2048]{1,0:T(8,128)(2,1)S(1)}, bf16[128,2048]{1,0:T(8,128)(2,1)S(1)}, u32[]{:S(2)}, u32[]{:S(2)}) collective-permute-start(bf16[128,2048]{1,0:T(8,128)(2,1)S(1)} %collective-permute-done.4.refs_5_), channel_id=1, source_target_pairs={{0,15},{1,0},{2,1},{3,2},{4,3},{5,4},{6,5},{7,6},{8,7},{9,8},{10,9... | collective-permute-start | bytes 1572872 | tf_op jit(solution)/shard_map/ppermute | solution.py:212
  76.6 94.3 %copy-start.16 = (bf16[128,2048]{1,0:T(8,128)(2,1)}, bf16[128,2048]{1,0:T(8,128)(2,1)S(1)}, u32[]{:S(2)}) copy-start(bf16[128,2048]{1,0:T(8,128)(2,1)S(1)} %collective-permute-done.7.refs_8_) | copy-start | bytes 1572868
  76.6 94.3 %collective-permute-start.9 = (bf16[128,2048]{1,0:T(8,128)(2,1)S(1)}, bf16[128,2048]{1,0:T(8,128)(2,1)S(1)}, u32[]{:S(2)}, u32[]{:S(2)}) collective-permute-start(bf16[128,2048]{1,0:T(8,128)(2,1)S(1)} %collective-permute-done.7.refs_8_), channel_id=1, source_target_pairs={{0,1},{1,2},{2,3},{3,4},{4,5},{5,6},{6,7},{7,8},{8,9},{9,10},{10,1... | collective-permute-start | bytes 1572872 | tf_op jit(solution)/shard_map/ppermute | solution.py:212
  78.6 94.6 %copy-start.18 = (bf16[128,2048]{1,0:T(8,128)(2,1)}, bf16[128,2048]{1,0:T(8,128)(2,1)S(1)}, u32[]{:S(2)}) copy-start(bf16[128,2048]{1,0:T(8,128)(2,1)S(1)} %collective-permute-done.6.refs_7_) | copy-start | bytes 1572868
  78.6 94.5 %collective-permute-start.8 = (bf16[128,2048]{1,0:T(8,128)(2,1)S(1)}, bf16[128,2048]{1,0:T(8,128)(2,1)S(1)}, u32[]{:S(2)}, u32[]{:S(2)}) collective-permute-start(bf16[128,2048]{1,0:T(8,128)(2,1)S(1)} %collective-permute-done.6.refs_7_), channel_id=1, source_target_pairs={{0,15},{1,0},{2,1},{3,2},{4,3},{5,4},{6,5},{7,6},{8,7},{9,8},{10,9... | collective-permute-start | bytes 1572872 | tf_op jit(solution)/shard_map/ppermute | solution.py:212
  168.7 1.0 copy-start.24
  170.8 34.1 %copy-start.30 = (s32[32,128]{1,0:T(8,128)}, s32[32,128]{1,0:T(8,128)S(1)}, u32[]{:S(2)}) copy-start(s32[32,128]{1,0:T(8,128)S(1)} %get-tuple-element.26.far_ref) | copy-start | bytes 49156
  170.8 34.1 %copy-start.27 = (f32[672,1]{1,0:T(8,128)}, f32[672,1]{1,0:T(8,128)S(1)}, u32[]{:S(2)}) copy-start(f32[672,1]{1,0:T(8,128)S(1)} %get-tuple-element.24) | copy-start | bytes 8068
  171.2 11.6 %collective-permute-start.10 = (bf16[112,2048]{1,0:T(8,128)(2,1)S(1)}, bf16[112,2048]{1,0:T(8,128)(2,1)S(1)}, u32[]{:S(2)}, u32[]{:S(2)}) collective-permute-start(bf16[112,2048]{1,0:T(8,128)(2,1)S(1)} %shard_map.151), channel_id=1, source_target_pairs={{0,1},{1,2},{2,3},{3,4},{4,5},{5,6},{6,7},{7,8},{8,9},{9,10},{10,1... | collective-permute-start | bytes 1376264 | tf_op jit(solution)/shard_map/ppermute | solution.py:212
  173.4 35.2 %copy-start.3 = (bf16[1,128,2048]{2,1,0:T(8,128)(2,1)S(1)}, bf16[1,128,2048]{2,1,0:T(8,128)(2,1)}, u32[]{:S(2)}) copy-start(bf16[1,128,2048]{2,1,0:T(8,128)(2,1)} %param.12) | copy-start | bytes 1572868
  173.5 11.3 %collective-permute-start.11 = (bf16[112,2048]{1,0:T(8,128)(2,1)S(1)}, bf16[112,2048]{1,0:T(8,128)(2,1)S(1)}, u32[]{:S(2)}, u32[]{:S(2)}) collective-permute-start(bf16[112,2048]{1,0:T(8,128)(2,1)S(1)} %shard_map.152), channel_id=1, source_target_pairs={{0,15},{1,0},{2,1},{3,2},{4,3},{5,4},{6,5},{7,6},{8,7},{9,8},{10,9... | collective-permute-start | bytes 1376264 | tf_op jit(solution)/shard_map/ppermute | solution.py:212
  182.8 9.5 %collective-permute-start.12 = (bf16[64,2048]{1,0:T(8,128)(2,1)S(1)}, bf16[64,2048]{1,0:T(8,128)(2,1)S(1)}, u32[]{:S(2)}, u32[]{:S(2)}) collective-permute-start(bf16[64,2048]{1,0:T(8,128)(2,1)S(1)} %slice.65), channel_id=1, source_target_pairs={{0,1},{1,2},{2,3},{3,4},{4,5},{5,6},{6,7},{7,8},{8,9},{9,10},{10,1... | collective-permute-start | bytes 786440 | tf_op jit(solution)/shard_map/ppermute | solution.py:212
  184.7 9.5 %collective-permute-start.13 = (bf16[64,2048]{1,0:T(8,128)(2,1)S(1)}, bf16[64,2048]{1,0:T(8,128)(2,1)S(1)}, u32[]{:S(2)}, u32[]{:S(2)}) collective-permute-start(bf16[64,2048]{1,0:T(8,128)(2,1)S(1)} %slice.66), channel_id=1, source_target_pairs={{0,15},{1,0},{2,1},{3,2},{4,3},{5,4},{6,5},{7,6},{8,7},{9,8},{10,9... | collective-permute-start | bytes 786440 | tf_op jit(solution)/shard_map/ppermute | solution.py:212
  192.3 8.1 %collective-permute-start.14 = (bf16[32,2048]{1,0:T(8,128)(2,1)S(1)}, bf16[32,2048]{1,0:T(8,128)(2,1)S(1)}, u32[]{:S(2)}, u32[]{:S(2)}) collective-permute-start(bf16[32,2048]{1,0:T(8,128)(2,1)S(1)} %slice.67), channel_id=1, source_target_pairs={{0,1},{1,2},{2,3},{3,4},{4,5},{5,6},{6,7},{7,8},{8,9},{9,10},{10,1... | collective-permute-start | bytes 393224 | tf_op jit(solution)/shard_map/ppermute | solution.py:212
  194.2 8.1 %collective-permute-start.15 = (bf16[32,2048]{1,0:T(8,128)(2,1)S(1)}, bf16[32,2048]{1,0:T(8,128)(2,1)S(1)}, u32[]{:S(2)}, u32[]{:S(2)}) collective-permute-start(bf16[32,2048]{1,0:T(8,128)(2,1)S(1)} %slice.68), channel_id=1, source_target_pairs={{0,15},{1,0},{2,1},{3,2},{4,3},{5,4},{6,5},{7,6},{8,7},{9,8},{10,9... | collective-permute-start | bytes 393224 | tf_op jit(solution)/shard_map/ppermute | solution.py:212
  204.9 16.8 %all-to-all-start.1 = ((bf16[4,56,2048]{2,1,0:T(8,128)(2,1)}), bf16[4,56,2048]{2,1,0:T(8,128)(2,1)S(1)}, u32[]{:S(2)}, u32[]{:S(2)}) async-start(bf16[4,56,2048]{2,1,0:T(8,128)(2,1)} %bitcast.14), calls=%async_computation.1 | async-start | bytes 1835008 | tf_op jit(solution)/shard_map/all_to_all | solution.py:266
  208.7 1.0 copy-start.5
  209.7 1.0 copy-start.7
  210.7 1.0 copy-start.9
  211.8 1.0 copy-start.11
  212.8 1.0 copy-start.13
  213.9 1.0 copy-start.15
  214.9 1.0 copy-start.17
  216.0 1.0 copy-start.19
  221.7 19.9 %all-to-all-start = ((bf16[4,112,2048]{2,1,0:T(8,128)(2,1)}), bf16[4,112,2048]{2,1,0:T(8,128)(2,1)S(1)}, u32[]{:S(2)}, u32[]{:S(2)}) async-start(bf16[4,112,2048]{2,1,0:T(8,128)(2,1)} %bitcast.57), calls=%async_computation | async-start | bytes 3670016 | tf_op jit(solution)/shard_map/all_to_all | solution.py:266
  227.6 1.0 copy-start.20
  231.1 1.9 copy-start
  235.4 0.9 copy-start.2
  241.6 19.5 %all-to-all-start.2 = ((bf16[4,56,2048]{2,1,0:T(8,128)(2,1)}), bf16[4,56,2048]{2,1,0:T(8,128)(2,1)}, u32[]{:S(2)}, u32[]{:S(2)}) async-start(bf16[4,56,2048]{2,1,0:T(8,128)(2,1)} %bitcast.52), calls=%async_computation.2 | async-start | bytes 1835008 | tf_op jit(solution)/shard_map/all_to_all | solution.py:266
  245.8 148.8 %reduce-scatter.2.cloned.1.call-start = ((), (), s32[]{:S(2)}) async-start(), calls=%async_computation.6 | async-start | bytes 3538944 | tf_op jit(solution)/shard_map/reduce_scatter | solution.py:334
  253.7 1.2 copy-start.1
  255.7 0.9 copy-start.34
  261.1 3.0 copy-start.29
  269.2 11.2 %collective-permute-start.24 = (bf16[32,2048]{1,0:T(8,128)(2,1)S(1)}, bf16[32,2048]{1,0:T(8,128)(2,1)S(1)}, u32[]{:S(2)}, u32[]{:S(2)}) collective-permute-start(bf16[32,2048]{1,0:T(8,128)(2,1)S(1)} %get-tuple-element.37), channel_id=1, source_target_pairs={{0,1},{1,2},{2,3},{3,4},{4,5},{5,6},{6,7},{7,8},{8,9},{9,10},{10,1... | collective-permute-start | bytes 393224 | tf_op jit(solution)/shard_map/ppermute | solution.py:212
  271.1 41.8 %all-to-all-start.3 = ((bf16[4,112,2048]{2,1,0:T(8,128)(2,1)}), bf16[4,112,2048]{2,1,0:T(8,128)(2,1)S(1)}, u32[]{:S(2)}, u32[]{:S(2)}) async-start(bf16[4,112,2048]{2,1,0:T(8,128)(2,1)} %bitcast.51), calls=%async_computation.3 | async-start | bytes 3670016 | tf_op jit(solution)/shard_map/all_to_all | solution.py:266
  274.7 38.2 %copy-start.31 = (s32[32,128]{1,0:T(8,128)S(1)}, s32[32,128]{1,0:T(8,128)}, u32[]{:S(2)}) copy-start(s32[32,128]{1,0:T(8,128)} %copy-done.30) | copy-start | bytes 49156
  274.7 9.5 %collective-permute-start.16 = (bf16[32,2048]{1,0:T(8,128)(2,1)S(1)}, bf16[32,2048]{1,0:T(8,128)(2,1)S(1)}, u32[]{:S(2)}, u32[]{:S(2)}) collective-permute-start(bf16[32,2048]{1,0:T(8,128)(2,1)S(1)} %get-tuple-element.34), channel_id=1, source_target_pairs={{0,15},{1,0},{2,1},{3,2},{4,3},{5,4},{6,5},{7,6},{8,7},{9,8},{10,9... | collective-permute-start | bytes 393224 | tf_op jit(solution)/shard_map/ppermute | solution.py:212
  280.4 12.3 %collective-permute-start.25 = (bf16[64,2048]{1,0:T(8,128)(2,1)S(1)}, bf16[64,2048]{1,0:T(8,128)(2,1)S(1)}, u32[]{:S(2)}, u32[]{:S(2)}) collective-permute-start(bf16[64,2048]{1,0:T(8,128)(2,1)S(1)} %pad_maximum_fusion.2), channel_id=1, source_target_pairs={{0,1},{1,2},{2,3},{3,4},{4,5},{5,6},{6,7},{7,8},{8,9},{9,10},{10,1... | collective-permute-start | bytes 786440 | tf_op jit(solution)/shard_map/ppermute | solution.py:212
  284.2 12.0 %collective-permute-start.17 = (bf16[64,2048]{1,0:T(8,128)(2,1)S(1)}, bf16[64,2048]{1,0:T(8,128)(2,1)S(1)}, u32[]{:S(2)}, u32[]{:S(2)}) collective-permute-start(bf16[64,2048]{1,0:T(8,128)(2,1)S(1)} %pad_maximum_fusion.1), channel_id=1, source_target_pairs={{0,15},{1,0},{2,1},{3,2},{4,3},{5,4},{6,5},{7,6},{8,7},{9,8},{10,9... | collective-permute-start | bytes 786440 | tf_op jit(solution)/shard_map/ppermute | solution.py:212
  297.2 14.9 %collective-permute-start.18 = (bf16[112,2048]{1,0:T(8,128)(2,1)S(1)}, bf16[112,2048]{1,0:T(8,128)(2,1)S(1)}, u32[]{:S(2)}, u32[]{:S(2)}) collective-permute-start(bf16[112,2048]{1,0:T(8,128)(2,1)S(1)} %get-tuple-element.47), channel_id=1, source_target_pairs={{0,15},{1,0},{2,1},{3,2},{4,3},{5,4},{6,5},{7,6},{8,7},{9,8},{10,9... | collective-permute-start | bytes 1376264 | tf_op jit(solution)/shard_map/ppermute | solution.py:212
  302.8 17.4 %collective-permute-start.26 = (bf16[112,2048]{1,0:T(8,128)(2,1)}, bf16[112,2048]{1,0:T(8,128)(2,1)}, u32[]{:S(2)}, u32[]{:S(2)}) collective-permute-start(bf16[112,2048]{1,0:T(8,128)(2,1)} %get-tuple-element.46), channel_id=1, source_target_pairs={{0,1},{1,2},{2,3},{3,4},{4,5},{5,6},{6,7},{7,8},{8,9},{9,10},{10,1... | collective-permute-start | bytes 1376264 | tf_op jit(solution)/shard_map/ppermute | solution.py:212
  312.9 1.0 copy-start.22
  314.6 17.1 %collective-permute-start.19 = (bf16[128,2048]{1,0:T(8,128)(2,1)S(1)}, bf16[128,2048]{1,0:T(8,128)(2,1)S(1)}, u32[]{:S(2)}, u32[]{:S(2)}) collective-permute-start(bf16[128,2048]{1,0:T(8,128)(2,1)S(1)} %shard_map.157), channel_id=1, source_target_pairs={{0,15},{1,0},{2,1},{3,2},{4,3},{5,4},{6,5},{7,6},{8,7},{9,8},{10,9... | collective-permute-start | bytes 1572872 | tf_op jit(solution)/shard_map/ppermute | solution.py:212
  321.9 15.9 %collective-permute-start.27 = (bf16[128,2048]{1,0:T(8,128)(2,1)S(1)}, bf16[128,2048]{1,0:T(8,128)(2,1)S(1)}, u32[]{:S(2)}, u32[]{:S(2)}) collective-permute-start(bf16[128,2048]{1,0:T(8,128)(2,1)S(1)} %shard_map.162), channel_id=1, source_target_pairs={{0,1},{1,2},{2,3},{3,4},{4,5},{5,6},{6,7},{7,8},{8,9},{9,10},{10,1... | collective-permute-start | bytes 1572872 | tf_op jit(solution)/shard_map/ppermute | solution.py:212
  332.2 16.3 %collective-permute-start.20 = (bf16[128,2048]{1,0:T(8,128)(2,1)S(1)}, bf16[128,2048]{1,0:T(8,128)(2,1)S(1)}, u32[]{:S(2)}, u32[]{:S(2)}) collective-permute-start(bf16[128,2048]{1,0:T(8,128)(2,1)S(1)} %shard_map.158), channel_id=1, source_target_pairs={{0,15},{1,0},{2,1},{3,2},{4,3},{5,4},{6,5},{7,6},{8,7},{9,8},{10,9... | collective-permute-start | bytes 1572872 | tf_op jit(solution)/shard_map/ppermute | solution.py:212
  338.4 16.3 %collective-permute-start.28 = (bf16[128,2048]{1,0:T(8,128)(2,1)S(1)}, bf16[128,2048]{1,0:T(8,128)(2,1)S(1)}, u32[]{:S(2)}, u32[]{:S(2)}) collective-permute-start(bf16[128,2048]{1,0:T(8,128)(2,1)S(1)} %shard_map.163), channel_id=1, source_target_pairs={{0,1},{1,2},{2,3},{3,4},{4,5},{5,6},{6,7},{7,8},{8,9},{9,10},{10,1... | collective-permute-start | bytes 1572872 | tf_op jit(solution)/shard_map/ppermute | solution.py:212
  349.0 12.3 %collective-permute-start.21 = (bf16[128,2048]{1,0:T(8,128)(2,1)S(1)}, bf16[128,2048]{1,0:T(8,128)(2,1)S(1)}, u32[]{:S(2)}, u32[]{:S(2)}) collective-permute-start(bf16[128,2048]{1,0:T(8,128)(2,1)S(1)} %shard_map.159), channel_id=1, source_target_pairs={{0,15},{1,0},{2,1},{3,2},{4,3},{5,4},{6,5},{7,6},{8,7},{9,8},{10,9... | collective-permute-start | bytes 1572872 | tf_op jit(solution)/shard_map/ppermute | solution.py:212
  355.1 12.3 %collective-permute-start.29 = (bf16[128,2048]{1,0:T(8,128)(2,1)S(1)}, bf16[128,2048]{1,0:T(8,128)(2,1)S(1)}, u32[]{:S(2)}, u32[]{:S(2)}) collective-permute-start(bf16[128,2048]{1,0:T(8,128)(2,1)S(1)} %shard_map.164), channel_id=1, source_target_pairs={{0,1},{1,2},{2,3},{3,4},{4,5},{5,6},{6,7},{7,8},{8,9},{9,10},{10,1... | collective-permute-start | bytes 1572872 | tf_op jit(solution)/shard_map/ppermute | solution.py:212
  361.8 12.3 %collective-permute-start.22 = (bf16[128,2048]{1,0:T(8,128)(2,1)S(1)}, bf16[128,2048]{1,0:T(8,128)(2,1)S(1)}, u32[]{:S(2)}, u32[]{:S(2)}) collective-permute-start(bf16[128,2048]{1,0:T(8,128)(2,1)S(1)} %shard_map.160), channel_id=1, source_target_pairs={{0,15},{1,0},{2,1},{3,2},{4,3},{5,4},{6,5},{7,6},{8,7},{9,8},{10,9... | collective-permute-start | bytes 1572872 | tf_op jit(solution)/shard_map/ppermute | solution.py:212
  367.9 14.9 %copy-start.26 = (bf16[448,384]{1,0:T(8,128)(2,1)S(1)}, bf16[448,384]{1,0:T(8,128)(2,1)}, u32[]{:S(2)}) copy-start(bf16[448,384]{1,0:T(8,128)(2,1)} %copy-done.25) | copy-start | bytes 1032196
  368.0 14.9 %copy-start.33 = (bf16[224,384]{1,0:T(8,128)(2,1)S(1)}, bf16[224,384]{1,0:T(8,128)(2,1)}, u32[]{:S(2)}) copy-start(bf16[224,384]{1,0:T(8,128)(2,1)} %copy-done.32) | copy-start | bytes 516100
  368.0 12.4 %collective-permute-start.30 = (bf16[128,2048]{1,0:T(8,128)(2,1)S(1)}, bf16[128,2048]{1,0:T(8,128)(2,1)S(1)}, u32[]{:S(2)}, u32[]{:S(2)}) collective-permute-start(bf16[128,2048]{1,0:T(8,128)(2,1)S(1)} %shard_map.165), channel_id=1, source_target_pairs={{0,1},{1,2},{2,3},{3,4},{4,5},{5,6},{6,7},{7,8},{8,9},{9,10},{10,1... | collective-permute-start | bytes 1572872 | tf_op jit(solution)/shard_map/ppermute | solution.py:212
  374.6 12.3 %collective-permute-start.23 = (bf16[128,2048]{1,0:T(8,128)(2,1)S(1)}, bf16[128,2048]{1,0:T(8,128)(2,1)S(1)}, u32[]{:S(2)}, u32[]{:S(2)}) collective-permute-start(bf16[128,2048]{1,0:T(8,128)(2,1)S(1)} %shard_map.161), channel_id=1, source_target_pairs={{0,15},{1,0},{2,1},{3,2},{4,3},{5,4},{6,5},{7,6},{8,7},{9,8},{10,9... | collective-permute-start | bytes 1572872 | tf_op jit(solution)/shard_map/ppermute | solution.py:212
  380.9 12.3 %collective-permute-start.31 = (bf16[128,2048]{1,0:T(8,128)(2,1)S(1)}, bf16[128,2048]{1,0:T(8,128)(2,1)S(1)}, u32[]{:S(2)}, u32[]{:S(2)}) collective-permute-start(bf16[128,2048]{1,0:T(8,128)(2,1)S(1)} %shard_map.166), channel_id=1, source_target_pairs={{0,1},{1,2},{2,3},{3,4},{4,5},{5,6},{6,7},{7,8},{8,9},{9,10},{10,1... | collective-permute-start | bytes 1572872 | tf_op jit(solution)/shard_map/ppermute | solution.py:212
  (9 other events, 6.9 us)
Sparse Core Ops, SparseCore 0:
  22.5 32.4 all-gather.1
  266.9 35.9 reduce-scatter.1

commit v3 on v0

v3 whole, which is shorter than its diff:
```python
import functools

import jax
import jax.numpy as jnp
import numpy as np
from jax import lax
from jax.experimental import pallas as pl
from jax.experimental.pallas import tpu as pltpu
from jax.sharding import Mesh, PartitionSpec as P

N_Y = 4
N_Z = 16
SLOTS = 10
REACH = 5
NEAR = (0, 1, -1, 2, -2, 3, -3, 4, -4)
LAST = (5, -5, 6, 7, 8, -7, -6)
NEAR_ROWS = 96
LAST_ROWS = 72
MESSAGE = (48, 48, 32)
MESSAGE_SLOTS = (40, 40, 20)
MESSAGE_ROWS = sum(MESSAGE)
LANES = 128
VMEM_BYTES = 48 * 1024 * 1024
F32 = jnp.float32
BF16 = jnp.bfloat16


def call(kernel, out_shape, *operands, scalars=0):
    whole = pl.BlockSpec(memory_space=pltpu.VMEM)
    small = pl.BlockSpec(memory_space=pltpu.SMEM)
    return pl.pallas_call(
        kernel,
        out_shape=out_shape,
        in_specs=[small] * scalars + [whole] * (len(operands) - scalars),
        out_specs=jax.tree.map(lambda _: whole, out_shape),
        compiler_params=pltpu.CompilerParams(vmem_limit_bytes=VMEM_BYTES),
    )(*operands)


def array(shape, dtype=BF16):
    return jax.ShapeDtypeStruct(shape, dtype)


def iota(shape, dimension):
    return lax.broadcasted_iota(jnp.int32, shape, dimension)


def one_hot(condition):
    return jnp.where(condition, 1.0, 0.0).astype(BF16)


def dot(a, b, contract=(1, 0)):
    return lax.dot_general(a, b, (((contract[0],), (contract[1],)), ((), ())), preferred_element_type=F32)


def block_kernel(ids_ref, weights_ref, tokens_ref, out_ref):
    tokens, width = tokens_ref.shape
    lane = iota((tokens, LANES), 1)
    expert = lane & (N_Y * N_Z - 1)
    hits = jnp.zeros((tokens, LANES), F32)
    eighths = jnp.zeros((tokens, LANES), F32)
    weights = weights_ref[...].astype(F32)
    for choice in range(ids_ref.shape[1]):
        named = ids_ref[:, choice : choice + 1] == expert
        hits = hits + jnp.where(named, 1.0, 0.0)
        eighths = eighths + jnp.where(named, weights[:, choice : choice + 1], 0.0)
    earlier = one_hot(iota((tokens, tokens), 1) < iota((tokens, tokens), 0))
    rank = jnp.where(hits > 0.0, dot(earlier, hits.astype(BF16)), -1.0)
    out_ref[:, :width] = tokens_ref[...]
    out_ref[:, width:] = jnp.where(lane < N_Y * N_Z, rank, eighths).astype(BF16)


def slots_of(routing, expert, slot):
    lane = iota((LANES, expert.shape[1]), 0)
    rank = dot(routing, one_hot(lane == expert))
    eighths = dot(routing, one_hot(lane == expert + N_Y * N_Z))
    here = rank == slot.astype(F32)
    return here, jnp.where(here, eighths, 0.0)


def message_kernel(sign, z_ref, map_ref, block_ref, first_ref, second_ref, third_ref, select_ref):
    width = first_ref.shape[1]
    expert = map_ref[0:1, :] + ((z_ref[0] + sign * map_ref[1:2, :] + N_Z) & (N_Z - 1))
    here, eighths = slots_of(block_ref[:, width:], expert, map_ref[2:3, :])
    select = one_hot(here)
    select_ref[...] = select
    picked = dot(select, block_ref[:, :width], (0, 0))
    weights = jnp.sum(eighths, axis=0, keepdims=True)
    first = 0
    for ref, rows, slots in zip((first_ref, second_ref, third_ref), MESSAGE, MESSAGE_SLOTS):
        part = picked[first : first + rows]
        ref[...] = part.astype(BF16)
        is_weights = iota((rows, LANES), 0) == slots
        ref[:, :LANES] = jnp.where(is_weights, weights, part[:, :LANES]).astype(BF16)
        first += rows


def pick_kernel(blocks, z_ref, map_ref, *refs):
    messages = refs[blocks + 1 : -2] if len(refs) > blocks + 2 else ()
    out_ref, select_ref = refs[-2:]
    rows, width = out_ref.shape
    tokens = refs[0].shape[0]
    routing = jnp.concatenate([ref[:, width:] for ref in refs[:blocks]], axis=0)
    here, eighths = slots_of(routing, map_ref[0:1, :] + z_ref[0], map_ref[1:2, :])
    here = here & ((iota(here.shape, 0) >> (tokens.bit_length() - 1)) == map_ref[2:3, :])
    select = one_hot(here)
    select_ref[...] = select
    weights = jnp.sum(jnp.where(here, eighths, 0.0), axis=0, keepdims=True)
    picked = dot(select, jnp.concatenate([ref[:, :width] for ref in refs[:blocks]], axis=0), (0, 0))
    for index, ref in enumerate(messages):
        place_ref = refs[blocks]
        count = ref.shape[0]
        picked = picked + dot(one_hot(iota((rows, count), 1) == place_ref[:, index : index + 1]), ref[...])
        line = (index // 2) if index < 4 else 2
        spread = one_hot(iota((LANES, rows), 0) == map_ref[3 + index : 4 + index, :])
        lines = dot(ref[:, :LANES], spread)
        weights = weights + jnp.sum(
            jnp.where(iota(lines.shape, 0) == MESSAGE_SLOTS[line], lines, 0.0), axis=0, keepdims=True
        )
    out_ref[...] = picked.astype(BF16)
    used = (rows // N_Y - 1) // SLOTS * SLOTS
    row = iota((rows, rows), 0)
    is_weights = row == used
    for y in range(1, N_Y):
        is_weights = is_weights | (row == used + y * (rows // N_Y))
    out_ref[:, :rows] = jnp.where(is_weights, weights, picked[:, :rows]).astype(BF16)


MESSAGE_KEYS = tuple((step, way) for step in range(3) for way in range(2))


def message_map():
    maps = np.full((2, 8, MESSAGE_ROWS), -5, np.int32)
    for way in range(2):
        for step in range(3):
            for place in range(MESSAGE_SLOTS[step]):
                row = sum(MESSAGE[:step]) + place
                y = place // SLOTS + (2 if step == 2 and way == 1 else 0)
                maps[way, :3, row] = y * N_Z, step + 1, place % SLOTS
    return maps


def row_maps(sources, rows_of_y, blocks):
    rows = N_Y * rows_of_y
    lanes = np.full((16, rows), -5, np.int32)
    places = np.full((rows, 8), -5, np.int32)
    origin = np.full((3, rows), -1, np.int32)
    for y in range(N_Y):
        for index, source in enumerate(sources):
            for slot in range(SLOTS):
                row = y * rows_of_y + index * SLOTS + slot
                origin[:, row] = y, source, slot
                if index < blocks:
                    lanes[:3, row] = y * N_Z, slot, index
                    continue
                step = abs(source) - REACH - 1
                way = (y // 2) if step == 2 else (0 if source < 0 else 1)
                place = (y % 2 if step == 2 else y) * SLOTS + slot
                key = MESSAGE_KEYS.index((step, way))
                lanes[3 + key, row] = sum(MESSAGE[:step]) + place
                places[row, key] = place
    return lanes, places, origin


def part_kernel(place_ref, grads_ref, *out_refs):
    for index, ref in enumerate(out_refs):
        move = one_hot(iota((grads_ref.shape[0], ref.shape[0]), 1) == place_ref[:, index : index + 1])
        ref[...] = dot(move, grads_ref[...], (0, 0)).astype(BF16)


def relative_kernel(row_ref, values_ref, out_ref):
    move = one_hot(iota((row_ref.shape[0], values_ref.shape[0]), 1) == row_ref[...])
    out_ref[...] = dot(move, values_ref[...]).astype(BF16)


def absolute_kernel(row_ref, near_ref, last_ref, out_ref):
    move = one_hot(iota((row_ref.shape[0], out_ref.shape[0]), 1) == row_ref[...])
    count = near_ref.shape[0]
    out = dot(move[:count], near_ref[...], (0, 0)) + dot(move[count:], last_ref[...], (0, 0))
    out_ref[...] = out.astype(BF16)


def expert_kernel(y_ref, rows_ref, matrix_ref, cotangent_ref, hidden_ref, grad_ref, row_grads_ref):
    rows = rows_ref.shape[0]
    of_y = rows // N_Y
    units = hidden_ref.shape[1]
    row, lane = iota((rows, rows), 0), iota((rows, rows), 1)
    first = jnp.zeros((rows, rows), jnp.int32)
    for y in range(1, N_Y):
        first = jnp.where(row >= y * of_y, y * of_y, first)
    used = (of_y - 1) // SLOTS * SLOTS
    eighths = dot(one_hot(lane == first + used), rows_ref[:, :rows])
    eighths = jnp.where(lane == row - first + y_ref[0] * of_y, eighths, 0.0)
    weight = jnp.sum(eighths, axis=1, keepdims=True) * 0.125

    pre = dot(rows_ref[...], matrix_ref[...])
    gate_pre, up_pre = pre[:, :units], pre[:, units:]
    sigmoid_gate = jax.nn.sigmoid(gate_pre)
    activation = gate_pre * sigmoid_gate
    hidden_ref[...] = (activation * up_pre * weight).astype(BF16)
    act_slope = sigmoid_gate * (1.0 + gate_pre * (1.0 - sigmoid_gate))
    scaled = cotangent_ref[...].astype(F32) * weight
    grad_ref[:, :units] = (scaled * up_pre * act_slope).astype(BF16)
    grad_ref[:, units:] = (scaled * activation).astype(BF16)
    row_grads_ref[...] = dot(grad_ref[...], matrix_ref[...], (1, 1)).astype(BF16)


def meet_kernel(first_ref, second_ref, third_ref, messages_ref, grads_ref, own_ref, out_ref):
    rows = jnp.concatenate((first_ref[...], second_ref[...], third_ref[...]), axis=0)
    out_ref[...] = (dot(messages_ref[...], rows) + dot(own_ref[...], grads_ref[...])).astype(BF16)


def pass_kernel(sum_ref, grads_ref, own_ref, out_ref):
    out_ref[...] = (sum_ref[...].astype(F32) + dot(own_ref[...], grads_ref[...])).astype(BF16)


def end_kernel(up_ref, down_ref, grads_ref, own_ref, out_ref):
    out_ref[...] = up_ref[...].astype(F32) + down_ref[...].astype(F32) + dot(own_ref[...], grads_ref[...])


def call_block(kernel, out_shape, index, tokens, *operands):
    whole = pl.BlockSpec(memory_space=pltpu.VMEM)
    rows = operands[-1].shape[1]
    part = pl.BlockSpec((tokens, rows), lambda step: (index, 0))
    out_block = pl.BlockSpec(out_shape.shape, lambda step: (0, 0))
    return pl.pallas_call(
        kernel,
        grid=(1,),
        out_shape=out_shape,
        in_specs=[whole] * (len(operands) - 1) + [part],
        out_specs=out_block,
        compiler_params=pltpu.CompilerParams(vmem_limit_bytes=VMEM_BYTES),
    )(*operands)


def after(value, *others):
    return lax.optimization_barrier((value,) + others)[0]


def shards(tokens, expert_ids, route_weights, gate_weight, up_weight, cotangent):
    slot_count, units = cotangent.shape[2:]
    block, width = tokens.shape[1:]
    y, z = lax.axis_index("y").astype(jnp.int32), lax.axis_index("z").astype(jnp.int32)
    y_of, z_of = y.reshape(1), z.reshape(1)
    near_lanes, _, near_origin = row_maps(NEAR, NEAR_ROWS, len(NEAR))
    last_lanes, last_places, last_origin = row_maps(LAST, LAST_ROWS, 2)
    near_count, last_count = N_Y * NEAR_ROWS, N_Y * LAST_ROWS

    def send(value, distance):
        return lax.ppermute(value, "z", [(i, (i + distance) % N_Z) for i in range(N_Z)])

    def exchange(rows):
        parts = rows.reshape(N_Y, rows.shape[0] // N_Y, width)
        return lax.all_to_all(parts, "y", 0, 0, tiled=True).reshape(rows.shape)

    own = call(block_kernel, array((block, width + LANES)), expert_ids[0], route_weights[0], tokens[0])
    stacked = jnp.concatenate((gate_weight[0], up_weight[0]), axis=1)
    matrix = lax.all_gather(stacked, "dp", axis=0, tiled=True)

    group, offset, slot = np.concatenate((near_origin, last_origin), axis=1)
    row_of = ((group * N_Z + (z + offset + N_Z) % N_Z) * SLOTS + slot).astype(jnp.int32)
    row_of = jnp.where(group >= 0, row_of, -1)[:, None]
    cotangent_rows = call(relative_kernel, array((near_count + last_count, units)), row_of, cotangent[0, 0])

    blocks = {0: own}
    going = [own, own]
    for hop in range(1, REACH + 1):
        going = [send(going[0], 1), send(going[1], -1)]
        blocks[-hop], blocks[hop] = going
        if hop == REACH - 1:
            near_rows, near_select = call(
                functools.partial(pick_kernel, len(NEAR)),
                (array((near_count, width)), array((len(NEAR) * block, near_count))),
                z_of,
                jnp.asarray(near_lanes),
                *[blocks[source] for source in NEAR],
                scalars=1,
            )
    going = [after(part, near_rows) for part in going]
    near_rows = exchange(near_rows)
    messages = [
        call(
            functools.partial(message_kernel, sign),
            tuple(array((rows, width)) for rows in MESSAGE) + (array((block, MESSAGE_ROWS)),),
            z_of,
            jnp.asarray(message_map()[way]),
            going[way],
            scalars=1,
        )
        for way, sign in enumerate((1, -1))
    ]
    arrived = [send(messages[way][step], (step + 1) * (1 - 2 * way)) for step, way in MESSAGE_KEYS]
    last_rows, last_select = call(
        functools.partial(pick_kernel, 2),
        (array((last_count, width)), array((2 * block, last_count))),
        z_of,
        jnp.asarray(last_lanes),
        *[blocks[source] for source in LAST[:2]],
        jnp.asarray(last_places),
        *arrived,
        scalars=1,
    )
    last_rows = exchange(last_rows)

    def expert(rows, first):
        count = rows.shape[0]
        return call(
            expert_kernel,
            (array((count, units)), array((count, 2 * units)), array((count, width))),
            y_of,
            rows,
            matrix,
            cotangent_rows[first : first + count],
            scalars=1,
        )

    near_hidden, near_grads, near_back = expert(near_rows, 0)
    last_hidden, last_grads, last_back = expert(last_rows, near_count)
    near_terms = after(near_rows, last_grads)
    terms = (dot(near_terms, near_grads, (0, 0)) + dot(last_rows, last_grads, (0, 0))).astype(BF16)
    weight_grads = lax.psum_scatter(terms, "dp", scatter_dimension=0, tiled=True).astype(F32)
    gate_grads, up_grads = weight_grads[None, :, :units], weight_grads[None, :, units:]

    last_back = exchange(last_back)
    parts = call(
        part_kernel,
        tuple(array((MESSAGE[step], width)) for step, _ in MESSAGE_KEYS),
        jnp.asarray(last_places),
        last_back,
    )
    near_back = exchange(after(near_back, parts[0]))
    hidden = call(
        absolute_kernel, array((slot_count, units)), row_of, after(near_hidden, parts[0]), last_hidden
    )
    arrived = {
        key: send(part, -(key[0] + 1) * (1 - 2 * key[1])) for key, part in zip(MESSAGE_KEYS, parts)
    }
    whole = array((block, width))
    going = [
        call_block(
            meet_kernel,
            whole,
            LAST.index(REACH * (2 * way - 1)),
            block,
            *[arrived[step, way] for step in range(3)],
            messages[way][3],
            last_back,
            last_select,
        )
        for way in range(2)
    ]
    for hop in range(REACH - 1, -1, -1):
        going = [send(going[0], -1), send(going[1], 1)]
        if hop:
            going = [
                call_block(
                    pass_kernel, whole, NEAR.index(hop * (2 * way - 1)), block, going[way], near_back, near_select
                )
                for way in range(2)
            ]
    going[0] = after(going[0], gate_grads, up_grads, hidden)
    token_grads = call_block(end_kernel, array((block, width), F32), 0, block, *going, near_back, near_select)
    return hidden[None, None], token_grads[None], gate_grads, up_grads


def solution(mesh):
    grid = Mesh(mesh.devices.reshape(mesh.shape["dp"], N_Y, N_Z), ("dp", "y", "z"))
    expert = ("y", "z")
    in_specs = (
        P("dp", expert, None),
        P("dp", expert, None),
        P("dp", expert, None),
        P(expert, "dp", None),
        P(expert, "dp", None),
        P("dp", expert, None, None),
    )
    out_specs = (
        P("dp", expert, None, None),
        P("dp", expert, None),
        P(expert, "dp", None),
        P(expert, "dp", None),
    )
    return jax.shard_map(shards, mesh=grid, in_specs=in_specs, out_specs=out_specs, check_vma=False)
```

time: 469 us -> 342 us (0.73); the launches traced: 469 us -> 336 us
  waiting for transfers between devices: 373 us -> 92.1 us
  starting transfers between devices: 32.4 us -> 134 us
  Pallas kernels: 0 us -> 33.5 us
  blocking collectives: 0 us -> 30 us
  matrix products: 17.2 us -> 5.31 us
    all_to_all x3 -> x2, waiting for transfers between devices: 334 us -> 3.96 us  [exchange(): return lax.all_to_all(parts, 'y', 0, 0, tiled=True).reshape(rows.shape)]
    ppermute x0 -> x32, starting transfers between devices: none -> 127 us  [send(): lax.ppermute(value, 'z', [(i, (i + distance) % N_Z) for i in range(N_Z)])]
    ppermute x0 -> x32, waiting for transfers between devices: none -> 88.1 us  [send(): lax.ppermute(value, 'z', [(i, (i + distance) % N_Z) for i in range(N_Z)])]
    reduce_scatter x1, waiting for transfers between devices: 39.8 us -> 0.01 us  [shards(): lax.psum_scatter(terms, 'dp', scatter_dimension=0, tiled=True).astype(F32)]
    pallas_call x0 -> x21, Pallas kernels: none -> 33.5 us  [the longest x10 23.8 us: call(): pl.pallas_call(kernel, out_shape=out_shape, in_specs=[small] * scalars +...]
    all_to_all x0 -> x2, blocking collectives: none -> 30 us  [exchange(): return lax.all_to_all(parts, 'y', 0, 0, tiled=True).reshape(rows.shape)]
    all_to_all x3 -> x2, starting transfers between devices: 32.1 us -> 7.27 us  [exchange(): return lax.all_to_all(parts, 'y', 0, 0, tiled=True).reshape(rows.shape)]
    unnamed x25 -> x84, local copies, waits for them, and re-layouts: 3.83 us -> 21.6 us
  transfers between devices with their start and end apart: 5 -> 36, of which waited for: 4 -> 15; matrix products, arithmetic and copies ran while one was open for 4% -> 1% of each run, Pallas kernels for 0% -> 8%
where the time goes in v3:
time: 342 us; the launch traced here: 336 us
  starting transfers between devices  134 us (39%)
  waiting for transfers between devices  92.1 us (27%)
  Pallas kernels  33.5 us (10%)
  blocking collectives  30 us (9%)
  local copies, waits for them, and re-layouts  22.7 us (7%)
  between operations  14.8 us (4%)
  matrix products  5.31 us (2%)
    ppermute x32, starting transfers between devices, send(): lax.ppermute(value, 'z', [(i, (i + distance) % N_Z) for i in range(N_Z)])  127 us
    ppermute x32, waiting for transfers between devices, send(): lax.ppermute(value, 'z', [(i, (i + distance) % N_Z) for i in range(N_Z)])  88.1 us
    all_to_all x2, blocking collectives, exchange(): return lax.all_to_all(parts, 'y', 0, 0, tiled=True).reshape(rows.shape)  30 us
    pallas_call x10, Pallas kernels, call(): pl.pallas_call(kernel, out_shape=out_shape, in_specs=[small] * scalars +...  23.8 us
    unnamed x84, local copies, waits for them, and re-layouts  21.6 us
    pallas_call x11, Pallas kernels, call_block(): pl.pallas_call(kernel, grid=(1,), out_shape=out_shape, in_specs=[whole] *...  9.65 us
    all_to_all x2, starting transfers between devices, exchange(): return lax.all_to_all(parts, 'y', 0, 0, tiled=True).reshape(rows.shape)  7.27 us
  transfers between devices with their start and end apart: 36, of which 15 were waited for; matrix products, arithmetic and copies ran while one was open for 1% of the time, Pallas kernels for 8%

profile of v3, /device:TPU:6, one launch (start us, length us, event | category | flops | bytes accessed | tf_op | source)
XLA Modules:
  0.0 335.6 jit_solution(11993323831028231178)
XLA Ops:
  7.2 1.9 pad_maximum_fusion
  11.1 3.8 %collective-permute-start.1 = (bf16[128,2176]{1,0:T(8,128)(2,1)S(1)}, bf16[128,2176]{1,0:T(8,128)(2,1)S(1)}, u32[]{:S(2)}, u32[]{:S(2)}) collective-permute-start(bf16[128,2176]{1,0:T(8,128)(2,1)S(1)} %shard_map.174.refs_0_), channel_id=1, source_target_pairs={{0,1},{1,2},{2,3},{3,4},{4,5},{5,6},{6,7},{7,8},{8,9},{9,10},{10,1... | collective-permute-start | bytes 1671176 | tf_op jit(solution)/shard_map/ppermute | solution.py:250
  15.0 9.5 %collective-permute-start = (bf16[128,2176]{1,0:T(8,128)(2,1)S(1)}, bf16[128,2176]{1,0:T(8,128)(2,1)S(1)}, u32[]{:S(2)}, u32[]{:S(2)}) collective-permute-start(bf16[128,2176]{1,0:T(8,128)(2,1)S(1)} %shard_map.174.refs_0_), channel_id=1, source_target_pairs={{0,15},{1,0},{2,1},{3,2},{4,3},{5,4},{6,5},{7,6},{8,7},{9,8},{10,9... | collective-permute-start | bytes 1671176 | tf_op jit(solution)/shard_map/ppermute | solution.py:250
  24.5 10.7 %collective-permute-done.1.refs_2_ = bf16[128,2176]{1,0:T(8,128)(2,1)S(1)} collective-permute-done((bf16[128,2176]{1,0:T(8,128)(2,1)S(1)}, bf16[128,2176]{1,0:T(8,128)(2,1)S(1)}, u32[]{:S(2)}, u32[]{:S(2)}) %collective-permute-start.1) | collective-permute-done | bytes 557088 | tf_op jit(solution)/shard_map/ppermute | solution.py:250
  35.2 1.9 collective-permute-start.3
  37.1 5.1 %collective-permute-start.2 = (bf16[128,2176]{1,0:T(8,128)(2,1)S(1)}, bf16[128,2176]{1,0:T(8,128)(2,1)S(1)}, u32[]{:S(2)}, u32[]{:S(2)}) collective-permute-start(bf16[128,2176]{1,0:T(8,128)(2,1)S(1)} %collective-permute-done.refs_1_), channel_id=1, source_target_pairs={{0,15},{1,0},{2,1},{3,2},{4,3},{5,4},{6,5},{7,6},{8,7},{9,8},{10,9... | collective-permute-start | bytes 1671176 | tf_op jit(solution)/shard_map/ppermute | solution.py:250
  43.0 9.0 %collective-permute-done.3.refs_4_ = bf16[128,2176]{1,0:T(8,128)(2,1)S(1)} collective-permute-done((bf16[128,2176]{1,0:T(8,128)(2,1)S(1)}, bf16[128,2176]{1,0:T(8,128)(2,1)S(1)}, u32[]{:S(2)}, u32[]{:S(2)}) %collective-permute-start.3) | collective-permute-done | bytes 557088 | tf_op jit(solution)/shard_map/ppermute | solution.py:250
  52.1 1.9 collective-permute-start.5
  54.8 5.1 %collective-permute-start.4 = (bf16[128,2176]{1,0:T(8,128)(2,1)S(1)}, bf16[128,2176]{1,0:T(8,128)(2,1)S(1)}, u32[]{:S(2)}, u32[]{:S(2)}) collective-permute-start(bf16[128,2176]{1,0:T(8,128)(2,1)S(1)} %collective-permute-done.2.refs_3_), channel_id=1, source_target_pairs={{0,15},{1,0},{2,1},{3,2},{4,3},{5,4},{6,5},{7,6},{8,7},{9,8},{10,9... | collective-permute-start | bytes 1671176 | tf_op jit(solution)/shard_map/ppermute | solution.py:250
  60.7 7.3 %collective-permute-done.5.refs_6_ = bf16[128,2176]{1,0:T(8,128)(2,1)S(1)} collective-permute-done((bf16[128,2176]{1,0:T(8,128)(2,1)S(1)}, bf16[128,2176]{1,0:T(8,128)(2,1)S(1)}, u32[]{:S(2)}, u32[]{:S(2)}) %collective-permute-start.5) | collective-permute-done | bytes 557088 | tf_op jit(solution)/shard_map/ppermute | solution.py:250
  68.0 1.9 collective-permute-start.7
  70.8 5.1 %collective-permute-start.6 = (bf16[128,2176]{1,0:T(8,128)(2,1)S(1)}, bf16[128,2176]{1,0:T(8,128)(2,1)}, u32[]{:S(2)}, u32[]{:S(2)}) collective-permute-start(bf16[128,2176]{1,0:T(8,128)(2,1)S(1)} %collective-permute-done.4.refs_5_), channel_id=1, source_target_pairs={{0,15},{1,0},{2,1},{3,2},{4,3},{5,4},{6,5},{7,6},{8,7},{9,8},{10,9... | collective-permute-start | bytes 1671176 | tf_op jit(solution)/shard_map/ppermute | solution.py:250
  76.7 6.5 %collective-permute-done.7.refs_8_ = bf16[128,2176]{1,0:T(8,128)(2,1)} collective-permute-done((bf16[128,2176]{1,0:T(8,128)(2,1)S(1)}, bf16[128,2176]{1,0:T(8,128)(2,1)}, u32[]{:S(2)}, u32[]{:S(2)}) %collective-permute-start.7) | collective-permute-done | bytes 557088 | tf_op jit(solution)/shard_map/ppermute | solution.py:250
  83.2 1.9 collective-permute-start.9
  85.1 5.6 %collective-permute-start.8 = (bf16[128,2176]{1,0:T(8,128)(2,1)}, bf16[128,2176]{1,0:T(8,128)(2,1)S(1)}, u32[]{:S(2)}, u32[]{:S(2)}) collective-permute-start(bf16[128,2176]{1,0:T(8,128)(2,1)} %collective-permute-done.6.refs_7_), channel_id=1, source_target_pairs={{0,15},{1,0},{2,1},{3,2},{4,3},{5,4},{6,5},{7,6},{8,7},{9,8},{10,9... | collective-permute-start | bytes 1671176 | tf_op jit(solution)/shard_map/ppermute | solution.py:250
  96.1 5.4 %shard_map.175 = (bf16[384,2048]{1,0:T(8,128)(2,1)}, bf16[1152,384]{1,0:T(8,128)(2,1)S(1)}) custom-call(s32[1]{0:T(128)} %bitcast.1.z_ref, s32[16,384]{1,0:T(8,128)S(1)} %copy-done.32, bf16[128,2176]{1,0:T(8,128)(2,1)S(1)} %shard_map.174.refs_0_, bf16[128,2176]{1,0:T(8,128)(2,1)S(1)} %copy-done.10, bf16[128,2176]{1,0:T(8,128)(2,1)S(1)} %collective-permute-done.1.refs_2_, ...), custom_call_target="tpu_custom_call" | custom-call | tf_op jit(solution)/shard_map/pallas_call | solution.py:31
  102.0 1.9 collective-permute-start.14
  103.9 2.3 collective-permute-start.10
  106.2 4.1 %collective-permute-start.12 = (bf16[48,2048]{1,0:T(8,128)(2,1)S(1)}, bf16[48,2048]{1,0:T(8,128)(2,1)S(1)}, u32[]{:S(2)}, u32[]{:S(2)}) collective-permute-start(bf16[48,2048]{1,0:T(8,128)(2,1)S(1)} %get-tuple-element.40), channel_id=1, source_target_pairs={{0,2},{1,3},{2,4},{3,5},{4,6},{5,7},{6,8},{7,9},{8,10},{9,11},{10,... | collective-permute-start | bytes 589832 | tf_op jit(solution)/shard_map/ppermute | solution.py:250
  111.4 2.6 collective-permute-start.11
  114.0 4.8 %collective-permute-start.13 = (bf16[48,2048]{1,0:T(8,128)(2,1)S(1)}, bf16[48,2048]{1,0:T(8,128)(2,1)S(1)}, u32[]{:S(2)}, u32[]{:S(2)}) collective-permute-start(bf16[48,2048]{1,0:T(8,128)(2,1)S(1)} %get-tuple-element.41), channel_id=1, source_target_pairs={{0,14},{1,15},{2,0},{3,1},{4,2},{5,3},{6,4},{7,5},{8,6},{9,7},{10,... | collective-permute-start | bytes 589832 | tf_op jit(solution)/shard_map/ppermute | solution.py:250
  118.8 6.9 %collective-permute-start.15 = (bf16[32,2048]{1,0:T(8,128)(2,1)S(1)}, bf16[32,2048]{1,0:T(8,128)(2,1)S(1)}, u32[]{:S(2)}, u32[]{:S(2)}) collective-permute-start(bf16[32,2048]{1,0:T(8,128)(2,1)S(1)} %get-tuple-element.43), channel_id=1, source_target_pairs={{0,13},{1,14},{2,15},{3,0},{4,1},{5,2},{6,3},{7,4},{8,5},{9,6},{10... | collective-permute-start | bytes 393224 | tf_op jit(solution)/shard_map/ppermute | solution.py:250
  125.7 9.8 %collective-permute-done.15.refs_8_ = bf16[32,2048]{1,0:T(8,128)(2,1)S(1)} collective-permute-done((bf16[32,2048]{1,0:T(8,128)(2,1)S(1)}, bf16[32,2048]{1,0:T(8,128)(2,1)S(1)}, u32[]{:S(2)}, u32[]{:S(2)}) %collective-permute-start.15) | collective-permute-done | bytes 131104 | tf_op jit(solution)/shard_map/ppermute | solution.py:250
  135.6 2.5 shard_map.180
  138.1 16.0 %all_to_all.20 = bf16[4,72,2048]{2,1,0:T(8,128)(2,1)} all-to-all(bf16[4,72,2048]{2,1,0:T(8,128)(2,1)S(1)} %bitcast.44), channel_id=1, replica_groups=mesh['dp'=8,'y'=4,'z'=16] {'y'}, dimensions={0} | all-to-all | bytes 2359296 | tf_op jit(solution)/shard_map/all_to_all | solution.py:254
  154.1 3.7 %all-to-all-start = ((bf16[4,96,2048]{2,1,0:T(8,128)(2,1)}), bf16[4,96,2048]{2,1,0:T(8,128)(2,1)S(1)}, u32[]{:S(2)}, u32[]{:S(2)}) async-start(bf16[4,96,2048]{2,1,0:T(8,128)(2,1)} %bitcast.49), calls=%async_computation | async-start | bytes 3145728 | tf_op jit(solution)/shard_map/all_to_all | solution.py:254
  159.2 1.3 copy-done.2
  160.4 4.6 %shard_map.181 = (bf16[288,384]{1,0:T(8,128)(2,1)S(1)}, bf16[288,768]{1,0:T(8,128)(2,1)S(1)}, bf16[288,2048]{1,0:T(8,128)(2,1)S(1)}) custom-call(s32[1]{0:T(128)} %bitcast.y_ref, bf16[288,2048]{1,0:T(8,128)(2,1)S(1)} %bitcast.40, bf16[2048,768]{1,0:T(8,128)(2,1)} %all-gather.2.cloned.1.call-done.matrix_ref, bf16[288,384]{1,0:T(8,128)(2,1)S(1)} %slice.17.cotangent_ref), custom_call_target="tpu_custom_call" | custom-call | tf_op jit(solution)/shard_map/pallas_call | solution.py:31
  167.5 4.0 %all-to-all-done = bf16[4,96,2048]{2,1,0:T(8,128)(2,1)S(1)} async-done(((bf16[4,96,2048]{2,1,0:T(8,128)(2,1)}), bf16[4,96,2048]{2,1,0:T(8,128)(2,1)S(1)}, u32[]{:S(2)}, u32[]{:S(2)}) %all-to-all-start) | async-done | bytes 1572896 | tf_op jit(solution)/shard_map/all_to_all | solution.py:254
  171.5 5.4 %shard_map.177 = (bf16[384,384]{1,0:T(8,128)(2,1)S(1)}, bf16[384,768]{1,0:T(8,128)(2,1)S(1)}, bf16[384,2048]{1,0:T(8,128)(2,1)S(1)}) custom-call(s32[1]{0:T(128)} %bitcast.y_ref, bf16[384,2048]{1,0:T(8,128)(2,1)S(1)} %bitcast.38, bf16[2048,768]{1,0:T(8,128)(2,1)} %all-gather.2.cloned.1.call-done.matrix_ref, bf16[384,384]{1,0:T(8,128)(2,1)S(1)} %slice.16.cotangent_ref), custom_call_target="tpu_custom_call" | custom-call | tf_op jit(solution)/shard_map/pallas_call | solution.py:31
  176.9 1.8 fusion.5
  178.9 3.5 %add_convert_fusion = bf16[2048,768]{1,0:T(8,128)(2,1)} fusion(f32[2048,768]{1,0:T(8,128)S(1)} %fusion.5, bf16[288,2048]{1,0:T(8,128)(2,1)S(1)} %bitcast.41, bf16[288,768]{1,0:T(8,128)(2,1)S(1)} %copy-done.24), kind=kOutput, calls=%fused_computation | convolution fusion | flops 909115392 | bytes 11059200 | tf_op jit(solution)/shard_map/dot_general | solution.py:53
  183.7 14.0 %all_to_all.21 = bf16[4,72,2048]{2,1,0:T(8,128)(2,1)S(1)} all-to-all(bf16[4,72,2048]{2,1,0:T(8,128)(2,1)S(1)} %bitcast.43), channel_id=1, replica_groups=mesh['dp'=8,'y'=4,'z'=16] {'y'}, dimensions={0} | all-to-all | bytes 2359296 | tf_op jit(solution)/shard_map/all_to_all | solution.py:254
  197.7 2.1 shard_map.182
  201.6 3.6 %all-to-all-start.3 = ((bf16[4,96,2048]{2,1,0:T(8,128)(2,1)}), bf16[4,96,2048]{2,1,0:T(8,128)(2,1)S(1)}, u32[]{:S(2)}, u32[]{:S(2)}) async-start(bf16[4,96,2048]{2,1,0:T(8,128)(2,1)} %bitcast.42), calls=%async_computation.3 | async-start | bytes 3145728 | tf_op jit(solution)/shard_map/all_to_all | solution.py:254
  205.1 10.7 %collective-permute-start.18 = (bf16[32,2048]{1,0:T(8,128)(2,1)}, bf16[32,2048]{1,0:T(8,128)(2,1)S(1)}, u32[]{:S(2)}, u32[]{:S(2)}) collective-permute-start(bf16[32,2048]{1,0:T(8,128)(2,1)} %get-tuple-element.50), channel_id=1, source_target_pairs={{0,13},{1,14},{2,15},{3,0},{4,1},{5,2},{6,3},{7,4},{8,5},{9,6},{10... | collective-permute-start | bytes 393224 | tf_op jit(solution)/shard_map/ppermute | solution.py:250
  215.9 1.9 collective-permute-start.17
  217.8 8.1 %collective-permute-start.16 = (bf16[48,2048]{1,0:T(8,128)(2,1)}, bf16[48,2048]{1,0:T(8,128)(2,1)S(1)}, u32[]{:S(2)}, u32[]{:S(2)}) collective-permute-start(bf16[48,2048]{1,0:T(8,128)(2,1)} %get-tuple-element.46), channel_id=1, source_target_pairs={{0,15},{1,0},{2,1},{3,2},{4,3},{5,4},{6,5},{7,6},{8,7},{9,8},{10,9... | collective-permute-start | bytes 589832 | tf_op jit(solution)/shard_map/ppermute | solution.py:250
  225.9 1.9 collective-permute-start.24
  227.9 1.9 collective-permute-start.25
  229.8 1.9 collective-permute-start.26
  231.8 1.3 copy-done.1
  233.6 5.1 %collective-permute-start.19 = (bf16[128,2048]{1,0:T(8,128)(2,1)S(1)}, bf16[128,2048]{1,0:T(8,128)(2,1)S(1)}, u32[]{:S(2)}, u32[]{:S(2)}) collective-permute-start(bf16[128,2048]{1,0:T(8,128)(2,1)S(1)} %shard_map.184), channel_id=1, source_target_pairs={{0,15},{1,0},{2,1},{3,2},{4,3},{5,4},{6,5},{7,6},{8,7},{9,8},{10,9... | collective-permute-start | bytes 1572872 | tf_op jit(solution)/shard_map/ppermute | solution.py:250
  238.8 8.1 %collective-permute-done.26.third_ref = bf16[32,2048]{1,0:T(8,128)(2,1)S(1)} collective-permute-done((bf16[32,2048]{1,0:T(8,128)(2,1)}, bf16[32,2048]{1,0:T(8,128)(2,1)S(1)}, u32[]{:S(2)}, u32[]{:S(2)}) %collective-permute-start.26) | collective-permute-done | bytes 131104 | tf_op jit(solution)/shard_map/ppermute | solution.py:250
  246.8 1.4 shard_map.189
  248.2 3.8 %collective-permute-start.27 = (bf16[128,2048]{1,0:T(8,128)(2,1)}, bf16[128,2048]{1,0:T(8,128)(2,1)S(1)}, u32[]{:S(2)}, u32[]{:S(2)}) collective-permute-start(bf16[128,2048]{1,0:T(8,128)(2,1)} %shard_map.189), channel_id=1, source_target_pairs={{0,1},{1,2},{2,3},{3,4},{4,5},{5,6},{6,7},{7,8},{8,9},{9,10},{10,1... | collective-permute-start | bytes 1572872 | tf_op jit(solution)/shard_map/ppermute | solution.py:250
  254.4 3.5 %collective-permute-start.20 = (bf16[128,2048]{1,0:T(8,128)(2,1)S(1)}, bf16[128,2048]{1,0:T(8,128)(2,1)S(1)}, u32[]{:S(2)}, u32[]{:S(2)}) collective-permute-start(bf16[128,2048]{1,0:T(8,128)(2,1)S(1)} %shard_map.185), channel_id=1, source_target_pairs={{0,15},{1,0},{2,1},{3,2},{4,3},{5,4},{6,5},{7,6},{8,7},{9,8},{10,9... | collective-permute-start | bytes 1572872 | tf_op jit(solution)/shard_map/ppermute | solution.py:250
  257.8 4.9 %collective-permute-done.27.sum_ref = bf16[128,2048]{1,0:T(8,128)(2,1)S(1)} collective-permute-done((bf16[128,2048]{1,0:T(8,128)(2,1)}, bf16[128,2048]{1,0:T(8,128)(2,1)S(1)}, u32[]{:S(2)}, u32[]{:S(2)}) %collective-permute-start.27) | collective-permute-done | bytes 524320 | tf_op jit(solution)/shard_map/ppermute | solution.py:250
  263.2 4.2 %collective-permute-start.28 = (bf16[128,2048]{1,0:T(8,128)(2,1)S(1)}, bf16[128,2048]{1,0:T(8,128)(2,1)S(1)}, u32[]{:S(2)}, u32[]{:S(2)}) collective-permute-start(bf16[128,2048]{1,0:T(8,128)(2,1)S(1)} %shard_map.190), channel_id=1, source_target_pairs={{0,1},{1,2},{2,3},{3,4},{4,5},{5,6},{6,7},{7,8},{8,9},{9,10},{10,1... | collective-permute-start | bytes 1572872 | tf_op jit(solution)/shard_map/ppermute | solution.py:250
  267.4 2.6 collective-permute-done.20.sum_ref
  270.5 2.3 collective-permute-start.21
  272.8 5.8 %collective-permute-done.28.sum_ref = bf16[128,2048]{1,0:T(8,128)(2,1)S(1)} collective-permute-done((bf16[128,2048]{1,0:T(8,128)(2,1)S(1)}, bf16[128,2048]{1,0:T(8,128)(2,1)S(1)}, u32[]{:S(2)}, u32[]{:S(2)}) %collective-permute-start.28) | collective-permute-done | bytes 524320 | tf_op jit(solution)/shard_map/ppermute | solution.py:250
  279.0 4.3 %collective-permute-start.29 = (bf16[128,2048]{1,0:T(8,128)(2,1)S(1)}, bf16[128,2048]{1,0:T(8,128)(2,1)S(1)}, u32[]{:S(2)}, u32[]{:S(2)}) collective-permute-start(bf16[128,2048]{1,0:T(8,128)(2,1)S(1)} %shard_map.191), channel_id=1, source_target_pairs={{0,1},{1,2},{2,3},{3,4},{4,5},{5,6},{6,7},{7,8},{8,9},{9,10},{10,1... | collective-permute-start | bytes 1572872 | tf_op jit(solution)/shard_map/ppermute | solution.py:250
  283.3 3.7 %collective-permute-done.21.sum_ref = bf16[128,2048]{1,0:T(8,128)(2,1)S(1)} collective-permute-done((bf16[128,2048]{1,0:T(8,128)(2,1)S(1)}, bf16[128,2048]{1,0:T(8,128)(2,1)S(1)}, u32[]{:S(2)}, u32[]{:S(2)}) %collective-permute-start.21) | collective-permute-done | bytes 524320 | tf_op jit(solution)/shard_map/ppermute | solution.py:250
  287.5 1.9 collective-permute-start.22
  289.4 6.0 %collective-permute-done.29.sum_ref = bf16[128,2048]{1,0:T(8,128)(2,1)S(1)} collective-permute-done((bf16[128,2048]{1,0:T(8,128)(2,1)S(1)}, bf16[128,2048]{1,0:T(8,128)(2,1)S(1)}, u32[]{:S(2)}, u32[]{:S(2)}) %collective-permute-start.29) | collective-permute-done | bytes 524320 | tf_op jit(solution)/shard_map/ppermute | solution.py:250
  295.9 4.3 %collective-permute-start.30 = (bf16[128,2048]{1,0:T(8,128)(2,1)S(1)}, bf16[128,2048]{1,0:T(8,128)(2,1)S(1)}, u32[]{:S(2)}, u32[]{:S(2)}) collective-permute-start(bf16[128,2048]{1,0:T(8,128)(2,1)S(1)} %shard_map.192), channel_id=1, source_target_pairs={{0,1},{1,2},{2,3},{3,4},{4,5},{5,6},{6,7},{7,8},{8,9},{9,10},{10,1... | collective-permute-start | bytes 1572872 | tf_op jit(solution)/shard_map/ppermute | solution.py:250
  300.2 3.6 %collective-permute-done.22.sum_ref = bf16[128,2048]{1,0:T(8,128)(2,1)S(1)} collective-permute-done((bf16[128,2048]{1,0:T(8,128)(2,1)S(1)}, bf16[128,2048]{1,0:T(8,128)(2,1)S(1)}, u32[]{:S(2)}, u32[]{:S(2)}) %collective-permute-start.22) | collective-permute-done | bytes 524320 | tf_op jit(solution)/shard_map/ppermute | solution.py:250
  305.1 2.0 collective-permute-start.23
  307.2 5.3 %collective-permute-done.30.sum_ref = bf16[128,2048]{1,0:T(8,128)(2,1)S(1)} collective-permute-done((bf16[128,2048]{1,0:T(8,128)(2,1)S(1)}, bf16[128,2048]{1,0:T(8,128)(2,1)S(1)}, u32[]{:S(2)}, u32[]{:S(2)}) %collective-permute-start.30) | collective-permute-done | bytes 524320 | tf_op jit(solution)/shard_map/ppermute | solution.py:250
  313.7 4.1 %collective-permute-start.31 = (bf16[128,2048]{1,0:T(8,128)(2,1)}, bf16[128,2048]{1,0:T(8,128)(2,1)}, u32[]{:S(2)}, u32[]{:S(2)}) collective-permute-start(bf16[128,2048]{1,0:T(8,128)(2,1)} %shard_map.193), channel_id=1, source_target_pairs={{0,1},{1,2},{2,3},{3,4},{4,5},{5,6},{6,7},{7,8},{8,9},{9,10},{10,1... | collective-permute-start | bytes 1572872 | tf_op jit(solution)/shard_map/ppermute | solution.py:250
  317.8 1.7 shard_map.183
  321.5 4.8 %collective-permute-done.31.down_ref = bf16[128,2048]{1,0:T(8,128)(2,1)} collective-permute-done((bf16[128,2048]{1,0:T(8,128)(2,1)}, bf16[128,2048]{1,0:T(8,128)(2,1)}, u32[]{:S(2)}, u32[]{:S(2)}) %collective-permute-start.31) | collective-permute-done | bytes 524320 | tf_op jit(solution)/shard_map/ppermute | solution.py:250
  326.3 2.5 shard_map.194
  (126 shorter events, 29.5 us)
Async XLA Ops:
  7.2 83.6 %copy-start.32 = (s32[16,384]{1,0:T(8,128)S(1)}, s32[16,384]{1,0:T(8,128)}, u32[]{:S(2)}) copy-start(s32[16,384]{1,0:T(8,128)} %constant.51.clone.map_ref) | copy-start | bytes 73732
  7.2 3.5 %copy-start.19 = (bf16[1,128,2048]{2,1,0:T(8,128)(2,1)S(1)}, bf16[1,128,2048]{2,1,0:T(8,128)(2,1)}, u32[]{:S(2)}) copy-start(bf16[1,128,2048]{2,1,0:T(8,128)(2,1)} %param.15) | copy-start | bytes 1572868
  7.2 152.0 %all-gather.2.cloned.1.call-start = ((), (), s32[]{:S(2)}) async-start(), calls=%async_computation.5 | async-start | bytes 3538944 | tf_op jit(solution)/shard_map/all_gather | solution.py:258
  11.1 24.0 %collective-permute-start.1 = (bf16[128,2176]{1,0:T(8,128)(2,1)S(1)}, bf16[128,2176]{1,0:T(8,128)(2,1)S(1)}, u32[]{:S(2)}, u32[]{:S(2)}) collective-permute-start(bf16[128,2176]{1,0:T(8,128)(2,1)S(1)} %shard_map.174.refs_0_), channel_id=1, source_target_pairs={{0,1},{1,2},{2,3},{3,4},{4,5},{5,6},{6,7},{7,8},{8,9},{9,10},{10,1... | collective-permute-start | bytes 1671176 | tf_op jit(solution)/shard_map/ppermute | solution.py:250
  15.0 22.1 %collective-permute-start = (bf16[128,2176]{1,0:T(8,128)(2,1)S(1)}, bf16[128,2176]{1,0:T(8,128)(2,1)S(1)}, u32[]{:S(2)}, u32[]{:S(2)}) collective-permute-start(bf16[128,2176]{1,0:T(8,128)(2,1)S(1)} %shard_map.174.refs_0_), channel_id=1, source_target_pairs={{0,15},{1,0},{2,1},{3,2},{4,3},{5,4},{6,5},{7,6},{8,7},{9,8},{10,9... | collective-permute-start | bytes 1671176 | tf_op jit(solution)/shard_map/ppermute | solution.py:250
  35.2 16.9 %collective-permute-start.3 = (bf16[128,2176]{1,0:T(8,128)(2,1)S(1)}, bf16[128,2176]{1,0:T(8,128)(2,1)S(1)}, u32[]{:S(2)}, u32[]{:S(2)}) collective-permute-start(bf16[128,2176]{1,0:T(8,128)(2,1)S(1)} %collective-permute-done.1.refs_2_), channel_id=1, source_target_pairs={{0,1},{1,2},{2,3},{3,4},{4,5},{5,6},{6,7},{7,8},{8,9},{9,10},{10,1... | collective-permute-start | bytes 1671176 | tf_op jit(solution)/shard_map/ppermute | solution.py:250
  37.1 17.7 %collective-permute-start.2 = (bf16[128,2176]{1,0:T(8,128)(2,1)S(1)}, bf16[128,2176]{1,0:T(8,128)(2,1)S(1)}, u32[]{:S(2)}, u32[]{:S(2)}) collective-permute-start(bf16[128,2176]{1,0:T(8,128)(2,1)S(1)} %collective-permute-done.refs_1_), channel_id=1, source_target_pairs={{0,15},{1,0},{2,1},{3,2},{4,3},{5,4},{6,5},{7,6},{8,7},{9,8},{10,9... | collective-permute-start | bytes 1671176 | tf_op jit(solution)/shard_map/ppermute | solution.py:250
  52.1 16.0 %collective-permute-start.5 = (bf16[128,2176]{1,0:T(8,128)(2,1)S(1)}, bf16[128,2176]{1,0:T(8,128)(2,1)S(1)}, u32[]{:S(2)}, u32[]{:S(2)}) collective-permute-start(bf16[128,2176]{1,0:T(8,128)(2,1)S(1)} %collective-permute-done.3.refs_4_), channel_id=1, source_target_pairs={{0,1},{1,2},{2,3},{3,4},{4,5},{5,6},{6,7},{7,8},{8,9},{9,10},{10,1... | collective-permute-start | bytes 1671176 | tf_op jit(solution)/shard_map/ppermute | solution.py:250
  54.8 16.0 %collective-permute-start.4 = (bf16[128,2176]{1,0:T(8,128)(2,1)S(1)}, bf16[128,2176]{1,0:T(8,128)(2,1)S(1)}, u32[]{:S(2)}, u32[]{:S(2)}) collective-permute-start(bf16[128,2176]{1,0:T(8,128)(2,1)S(1)} %collective-permute-done.2.refs_3_), channel_id=1, source_target_pairs={{0,15},{1,0},{2,1},{3,2},{4,3},{5,4},{6,5},{7,6},{8,7},{9,8},{10,9... | collective-permute-start | bytes 1671176 | tf_op jit(solution)/shard_map/ppermute | solution.py:250
  68.0 15.2 %collective-permute-start.7 = (bf16[128,2176]{1,0:T(8,128)(2,1)S(1)}, bf16[128,2176]{1,0:T(8,128)(2,1)}, u32[]{:S(2)}, u32[]{:S(2)}) collective-permute-start(bf16[128,2176]{1,0:T(8,128)(2,1)S(1)} %collective-permute-done.5.refs_6_), channel_id=1, source_target_pairs={{0,1},{1,2},{2,3},{3,4},{4,5},{5,6},{6,7},{7,8},{8,9},{9,10},{10,1... | collective-permute-start | bytes 1671176 | tf_op jit(solution)/shard_map/ppermute | solution.py:250
  70.8 14.4 %collective-permute-start.6 = (bf16[128,2176]{1,0:T(8,128)(2,1)S(1)}, bf16[128,2176]{1,0:T(8,128)(2,1)}, u32[]{:S(2)}, u32[]{:S(2)}) collective-permute-start(bf16[128,2176]{1,0:T(8,128)(2,1)S(1)} %collective-permute-done.4.refs_5_), channel_id=1, source_target_pairs={{0,15},{1,0},{2,1},{3,2},{4,3},{5,4},{6,5},{7,6},{8,7},{9,8},{10,9... | collective-permute-start | bytes 1671176 | tf_op jit(solution)/shard_map/ppermute | solution.py:250
  83.2 18.3 %collective-permute-start.9 = (bf16[128,2176]{1,0:T(8,128)(2,1)}, bf16[128,2176]{1,0:T(8,128)(2,1)S(1)}, u32[]{:S(2)}, u32[]{:S(2)}) collective-permute-start(bf16[128,2176]{1,0:T(8,128)(2,1)} %collective-permute-done.7.refs_8_), channel_id=1, source_target_pairs={{0,1},{1,2},{2,3},{3,4},{4,5},{5,6},{6,7},{7,8},{8,9},{9,10},{10,1... | collective-permute-start | bytes 1671176 | tf_op jit(solution)/shard_map/ppermute | solution.py:250
  85.1 25.2 %collective-permute-start.8 = (bf16[128,2176]{1,0:T(8,128)(2,1)}, bf16[128,2176]{1,0:T(8,128)(2,1)S(1)}, u32[]{:S(2)}, u32[]{:S(2)}) collective-permute-start(bf16[128,2176]{1,0:T(8,128)(2,1)} %collective-permute-done.6.refs_7_), channel_id=1, source_target_pairs={{0,15},{1,0},{2,1},{3,2},{4,3},{5,4},{6,5},{7,6},{8,7},{9,8},{10,9... | collective-permute-start | bytes 1671176 | tf_op jit(solution)/shard_map/ppermute | solution.py:250
  90.8 1.1 copy-start.10
  91.9 1.1 copy-start.12
  92.9 1.1 copy-start.14
  94.0 1.1 copy-start.16
  95.0 1.1 copy-start.18
  96.1 5.4 %copy-start.34 = (s32[8,128]{1,0:T(8,128)S(1)}, s32[8,128]{1,0:T(8,128)}, u32[]{:S(2)}) copy-start(s32[8,128]{1,0:T(8,128)} %constant.52.clone.map_ref) | copy-start | bytes 12292
  96.1 14.2 %copy-start.33 = (s32[8,128]{1,0:T(8,128)S(1)}, s32[8,128]{1,0:T(8,128)}, u32[]{:S(2)}) copy-start(s32[8,128]{1,0:T(8,128)} %constant.53.clone.map_ref) | copy-start | bytes 12292
  96.1 39.5 %copy-start.7 = (s32[288,8]{1,0:T(8,128)S(1)}, s32[288,8]{1,0:T(8,128)}, u32[]{:S(2)}) copy-start(s32[288,8]{1,0:T(8,128)} %constant.55.clone.refs_2_.place_ref) | copy-start | bytes 27652
  96.1 39.5 %copy-start.31 = (s32[16,288]{1,0:T(8,128)S(1)}, s32[16,288]{1,0:T(8,128)}, u32[]{:S(2)}) copy-start(s32[16,288]{1,0:T(8,128)} %constant.54.clone.map_ref) | copy-start | bytes 55300
  102.0 16.8 %collective-permute-start.14 = (bf16[32,2048]{1,0:T(8,128)(2,1)S(1)}, bf16[32,2048]{1,0:T(8,128)(2,1)S(1)}, u32[]{:S(2)}, u32[]{:S(2)}) collective-permute-start(bf16[32,2048]{1,0:T(8,128)(2,1)S(1)} %get-tuple-element.42), channel_id=1, source_target_pairs={{0,3},{1,4},{2,5},{3,6},{4,7},{5,8},{6,9},{7,10},{8,11},{9,12},{10... | collective-permute-start | bytes 393224 | tf_op jit(solution)/shard_map/ppermute | solution.py:250
  103.9 31.6 %collective-permute-start.10 = (bf16[48,2048]{1,0:T(8,128)(2,1)S(1)}, bf16[48,2048]{1,0:T(8,128)(2,1)S(1)}, u32[]{:S(2)}, u32[]{:S(2)}) collective-permute-start(bf16[48,2048]{1,0:T(8,128)(2,1)S(1)} %get-tuple-element.37), channel_id=1, source_target_pairs={{0,1},{1,2},{2,3},{3,4},{4,5},{5,6},{6,7},{7,8},{8,9},{9,10},{10,1... | collective-permute-start | bytes 589832 | tf_op jit(solution)/shard_map/ppermute | solution.py:250
  106.2 29.3 %collective-permute-start.12 = (bf16[48,2048]{1,0:T(8,128)(2,1)S(1)}, bf16[48,2048]{1,0:T(8,128)(2,1)S(1)}, u32[]{:S(2)}, u32[]{:S(2)}) collective-permute-start(bf16[48,2048]{1,0:T(8,128)(2,1)S(1)} %get-tuple-element.40), channel_id=1, source_target_pairs={{0,2},{1,3},{2,4},{3,5},{4,6},{5,7},{6,8},{7,9},{8,10},{9,11},{10,... | collective-permute-start | bytes 589832 | tf_op jit(solution)/shard_map/ppermute | solution.py:250
  111.4 24.1 %collective-permute-start.11 = (bf16[48,2048]{1,0:T(8,128)(2,1)S(1)}, bf16[48,2048]{1,0:T(8,128)(2,1)S(1)}, u32[]{:S(2)}, u32[]{:S(2)}) collective-permute-start(bf16[48,2048]{1,0:T(8,128)(2,1)S(1)} %get-tuple-element.39), channel_id=1, source_target_pairs={{0,15},{1,0},{2,1},{3,2},{4,3},{5,4},{6,5},{7,6},{8,7},{9,8},{10,9... | collective-permute-start | bytes 589832 | tf_op jit(solution)/shard_map/ppermute | solution.py:250
  114.0 21.6 %collective-permute-start.13 = (bf16[48,2048]{1,0:T(8,128)(2,1)S(1)}, bf16[48,2048]{1,0:T(8,128)(2,1)S(1)}, u32[]{:S(2)}, u32[]{:S(2)}) collective-permute-start(bf16[48,2048]{1,0:T(8,128)(2,1)S(1)} %get-tuple-element.41), channel_id=1, source_target_pairs={{0,14},{1,15},{2,0},{3,1},{4,2},{5,3},{6,4},{7,5},{8,6},{9,7},{10,... | collective-permute-start | bytes 589832 | tf_op jit(solution)/shard_map/ppermute | solution.py:250
  118.8 16.7 %collective-permute-start.15 = (bf16[32,2048]{1,0:T(8,128)(2,1)S(1)}, bf16[32,2048]{1,0:T(8,128)(2,1)S(1)}, u32[]{:S(2)}, u32[]{:S(2)}) collective-permute-start(bf16[32,2048]{1,0:T(8,128)(2,1)S(1)} %get-tuple-element.43), channel_id=1, source_target_pairs={{0,13},{1,14},{2,15},{3,0},{4,1},{5,2},{6,3},{7,4},{8,5},{9,6},{10... | collective-permute-start | bytes 393224 | tf_op jit(solution)/shard_map/ppermute | solution.py:250
  154.1 4.0 %copy-start.37 = (s32[672]{0:T(1024)S(1)}, s32[672]{0:T(1024)}, u32[]{:S(2)}) copy-start(s32[672]{0:T(1024)} %constant.49.clone) | copy-start | bytes 8068
  154.1 4.0 %copy-start.38 = (s32[672]{0:T(1024)S(1)}, s32[672]{0:T(1024)}, u32[]{:S(2)}) copy-start(s32[672]{0:T(1024)} %constant.48.clone) | copy-start | bytes 8068
  154.1 4.0 %copy-start.39 = (s32[672]{0:T(1024)S(1)}, s32[672]{0:T(1024)}, u32[]{:S(2)}) copy-start(s32[672]{0:T(1024)} %constant.47.clone) | copy-start | bytes 8068
  154.1 4.0 %copy-start.40 = (pred[672]{0:T(1024)(128)(4,1)S(1)}, pred[672]{0:T(1024)(128)(4,1)}, u32[]{:S(2)}) copy-start(pred[672]{0:T(1024)(128)(4,1)} %constant.50.clone) | copy-start | bytes 2020
  154.1 4.2 %copy-start.22 = (bf16[1,1,640,384]{3,2,1,0:T(8,128)(2,1)S(1)}, bf16[1,1,640,384]{3,2,1,0:T(8,128)(2,1)}, u32[]{:S(2)}) copy-start(bf16[1,1,640,384]{3,2,1,0:T(8,128)(2,1)} %param.20) | copy-start | bytes 1474564
  154.1 17.4 %all-to-all-start = ((bf16[4,96,2048]{2,1,0:T(8,128)(2,1)}), bf16[4,96,2048]{2,1,0:T(8,128)(2,1)S(1)}, u32[]{:S(2)}, u32[]{:S(2)}) async-start(bf16[4,96,2048]{2,1,0:T(8,128)(2,1)} %bitcast.49), calls=%async_computation | async-start | bytes 3145728 | tf_op jit(solution)/shard_map/all_to_all | solution.py:254
  157.8 161.7 %reduce-scatter.2.cloned.1.call-start = ((), (), s32[]{:S(2)}) async-start(), calls=%async_computation.6 | async-start | bytes 3538944 | tf_op jit(solution)/shard_map/reduce_scatter | solution.py:321
  159.1 1.3 copy-start.2
  165.0 1.0 copy-start.5
  176.9 1.9 copy-start.4
  176.9 1.9 copy-start.25
  176.9 1.9 copy-start.3
  176.9 2.0 copy-start.24
  182.4 1.3 copy-start.6
  182.4 15.3 %copy-start.8 = (s32[288,8]{1,0:T(8,128)S(1)}, s32[288,8]{1,0:T(8,128)}, u32[]{:S(2)}) copy-start(s32[288,8]{1,0:T(8,128)} %constant.55.clone.refs_2_.place_ref) | copy-start | bytes 27652
  201.5 45.4 %copy-start.30 = (bf16[128,128]{1,0:T(8,128)(2,1)S(1)}, bf16[128,128]{1,0:T(8,128)(2,1)}, u32[]{:S(2)}) copy-start(bf16[128,128]{1,0:T(8,128)(2,1)} %copy-done.29) | copy-start | bytes 98308
  201.6 51.3 %all-to-all-start.3 = ((bf16[4,96,2048]{2,1,0:T(8,128)(2,1)}), bf16[4,96,2048]{2,1,0:T(8,128)(2,1)S(1)}, u32[]{:S(2)}, u32[]{:S(2)}) async-start(bf16[4,96,2048]{2,1,0:T(8,128)(2,1)} %bitcast.42), calls=%async_computation.3 | async-start | bytes 3145728 | tf_op jit(solution)/shard_map/all_to_all | solution.py:254
  205.1 24.6 %collective-permute-start.18 = (bf16[32,2048]{1,0:T(8,128)(2,1)}, bf16[32,2048]{1,0:T(8,128)(2,1)S(1)}, u32[]{:S(2)}, u32[]{:S(2)}) collective-permute-start(bf16[32,2048]{1,0:T(8,128)(2,1)} %get-tuple-element.50), channel_id=1, source_target_pairs={{0,13},{1,14},{2,15},{3,0},{4,1},{5,2},{6,3},{7,4},{8,5},{9,6},{10... | collective-permute-start | bytes 393224 | tf_op jit(solution)/shard_map/ppermute | solution.py:250
  215.9 15.9 %collective-permute-start.17 = (bf16[48,2048]{1,0:T(8,128)(2,1)}, bf16[48,2048]{1,0:T(8,128)(2,1)S(1)}, u32[]{:S(2)}, u32[]{:S(2)}) collective-permute-start(bf16[48,2048]{1,0:T(8,128)(2,1)} %get-tuple-element.49), channel_id=1, source_target_pairs={{0,14},{1,15},{2,0},{3,1},{4,2},{5,3},{6,4},{7,5},{8,6},{9,7},{10,... | collective-permute-start | bytes 589832 | tf_op jit(solution)/shard_map/ppermute | solution.py:250
  217.8 14.0 %collective-permute-start.16 = (bf16[48,2048]{1,0:T(8,128)(2,1)}, bf16[48,2048]{1,0:T(8,128)(2,1)S(1)}, u32[]{:S(2)}, u32[]{:S(2)}) collective-permute-start(bf16[48,2048]{1,0:T(8,128)(2,1)} %get-tuple-element.46), channel_id=1, source_target_pairs={{0,15},{1,0},{2,1},{3,2},{4,3},{5,4},{6,5},{7,6},{8,7},{9,8},{10,9... | collective-permute-start | bytes 589832 | tf_op jit(solution)/shard_map/ppermute | solution.py:250
  225.9 20.9 %collective-permute-start.24 = (bf16[48,2048]{1,0:T(8,128)(2,1)}, bf16[48,2048]{1,0:T(8,128)(2,1)S(1)}, u32[]{:S(2)}, u32[]{:S(2)}) collective-permute-start(bf16[48,2048]{1,0:T(8,128)(2,1)} %get-tuple-element.60), channel_id=1, source_target_pairs={{0,1},{1,2},{2,3},{3,4},{4,5},{5,6},{6,7},{7,8},{8,9},{9,10},{10,1... | collective-permute-start | bytes 589832 | tf_op jit(solution)/shard_map/ppermute | solution.py:250
  227.9 19.0 %collective-permute-start.25 = (bf16[48,2048]{1,0:T(8,128)(2,1)}, bf16[48,2048]{1,0:T(8,128)(2,1)S(1)}, u32[]{:S(2)}, u32[]{:S(2)}) collective-permute-start(bf16[48,2048]{1,0:T(8,128)(2,1)} %copy-done.35), channel_id=1, source_target_pairs={{0,2},{1,3},{2,4},{3,5},{4,6},{5,7},{6,8},{7,9},{8,10},{9,11},{10,... | collective-permute-start | bytes 589832 | tf_op jit(solution)/shard_map/ppermute | solution.py:250
  229.8 17.0 %collective-permute-start.26 = (bf16[32,2048]{1,0:T(8,128)(2,1)}, bf16[32,2048]{1,0:T(8,128)(2,1)S(1)}, u32[]{:S(2)}, u32[]{:S(2)}) collective-permute-start(bf16[32,2048]{1,0:T(8,128)(2,1)} %copy-done.36), channel_id=1, source_target_pairs={{0,3},{1,4},{2,5},{3,6},{4,7},{5,8},{6,9},{7,10},{8,11},{9,12},{10... | collective-permute-start | bytes 393224 | tf_op jit(solution)/shard_map/ppermute | solution.py:250
  231.8 1.3 copy-start.1
  233.6 18.5 %collective-permute-start.19 = (bf16[128,2048]{1,0:T(8,128)(2,1)S(1)}, bf16[128,2048]{1,0:T(8,128)(2,1)S(1)}, u32[]{:S(2)}, u32[]{:S(2)}) collective-permute-start(bf16[128,2048]{1,0:T(8,128)(2,1)S(1)} %shard_map.184), channel_id=1, source_target_pairs={{0,15},{1,0},{2,1},{3,2},{4,3},{5,4},{6,5},{7,6},{8,7},{9,8},{10,9... | collective-permute-start | bytes 1572872 | tf_op jit(solution)/shard_map/ppermute | solution.py:250
  248.2 14.5 %collective-permute-start.27 = (bf16[128,2048]{1,0:T(8,128)(2,1)}, bf16[128,2048]{1,0:T(8,128)(2,1)S(1)}, u32[]{:S(2)}, u32[]{:S(2)}) collective-permute-start(bf16[128,2048]{1,0:T(8,128)(2,1)} %shard_map.189), channel_id=1, source_target_pairs={{0,1},{1,2},{2,3},{3,4},{4,5},{5,6},{6,7},{7,8},{8,9},{9,10},{10,1... | collective-permute-start | bytes 1572872 | tf_op jit(solution)/shard_map/ppermute | solution.py:250
  254.4 15.7 %collective-permute-start.20 = (bf16[128,2048]{1,0:T(8,128)(2,1)S(1)}, bf16[128,2048]{1,0:T(8,128)(2,1)S(1)}, u32[]{:S(2)}, u32[]{:S(2)}) collective-permute-start(bf16[128,2048]{1,0:T(8,128)(2,1)S(1)} %shard_map.185), channel_id=1, source_target_pairs={{0,15},{1,0},{2,1},{3,2},{4,3},{5,4},{6,5},{7,6},{8,7},{9,8},{10,9... | collective-permute-start | bytes 1572872 | tf_op jit(solution)/shard_map/ppermute | solution.py:250
  263.2 15.4 %collective-permute-start.28 = (bf16[128,2048]{1,0:T(8,128)(2,1)S(1)}, bf16[128,2048]{1,0:T(8,128)(2,1)S(1)}, u32[]{:S(2)}, u32[]{:S(2)}) collective-permute-start(bf16[128,2048]{1,0:T(8,128)(2,1)S(1)} %shard_map.190), channel_id=1, source_target_pairs={{0,1},{1,2},{2,3},{3,4},{4,5},{5,6},{6,7},{7,8},{8,9},{9,10},{10,1... | collective-permute-start | bytes 1572872 | tf_op jit(solution)/shard_map/ppermute | solution.py:250
  270.5 16.5 %collective-permute-start.21 = (bf16[128,2048]{1,0:T(8,128)(2,1)S(1)}, bf16[128,2048]{1,0:T(8,128)(2,1)S(1)}, u32[]{:S(2)}, u32[]{:S(2)}) collective-permute-start(bf16[128,2048]{1,0:T(8,128)(2,1)S(1)} %shard_map.186), channel_id=1, source_target_pairs={{0,15},{1,0},{2,1},{3,2},{4,3},{5,4},{6,5},{7,6},{8,7},{9,8},{10,9... | collective-permute-start | bytes 1572872 | tf_op jit(solution)/shard_map/ppermute | solution.py:250
  279.0 16.4 %collective-permute-start.29 = (bf16[128,2048]{1,0:T(8,128)(2,1)S(1)}, bf16[128,2048]{1,0:T(8,128)(2,1)S(1)}, u32[]{:S(2)}, u32[]{:S(2)}) collective-permute-start(bf16[128,2048]{1,0:T(8,128)(2,1)S(1)} %shard_map.191), channel_id=1, source_target_pairs={{0,1},{1,2},{2,3},{3,4},{4,5},{5,6},{6,7},{7,8},{8,9},{9,10},{10,1... | collective-permute-start | bytes 1572872 | tf_op jit(solution)/shard_map/ppermute | solution.py:250
  287.5 16.4 %collective-permute-start.22 = (bf16[128,2048]{1,0:T(8,128)(2,1)S(1)}, bf16[128,2048]{1,0:T(8,128)(2,1)S(1)}, u32[]{:S(2)}, u32[]{:S(2)}) collective-permute-start(bf16[128,2048]{1,0:T(8,128)(2,1)S(1)} %shard_map.187), channel_id=1, source_target_pairs={{0,15},{1,0},{2,1},{3,2},{4,3},{5,4},{6,5},{7,6},{8,7},{9,8},{10,9... | collective-permute-start | bytes 1572872 | tf_op jit(solution)/shard_map/ppermute | solution.py:250
  295.9 16.5 %collective-permute-start.30 = (bf16[128,2048]{1,0:T(8,128)(2,1)S(1)}, bf16[128,2048]{1,0:T(8,128)(2,1)S(1)}, u32[]{:S(2)}, u32[]{:S(2)}) collective-permute-start(bf16[128,2048]{1,0:T(8,128)(2,1)S(1)} %shard_map.192), channel_id=1, source_target_pairs={{0,1},{1,2},{2,3},{3,4},{4,5},{5,6},{6,7},{7,8},{8,9},{9,10},{10,1... | collective-permute-start | bytes 1572872 | tf_op jit(solution)/shard_map/ppermute | solution.py:250
  305.1 12.7 %copy-start.26 = (bf16[384,384]{1,0:T(8,128)(2,1)S(1)}, bf16[384,384]{1,0:T(8,128)(2,1)}, u32[]{:S(2)}) copy-start(bf16[384,384]{1,0:T(8,128)(2,1)} %copy-done.25) | copy-start | bytes 884740
  305.1 12.7 %copy-start.28 = (bf16[288,384]{1,0:T(8,128)(2,1)S(1)}, bf16[288,384]{1,0:T(8,128)(2,1)}, u32[]{:S(2)}) copy-start(bf16[288,384]{1,0:T(8,128)(2,1)} %copy-done.27) | copy-start | bytes 663556
  305.1 16.4 %collective-permute-start.23 = (bf16[128,2048]{1,0:T(8,128)(2,1)}, bf16[128,2048]{1,0:T(8,128)(2,1)S(1)}, u32[]{:S(2)}, u32[]{:S(2)}) collective-permute-start(bf16[128,2048]{1,0:T(8,128)(2,1)} %shard_map.188), channel_id=1, source_target_pairs={{0,15},{1,0},{2,1},{3,2},{4,3},{5,4},{6,5},{7,6},{8,7},{9,8},{10,9... | collective-permute-start | bytes 1572872 | tf_op jit(solution)/shard_map/ppermute | solution.py:250
  313.7 12.6 %collective-permute-start.31 = (bf16[128,2048]{1,0:T(8,128)(2,1)}, bf16[128,2048]{1,0:T(8,128)(2,1)}, u32[]{:S(2)}, u32[]{:S(2)}) collective-permute-start(bf16[128,2048]{1,0:T(8,128)(2,1)} %shard_map.193), channel_id=1, source_target_pairs={{0,1},{1,2},{2,3},{3,4},{4,5},{5,6},{6,7},{7,8},{8,9},{9,10},{10,1... | collective-permute-start | bytes 1572872 | tf_op jit(solution)/shard_map/ppermute | solution.py:250
  (13 other events, 10.4 us)
Sparse Core Ops, SparseCore 0:
  10.7 38.7 all-gather.1
  182.6 42.2 reduce-scatter.1

commit v4 on v1

v4 whole, which is shorter than its diff:
```python
import functools

import jax
import jax.numpy as jnp
import numpy as np
from jax import lax
from jax.experimental import pallas as pl
from jax.experimental.pallas import tpu as pltpu
from jax.sharding import Mesh, PartitionSpec as P

N_Y = 4
N_Z = 16
DIRECT = 512
VMEM_BYTES = 48 * 1024 * 1024


def routing_kernel(ids_ref, weights_ref, out_ref):
    rows, tokens = out_ref.shape
    row = lax.broadcasted_iota(jnp.int32, (rows, tokens), 0)
    kind = row % 8
    device = row // 8
    expert = jnp.where(kind < N_Y, kind * N_Z + device % N_Z, device)
    hits = jnp.zeros((rows, tokens), jnp.float32)
    eighths = jnp.zeros((rows, tokens), jnp.float32)
    for choice in range(ids_ref.shape[0]):
        named = ids_ref[choice : choice + 1, :] == expert
        hits = hits + jnp.where(named, 1.0, 0.0)
        eighths = eighths + jnp.where(named, weights_ref[choice : choice + 1, :].astype(jnp.float32), 0.0)
    earlier = lax.broadcasted_iota(jnp.int32, (tokens, tokens), 0)
    later = lax.broadcasted_iota(jnp.int32, (tokens, tokens), 1)
    triangle = jnp.where(earlier < later, 1.0, 0.0).astype(jnp.bfloat16)
    rank = jnp.dot(hits.astype(jnp.bfloat16), triangle, preferred_element_type=jnp.float32)
    rank = jnp.where(hits > 0.0, rank, -1.0)
    out_ref[...] = jnp.where(kind <= N_Y, rank, eighths).astype(jnp.bfloat16)


def slot_matrix(slot_ref, part, part_slots, part_tokens):
    columns = slice(part * part_tokens, (part + 1) * part_tokens)
    slot = lax.broadcasted_iota(jnp.int32, (part_slots, part_tokens), 0) + part * part_slots
    return jnp.concatenate(
        [jnp.where(slot_ref[y : y + 1, columns] == slot, 1.0, 0.0).astype(jnp.bfloat16) for y in range(N_Y)],
        axis=0,
    )


def pick_kernel(parts, slot_ref, tokens_ref, out_ref):
    part_slots = out_ref.shape[1] // parts
    part_tokens = tokens_ref.shape[0] // parts
    for part in range(parts):
        select = slot_matrix(slot_ref, part, part_slots, part_tokens)
        picked = jnp.dot(
            select,
            tokens_ref[part * part_tokens : (part + 1) * part_tokens, :],
            preferred_element_type=jnp.float32,
        ).astype(jnp.bfloat16)
        for y in range(N_Y):
            out_ref[y, part * part_slots : (part + 1) * part_slots, :] = picked[
                y * part_slots : (y + 1) * part_slots, :
            ]


def add_kernel(parts, slot_ref, grads_ref, out_ref):
    part_slots = grads_ref.shape[1] // parts
    part_tokens = out_ref.shape[0] // parts
    for part in range(parts):
        select = slot_matrix(slot_ref, part, part_slots, part_tokens)
        rows = jnp.concatenate(
            [grads_ref[y, part * part_slots : (part + 1) * part_slots, :] for y in range(N_Y)], axis=0
        )
        out_ref[part * part_tokens : (part + 1) * part_tokens, :] = lax.dot_general(
            select, rows, (((0,), (0,)), ((), ())), preferred_element_type=jnp.float32
        ).astype(jnp.bfloat16)


def dot(a, b, contract=(1, 0)):
    return lax.dot_general(
        a, b, (((contract[0],), (contract[1],)), ((), ())), preferred_element_type=jnp.float32
    )


def direct_pick_kernel(rank_ref, expert_ref, place_ref, tokens_ref, out_ref, select_ref):
    rows = out_ref.shape[0]
    spread = lax.broadcasted_iota(jnp.int32, (rows, rank_ref.shape[0]), 1) == expert_ref[...]
    rank = dot(jnp.where(spread, 1.0, 0.0).astype(jnp.bfloat16), rank_ref[...])
    select = jnp.where(rank == place_ref[...].astype(jnp.float32), 1.0, 0.0).astype(jnp.bfloat16)
    select_ref[...] = select
    out_ref[...] = dot(select, tokens_ref[...]).astype(jnp.bfloat16)


def expert_kernel(
    direct_ref, rows_ref, matrix_ref, weight_ref, cotangent_ref, hidden_ref, grad_ref, row_grads_ref
):
    units = hidden_ref.shape[1]
    width = direct_ref.shape[1]
    pre = dot(direct_ref[...], matrix_ref[:width, :]) + dot(rows_ref[...], matrix_ref[width:, :])
    gate_pre, up_pre = pre[:, :units], pre[:, units:]
    weight = weight_ref[...]
    sigmoid_gate = jax.nn.sigmoid(gate_pre)
    activation = gate_pre * sigmoid_gate
    hidden_ref[...] = (activation * up_pre * weight).astype(jnp.bfloat16)
    act_slope = sigmoid_gate * (1.0 + gate_pre * (1.0 - sigmoid_gate))
    scaled = cotangent_ref[...].astype(jnp.float32) * weight
    grad_ref[:, :units] = (scaled * up_pre * act_slope).astype(jnp.bfloat16)
    grad_ref[:, units:] = (scaled * activation).astype(jnp.bfloat16)
    row_grads_ref[...] = dot(grad_ref[...], matrix_ref[width:, :], (1, 1)).astype(jnp.bfloat16)


def call(kernel, out_shape, *operands):
    whole = pl.BlockSpec(memory_space=pltpu.VMEM)
    return pl.pallas_call(
        kernel,
        out_shape=out_shape,
        in_specs=[whole] * len(operands),
        out_specs=jax.tree.map(lambda _: whole, out_shape),
        compiler_params=pltpu.CompilerParams(vmem_limit_bytes=VMEM_BYTES),
    )(*operands)


def array(shape):
    return jax.ShapeDtypeStruct(shape, jnp.bfloat16)


def after(value, *others):
    return lax.optimization_barrier((value,) + others)[0]


def shards(tokens, expert_ids, route_weights, gate_weight, up_weight, cotangent):
    experts = N_Y * N_Z
    groups = lax.axis_size("dp")
    slot_count, units = cotangent.shape[2:]
    capacity = slot_count // experts
    row_slots = N_Z * capacity
    block, model_width = tokens.shape[1:]
    width = model_width - DIRECT

    def exchange(rows):
        parts = rows.reshape(N_Y, row_slots, rows.shape[1])
        return lax.all_to_all(parts, "y", 0, 0, tiled=True).reshape(rows.shape)

    def exchange_direct(rows):
        parts = rows.reshape(experts, 8, capacity * DIRECT // 8)
        return lax.all_to_all(parts, ("y", "z"), 0, 0, tiled=True).reshape(rows.shape)

    gathered = lax.all_gather(tokens[0, :, DIRECT:], "z", axis=0, tiled=True)

    told = call(routing_kernel, array((experts * 8, block)), expert_ids[0].T, route_weights[0].T)
    told = told.reshape(experts, 8, block)
    heard = lax.all_to_all(told, ("y", "z"), 0, 0, tiled=True)
    own_row = lax.dynamic_slice_in_dim(heard, lax.axis_index("y") * N_Z, N_Z, axis=0)
    rank = jnp.transpose(own_row[:, :N_Y], (1, 0, 2)).astype(jnp.int32)
    base = capacity * jnp.arange(N_Z, dtype=jnp.int32)[None, :, None]
    slot_of = jnp.where(rank >= 0, rank + base, -1).reshape(N_Y, N_Z * block)
    places = jnp.arange(capacity, dtype=jnp.int32).astype(jnp.bfloat16)
    weight_col = jnp.sum(
        jnp.where(
            heard[:, N_Y, None, :] == places[None, :, None],
            heard[:, N_Y + 1, None, :].astype(jnp.float32),
            0.0,
        ),
        axis=2,
    ).reshape(slot_count, 1) / 8.0

    slots = np.arange(slot_count, dtype=np.int32)[:, None]
    direct, select = call(
        direct_pick_kernel,
        (array((slot_count, DIRECT)), array((slot_count, block))),
        told[:, N_Y],
        jnp.asarray(slots // capacity),
        jnp.asarray(slots % capacity),
        tokens[0, :, :DIRECT],
    )
    direct = exchange_direct(direct)

    stacked = jnp.concatenate((gate_weight[0], up_weight[0]), axis=1)
    matrix = lax.all_to_all(
        jnp.broadcast_to(stacked[None], (groups,) + stacked.shape), "dp", 0, 0, tiled=True
    ).reshape(model_width, 2 * units)

    picked = call(functools.partial(pick_kernel, 2), array((N_Y, row_slots, width)), slot_of, gathered)
    rows = exchange(picked.reshape(slot_count, width))
    hidden, grads, row_grads = call(
        expert_kernel,
        (array((slot_count, units)), array((slot_count, 2 * units)), array((slot_count, width))),
        direct,
        rows,
        matrix,
        weight_col,
        cotangent[0, 0],
    )

    returned = exchange(row_grads).reshape(N_Y, row_slots, width)
    sums = call(functools.partial(add_kernel, 2), array((N_Z * block, width)), slot_of, returned)
    token_grads = lax.psum_scatter(sums, "z", scatter_dimension=0, tiled=True).astype(jnp.float32)

    late_grads = after(grads, sums)
    direct_grads = dot(late_grads, matrix[:DIRECT], (1, 1)).astype(jnp.bfloat16)
    direct_grads = dot(select, exchange_direct(direct_grads), (0, 0))
    terms = jnp.concatenate(
        (
            dot(direct, late_grads, (0, 0)).astype(jnp.bfloat16),
            dot(rows, late_grads, (0, 0)).astype(jnp.bfloat16),
        ),
        axis=0,
    ).reshape(groups, model_width // groups, 2 * units)
    weight_grads = jnp.sum(lax.all_to_all(terms, "dp", 0, 0, tiled=True).astype(jnp.float32), axis=0)
    return (
        hidden[None, None],
        jnp.concatenate((direct_grads, token_grads), axis=1)[None],
        weight_grads[None, :, :units],
        weight_grads[None, :, units:],
    )


def solution(mesh):
    grid = Mesh(mesh.devices.reshape(mesh.shape["dp"], N_Y, N_Z), ("dp", "y", "z"))
    expert = ("y", "z")
    in_specs = (
        P("dp", expert, None),
        P("dp", expert, None),
        P("dp", expert, None),
        P(expert, "dp", None),
        P(expert, "dp", None),
        P("dp", expert, None, None),
    )
    out_specs = (
        P("dp", expert, None, None),
        P("dp", expert, None),
        P(expert, "dp", None),
        P(expert, "dp", None),
    )
    return jax.shard_map(shards, mesh=grid, in_specs=in_specs, out_specs=out_specs, check_vma=False)
```

time: 385 us -> 329 us (0.85)
  blocking collectives: 70.9 us -> 26.6 us
  waiting for transfers between devices: 221 us -> 188 us
  starting transfers between devices: 32.3 us -> 46.9 us
  Pallas kernels: 11.1 us -> 21.3 us
  matrix products: 15 us -> 7.2 us
    all_to_all x3 -> x5, waiting for transfers between devices: 22.2 us -> 148 us  [the longest x2 80.8 us: exchange_direct(): lax.all_to_all(parts, ('y', 'z'), 0, 0, tiled=True).reshape(rows.shape)]
    all_gather x2 -> x1, waiting for transfers between devices: 112 us -> 27.8 us  [shards(): gathered = lax.all_gather(tokens[0, :, DIRECT:], 'z', axis=0, tiled=True)]
    reduce_scatter x2 -> x1, waiting for transfers between devices: 85.8 us -> 9.7 us  [shards(): lax.psum_scatter(sums, 'z', scatter_dimension=0, tiled=True)]
    all_to_all x3 -> x1, blocking collectives: 70.9 us -> 26.6 us  [exchange(): return lax.all_to_all(parts, 'y', 0, 0, tiled=True).reshape(rows.shape)]
    all_to_all x3 -> x5, starting transfers between devices: 27.3 us -> 42 us  [the longest x1 18.7 us: shards(): heard = lax.all_to_all(told, ('y', 'z'), 0, 0, tiled=True)]
    pallas_call x5, Pallas kernels: 11.1 us -> 21.3 us  [call(): pl.pallas_call(kernel, out_shape=out_shape, in_specs=[whole] * len(operan...]
    dot_general x6 -> x4, matrix products: 15 us -> 7.2 us  [dot(): lax.dot_general(a, b, (((contract[0],), (contract[1],)), ((), ())), prefe...]
    reshape x0 -> x4, local copies, waits for them, and re-layouts: none -> 5.9 us  [the longest x2 3 us: exchange_direct(): lax.all_to_all(parts, ('y', 'z'), 0, 0, tiled=True).reshape(rows.shape)]
  transfers between devices with their start and end apart: 8 -> 8, of which waited for: 6 -> 8; matrix products, arithmetic and copies ran while one was open for 4% -> 7% of each run, Pallas kernels for 2% -> 2%
where the time goes in v4:
time: 329 us; the launch traced here: 328 us
  waiting for transfers between devices  188 us (57%)
  starting transfers between devices  46.9 us (14%)
  blocking collectives  26.6 us (8%)
  Pallas kernels  21.3 us (6%)
  local copies, waits for them, and re-layouts  18 us (5%)
  between operations  14.3 us (4%)
  matrix products  7.2 us (2%)
  other arithmetic  5.82 us (2%)
    all_to_all x2, waiting for transfers between devices, exchange_direct(): lax.all_to_all(parts, ('y', 'z'), 0, 0, tiled=True).reshape(rows.shape)  80.8 us
    all_to_all x1, waiting for transfers between devices, shards(): lax.all_to_all(terms, 'dp', 0, 0, tiled=True).astype(jnp.float32)  31.9 us
    all_gather x1, waiting for transfers between devices, shards(): gathered = lax.all_gather(tokens[0, :, DIRECT:], 'z', axis=0, tiled=True)  27.8 us
    all_to_all x1, blocking collectives, exchange(): return lax.all_to_all(parts, 'y', 0, 0, tiled=True).reshape(rows.shape)  26.6 us
    all_to_all x1, waiting for transfers between devices, exchange(): return lax.all_to_all(parts, 'y', 0, 0, tiled=True).reshape(rows.shape)  23.8 us
    pallas_call x5, Pallas kernels, call(): pl.pallas_call(kernel, out_shape=out_shape, in_specs=[whole] * len(operan...  21.3 us
    all_to_all x1, starting transfers between devices, shards(): heard = lax.all_to_all(told, ('y', 'z'), 0, 0, tiled=True)  18.7 us
    all_to_all x2, starting transfers between devices, exchange_direct(): lax.all_to_all(parts, ('y', 'z'), 0, 0, tiled=True).reshape(rows.shape)  14.1 us
  transfers between devices with their start and end apart: 8, of which 8 were waited for; matrix products, arithmetic and copies ran while one was open for 7% of the time, Pallas kernels for 2%

profile of v4, /device:TPU:6, one launch (start us, length us, event | category | flops | bytes accessed | tf_op | source)
XLA Modules:
  0.0 327.6 jit_solution(17795046104292921929)
XLA Ops:
  7.2 0.0 copy-start.6
  7.2 0.0 copy-start.7
  7.2 0.0 all-gather.3.cloned.1.call-start
  7.2 1.9 slice.33
  9.1 0.0 all-gather.3.cloned.1.call-update
  9.1 0.0 copy-start.3
  9.1 0.7 copy-done.3
  9.8 0.0 copy-start.4
  9.8 0.7 copy-done.4
  10.5 1.2 shard_map.111
  11.7 18.7 %all-to-all-start.1 = ((bf16[64,8,128]{2,1,0:T(8,128)(2,1)}), bf16[64,8,128]{2,1,0:T(8,128)(2,1)S(1)}, u32[]{:S(2)}, u32[]{:S(2)}) async-start(bf16[64,8,128]{2,1,0:T(8,128)(2,1)} %bitcast.4), calls=%async_computation.1 | async-start | bytes 262144 | tf_op jit(solution)/shard_map/all_to_all | solution.py:148
  30.4 1.0 slice.40
  31.4 0.9 slice_bitcast_fusion.2.tokens_ref
  32.3 0.0 copy-start.1
  32.3 1.0 copy-done.1
  33.3 0.0 copy-start.2
  33.3 1.0 copy-done.2
  34.3 0.5 shard_map.112
  34.8 1.5 reshape.65
  36.2 11.2 %all-to-all-done.1 = bf16[64,8,128]{2,1,0:T(8,128)(2,1)S(1)} async-done(((bf16[64,8,128]{2,1,0:T(8,128)(2,1)}), bf16[64,8,128]{2,1,0:T(8,128)(2,1)S(1)}, u32[]{:S(2)}, u32[]{:S(2)}) %all-to-all-start.1) | async-done | bytes 131104 | tf_op jit(solution)/shard_map/all_to_all | solution.py:148
  47.4 6.2 %all-to-all-start = ((bf16[64,8,640]{2,1,0:T(8,128)(2,1)}), bf16[64,8,640]{2,1,0:T(8,128)(2,1)S(1)}, u32[]{:S(2)}, u32[]{:S(2)}) async-start(bf16[64,8,640]{2,1,0:T(8,128)(2,1)} %reshape.65), calls=%async_computation | async-start | bytes 1310720 | tf_op jit(solution)/shard_map/all_to_all | solution.py:142
  53.6 0.0 copy-done.6
  53.7 0.0 copy-done.7
  53.7 44.6 %all-to-all-done = bf16[64,8,640]{2,1,0:T(8,128)(2,1)S(1)} async-done(((bf16[64,8,640]{2,1,0:T(8,128)(2,1)}), bf16[64,8,640]{2,1,0:T(8,128)(2,1)S(1)}, u32[]{:S(2)}, u32[]{:S(2)}) %all-to-all-start) | async-done | bytes 655392 | tf_op jit(solution)/shard_map/all_to_all | solution.py:142
  98.3 1.9 broadcast_in_dim.42
  100.1 4.8 %all-to-all-start.3 = ((bf16[8,256,768]{2,1,0:T(8,128)(2,1)}), bf16[8,256,768]{2,1,0:T(8,128)(2,1)}, u32[]{:S(2)}, u32[]{:S(2)}) async-start(bf16[8,256,768]{2,1,0:T(8,128)(2,1)} %broadcast_in_dim.42), calls=%async_computation.3 | async-start | bytes 6291456 | tf_op jit(solution)/shard_map/all_to_all | solution.py:175
  104.9 0.1 fusion.1.slot_ref
  105.0 27.8 %all-gather.3.cloned.1.call-done = bf16[1,2048,1536]{2,1,0:T(8,128)(2,1)} async-done(((bf16[1,128,1536]{2,1,0:T(8,128)(2,1)}), bf16[1,2048,1536]{2,1,0:T(8,128)(2,1)}) %all-gather.3.cloned.1.call-update) | async-done | bytes 6291472 | tf_op jit(solution)/shard_map/all_gather | solution.py:144
  132.8 6.3 %shard_map.113 = bf16[4,160,1536]{2,1,0:T(8,128)(2,1)} custom-call(s32[4,2048]{1,0:T(4,128)S(1)} %fusion.1.slot_ref, bf16[2048,1536]{1,0:T(8,128)(2,1)} %bitcast.49), custom_call_target="tpu_custom_call" | custom-call | tf_op jit(solution)/shard_map/pallas_call | solution.py:110
  139.1 0.0 copy-start
  139.1 2.3 all-to-all-done.3
  141.4 4.4 %all-to-all-start.2 = ((bf16[4,160,1536]{2,1,0:T(8,128)(2,1)}), bf16[4,160,1536]{2,1,0:T(8,128)(2,1)}, u32[]{:S(2)}, u32[]{:S(2)}) async-start(bf16[4,160,1536]{2,1,0:T(8,128)(2,1)} %shard_map.113), calls=%async_computation.2 | async-start | bytes 3932160 | tf_op jit(solution)/shard_map/all_to_all | solution.py:138
  145.8 0.0 reduce-scatter.2.cloned.1.call-start
  145.9 0.1 fusion.2
  146.0 0.2 select_reduce_fusion
  146.2 0.1 copy.17
  146.3 0.1 div.11.weight_ref
  146.5 0.6 reshape.66.direct_ref
  147.1 23.8 %all-to-all-done.2 = bf16[4,160,1536]{2,1,0:T(8,128)(2,1)} async-done(((bf16[4,160,1536]{2,1,0:T(8,128)(2,1)}), bf16[4,160,1536]{2,1,0:T(8,128)(2,1)}, u32[]{:S(2)}, u32[]{:S(2)}) %all-to-all-start.2) | async-done | bytes 1966112 | tf_op jit(solution)/shard_map/all_to_all | solution.py:138
  170.9 0.0 copy-done
  170.9 7.2 %shard_map.114 = (bf16[640,384]{1,0:T(8,128)(2,1)}, bf16[640,768]{1,0:T(8,128)(2,1)S(1)}, bf16[640,1536]{1,0:T(8,128)(2,1)S(1)}) custom-call(bf16[640,512]{1,0:T(8,128)(2,1)S(1)} %reshape.66.direct_ref, bf16[640,1536]{1,0:T(8,128)(2,1)} %bitcast.10.rows_ref, bf16[2048,768]{1,0:T(8,128)(2,1)} %bitcast.13.matrix_ref, f32[640,1]{1,0:T(8,128)S(1)} %div.11.weight_ref, ...), custom_call_target="tpu_custom_call" | custom-call | tf_op jit(solution)/shard_map/pallas_call | solution.py:110
  178.1 26.6 %all_to_all.35.grads_ref = bf16[4,160,1536]{2,1,0:T(8,128)(2,1)S(1)} all-to-all(bf16[4,160,1536]{2,1,0:T(8,128)(2,1)S(1)} %bitcast.44), channel_id=1, replica_groups=mesh['dp'=8,'y'=4,'z'=16] {'y'}, dimensions={0} | all-to-all | bytes 3932160 | tf_op jit(solution)/shard_map/all_to_all | solution.py:138
  204.7 6.1 %shard_map.115 = bf16[2048,1536]{1,0:T(8,128)(2,1)} custom-call(s32[4,2048]{1,0:T(4,128)S(1)} %fusion.1.slot_ref, bf16[4,160,1536]{2,1,0:T(8,128)(2,1)S(1)} %all_to_all.35.grads_ref), custom_call_target="tpu_custom_call" | custom-call | tf_op jit(solution)/shard_map/pallas_call | solution.py:110
  210.8 0.0 reduce-scatter.2.cloned.1.call-update
  210.8 1.2 slice.43
  212.0 0.7 convolution_convert_fusion.2
  212.7 1.5 reshape.71
  214.2 7.9 %all-to-all-start.5 = ((bf16[64,8,640]{2,1,0:T(8,128)(2,1)}), bf16[64,8,640]{2,1,0:T(8,128)(2,1)S(1)}, u32[]{:S(2)}, u32[]{:S(2)}) async-start(bf16[64,8,640]{2,1,0:T(8,128)(2,1)} %reshape.71), calls=%async_computation.5 | async-start | bytes 1310720 | tf_op jit(solution)/shard_map/all_to_all | solution.py:142
  222.1 0.8 convolution_convert_fusion.1
  222.9 3.6 %convolution_convert_fusion = bf16[1536,768]{1,0:T(8,128)(2,1)S(1)} fusion(bf16[640,1536]{1,0:T(8,128)(2,1)} %bitcast.10.rows_ref, bf16[640,768]{1,0:T(8,128)(2,1)S(1)} %get-tuple-element.15), kind=kOutput, calls=%fused_computation.1 | convolution fusion | flops 1511129088 | bytes 5308416 | tf_op jit(solution)/shard_map/dot_general | solution.py:76
  226.5 1.9 pad_maximum_fusion
  228.4 36.3 %all-to-all-done.5 = bf16[64,8,640]{2,1,0:T(8,128)(2,1)S(1)} async-done(((bf16[64,8,640]{2,1,0:T(8,128)(2,1)}), bf16[64,8,640]{2,1,0:T(8,128)(2,1)S(1)}, u32[]{:S(2)}, u32[]{:S(2)}) %all-to-all-start.5) | async-done | bytes 655392 | tf_op jit(solution)/shard_map/all_to_all | solution.py:142
  264.7 0.0 copy-start.5
  264.7 0.8 copy-done.5
  265.5 4.8 %all-to-all-start.6 = ((bf16[8,256,768]{2,1,0:T(8,128)(2,1)}), bf16[8,256,768]{2,1,0:T(8,128)(2,1)S(1)}, u32[]{:S(2)}, u32[]{:S(2)}) async-start(bf16[8,256,768]{2,1,0:T(8,128)(2,1)} %bitcast.21), calls=%async_computation.7 | async-start | bytes 6291456 | tf_op jit(solution)/shard_map/all_to_all | solution.py:205
  270.3 2.4 reshape.72
  272.7 2.1 fusion.3
  274.8 31.9 %all-to-all-done.6 = bf16[8,256,768]{2,1,0:T(8,128)(2,1)S(1)} async-done(((bf16[8,256,768]{2,1,0:T(8,128)(2,1)}), bf16[8,256,768]{2,1,0:T(8,128)(2,1)S(1)}, u32[]{:S(2)}, u32[]{:S(2)}) %all-to-all-start.6) | async-done | bytes 3145760 | tf_op jit(solution)/shard_map/all_to_all | solution.py:205
  306.6 0.4 convert_reduce_fusion
  307.1 0.9 slice_bitcast_fusion
  308.0 9.7 %reduce-scatter.2.cloned.1.call-done = bf16[128,1536]{1,0:T(8,128)(2,1)} async-done(((bf16[2048,1536]{1,0:T(8,128)(2,1)}), bf16[128,1536]{1,0:T(8,128)(2,1)}) %reduce-scatter.2.cloned.1.call-update) | async-done | bytes 393232 | tf_op jit(solution)/shard_map/reduce_scatter | solution.py:193
  317.7 1.1 convert_element_type.30
  318.8 2.0 maximum_bitcast_fusion
  (6 shorter events, 0.1 us)
Async XLA Ops:
  7.2 46.5 %copy-start.6 = (bf16[1,256,384]{2,1,0:T(8,128)(2,1)S(1)}, bf16[1,256,384]{2,1,0:T(8,128)(2,1)}, u32[]{:S(2)}) copy-start(bf16[1,256,384]{2,1,0:T(8,128)(2,1)} %param.12) | copy-start | bytes 589828
  7.2 46.5 %copy-start.7 = (bf16[1,256,384]{2,1,0:T(8,128)(2,1)S(1)}, bf16[1,256,384]{2,1,0:T(8,128)(2,1)}, u32[]{:S(2)}) copy-start(bf16[1,256,384]{2,1,0:T(8,128)(2,1)} %param.11) | copy-start | bytes 589828
  7.2 125.6 %all-gather.3.cloned.1.call-start = ((), (), s32[]{:S(2)}) async-start(), calls=%async_computation.9 | async-start | bytes 6684672 | tf_op jit(solution)/shard_map/all_gather | solution.py:144
  9.1 0.7 copy-start.3
  9.8 0.7 copy-start.4
  11.7 35.8 %all-to-all-start.1 = ((bf16[64,8,128]{2,1,0:T(8,128)(2,1)}), bf16[64,8,128]{2,1,0:T(8,128)(2,1)S(1)}, u32[]{:S(2)}, u32[]{:S(2)}) async-start(bf16[64,8,128]{2,1,0:T(8,128)(2,1)} %bitcast.4), calls=%async_computation.1 | async-start | bytes 262144 | tf_op jit(solution)/shard_map/all_to_all | solution.py:148
  32.3 1.0 copy-start.1
  33.3 1.0 copy-start.2
  47.4 50.9 %all-to-all-start = ((bf16[64,8,640]{2,1,0:T(8,128)(2,1)}), bf16[64,8,640]{2,1,0:T(8,128)(2,1)S(1)}, u32[]{:S(2)}, u32[]{:S(2)}) async-start(bf16[64,8,640]{2,1,0:T(8,128)(2,1)} %reshape.65), calls=%async_computation | async-start | bytes 1310720 | tf_op jit(solution)/shard_map/all_to_all | solution.py:142
  100.1 41.3 %all-to-all-start.3 = ((bf16[8,256,768]{2,1,0:T(8,128)(2,1)}), bf16[8,256,768]{2,1,0:T(8,128)(2,1)}, u32[]{:S(2)}, u32[]{:S(2)}) async-start(bf16[8,256,768]{2,1,0:T(8,128)(2,1)} %broadcast_in_dim.42), calls=%async_computation.3 | async-start | bytes 6291456 | tf_op jit(solution)/shard_map/all_to_all | solution.py:175
  139.1 31.8 %copy-start = (bf16[1,1,640,384]{3,2,1,0:T(8,128)(2,1)S(1)}, bf16[1,1,640,384]{3,2,1,0:T(8,128)(2,1)}, u32[]{:S(2)}) copy-start(bf16[1,1,640,384]{3,2,1,0:T(8,128)(2,1)} %param.13) | copy-start | bytes 1474564
  141.4 29.5 %all-to-all-start.2 = ((bf16[4,160,1536]{2,1,0:T(8,128)(2,1)}), bf16[4,160,1536]{2,1,0:T(8,128)(2,1)}, u32[]{:S(2)}, u32[]{:S(2)}) async-start(bf16[4,160,1536]{2,1,0:T(8,128)(2,1)} %shard_map.113), calls=%async_computation.2 | async-start | bytes 3932160 | tf_op jit(solution)/shard_map/all_to_all | solution.py:138
  145.8 171.9 %reduce-scatter.2.cloned.1.call-start = ((), (), s32[]{:S(2)}) async-start(), calls=%async_computation.8 | async-start | bytes 6684672 | tf_op jit(solution)/shard_map/reduce_scatter | solution.py:193
  214.2 50.5 %all-to-all-start.5 = ((bf16[64,8,640]{2,1,0:T(8,128)(2,1)}), bf16[64,8,640]{2,1,0:T(8,128)(2,1)S(1)}, u32[]{:S(2)}, u32[]{:S(2)}) async-start(bf16[64,8,640]{2,1,0:T(8,128)(2,1)} %reshape.71), calls=%async_computation.5 | async-start | bytes 1310720 | tf_op jit(solution)/shard_map/all_to_all | solution.py:142
  264.7 0.8 copy-start.5
  265.5 41.1 %all-to-all-start.6 = ((bf16[8,256,768]{2,1,0:T(8,128)(2,1)}), bf16[8,256,768]{2,1,0:T(8,128)(2,1)S(1)}, u32[]{:S(2)}, u32[]{:S(2)}) async-start(bf16[8,256,768]{2,1,0:T(8,128)(2,1)} %bitcast.21), calls=%async_computation.7 | async-start | bytes 6291456 | tf_op jit(solution)/shard_map/all_to_all | solution.py:205
Sparse Core Ops, SparseCore 0:
  10.7 122.0 all-gather.2
  210.9 106.7 reduce-scatter.1

commit v5 on v3

--- a/solution.py
+++ b/solution.py
@@ -55,19 +55,21 @@
 
 def block_kernel(ids_ref, weights_ref, tokens_ref, out_ref):
     tokens, width = tokens_ref.shape
-    lane = iota((tokens, LANES), 1)
-    expert = lane & (N_Y * N_Z - 1)
-    hits = jnp.zeros((tokens, LANES), F32)
-    eighths = jnp.zeros((tokens, LANES), F32)
+    line = iota((LANES, tokens), 0)
+    expert = line & (N_Y * N_Z - 1)
+    hits = jnp.zeros((LANES, tokens), F32)
+    eighths = jnp.zeros((LANES, tokens), F32)
     weights = weights_ref[...].astype(F32)
-    for choice in range(ids_ref.shape[1]):
-        named = ids_ref[:, choice : choice + 1] == expert
+    for choice in range(ids_ref.shape[0]):
+        named = ids_ref[choice : choice + 1, :] == expert
         hits = hits + jnp.where(named, 1.0, 0.0)
-        eighths = eighths + jnp.where(named, weights[:, choice : choice + 1], 0.0)
-    earlier = one_hot(iota((tokens, tokens), 1) < iota((tokens, tokens), 0))
-    rank = jnp.where(hits > 0.0, dot(earlier, hits.astype(BF16)), -1.0)
+        eighths = eighths + jnp.where(named, weights[choice : choice + 1, :], 0.0)
+    earlier = one_hot(iota((tokens, tokens), 0) < iota((tokens, tokens), 1))
+    rank = jnp.where(hits > 0.0, dot(hits.astype(BF16), earlier), -1.0)
+    routing = jnp.where(line < N_Y * N_Z, rank, eighths).astype(BF16)
+    same = one_hot(iota((LANES, LANES), 0) == iota((LANES, LANES), 1))
     out_ref[:, :width] = tokens_ref[...]
-    out_ref[:, width:] = jnp.where(lane < N_Y * N_Z, rank, eighths).astype(BF16)
+    out_ref[:, width:] = dot(routing, same, (0, 0)).astype(BF16)
 
 
 def slots_of(routing, expert, slot):
@@ -95,35 +97,66 @@
         first += rows
 
 
-def pick_kernel(blocks, z_ref, map_ref, *refs):
-    messages = refs[blocks + 1 : -2] if len(refs) > blocks + 2 else ()
+def pick_kernel(blocks, messages, z_ref, map_ref, *refs):
+    token_refs, routing_refs, refs = refs[:blocks], refs[blocks : 2 * blocks], refs[2 * blocks :]
     out_ref, select_ref = refs[-2:]
-    rows, width = out_ref.shape
-    tokens = refs[0].shape[0]
-    routing = jnp.concatenate([ref[:, width:] for ref in refs[:blocks]], axis=0)
-    here, eighths = slots_of(routing, map_ref[0:1, :] + z_ref[0], map_ref[1:2, :])
-    here = here & ((iota(here.shape, 0) >> (tokens.bit_length() - 1)) == map_ref[2:3, :])
-    select = one_hot(here)
-    select_ref[...] = select
-    weights = jnp.sum(jnp.where(here, eighths, 0.0), axis=0, keepdims=True)
-    picked = dot(select, jnp.concatenate([ref[:, :width] for ref in refs[:blocks]], axis=0), (0, 0))
-    for index, ref in enumerate(messages):
-        place_ref = refs[blocks]
-        count = ref.shape[0]
-        picked = picked + dot(one_hot(iota((rows, count), 1) == place_ref[:, index : index + 1]), ref[...])
-        line = (index // 2) if index < 4 else 2
-        spread = one_hot(iota((LANES, rows), 0) == map_ref[3 + index : 4 + index, :])
-        lines = dot(ref[:, :LANES], spread)
-        weights = weights + jnp.sum(
-            jnp.where(iota(lines.shape, 0) == MESSAGE_SLOTS[line], lines, 0.0), axis=0, keepdims=True
-        )
+    rows = out_ref.shape[0]
+    tokens = token_refs[0].shape[0]
+    first = pl.program_id(0) == 0
+
+    @pl.when(first)
+    def _():
+        routing = jnp.concatenate([ref[...] for ref in routing_refs], axis=0)
+        here, _ = slots_of(routing, map_ref[0:1, :] + z_ref[0], map_ref[1:2, :])
+        here = here & ((iota(here.shape, 0) >> (tokens.bit_length() - 1)) == map_ref[2:3, :])
+        select_ref[...] = one_hot(here)
+
+    picked = dot(select_ref[...], jnp.concatenate([ref[...] for ref in token_refs], axis=0), (0, 0))
+    for index in range(messages):
+        place_ref, ref = refs[0], refs[1 + index]
+        picked = picked + dot(one_hot(iota((rows, ref.shape[0]), 1) == place_ref[:, index : index + 1]), ref[...])
     out_ref[...] = picked.astype(BF16)
-    used = (rows // N_Y - 1) // SLOTS * SLOTS
-    row = iota((rows, rows), 0)
-    is_weights = row == used
-    for y in range(1, N_Y):
-        is_weights = is_weights | (row == used + y * (rows // N_Y))
-    out_ref[:, :rows] = jnp.where(is_weights, weights, picked[:, :rows]).astype(BF16)
+
+    @pl.when(first)
+    def _():
+        routing = jnp.concatenate([ref[...] for ref in routing_refs], axis=0)
+        lane = iota((LANES, rows), 0)
+        eighths = dot(routing, one_hot(lane == map_ref[0:1, :] + z_ref[0] + N_Y * N_Z))
+        weights = jnp.sum(select_ref[...].astype(F32) * eighths, axis=0, keepdims=True)
+        for index in range(messages):
+            ref = refs[1 + index]
+            lines = dot(ref[:, :LANES], one_hot(lane == map_ref[3 + index : 4 + index, :]))
+            line = MESSAGE_SLOTS[index // 2]
+            weights = weights + jnp.sum(
+                jnp.where(iota(lines.shape, 0) == line, lines, 0.0), axis=0, keepdims=True
+            )
+        used = (rows // N_Y - 1) // SLOTS * SLOTS
+        row = iota((rows, rows), 0)
+        is_weights = row == used
+        for y in range(1, N_Y):
+            is_weights = is_weights | (row == used + y * (rows // N_Y))
+        out_ref[:, :rows] = jnp.where(is_weights, weights, picked[:, :rows]).astype(BF16)
+
+
+def pick(z_of, lanes, places, blocks, messages, width):
+    rows, tokens, step = lanes.shape[1], blocks[0].shape[0], 512
+    whole = lambda value: pl.BlockSpec(value.shape, lambda part: (0, 0))
+    others = (jnp.asarray(places),) + tuple(messages) if messages else ()
+    return pl.pallas_call(
+        functools.partial(pick_kernel, len(blocks), len(messages)),
+        grid=(width // step,),
+        out_shape=(array((rows, width)), array((len(blocks) * tokens, rows))),
+        in_specs=[pl.BlockSpec(memory_space=pltpu.SMEM), whole(lanes)]
+        + [pl.BlockSpec((tokens, step), lambda part: (0, part))] * len(blocks)
+        + [pl.BlockSpec((tokens, LANES), lambda part: (0, width // LANES))] * len(blocks)
+        + [whole(value) for value in others[:1]]
+        + [pl.BlockSpec((value.shape[0], step), lambda part: (0, part)) for value in others[1:]],
+        out_specs=(
+            pl.BlockSpec((rows, step), lambda part: (0, part)),
+            pl.BlockSpec((len(blocks) * tokens, rows), lambda part: (0, 0)),
+        ),
+        compiler_params=pltpu.CompilerParams(vmem_limit_bytes=VMEM_BYTES),
+    )(z_of, jnp.asarray(lanes), *blocks, *blocks, *others)
 
 
 MESSAGE_KEYS = tuple((step, way) for step in range(3) for way in range(2))
@@ -253,8 +286,8 @@
         parts = rows.reshape(N_Y, rows.shape[0] // N_Y, width)
         return lax.all_to_all(parts, "y", 0, 0, tiled=True).reshape(rows.shape)
 
-    own = call(block_kernel, array((block, width + LANES)), expert_ids[0], route_weights[0], tokens[0])
-    stacked = jnp.concatenate((gate_weight[0], up_weight[0]), axis=1)
+    own = call(block_kernel, array((block, width + LANES)), expert_ids[0].T, route_weights[0].T, tokens[0])
+    stacked = jnp.concatenate((after(gate_weight[0], own), up_weight[0]), axis=1)
     matrix = lax.all_gather(stacked, "dp", axis=0, tiled=True)
 
     group, offset, slot = np.concatenate((near_origin, last_origin), axis=1)
@@ -268,13 +301,8 @@
         going = [send(going[0], 1), send(going[1], -1)]
         blocks[-hop], blocks[hop] = going
         if hop == REACH - 1:
-            near_rows, near_select = call(
-                functools.partial(pick_kernel, len(NEAR)),
-                (array((near_count, width)), array((len(NEAR) * block, near_count))),
-                z_of,
-                jnp.asarray(near_lanes),
-                *[blocks[source] for source in NEAR],
-                scalars=1,
+            near_rows, near_select = pick(
+                z_of, near_lanes, None, [blocks[source] for source in NEAR], (), width
             )
     going = [after(part, near_rows) for part in going]
     near_rows = exchange(near_rows)
@@ -290,15 +318,9 @@
         for way, sign in enumerate((1, -1))
     ]
     arrived = [send(messages[way][step], (step + 1) * (1 - 2 * way)) for step, way in MESSAGE_KEYS]
-    last_rows, last_select = call(
-        functools.partial(pick_kernel, 2),
-        (array((last_count, width)), array((2 * block, last_count))),
-        z_of,
-        jnp.asarray(last_lanes),
-        *[blocks[source] for source in LAST[:2]],
-        jnp.asarray(last_places),
-        *arrived,
-        scalars=1,
+    arrived[0] = after(arrived[0], near_rows)
+    last_rows, last_select = pick(
+        z_of, last_lanes, last_places, [blocks[source] for source in LAST[:2]], arrived, width
     )
     last_rows = exchange(last_rows)
 

time: 342 us -> 341 us (level)
  the two profiles are of different devices: /device:TPU:6 before, /device:TPU:260 now
where the time goes in v5:
time: 341 us; the launch traced here: 339 us
  starting transfers between devices  136 us (40%)
  waiting for transfers between devices  102 us (30%)
  Pallas kernels  39.8 us (12%)
  local copies, waits for them, and re-layouts  23 us (7%)
  between operations  14.8 us (4%)
  blocking collectives  14 us (4%)
  matrix products  6.72 us (2%)
    ppermute x32, starting transfers between devices, send(): lax.ppermute(value, 'z', [(i, (i + distance) % N_Z) for i in range(N_Z)])  123 us
    ppermute x32, waiting for transfers between devices, send(): lax.ppermute(value, 'z', [(i, (i + distance) % N_Z) for i in range(N_Z)])  91.1 us
    unnamed x82, local copies, waits for them, and re-layouts  21.8 us
    pallas_call x8, Pallas kernels, call(): pl.pallas_call(kernel, out_shape=out_shape, in_specs=[small] * scalars +...  17.9 us
    all_to_all x1, blocking collectives, exchange(): return lax.all_to_all(parts, 'y', 0, 0, tiled=True).reshape(rows.shape)  14 us
    all_to_all x3, starting transfers between devices, exchange(): return lax.all_to_all(parts, 'y', 0, 0, tiled=True).reshape(rows.shape)  13 us
    pallas_call x2, Pallas kernels, pick(): pl.pallas_call(functools.partial(pick_kernel, len(blocks), len(messages))...  11.3 us
    all_to_all x3, waiting for transfers between devices, exchange(): return lax.all_to_all(parts, 'y', 0, 0, tiled=True).reshape(rows.shape)  11 us
  transfers between devices with their start and end apart: 37, of which 16 were waited for; matrix products, arithmetic and copies ran while one was open for 1% of the time, Pallas kernels for 8%

profile of v5, /device:TPU:260, one launch (start us, length us, event | category | flops | bytes accessed | tf_op | source)
XLA Modules:
  0.0 339.1 jit_solution(1976086172109657191)
XLA Ops:
  10.0 1.8 pad_maximum_fusion
  11.8 2.9 collective-permute-start.1
  14.7 4.1 %collective-permute-start = (bf16[128,2176]{1,0:T(8,128)(2,1)S(1)}, bf16[128,2176]{1,0:T(8,128)(2,1)S(1)}, u32[]{:S(2)}, u32[]{:S(2)}) collective-permute-start(bf16[128,2176]{1,0:T(8,128)(2,1)S(1)} %shard_map.174.refs_0_.refs_9_), channel_id=1, source_target_pairs={{0,15},{1,0},{2,1},{3,2},{4,3},{5,4},{6,5},{7,6},{8,7},{9,8},{10,9... | collective-permute-start | bytes 1671176 | tf_op jit(solution)/shard_map/ppermute | solution.py:283
  18.9 10.4 %collective-permute-done.1.refs_2_.refs_11_ = bf16[128,2176]{1,0:T(8,128)(2,1)S(1)} collective-permute-done((bf16[128,2176]{1,0:T(8,128)(2,1)S(1)}, bf16[128,2176]{1,0:T(8,128)(2,1)S(1)}, u32[]{:S(2)}, u32[]{:S(2)}) %collective-permute-start.1) | collective-permute-done | bytes 557088 | tf_op jit(solution)/shard_map/ppermute | solution.py:283
  29.3 1.9 collective-permute-start.3
  31.2 5.1 %collective-permute-start.2 = (bf16[128,2176]{1,0:T(8,128)(2,1)S(1)}, bf16[128,2176]{1,0:T(8,128)(2,1)S(1)}, u32[]{:S(2)}, u32[]{:S(2)}) collective-permute-start(bf16[128,2176]{1,0:T(8,128)(2,1)S(1)} %collective-permute-done.refs_1_.refs_10_), channel_id=1, source_target_pairs={{0,15},{1,0},{2,1},{3,2},{4,3},{5,4},{6,5},{7,6},{8,7},{9,8},{10,9... | collective-permute-start | bytes 1671176 | tf_op jit(solution)/shard_map/ppermute | solution.py:283
  36.3 9.5 %collective-permute-done.3.refs_4_.refs_13_ = bf16[128,2176]{1,0:T(8,128)(2,1)S(1)} collective-permute-done((bf16[128,2176]{1,0:T(8,128)(2,1)S(1)}, bf16[128,2176]{1,0:T(8,128)(2,1)S(1)}, u32[]{:S(2)}, u32[]{:S(2)}) %collective-permute-start.3) | collective-permute-done | bytes 557088 | tf_op jit(solution)/shard_map/ppermute | solution.py:283
  45.9 1.9 collective-permute-start.5
  48.6 5.1 %collective-permute-start.4 = (bf16[128,2176]{1,0:T(8,128)(2,1)S(1)}, bf16[128,2176]{1,0:T(8,128)(2,1)}, u32[]{:S(2)}, u32[]{:S(2)}) collective-permute-start(bf16[128,2176]{1,0:T(8,128)(2,1)S(1)} %collective-permute-done.2.refs_3_.refs_12_), channel_id=1, source_target_pairs={{0,15},{1,0},{2,1},{3,2},{4,3},{5,4},{6,5},{7,6},{8,7},{9,8},{10,9... | collective-permute-start | bytes 1671176 | tf_op jit(solution)/shard_map/ppermute | solution.py:283
  54.5 7.1 %collective-permute-done.5.refs_6_.refs_15_ = bf16[128,2176]{1,0:T(8,128)(2,1)} collective-permute-done((bf16[128,2176]{1,0:T(8,128)(2,1)S(1)}, bf16[128,2176]{1,0:T(8,128)(2,1)}, u32[]{:S(2)}, u32[]{:S(2)}) %collective-permute-start.5) | collective-permute-done | bytes 557088 | tf_op jit(solution)/shard_map/ppermute | solution.py:283
  61.6 1.9 collective-permute-start.7
  63.6 5.7 %collective-permute-start.6 = (bf16[128,2176]{1,0:T(8,128)(2,1)}, bf16[128,2176]{1,0:T(8,128)(2,1)S(1)}, u32[]{:S(2)}, u32[]{:S(2)}) collective-permute-start(bf16[128,2176]{1,0:T(8,128)(2,1)} %collective-permute-done.4.refs_5_.refs_14_), channel_id=1, source_target_pairs={{0,15},{1,0},{2,1},{3,2},{4,3},{5,4},{6,5},{7,6},{8,7},{9,8},{10,9... | collective-permute-start | bytes 1671176 | tf_op jit(solution)/shard_map/ppermute | solution.py:283
  69.2 7.4 %collective-permute-done.7.refs_8_.refs_17_ = bf16[128,2176]{1,0:T(8,128)(2,1)S(1)} collective-permute-done((bf16[128,2176]{1,0:T(8,128)(2,1)}, bf16[128,2176]{1,0:T(8,128)(2,1)S(1)}, u32[]{:S(2)}, u32[]{:S(2)}) %collective-permute-start.7) | collective-permute-done | bytes 557088 | tf_op jit(solution)/shard_map/ppermute | solution.py:283
  81.8 6.5 %shard_map.175 = (bf16[384,2048]{1,0:T(8,128)(2,1)}, bf16[1152,384]{1,0:T(8,128)(2,1)S(1)}) custom-call(s32[1]{0:T(128)} %bitcast.1.z_ref, s32[16,384]{1,0:T(8,128)S(1)} %copy-done.32, bf16[128,2176]{1,0:T(8,128)(2,1)S(1)} %shard_map.174.refs_0_.refs_9_, bf16[128,2176]{1,0:T(8,128)(2,1)S(1)} %collective-permute-done.refs_1_.refs_10_, ...), custom_call_target="tpu_custom_call" | custom-call | tf_op jit(solution)/shard_map/pallas_call | solution.py:145
  88.3 4.6 %all-to-all-start = ((bf16[4,96,2048]{2,1,0:T(8,128)(2,1)}), bf16[4,96,2048]{2,1,0:T(8,128)(2,1)S(1)}, u32[]{:S(2)}, u32[]{:S(2)}) async-start(bf16[4,96,2048]{2,1,0:T(8,128)(2,1)} %bitcast.51), calls=%async_computation | async-start | bytes 3145728 | tf_op jit(solution)/shard_map/all_to_all | solution.py:287
  92.9 1.9 collective-permute-start.9
  94.8 5.5 %collective-permute-start.8 = (bf16[128,2176]{1,0:T(8,128)(2,1)}, bf16[128,2176]{1,0:T(8,128)(2,1)S(1)}, u32[]{:S(2)}, u32[]{:S(2)}) collective-permute-start(bf16[128,2176]{1,0:T(8,128)(2,1)} %copy-done.6), channel_id=1, source_target_pairs={{0,15},{1,0},{2,1},{3,2},{4,3},{5,4},{6,5},{7,6},{8,7},{9,8},{10,9... | collective-permute-start | bytes 1671176 | tf_op jit(solution)/shard_map/ppermute | solution.py:283
  100.3 6.7 %collective-permute-done.9.block_ref.refs_1_.refs_3_ = bf16[128,2176]{1,0:T(8,128)(2,1)S(1)} collective-permute-done((bf16[128,2176]{1,0:T(8,128)(2,1)}, bf16[128,2176]{1,0:T(8,128)(2,1)S(1)}, u32[]{:S(2)}, u32[]{:S(2)}) %collective-permute-start.9) | collective-permute-done | bytes 557088 | tf_op jit(solution)/shard_map/ppermute | solution.py:283
  108.8 1.9 collective-permute-start.10
  110.7 3.9 %collective-permute-start.12 = (bf16[48,2048]{1,0:T(8,128)(2,1)}, bf16[48,2048]{1,0:T(8,128)(2,1)S(1)}, u32[]{:S(2)}, u32[]{:S(2)}) collective-permute-start(bf16[48,2048]{1,0:T(8,128)(2,1)} %get-tuple-element.44), channel_id=1, source_target_pairs={{0,2},{1,3},{2,4},{3,5},{4,6},{5,7},{6,8},{7,9},{8,10},{9,11},{10,... | collective-permute-start | bytes 589832 | tf_op jit(solution)/shard_map/ppermute | solution.py:283
  117.2 3.2 collective-permute-start.11
  120.4 4.8 %collective-permute-start.13 = (bf16[48,2048]{1,0:T(8,128)(2,1)}, bf16[48,2048]{1,0:T(8,128)(2,1)}, u32[]{:S(2)}, u32[]{:S(2)}) collective-permute-start(bf16[48,2048]{1,0:T(8,128)(2,1)} %get-tuple-element.45), channel_id=1, source_target_pairs={{0,14},{1,15},{2,0},{3,1},{4,2},{5,3},{6,4},{7,5},{8,6},{9,7},{10,... | collective-permute-start | bytes 589832 | tf_op jit(solution)/shard_map/ppermute | solution.py:283
  125.2 2.1 collective-permute-start.14
  127.3 6.7 %collective-permute-start.15 = (bf16[32,2048]{1,0:T(8,128)(2,1)}, bf16[32,2048]{1,0:T(8,128)(2,1)}, u32[]{:S(2)}, u32[]{:S(2)}) collective-permute-start(bf16[32,2048]{1,0:T(8,128)(2,1)} %get-tuple-element.47), channel_id=1, source_target_pairs={{0,13},{1,14},{2,15},{3,0},{4,1},{5,2},{6,3},{7,4},{8,5},{9,6},{10... | collective-permute-start | bytes 393224 | tf_op jit(solution)/shard_map/ppermute | solution.py:283
  134.1 2.6 collective-permute-done.14.refs_9_
  136.7 2.8 collective-permute-done.15.refs_10_
  142.9 4.8 %shard_map.180 = (bf16[288,2048]{1,0:T(8,128)(2,1)S(1)}, bf16[256,288]{1,0:T(8,128)(2,1)S(1)}) custom-call(s32[1]{0:T(128)} %bitcast.1.z_ref, s32[16,288]{1,0:T(8,128)S(1)} %copy-done.31, bf16[128,2176]{1,0:T(8,128)(2,1)S(1)} %copy-done.3, bf16[128,2176]{1,0:T(8,128)(2,1)S(1)} %collective-permute-done.9.block_ref.refs_1_.refs_3_, ...), custom_call_target="tpu_custom_call" | custom-call | tf_op jit(solution)/shard_map/pallas_call | solution.py:145
  148.8 4.6 %all-to-all-start.1 = ((bf16[4,72,2048]{2,1,0:T(8,128)(2,1)}), bf16[4,72,2048]{2,1,0:T(8,128)(2,1)}, u32[]{:S(2)}, u32[]{:S(2)}) async-start(bf16[4,72,2048]{2,1,0:T(8,128)(2,1)} %bitcast.45), calls=%async_computation.1 | async-start | bytes 2359296 | tf_op jit(solution)/shard_map/all_to_all | solution.py:287
  154.6 11.0 %all-to-all-done.1 = bf16[4,72,2048]{2,1,0:T(8,128)(2,1)} async-done(((bf16[4,72,2048]{2,1,0:T(8,128)(2,1)}), bf16[4,72,2048]{2,1,0:T(8,128)(2,1)}, u32[]{:S(2)}, u32[]{:S(2)}) %all-to-all-start.1) | async-done | bytes 1179680 | tf_op jit(solution)/shard_map/all_to_all | solution.py:287
  165.6 5.0 %shard_map.181 = (bf16[288,384]{1,0:T(8,128)(2,1)S(1)}, bf16[288,768]{1,0:T(8,128)(2,1)S(1)}, bf16[288,2048]{1,0:T(8,128)(2,1)S(1)}) custom-call(s32[1]{0:T(128)} %bitcast.y_ref, bf16[288,2048]{1,0:T(8,128)(2,1)} %bitcast.13.rows_ref, bf16[2048,768]{1,0:T(8,128)(2,1)} %all-gather.2.cloned.1.call-done.matrix_ref, bf16[288,384]{1,0:T(8,128)(2,1)S(1)} %slice.17.cotangent_ref), custom_call_target="tpu_custom_call" | custom-call | tf_op jit(solution)/shard_map/pallas_call | solution.py:31
  171.6 5.5 %shard_map.177 = (bf16[384,384]{1,0:T(8,128)(2,1)S(1)}, bf16[384,768]{1,0:T(8,128)(2,1)S(1)}, bf16[384,2048]{1,0:T(8,128)(2,1)S(1)}) custom-call(s32[1]{0:T(128)} %bitcast.y_ref, bf16[384,2048]{1,0:T(8,128)(2,1)S(1)} %bitcast.42, bf16[2048,768]{1,0:T(8,128)(2,1)} %all-gather.2.cloned.1.call-done.matrix_ref, bf16[384,384]{1,0:T(8,128)(2,1)S(1)} %slice.16.cotangent_ref), custom_call_target="tpu_custom_call" | custom-call | tf_op jit(solution)/shard_map/pallas_call | solution.py:31
  177.1 1.8 fusion.5
  179.0 4.9 %add_convert_fusion = bf16[2048,768]{1,0:T(8,128)(2,1)} fusion(f32[2048,768]{1,0:T(8,128)S(1)} %fusion.5, bf16[288,2048]{1,0:T(8,128)(2,1)} %bitcast.13.rows_ref, bf16[288,768]{1,0:T(8,128)(2,1)S(1)} %get-tuple-element.60), kind=kOutput, calls=%fused_computation | convolution fusion | flops 909115392 | bytes 11059200 | tf_op jit(solution)/shard_map/dot_general | solution.py:53
  185.1 14.0 %all_to_all.20 = bf16[4,72,2048]{2,1,0:T(8,128)(2,1)S(1)} all-to-all(bf16[4,72,2048]{2,1,0:T(8,128)(2,1)S(1)} %bitcast.46), channel_id=1, replica_groups=mesh['dp'=8,'y'=4,'z'=16] {'y'}, dimensions={0} | all-to-all | bytes 2359296 | tf_op jit(solution)/shard_map/all_to_all | solution.py:287
  199.1 2.3 shard_map.182
  202.4 3.7 %all-to-all-start.3 = ((bf16[4,96,2048]{2,1,0:T(8,128)(2,1)}), bf16[4,96,2048]{2,1,0:T(8,128)(2,1)S(1)}, u32[]{:S(2)}, u32[]{:S(2)}) async-start(bf16[4,96,2048]{2,1,0:T(8,128)(2,1)} %bitcast.44), calls=%async_computation.3 | async-start | bytes 3145728 | tf_op jit(solution)/shard_map/all_to_all | solution.py:287
  206.1 7.3 %collective-permute-start.18 = (bf16[32,2048]{1,0:T(8,128)(2,1)S(1)}, bf16[32,2048]{1,0:T(8,128)(2,1)S(1)}, u32[]{:S(2)}, u32[]{:S(2)}) collective-permute-start(bf16[32,2048]{1,0:T(8,128)(2,1)S(1)} %get-tuple-element.54), channel_id=1, source_target_pairs={{0,13},{1,14},{2,15},{3,0},{4,1},{5,2},{6,3},{7,4},{8,5},{9,6},{10... | collective-permute-start | bytes 393224 | tf_op jit(solution)/shard_map/ppermute | solution.py:283
  213.4 2.4 collective-permute-start.17
  215.8 3.4 collective-permute-start.16
  219.2 2.5 collective-permute-start.24
  221.6 4.4 %collective-permute-start.25 = (bf16[48,2048]{1,0:T(8,128)(2,1)}, bf16[48,2048]{1,0:T(8,128)(2,1)S(1)}, u32[]{:S(2)}, u32[]{:S(2)}) collective-permute-start(bf16[48,2048]{1,0:T(8,128)(2,1)} %get-tuple-element.65), channel_id=1, source_target_pairs={{0,2},{1,3},{2,4},{3,5},{4,6},{5,7},{6,8},{7,9},{8,10},{9,11},{10,... | collective-permute-start | bytes 589832 | tf_op jit(solution)/shard_map/ppermute | solution.py:283
  226.0 4.8 %collective-permute-start.26 = (bf16[32,2048]{1,0:T(8,128)(2,1)}, bf16[32,2048]{1,0:T(8,128)(2,1)S(1)}, u32[]{:S(2)}, u32[]{:S(2)}) collective-permute-start(bf16[32,2048]{1,0:T(8,128)(2,1)} %get-tuple-element.66), channel_id=1, source_target_pairs={{0,3},{1,4},{2,5},{3,6},{4,7},{5,8},{6,9},{7,10},{8,11},{9,12},{10... | collective-permute-start | bytes 393224 | tf_op jit(solution)/shard_map/ppermute | solution.py:283
  230.8 1.3 copy-done.1
  233.4 3.0 collective-permute-start.19
  236.4 3.2 collective-permute-done.26.third_ref
  239.6 1.4 shard_map.189
  241.0 4.2 %collective-permute-start.27 = (bf16[128,2048]{1,0:T(8,128)(2,1)}, bf16[128,2048]{1,0:T(8,128)(2,1)}, u32[]{:S(2)}, u32[]{:S(2)}) collective-permute-start(bf16[128,2048]{1,0:T(8,128)(2,1)} %shard_map.189), channel_id=1, source_target_pairs={{0,1},{1,2},{2,3},{3,4},{4,5},{5,6},{6,7},{7,8},{8,9},{9,10},{10,1... | collective-permute-start | bytes 1572872 | tf_op jit(solution)/shard_map/ppermute | solution.py:283
  247.6 8.1 %collective-permute-start.20 = (bf16[128,2048]{1,0:T(8,128)(2,1)S(1)}, bf16[128,2048]{1,0:T(8,128)(2,1)S(1)}, u32[]{:S(2)}, u32[]{:S(2)}) collective-permute-start(bf16[128,2048]{1,0:T(8,128)(2,1)S(1)} %shard_map.185), channel_id=1, source_target_pairs={{0,15},{1,0},{2,1},{3,2},{4,3},{5,4},{6,5},{7,6},{8,7},{9,8},{10,9... | collective-permute-start | bytes 1572872 | tf_op jit(solution)/shard_map/ppermute | solution.py:283
  255.7 5.7 %collective-permute-done.27.sum_ref = bf16[128,2048]{1,0:T(8,128)(2,1)} collective-permute-done((bf16[128,2048]{1,0:T(8,128)(2,1)}, bf16[128,2048]{1,0:T(8,128)(2,1)}, u32[]{:S(2)}, u32[]{:S(2)}) %collective-permute-start.27) | collective-permute-done | bytes 524320 | tf_op jit(solution)/shard_map/ppermute | solution.py:283
  261.4 1.5 shard_map.190
  262.9 1.9 collective-permute-start.28
  265.9 5.6 %collective-permute-start.21 = (bf16[128,2048]{1,0:T(8,128)(2,1)S(1)}, bf16[128,2048]{1,0:T(8,128)(2,1)S(1)}, u32[]{:S(2)}, u32[]{:S(2)}) collective-permute-start(bf16[128,2048]{1,0:T(8,128)(2,1)S(1)} %shard_map.186), channel_id=1, source_target_pairs={{0,15},{1,0},{2,1},{3,2},{4,3},{5,4},{6,5},{7,6},{8,7},{9,8},{10,9... | collective-permute-start | bytes 1572872 | tf_op jit(solution)/shard_map/ppermute | solution.py:283
  271.5 8.8 %collective-permute-done.28.sum_ref = bf16[128,2048]{1,0:T(8,128)(2,1)S(1)} collective-permute-done((bf16[128,2048]{1,0:T(8,128)(2,1)S(1)}, bf16[128,2048]{1,0:T(8,128)(2,1)S(1)}, u32[]{:S(2)}, u32[]{:S(2)}) %collective-permute-start.28) | collective-permute-done | bytes 524320 | tf_op jit(solution)/shard_map/ppermute | solution.py:283
  280.7 1.9 collective-permute-start.29
  283.1 5.6 %collective-permute-start.22 = (bf16[128,2048]{1,0:T(8,128)(2,1)S(1)}, bf16[128,2048]{1,0:T(8,128)(2,1)S(1)}, u32[]{:S(2)}, u32[]{:S(2)}) collective-permute-start(bf16[128,2048]{1,0:T(8,128)(2,1)S(1)} %shard_map.187), channel_id=1, source_target_pairs={{0,15},{1,0},{2,1},{3,2},{4,3},{5,4},{6,5},{7,6},{8,7},{9,8},{10,9... | collective-permute-start | bytes 1572872 | tf_op jit(solution)/shard_map/ppermute | solution.py:283
  288.7 9.3 %collective-permute-done.29.sum_ref = bf16[128,2048]{1,0:T(8,128)(2,1)S(1)} collective-permute-done((bf16[128,2048]{1,0:T(8,128)(2,1)S(1)}, bf16[128,2048]{1,0:T(8,128)(2,1)S(1)}, u32[]{:S(2)}, u32[]{:S(2)}) %collective-permute-start.29) | collective-permute-done | bytes 524320 | tf_op jit(solution)/shard_map/ppermute | solution.py:283
  298.5 1.9 collective-permute-start.30
  300.4 1.3 shard_map.188
  301.7 5.2 %collective-permute-start.23 = (bf16[128,2048]{1,0:T(8,128)(2,1)}, bf16[128,2048]{1,0:T(8,128)(2,1)S(1)}, u32[]{:S(2)}, u32[]{:S(2)}) collective-permute-start(bf16[128,2048]{1,0:T(8,128)(2,1)} %shard_map.188), channel_id=1, source_target_pairs={{0,15},{1,0},{2,1},{3,2},{4,3},{5,4},{6,5},{7,6},{8,7},{9,8},{10,9... | collective-permute-start | bytes 1572872 | tf_op jit(solution)/shard_map/ppermute | solution.py:283
  306.9 9.0 %collective-permute-done.30.sum_ref = bf16[128,2048]{1,0:T(8,128)(2,1)S(1)} collective-permute-done((bf16[128,2048]{1,0:T(8,128)(2,1)S(1)}, bf16[128,2048]{1,0:T(8,128)(2,1)S(1)}, u32[]{:S(2)}, u32[]{:S(2)}) %collective-permute-start.30) | collective-permute-done | bytes 524320 | tf_op jit(solution)/shard_map/ppermute | solution.py:283
  317.2 1.9 collective-permute-start.31
  319.2 1.7 shard_map.183
  322.8 7.0 %collective-permute-done.31.down_ref = bf16[128,2048]{1,0:T(8,128)(2,1)} collective-permute-done((bf16[128,2048]{1,0:T(8,128)(2,1)}, bf16[128,2048]{1,0:T(8,128)(2,1)}, u32[]{:S(2)}, u32[]{:S(2)}) %collective-permute-start.31) | collective-permute-done | bytes 524320 | tf_op jit(solution)/shard_map/ppermute | solution.py:283
  329.8 2.5 shard_map.194
  (125 shorter events, 32.1 us)
Async XLA Ops:
  7.2 71.2 %copy-start.32 = (s32[16,384]{1,0:T(8,128)S(1)}, s32[16,384]{1,0:T(8,128)}, u32[]{:S(2)}) copy-start(s32[16,384]{1,0:T(8,128)} %constant.51.clone.map_ref) | copy-start | bytes 73732
  7.2 158.4 %all-gather.2.cloned.1.call-start = ((), (), s32[]{:S(2)}) async-start(), calls=%async_computation.5 | async-start | bytes 3538944 | tf_op jit(solution)/shard_map/all_gather | solution.py:291
  7.2 1.0 copy-start.17
  11.8 17.5 %collective-permute-start.1 = (bf16[128,2176]{1,0:T(8,128)(2,1)S(1)}, bf16[128,2176]{1,0:T(8,128)(2,1)S(1)}, u32[]{:S(2)}, u32[]{:S(2)}) collective-permute-start(bf16[128,2176]{1,0:T(8,128)(2,1)S(1)} %shard_map.174.refs_0_.refs_9_), channel_id=1, source_target_pairs={{0,1},{1,2},{2,3},{3,4},{4,5},{5,6},{6,7},{7,8},{8,9},{9,10},{10,1... | collective-permute-start | bytes 1671176 | tf_op jit(solution)/shard_map/ppermute | solution.py:283
  14.7 16.5 %collective-permute-start = (bf16[128,2176]{1,0:T(8,128)(2,1)S(1)}, bf16[128,2176]{1,0:T(8,128)(2,1)S(1)}, u32[]{:S(2)}, u32[]{:S(2)}) collective-permute-start(bf16[128,2176]{1,0:T(8,128)(2,1)S(1)} %shard_map.174.refs_0_.refs_9_), channel_id=1, source_target_pairs={{0,15},{1,0},{2,1},{3,2},{4,3},{5,4},{6,5},{7,6},{8,7},{9,8},{10,9... | collective-permute-start | bytes 1671176 | tf_op jit(solution)/shard_map/ppermute | solution.py:283
  29.3 16.6 %collective-permute-start.3 = (bf16[128,2176]{1,0:T(8,128)(2,1)S(1)}, bf16[128,2176]{1,0:T(8,128)(2,1)S(1)}, u32[]{:S(2)}, u32[]{:S(2)}) collective-permute-start(bf16[128,2176]{1,0:T(8,128)(2,1)S(1)} %collective-permute-done.1.refs_2_.refs_11_), channel_id=1, source_target_pairs={{0,1},{1,2},{2,3},{3,4},{4,5},{5,6},{6,7},{7,8},{8,9},{9,10},{10,1... | collective-permute-start | bytes 1671176 | tf_op jit(solution)/shard_map/ppermute | solution.py:283
  31.2 17.4 %collective-permute-start.2 = (bf16[128,2176]{1,0:T(8,128)(2,1)S(1)}, bf16[128,2176]{1,0:T(8,128)(2,1)S(1)}, u32[]{:S(2)}, u32[]{:S(2)}) collective-permute-start(bf16[128,2176]{1,0:T(8,128)(2,1)S(1)} %collective-permute-done.refs_1_.refs_10_), channel_id=1, source_target_pairs={{0,15},{1,0},{2,1},{3,2},{4,3},{5,4},{6,5},{7,6},{8,7},{9,8},{10,9... | collective-permute-start | bytes 1671176 | tf_op jit(solution)/shard_map/ppermute | solution.py:283
  45.9 15.8 %collective-permute-start.5 = (bf16[128,2176]{1,0:T(8,128)(2,1)S(1)}, bf16[128,2176]{1,0:T(8,128)(2,1)}, u32[]{:S(2)}, u32[]{:S(2)}) collective-permute-start(bf16[128,2176]{1,0:T(8,128)(2,1)S(1)} %collective-permute-done.3.refs_4_.refs_13_), channel_id=1, source_target_pairs={{0,1},{1,2},{2,3},{3,4},{4,5},{5,6},{6,7},{7,8},{8,9},{9,10},{10,1... | collective-permute-start | bytes 1671176 | tf_op jit(solution)/shard_map/ppermute | solution.py:283
  48.6 14.9 %collective-permute-start.4 = (bf16[128,2176]{1,0:T(8,128)(2,1)S(1)}, bf16[128,2176]{1,0:T(8,128)(2,1)}, u32[]{:S(2)}, u32[]{:S(2)}) collective-permute-start(bf16[128,2176]{1,0:T(8,128)(2,1)S(1)} %collective-permute-done.2.refs_3_.refs_12_), channel_id=1, source_target_pairs={{0,15},{1,0},{2,1},{3,2},{4,3},{5,4},{6,5},{7,6},{8,7},{9,8},{10,9... | collective-permute-start | bytes 1671176 | tf_op jit(solution)/shard_map/ppermute | solution.py:283
  61.6 15.0 %collective-permute-start.7 = (bf16[128,2176]{1,0:T(8,128)(2,1)}, bf16[128,2176]{1,0:T(8,128)(2,1)S(1)}, u32[]{:S(2)}, u32[]{:S(2)}) collective-permute-start(bf16[128,2176]{1,0:T(8,128)(2,1)} %collective-permute-done.5.refs_6_.refs_15_), channel_id=1, source_target_pairs={{0,1},{1,2},{2,3},{3,4},{4,5},{5,6},{6,7},{7,8},{8,9},{9,10},{10,1... | collective-permute-start | bytes 1671176 | tf_op jit(solution)/shard_map/ppermute | solution.py:283
  63.6 14.9 %collective-permute-start.6 = (bf16[128,2176]{1,0:T(8,128)(2,1)}, bf16[128,2176]{1,0:T(8,128)(2,1)S(1)}, u32[]{:S(2)}, u32[]{:S(2)}) collective-permute-start(bf16[128,2176]{1,0:T(8,128)(2,1)} %collective-permute-done.4.refs_5_.refs_14_), channel_id=1, source_target_pairs={{0,15},{1,0},{2,1},{3,2},{4,3},{5,4},{6,5},{7,6},{8,7},{9,8},{10,9... | collective-permute-start | bytes 1671176 | tf_op jit(solution)/shard_map/ppermute | solution.py:283
  78.4 9.8 %copy-start.6 = (bf16[128,2176]{1,0:T(8,128)(2,1)}, bf16[128,2176]{1,0:T(8,128)(2,1)S(1)}, u32[]{:S(2)}) copy-start(bf16[128,2176]{1,0:T(8,128)(2,1)S(1)} %collective-permute-done.6.refs_7_.refs_16_) | copy-start | bytes 1671172
  78.4 1.3 copy-start.5
  79.7 1.1 copy-start.8
  80.7 1.1 copy-start.10
  88.3 18.8 %copy-start.36 = (s32[8,128]{1,0:T(8,128)S(1)}, s32[8,128]{1,0:T(8,128)}, u32[]{:S(2)}) copy-start(s32[8,128]{1,0:T(8,128)} %constant.52.clone.map_ref) | copy-start | bytes 12292
  88.3 51.9 %copy-start.15 = (s32[288,8]{1,0:T(8,128)S(1)}, s32[288,8]{1,0:T(8,128)}, u32[]{:S(2)}) copy-start(s32[288,8]{1,0:T(8,128)} %constant.54.clone.refs_4_.place_ref) | copy-start | bytes 27652
  88.3 45.8 %all-to-all-start = ((bf16[4,96,2048]{2,1,0:T(8,128)(2,1)}), bf16[4,96,2048]{2,1,0:T(8,128)(2,1)S(1)}, u32[]{:S(2)}, u32[]{:S(2)}) async-start(bf16[4,96,2048]{2,1,0:T(8,128)(2,1)} %bitcast.51), calls=%async_computation | async-start | bytes 3145728 | tf_op jit(solution)/shard_map/all_to_all | solution.py:287
  92.9 14.1 %collective-permute-start.9 = (bf16[128,2176]{1,0:T(8,128)(2,1)}, bf16[128,2176]{1,0:T(8,128)(2,1)S(1)}, u32[]{:S(2)}, u32[]{:S(2)}) collective-permute-start(bf16[128,2176]{1,0:T(8,128)(2,1)} %copy-done.9), channel_id=1, source_target_pairs={{0,1},{1,2},{2,3},{3,4},{4,5},{5,6},{6,7},{7,8},{8,9},{9,10},{10,1... | collective-permute-start | bytes 1671176 | tf_op jit(solution)/shard_map/ppermute | solution.py:283
  94.8 19.8 %collective-permute-start.8 = (bf16[128,2176]{1,0:T(8,128)(2,1)}, bf16[128,2176]{1,0:T(8,128)(2,1)S(1)}, u32[]{:S(2)}, u32[]{:S(2)}) collective-permute-start(bf16[128,2176]{1,0:T(8,128)(2,1)} %copy-done.6), channel_id=1, source_target_pairs={{0,15},{1,0},{2,1},{3,2},{4,3},{5,4},{6,5},{7,6},{8,7},{9,8},{10,9... | collective-permute-start | bytes 1671176 | tf_op jit(solution)/shard_map/ppermute | solution.py:283
  108.8 18.5 %collective-permute-start.10 = (bf16[48,2048]{1,0:T(8,128)(2,1)S(1)}, bf16[48,2048]{1,0:T(8,128)(2,1)S(1)}, u32[]{:S(2)}, u32[]{:S(2)}) collective-permute-start(bf16[48,2048]{1,0:T(8,128)(2,1)S(1)} %get-tuple-element.40), channel_id=1, source_target_pairs={{0,1},{1,2},{2,3},{3,4},{4,5},{5,6},{6,7},{7,8},{8,9},{9,10},{10,1... | collective-permute-start | bytes 589832 | tf_op jit(solution)/shard_map/ppermute | solution.py:283
  110.7 28.8 %collective-permute-start.12 = (bf16[48,2048]{1,0:T(8,128)(2,1)}, bf16[48,2048]{1,0:T(8,128)(2,1)S(1)}, u32[]{:S(2)}, u32[]{:S(2)}) collective-permute-start(bf16[48,2048]{1,0:T(8,128)(2,1)} %get-tuple-element.44), channel_id=1, source_target_pairs={{0,2},{1,3},{2,4},{3,5},{4,6},{5,7},{6,8},{7,9},{8,10},{9,11},{10,... | collective-permute-start | bytes 589832 | tf_op jit(solution)/shard_map/ppermute | solution.py:283
  115.3 12.0 %copy-start.2 = (bf16[128,2176]{1,0:T(8,128)(2,1)}, bf16[128,2176]{1,0:T(8,128)(2,1)S(1)}, u32[]{:S(2)}) copy-start(bf16[128,2176]{1,0:T(8,128)(2,1)S(1)} %collective-permute-done.8.block_ref.refs_0_.refs_2_) | copy-start | bytes 1671172
  117.2 23.0 %collective-permute-start.11 = (bf16[48,2048]{1,0:T(8,128)(2,1)}, bf16[48,2048]{1,0:T(8,128)(2,1)}, u32[]{:S(2)}, u32[]{:S(2)}) collective-permute-start(bf16[48,2048]{1,0:T(8,128)(2,1)} %get-tuple-element.43), channel_id=1, source_target_pairs={{0,15},{1,0},{2,1},{3,2},{4,3},{5,4},{6,5},{7,6},{8,7},{9,8},{10,9... | collective-permute-start | bytes 589832 | tf_op jit(solution)/shard_map/ppermute | solution.py:283
  120.4 19.8 %collective-permute-start.13 = (bf16[48,2048]{1,0:T(8,128)(2,1)}, bf16[48,2048]{1,0:T(8,128)(2,1)}, u32[]{:S(2)}, u32[]{:S(2)}) collective-permute-start(bf16[48,2048]{1,0:T(8,128)(2,1)} %get-tuple-element.45), channel_id=1, source_target_pairs={{0,14},{1,15},{2,0},{3,1},{4,2},{5,3},{6,4},{7,5},{8,6},{9,7},{10,... | collective-permute-start | bytes 589832 | tf_op jit(solution)/shard_map/ppermute | solution.py:283
  125.2 11.5 %collective-permute-start.14 = (bf16[32,2048]{1,0:T(8,128)(2,1)}, bf16[32,2048]{1,0:T(8,128)(2,1)}, u32[]{:S(2)}, u32[]{:S(2)}) collective-permute-start(bf16[32,2048]{1,0:T(8,128)(2,1)} %get-tuple-element.46), channel_id=1, source_target_pairs={{0,3},{1,4},{2,5},{3,6},{4,7},{5,8},{6,9},{7,10},{8,11},{9,12},{10... | collective-permute-start | bytes 393224 | tf_op jit(solution)/shard_map/ppermute | solution.py:283
  127.3 12.2 %collective-permute-start.15 = (bf16[32,2048]{1,0:T(8,128)(2,1)}, bf16[32,2048]{1,0:T(8,128)(2,1)}, u32[]{:S(2)}, u32[]{:S(2)}) collective-permute-start(bf16[32,2048]{1,0:T(8,128)(2,1)} %get-tuple-element.47), channel_id=1, source_target_pairs={{0,13},{1,14},{2,15},{3,0},{4,1},{5,2},{6,3},{7,4},{8,5},{9,6},{10... | collective-permute-start | bytes 393224 | tf_op jit(solution)/shard_map/ppermute | solution.py:283
  140.2 1.1 copy-start.3
  147.7 1.1 copy-start.12
  148.8 4.7 %copy-start.37 = (s32[672]{0:T(1024)S(1)}, s32[672]{0:T(1024)}, u32[]{:S(2)}) copy-start(s32[672]{0:T(1024)} %constant.49.clone) | copy-start | bytes 8068
  148.8 4.7 %copy-start.38 = (s32[672]{0:T(1024)S(1)}, s32[672]{0:T(1024)}, u32[]{:S(2)}) copy-start(s32[672]{0:T(1024)} %constant.48.clone) | copy-start | bytes 8068
  148.8 4.7 %copy-start.39 = (s32[672]{0:T(1024)S(1)}, s32[672]{0:T(1024)}, u32[]{:S(2)}) copy-start(s32[672]{0:T(1024)} %constant.47.clone) | copy-start | bytes 8068
  148.8 4.7 %copy-start.40 = (pred[672]{0:T(1024)(128)(4,1)S(1)}, pred[672]{0:T(1024)(128)(4,1)}, u32[]{:S(2)}) copy-start(pred[672]{0:T(1024)(128)(4,1)} %constant.50.clone) | copy-start | bytes 2020
  148.8 4.9 %copy-start.20 = (bf16[1,1,640,384]{3,2,1,0:T(8,128)(2,1)S(1)}, bf16[1,1,640,384]{3,2,1,0:T(8,128)(2,1)}, u32[]{:S(2)}) copy-start(bf16[1,1,640,384]{3,2,1,0:T(8,128)(2,1)} %param.20) | copy-start | bytes 1474564
  148.8 16.7 %all-to-all-start.1 = ((bf16[4,72,2048]{2,1,0:T(8,128)(2,1)}), bf16[4,72,2048]{2,1,0:T(8,128)(2,1)}, u32[]{:S(2)}, u32[]{:S(2)}) async-start(bf16[4,72,2048]{2,1,0:T(8,128)(2,1)} %bitcast.45), calls=%async_computation.1 | async-start | bytes 2359296 | tf_op jit(solution)/shard_map/all_to_all | solution.py:287
  153.5 167.4 %reduce-scatter.2.cloned.1.call-start = ((), (), s32[]{:S(2)}) async-start(), calls=%async_computation.6 | async-start | bytes 3538944 | tf_op jit(solution)/shard_map/reduce_scatter | solution.py:343
  170.5 1.1 copy-start.13
  171.6 5.5 %copy-start.23 = (bf16[288,384]{1,0:T(8,128)(2,1)}, bf16[288,384]{1,0:T(8,128)(2,1)S(1)}, u32[]{:S(2)}) copy-start(bf16[288,384]{1,0:T(8,128)(2,1)S(1)} %get-tuple-element.52.last_ref) | copy-start | bytes 663556
  177.1 1.9 copy-start.11
  177.1 1.9 copy-start.21
  183.8 1.3 copy-start.14
  183.9 15.3 %copy-start.16 = (s32[288,8]{1,0:T(8,128)S(1)}, s32[288,8]{1,0:T(8,128)}, u32[]{:S(2)}) copy-start(s32[288,8]{1,0:T(8,128)} %constant.54.clone.refs_4_.place_ref) | copy-start | bytes 27652
  202.4 37.2 %copy-start.28 = (bf16[128,128]{1,0:T(8,128)(2,1)S(1)}, bf16[128,128]{1,0:T(8,128)(2,1)}, u32[]{:S(2)}) copy-start(bf16[128,128]{1,0:T(8,128)(2,1)} %copy-done.27) | copy-start | bytes 98308
  202.4 43.7 %all-to-all-start.3 = ((bf16[4,96,2048]{2,1,0:T(8,128)(2,1)}), bf16[4,96,2048]{2,1,0:T(8,128)(2,1)S(1)}, u32[]{:S(2)}, u32[]{:S(2)}) async-start(bf16[4,96,2048]{2,1,0:T(8,128)(2,1)} %bitcast.44), calls=%async_computation.3 | async-start | bytes 3145728 | tf_op jit(solution)/shard_map/all_to_all | solution.py:287
  206.1 19.9 %collective-permute-start.18 = (bf16[32,2048]{1,0:T(8,128)(2,1)S(1)}, bf16[32,2048]{1,0:T(8,128)(2,1)S(1)}, u32[]{:S(2)}, u32[]{:S(2)}) collective-permute-start(bf16[32,2048]{1,0:T(8,128)(2,1)S(1)} %get-tuple-element.54), channel_id=1, source_target_pairs={{0,13},{1,14},{2,15},{3,0},{4,1},{5,2},{6,3},{7,4},{8,5},{9,6},{10... | collective-permute-start | bytes 393224 | tf_op jit(solution)/shard_map/ppermute | solution.py:283
  213.4 17.4 %collective-permute-start.17 = (bf16[48,2048]{1,0:T(8,128)(2,1)S(1)}, bf16[48,2048]{1,0:T(8,128)(2,1)S(1)}, u32[]{:S(2)}, u32[]{:S(2)}) collective-permute-start(bf16[48,2048]{1,0:T(8,128)(2,1)S(1)} %get-tuple-element.53), channel_id=1, source_target_pairs={{0,14},{1,15},{2,0},{3,1},{4,2},{5,3},{6,4},{7,5},{8,6},{9,7},{10,... | collective-permute-start | bytes 589832 | tf_op jit(solution)/shard_map/ppermute | solution.py:283
  215.8 15.0 %collective-permute-start.16 = (bf16[48,2048]{1,0:T(8,128)(2,1)S(1)}, bf16[48,2048]{1,0:T(8,128)(2,1)S(1)}, u32[]{:S(2)}, u32[]{:S(2)}) collective-permute-start(bf16[48,2048]{1,0:T(8,128)(2,1)S(1)} %get-tuple-element.50), channel_id=1, source_target_pairs={{0,15},{1,0},{2,1},{3,2},{4,3},{5,4},{6,5},{7,6},{8,7},{9,8},{10,9... | collective-permute-start | bytes 589832 | tf_op jit(solution)/shard_map/ppermute | solution.py:283
  219.2 20.5 %collective-permute-start.24 = (bf16[48,2048]{1,0:T(8,128)(2,1)}, bf16[48,2048]{1,0:T(8,128)(2,1)S(1)}, u32[]{:S(2)}, u32[]{:S(2)}) collective-permute-start(bf16[48,2048]{1,0:T(8,128)(2,1)} %get-tuple-element.64), channel_id=1, source_target_pairs={{0,1},{1,2},{2,3},{3,4},{4,5},{5,6},{6,7},{7,8},{8,9},{9,10},{10,1... | collective-permute-start | bytes 589832 | tf_op jit(solution)/shard_map/ppermute | solution.py:283
  221.6 18.0 %collective-permute-start.25 = (bf16[48,2048]{1,0:T(8,128)(2,1)}, bf16[48,2048]{1,0:T(8,128)(2,1)S(1)}, u32[]{:S(2)}, u32[]{:S(2)}) collective-permute-start(bf16[48,2048]{1,0:T(8,128)(2,1)} %get-tuple-element.65), channel_id=1, source_target_pairs={{0,2},{1,3},{2,4},{3,5},{4,6},{5,7},{6,8},{7,9},{8,10},{9,11},{10,... | collective-permute-start | bytes 589832 | tf_op jit(solution)/shard_map/ppermute | solution.py:283
  226.0 13.6 %collective-permute-start.26 = (bf16[32,2048]{1,0:T(8,128)(2,1)}, bf16[32,2048]{1,0:T(8,128)(2,1)S(1)}, u32[]{:S(2)}, u32[]{:S(2)}) collective-permute-start(bf16[32,2048]{1,0:T(8,128)(2,1)} %get-tuple-element.66), channel_id=1, source_target_pairs={{0,3},{1,4},{2,5},{3,6},{4,7},{5,8},{6,9},{7,10},{8,11},{9,12},{10... | collective-permute-start | bytes 393224 | tf_op jit(solution)/shard_map/ppermute | solution.py:283
  230.8 1.3 copy-start.1
  233.4 11.9 %collective-permute-start.19 = (bf16[128,2048]{1,0:T(8,128)(2,1)S(1)}, bf16[128,2048]{1,0:T(8,128)(2,1)S(1)}, u32[]{:S(2)}, u32[]{:S(2)}) collective-permute-start(bf16[128,2048]{1,0:T(8,128)(2,1)S(1)} %shard_map.184), channel_id=1, source_target_pairs={{0,15},{1,0},{2,1},{3,2},{4,3},{5,4},{6,5},{7,6},{8,7},{9,8},{10,9... | collective-permute-start | bytes 1572872 | tf_op jit(solution)/shard_map/ppermute | solution.py:283
  241.0 20.4 %collective-permute-start.27 = (bf16[128,2048]{1,0:T(8,128)(2,1)}, bf16[128,2048]{1,0:T(8,128)(2,1)}, u32[]{:S(2)}, u32[]{:S(2)}) collective-permute-start(bf16[128,2048]{1,0:T(8,128)(2,1)} %shard_map.189), channel_id=1, source_target_pairs={{0,1},{1,2},{2,3},{3,4},{4,5},{5,6},{6,7},{7,8},{8,9},{9,10},{10,1... | collective-permute-start | bytes 1572872 | tf_op jit(solution)/shard_map/ppermute | solution.py:283
  246.1 1.0 copy-start.19
  247.6 17.9 %collective-permute-start.20 = (bf16[128,2048]{1,0:T(8,128)(2,1)S(1)}, bf16[128,2048]{1,0:T(8,128)(2,1)S(1)}, u32[]{:S(2)}, u32[]{:S(2)}) collective-permute-start(bf16[128,2048]{1,0:T(8,128)(2,1)S(1)} %shard_map.185), channel_id=1, source_target_pairs={{0,15},{1,0},{2,1},{3,2},{4,3},{5,4},{6,5},{7,6},{8,7},{9,8},{10,9... | collective-permute-start | bytes 1572872 | tf_op jit(solution)/shard_map/ppermute | solution.py:283
  262.9 17.4 %collective-permute-start.28 = (bf16[128,2048]{1,0:T(8,128)(2,1)S(1)}, bf16[128,2048]{1,0:T(8,128)(2,1)S(1)}, u32[]{:S(2)}, u32[]{:S(2)}) collective-permute-start(bf16[128,2048]{1,0:T(8,128)(2,1)S(1)} %shard_map.190), channel_id=1, source_target_pairs={{0,1},{1,2},{2,3},{3,4},{4,5},{5,6},{6,7},{7,8},{8,9},{9,10},{10,1... | collective-permute-start | bytes 1572872 | tf_op jit(solution)/shard_map/ppermute | solution.py:283
  265.9 16.8 %collective-permute-start.21 = (bf16[128,2048]{1,0:T(8,128)(2,1)S(1)}, bf16[128,2048]{1,0:T(8,128)(2,1)S(1)}, u32[]{:S(2)}, u32[]{:S(2)}) collective-permute-start(bf16[128,2048]{1,0:T(8,128)(2,1)S(1)} %shard_map.186), channel_id=1, source_target_pairs={{0,15},{1,0},{2,1},{3,2},{4,3},{5,4},{6,5},{7,6},{8,7},{9,8},{10,9... | collective-permute-start | bytes 1572872 | tf_op jit(solution)/shard_map/ppermute | solution.py:283
  280.7 17.3 %collective-permute-start.29 = (bf16[128,2048]{1,0:T(8,128)(2,1)S(1)}, bf16[128,2048]{1,0:T(8,128)(2,1)S(1)}, u32[]{:S(2)}, u32[]{:S(2)}) collective-permute-start(bf16[128,2048]{1,0:T(8,128)(2,1)S(1)} %shard_map.191), channel_id=1, source_target_pairs={{0,1},{1,2},{2,3},{3,4},{4,5},{5,6},{6,7},{7,8},{8,9},{9,10},{10,1... | collective-permute-start | bytes 1572872 | tf_op jit(solution)/shard_map/ppermute | solution.py:283
  283.1 17.3 %collective-permute-start.22 = (bf16[128,2048]{1,0:T(8,128)(2,1)S(1)}, bf16[128,2048]{1,0:T(8,128)(2,1)S(1)}, u32[]{:S(2)}, u32[]{:S(2)}) collective-permute-start(bf16[128,2048]{1,0:T(8,128)(2,1)S(1)} %shard_map.187), channel_id=1, source_target_pairs={{0,15},{1,0},{2,1},{3,2},{4,3},{5,4},{6,5},{7,6},{8,7},{9,8},{10,9... | collective-permute-start | bytes 1572872 | tf_op jit(solution)/shard_map/ppermute | solution.py:283
  298.5 17.5 %collective-permute-start.30 = (bf16[128,2048]{1,0:T(8,128)(2,1)S(1)}, bf16[128,2048]{1,0:T(8,128)(2,1)S(1)}, u32[]{:S(2)}, u32[]{:S(2)}) collective-permute-start(bf16[128,2048]{1,0:T(8,128)(2,1)S(1)} %shard_map.192), channel_id=1, source_target_pairs={{0,1},{1,2},{2,3},{3,4},{4,5},{5,6},{6,7},{7,8},{8,9},{9,10},{10,1... | collective-permute-start | bytes 1572872 | tf_op jit(solution)/shard_map/ppermute | solution.py:283
  301.7 17.5 %copy-start.22 = (bf16[384,384]{1,0:T(8,128)(2,1)S(1)}, bf16[384,384]{1,0:T(8,128)(2,1)}, u32[]{:S(2)}) copy-start(bf16[384,384]{1,0:T(8,128)(2,1)} %copy-done.21) | copy-start | bytes 884740
  301.7 17.5 %copy-start.24 = (bf16[288,384]{1,0:T(8,128)(2,1)S(1)}, bf16[288,384]{1,0:T(8,128)(2,1)}, u32[]{:S(2)}) copy-start(bf16[288,384]{1,0:T(8,128)(2,1)} %copy-done.23) | copy-start | bytes 663556
  301.7 21.1 %collective-permute-start.23 = (bf16[128,2048]{1,0:T(8,128)(2,1)}, bf16[128,2048]{1,0:T(8,128)(2,1)S(1)}, u32[]{:S(2)}, u32[]{:S(2)}) collective-permute-start(bf16[128,2048]{1,0:T(8,128)(2,1)} %shard_map.188), channel_id=1, source_target_pairs={{0,15},{1,0},{2,1},{3,2},{4,3},{5,4},{6,5},{7,6},{8,7},{9,8},{10,9... | collective-permute-start | bytes 1572872 | tf_op jit(solution)/shard_map/ppermute | solution.py:283
  317.2 12.6 %collective-permute-start.31 = (bf16[128,2048]{1,0:T(8,128)(2,1)}, bf16[128,2048]{1,0:T(8,128)(2,1)}, u32[]{:S(2)}, u32[]{:S(2)}) collective-permute-start(bf16[128,2048]{1,0:T(8,128)(2,1)} %shard_map.193), channel_id=1, source_target_pairs={{0,1},{1,2},{2,3},{3,4},{4,5},{5,6},{6,7},{7,8},{8,9},{9,10},{10,1... | collective-permute-start | bytes 1572872 | tf_op jit(solution)/shard_map/ppermute | solution.py:283
  (14 other events, 10.7 us)
Sparse Core Ops, SparseCore 0:
  11.9 35.6 all-gather.1
  184.0 40.5 reduce-scatter.1

commit v6 on v5

--- a/solution.py
+++ b/solution.py
@@ -97,66 +97,72 @@
         first += rows
 
 
-def pick_kernel(blocks, messages, z_ref, map_ref, *refs):
-    token_refs, routing_refs, refs = refs[:blocks], refs[blocks : 2 * blocks], refs[2 * blocks :]
-    out_ref, select_ref = refs[-2:]
-    rows = out_ref.shape[0]
-    tokens = token_refs[0].shape[0]
-    first = pl.program_id(0) == 0
-
-    @pl.when(first)
-    def _():
-        routing = jnp.concatenate([ref[...] for ref in routing_refs], axis=0)
-        here, _ = slots_of(routing, map_ref[0:1, :] + z_ref[0], map_ref[1:2, :])
-        here = here & ((iota(here.shape, 0) >> (tokens.bit_length() - 1)) == map_ref[2:3, :])
-        select_ref[...] = one_hot(here)
-
-    picked = dot(select_ref[...], jnp.concatenate([ref[...] for ref in token_refs], axis=0), (0, 0))
-    for index in range(messages):
-        place_ref, ref = refs[0], refs[1 + index]
+def pick_kernel(blocks, messages, z_ref, row_ref, lane_ref, place_ref, *refs):
+    arrays, refs = refs[: blocks + messages], refs[blocks + messages :]
+    out_ref, select_ref, tokens_ref = refs[:3]
+    message_refs, copied = refs[3:-1], refs[-1]
+    rows, width = out_ref.shape
+    tokens = arrays[0].shape[0]
+    targets = [tokens_ref.at[pl.ds(index * tokens, tokens), :] for index in range(blocks)] + list(message_refs)
+    copies = [
+        pltpu.make_async_copy(source, target, copied.at[index])
+        for index, (source, target) in enumerate(zip(arrays, targets))
+    ]
+    for copy in copies:
+        copy.start()
+    for copy in copies:
+        copy.wait()
+
+    routing = tokens_ref[:, width:]
+    line, lane = iota((rows, LANES), 1), iota((LANES, rows), 0)
+    expert = row_ref[:, 0:1] + z_ref[0]
+    rank = dot(one_hot(line == expert), routing, (1, 1))
+    here = (rank == row_ref[:, 1:2].astype(F32)) & ((iota(rank.shape, 1) >> 7) == row_ref[:, 2:3])
+    picked = dot(one_hot(here), tokens_ref[:, :width])
+
+    expert = lane_ref[0:1, :] + z_ref[0]
+    rank = dot(routing, one_hot(lane == expert))
+    here = (rank == lane_ref[1:2, :].astype(F32)) & ((iota(rank.shape, 0) >> 7) == lane_ref[2:3, :])
+    select_ref[...] = one_hot(here)
+    eighths = dot(routing, one_hot(lane == expert + N_Y * N_Z))
+    weights = jnp.sum(jnp.where(here, eighths, 0.0), axis=0, keepdims=True)
+    for index, ref in enumerate(message_refs):
         picked = picked + dot(one_hot(iota((rows, ref.shape[0]), 1) == place_ref[:, index : index + 1]), ref[...])
+        lines = dot(ref[:, :LANES], one_hot(lane == lane_ref[3 + index : 4 + index, :]))
+        slots = MESSAGE_SLOTS[index // 2]
+        weights = weights + jnp.sum(jnp.where(iota(lines.shape, 0) == slots, lines, 0.0), axis=0, keepdims=True)
     out_ref[...] = picked.astype(BF16)
-
-    @pl.when(first)
-    def _():
-        routing = jnp.concatenate([ref[...] for ref in routing_refs], axis=0)
-        lane = iota((LANES, rows), 0)
-        eighths = dot(routing, one_hot(lane == map_ref[0:1, :] + z_ref[0] + N_Y * N_Z))
-        weights = jnp.sum(select_ref[...].astype(F32) * eighths, axis=0, keepdims=True)
-        for index in range(messages):
-            ref = refs[1 + index]
-            lines = dot(ref[:, :LANES], one_hot(lane == map_ref[3 + index : 4 + index, :]))
-            line = MESSAGE_SLOTS[index // 2]
-            weights = weights + jnp.sum(
-                jnp.where(iota(lines.shape, 0) == line, lines, 0.0), axis=0, keepdims=True
-            )
-        used = (rows // N_Y - 1) // SLOTS * SLOTS
-        row = iota((rows, rows), 0)
-        is_weights = row == used
-        for y in range(1, N_Y):
-            is_weights = is_weights | (row == used + y * (rows // N_Y))
-        out_ref[:, :rows] = jnp.where(is_weights, weights, picked[:, :rows]).astype(BF16)
+    used = (rows // N_Y - 1) // SLOTS * SLOTS
+    row = iota((rows, rows), 0)
+    is_weights = row == used
+    for y in range(1, N_Y):
+        is_weights = is_weights | (row == used + y * (rows // N_Y))
+    out_ref[:, :rows] = jnp.where(is_weights, weights, picked[:, :rows]).astype(BF16)
 
 
 def pick(z_of, lanes, places, blocks, messages, width):
-    rows, tokens, step = lanes.shape[1], blocks[0].shape[0], 512
-    whole = lambda value: pl.BlockSpec(value.shape, lambda part: (0, 0))
-    others = (jnp.asarray(places),) + tuple(messages) if messages else ()
+    rows, tokens = lanes.shape[1], blocks[0].shape[0]
+    vmem = pl.BlockSpec(memory_space=pltpu.VMEM)
+    count = len(blocks) + len(messages)
     return pl.pallas_call(
         functools.partial(pick_kernel, len(blocks), len(messages)),
-        grid=(width // step,),
         out_shape=(array((rows, width)), array((len(blocks) * tokens, rows))),
-        in_specs=[pl.BlockSpec(memory_space=pltpu.SMEM), whole(lanes)]
-        + [pl.BlockSpec((tokens, step), lambda part: (0, part))] * len(blocks)
-        + [pl.BlockSpec((tokens, LANES), lambda part: (0, width // LANES))] * len(blocks)
-        + [whole(value) for value in others[:1]]
-        + [pl.BlockSpec((value.shape[0], step), lambda part: (0, part)) for value in others[1:]],
-        out_specs=(
-            pl.BlockSpec((rows, step), lambda part: (0, part)),
-            pl.BlockSpec((len(blocks) * tokens, rows), lambda part: (0, 0)),
-        ),
+        in_specs=[pl.BlockSpec(memory_space=pltpu.SMEM)]
+        + [vmem] * 3
+        + [pl.BlockSpec(memory_space=pltpu.HBM)] * count,
+        out_specs=(vmem, vmem),
+        scratch_shapes=[pltpu.VMEM((len(blocks) * tokens, blocks[0].shape[1]), BF16)]
+        + [pltpu.VMEM(message.shape, BF16) for message in messages]
+        + [pltpu.SemaphoreType.DMA((count,))],
         compiler_params=pltpu.CompilerParams(vmem_limit_bytes=VMEM_BYTES),
-    )(z_of, jnp.asarray(lanes), *blocks, *blocks, *others)
+    )(
+        z_of,
+        jnp.asarray(np.ascontiguousarray(lanes[:8].T)),
+        jnp.asarray(lanes),
+        jnp.asarray(places),
+        *blocks,
+        *messages,
+    )
 
 
 MESSAGE_KEYS = tuple((step, way) for step in range(3) for way in range(2))
@@ -213,7 +219,7 @@
     out_ref[...] = out.astype(BF16)
 
 
-def expert_kernel(y_ref, rows_ref, matrix_ref, cotangent_ref, hidden_ref, grad_ref, row_grads_ref):
+def expert_kernel(y_ref, rows_ref, gate_ref, up_ref, cotangent_ref, hidden_ref, grad_ref, row_grads_ref):
     rows = rows_ref.shape[0]
     of_y = rows // N_Y
     units = hidden_ref.shape[1]
@@ -226,16 +232,18 @@
     eighths = jnp.where(lane == row - first + y_ref[0] * of_y, eighths, 0.0)
     weight = jnp.sum(eighths, axis=1, keepdims=True) * 0.125
 
-    pre = dot(rows_ref[...], matrix_ref[...])
-    gate_pre, up_pre = pre[:, :units], pre[:, units:]
+    gate_pre, up_pre = dot(rows_ref[...], gate_ref[...]), dot(rows_ref[...], up_ref[...])
     sigmoid_gate = jax.nn.sigmoid(gate_pre)
     activation = gate_pre * sigmoid_gate
     hidden_ref[...] = (activation * up_pre * weight).astype(BF16)
     act_slope = sigmoid_gate * (1.0 + gate_pre * (1.0 - sigmoid_gate))
     scaled = cotangent_ref[...].astype(F32) * weight
-    grad_ref[:, :units] = (scaled * up_pre * act_slope).astype(BF16)
-    grad_ref[:, units:] = (scaled * activation).astype(BF16)
-    row_grads_ref[...] = dot(grad_ref[...], matrix_ref[...], (1, 1)).astype(BF16)
+    grad_gate = (scaled * up_pre * act_slope).astype(BF16)
+    grad_up = (scaled * activation).astype(BF16)
+    grad_ref[:, :units] = grad_gate
+    grad_ref[:, units:] = grad_up
+    row_grads = dot(grad_gate, gate_ref[...], (1, 1)) + dot(grad_up, up_ref[...], (1, 1))
+    row_grads_ref[...] = row_grads.astype(BF16)
 
 
 def meet_kernel(first_ref, second_ref, third_ref, messages_ref, grads_ref, own_ref, out_ref):
@@ -275,7 +283,7 @@
     block, width = tokens.shape[1:]
     y, z = lax.axis_index("y").astype(jnp.int32), lax.axis_index("z").astype(jnp.int32)
     y_of, z_of = y.reshape(1), z.reshape(1)
-    near_lanes, _, near_origin = row_maps(NEAR, NEAR_ROWS, len(NEAR))
+    near_lanes, near_places, near_origin = row_maps(NEAR, NEAR_ROWS, len(NEAR))
     last_lanes, last_places, last_origin = row_maps(LAST, LAST_ROWS, 2)
     near_count, last_count = N_Y * NEAR_ROWS, N_Y * LAST_ROWS
 
@@ -287,8 +295,9 @@
         return lax.all_to_all(parts, "y", 0, 0, tiled=True).reshape(rows.shape)
 
     own = call(block_kernel, array((block, width + LANES)), expert_ids[0].T, route_weights[0].T, tokens[0])
-    stacked = jnp.concatenate((after(gate_weight[0], own), up_weight[0]), axis=1)
-    matrix = lax.all_gather(stacked, "dp", axis=0, tiled=True)
+
+    gate_matrix = lax.all_gather(gate_weight[0], "dp", axis=0, tiled=True)
+    up_matrix = lax.all_gather(up_weight[0], "dp", axis=0, tiled=True)
 
     group, offset, slot = np.concatenate((near_origin, last_origin), axis=1)
     row_of = ((group * N_Z + (z + offset + N_Z) % N_Z) * SLOTS + slot).astype(jnp.int32)
@@ -302,7 +311,7 @@
         blocks[-hop], blocks[hop] = going
         if hop == REACH - 1:
             near_rows, near_select = pick(
-                z_of, near_lanes, None, [blocks[source] for source in NEAR], (), width
+                z_of, near_lanes, near_places, [blocks[source] for source in NEAR], (), width
             )
     going = [after(part, near_rows) for part in going]
     near_rows = exchange(near_rows)
@@ -331,17 +340,14 @@
             (array((count, units)), array((count, 2 * units)), array((count, width))),
             y_of,
             rows,
-            matrix,
+            gate_matrix,
+            up_matrix,
             cotangent_rows[first : first + count],
             scalars=1,
         )
 
     near_hidden, near_grads, near_back = expert(near_rows, 0)
-    last_hidden, last_grads, last_back = expert(last_rows, near_count)
-    near_terms = after(near_rows, last_grads)
-    terms = (dot(near_terms, near_grads, (0, 0)) + dot(last_rows, last_grads, (0, 0))).astype(BF16)
-    weight_grads = lax.psum_scatter(terms, "dp", scatter_dimension=0, tiled=True).astype(F32)
-    gate_grads, up_grads = weight_grads[None, :, :units], weight_grads[None, :, units:]
+    last_hidden, last_grads, last_back = expert(after(last_rows, near_grads), near_count)
 
     last_back = exchange(last_back)
     parts = call(
@@ -380,6 +386,11 @@
                 )
                 for way in range(2)
             ]
+        if hop == REACH - 1:
+            near_terms, last_terms = after(near_rows, *going), after(last_rows, *going)
+            terms = (dot(near_terms, near_grads, (0, 0)) + dot(last_terms, last_grads, (0, 0))).astype(BF16)
+            weight_grads = lax.psum_scatter(terms, "dp", scatter_dimension=0, tiled=True).astype(F32)
+            gate_grads, up_grads = weight_grads[None, :, :units], weight_grads[None, :, units:]
     going[0] = after(going[0], gate_grads, up_grads, hidden)
     token_grads = call_block(end_kernel, array((block, width), F32), 0, block, *going, near_back, near_select)
     return hidden[None, None], token_grads[None], gate_grads, up_grads

time: 341 us -> 336 us (0.985)
  the two profiles are of different devices: /device:TPU:260 before, /device:TPU:6 now
where the time goes in v6:
time: 336 us; the launch traced here: 333 us
  starting transfers between devices  137 us (41%)
  waiting for transfers between devices  94.9 us (28%)
  Pallas kernels  36.3 us (11%)
  local copies, waits for them, and re-layouts  27 us (8%)
  blocking collectives  16.2 us (5%)
  between operations  14.6 us (4%)
  matrix products  5.31 us (2%)
    ppermute x32, starting transfers between devices, send(): lax.ppermute(value, 'z', [(i, (i + distance) % N_Z) for i in range(N_Z)])  124 us
    ppermute x32, waiting for transfers between devices, send(): lax.ppermute(value, 'z', [(i, (i + distance) % N_Z) for i in range(N_Z)])  94.2 us
    unnamed x102, local copies, waits for them, and re-layouts  25.2 us
    all_to_all x1, blocking collectives, exchange(): return lax.all_to_all(parts, 'y', 0, 0, tiled=True).reshape(rows.shape)  16.2 us
    pallas_call x8, Pallas kernels, call(): pl.pallas_call(kernel, out_shape=out_shape, in_specs=[small] * scalars +...  16.1 us
    all_to_all x3, starting transfers between devices, exchange(): return lax.all_to_all(parts, 'y', 0, 0, tiled=True).reshape(rows.shape)  12.8 us
    pallas_call x2, Pallas kernels, pick(): pl.pallas_call(functools.partial(pick_kernel, len(blocks), len(messages))...  10.7 us
    pallas_call x11, Pallas kernels, call_block(): pl.pallas_call(kernel, grid=(1,), out_shape=out_shape, in_specs=[whole] *...  9.58 us
  transfers between devices with their start and end apart: 38, of which 16 were waited for; matrix products, arithmetic and copies ran while one was open for 1% of the time, Pallas kernels for 8%

profile of v6, /device:TPU:6, one launch (start us, length us, event | category | flops | bytes accessed | tf_op | source)
XLA Modules:
  0.0 332.5 jit_solution(7141431029760475575)
XLA Ops:
  10.7 3.8 %collective-permute-start.1 = (bf16[128,2176]{1,0:T(8,128)(2,1)S(1)}, bf16[128,2176]{1,0:T(8,128)(2,1)S(1)}, u32[]{:S(2)}, u32[]{:S(2)}) collective-permute-start(bf16[128,2176]{1,0:T(8,128)(2,1)S(1)} %shard_map.201.refs_0_), channel_id=1, source_target_pairs={{0,1},{1,2},{2,3},{3,4},{4,5},{5,6},{6,7},{7,8},{8,9},{9,10},{10,1... | collective-permute-start | bytes 1671176 | tf_op jit(solution)/shard_map/ppermute | solution.py:291
  14.5 9.5 %collective-permute-start = (bf16[128,2176]{1,0:T(8,128)(2,1)S(1)}, bf16[128,2176]{1,0:T(8,128)(2,1)S(1)}, u32[]{:S(2)}, u32[]{:S(2)}) collective-permute-start(bf16[128,2176]{1,0:T(8,128)(2,1)S(1)} %shard_map.201.refs_0_), channel_id=1, source_target_pairs={{0,15},{1,0},{2,1},{3,2},{4,3},{5,4},{6,5},{7,6},{8,7},{9,8},{10,9... | collective-permute-start | bytes 1671176 | tf_op jit(solution)/shard_map/ppermute | solution.py:291
  24.0 10.7 %collective-permute-done.1.refs_2_ = bf16[128,2176]{1,0:T(8,128)(2,1)S(1)} collective-permute-done((bf16[128,2176]{1,0:T(8,128)(2,1)S(1)}, bf16[128,2176]{1,0:T(8,128)(2,1)S(1)}, u32[]{:S(2)}, u32[]{:S(2)}) %collective-permute-start.1) | collective-permute-done | bytes 557088 | tf_op jit(solution)/shard_map/ppermute | solution.py:291
  34.7 1.9 collective-permute-start.3
  36.7 5.1 %collective-permute-start.2 = (bf16[128,2176]{1,0:T(8,128)(2,1)S(1)}, bf16[128,2176]{1,0:T(8,128)(2,1)S(1)}, u32[]{:S(2)}, u32[]{:S(2)}) collective-permute-start(bf16[128,2176]{1,0:T(8,128)(2,1)S(1)} %collective-permute-done.refs_1_), channel_id=1, source_target_pairs={{0,15},{1,0},{2,1},{3,2},{4,3},{5,4},{6,5},{7,6},{8,7},{9,8},{10,9... | collective-permute-start | bytes 1671176 | tf_op jit(solution)/shard_map/ppermute | solution.py:291
  41.8 9.8 %collective-permute-done.3.refs_4_ = bf16[128,2176]{1,0:T(8,128)(2,1)S(1)} collective-permute-done((bf16[128,2176]{1,0:T(8,128)(2,1)S(1)}, bf16[128,2176]{1,0:T(8,128)(2,1)S(1)}, u32[]{:S(2)}, u32[]{:S(2)}) %collective-permute-start.3) | collective-permute-done | bytes 557088 | tf_op jit(solution)/shard_map/ppermute | solution.py:291
  51.6 1.9 collective-permute-start.5
  53.6 5.1 %collective-permute-start.4 = (bf16[128,2176]{1,0:T(8,128)(2,1)S(1)}, bf16[128,2176]{1,0:T(8,128)(2,1)}, u32[]{:S(2)}, u32[]{:S(2)}) collective-permute-start(bf16[128,2176]{1,0:T(8,128)(2,1)S(1)} %collective-permute-done.2.refs_3_), channel_id=1, source_target_pairs={{0,15},{1,0},{2,1},{3,2},{4,3},{5,4},{6,5},{7,6},{8,7},{9,8},{10,9... | collective-permute-start | bytes 1671176 | tf_op jit(solution)/shard_map/ppermute | solution.py:291
  58.7 9.0 %collective-permute-done.5.refs_6_ = bf16[128,2176]{1,0:T(8,128)(2,1)} collective-permute-done((bf16[128,2176]{1,0:T(8,128)(2,1)S(1)}, bf16[128,2176]{1,0:T(8,128)(2,1)}, u32[]{:S(2)}, u32[]{:S(2)}) %collective-permute-start.5) | collective-permute-done | bytes 557088 | tf_op jit(solution)/shard_map/ppermute | solution.py:291
  67.7 1.9 collective-permute-start.7
  69.7 5.1 %collective-permute-start.6 = (bf16[128,2176]{1,0:T(8,128)(2,1)}, bf16[128,2176]{1,0:T(8,128)(2,1)S(1)}, u32[]{:S(2)}, u32[]{:S(2)}) collective-permute-start(bf16[128,2176]{1,0:T(8,128)(2,1)} %collective-permute-done.4.refs_5_), channel_id=1, source_target_pairs={{0,15},{1,0},{2,1},{3,2},{4,3},{5,4},{6,5},{7,6},{8,7},{9,8},{10,9... | collective-permute-start | bytes 1671176 | tf_op jit(solution)/shard_map/ppermute | solution.py:291
  74.8 8.3 %collective-permute-done.7.refs_8_ = bf16[128,2176]{1,0:T(8,128)(2,1)} collective-permute-done((bf16[128,2176]{1,0:T(8,128)(2,1)}, bf16[128,2176]{1,0:T(8,128)(2,1)}, u32[]{:S(2)}, u32[]{:S(2)}) %collective-permute-start.7) | collective-permute-done | bytes 557088 | tf_op jit(solution)/shard_map/ppermute | solution.py:291
  85.1 6.3 %shard_map.202 = (bf16[384,2048]{1,0:T(8,128)(2,1)}, bf16[1152,384]{1,0:T(8,128)(2,1)}) custom-call(s32[1]{0:T(128)} %bitcast.1.z_ref, s32[384,8]{1,0:T(8,128)S(1)} %copy-done.29, s32[16,384]{1,0:T(8,128)S(1)} %copy-done.36, s32[384,8]{1,0:T(8,128)S(1)} %jit_solution_.3.place_ref, bf16[128,2176]{1,0:T(8,128)(2,1)S(1)} %shard_map.201.refs_0_, ...), custom_call_target="tpu_custom_call" | custom-call | tf_op jit(solution)/shard_map/pallas_call | solution.py:147
  91.5 4.9 %all-to-all-start = ((bf16[4,96,2048]{2,1,0:T(8,128)(2,1)}), bf16[4,96,2048]{2,1,0:T(8,128)(2,1)S(1)}, u32[]{:S(2)}, u32[]{:S(2)}) async-start(bf16[4,96,2048]{2,1,0:T(8,128)(2,1)} %bitcast.57), calls=%async_computation | async-start | bytes 3145728 | tf_op jit(solution)/shard_map/all_to_all | solution.py:295
  96.4 1.9 collective-permute-start.9
  98.3 5.5 %collective-permute-start.8 = (bf16[128,2176]{1,0:T(8,128)(2,1)}, bf16[128,2176]{1,0:T(8,128)(2,1)S(1)}, u32[]{:S(2)}, u32[]{:S(2)}) collective-permute-start(bf16[128,2176]{1,0:T(8,128)(2,1)} %copy-done.17), channel_id=1, source_target_pairs={{0,15},{1,0},{2,1},{3,2},{4,3},{5,4},{6,5},{7,6},{8,7},{9,8},{10,9... | collective-permute-start | bytes 1671176 | tf_op jit(solution)/shard_map/ppermute | solution.py:291
  103.8 7.1 %collective-permute-done.9.block_ref.refs_1_ = bf16[128,2176]{1,0:T(8,128)(2,1)S(1)} collective-permute-done((bf16[128,2176]{1,0:T(8,128)(2,1)}, bf16[128,2176]{1,0:T(8,128)(2,1)S(1)}, u32[]{:S(2)}, u32[]{:S(2)}) %collective-permute-start.9) | collective-permute-done | bytes 557088 | tf_op jit(solution)/shard_map/ppermute | solution.py:291
  112.7 1.9 collective-permute-start.10
  114.6 1.9 collective-permute-start.12
  118.4 5.1 %collective-permute-start.11 = (bf16[48,2048]{1,0:T(8,128)(2,1)}, bf16[48,2048]{1,0:T(8,128)(2,1)}, u32[]{:S(2)}, u32[]{:S(2)}) collective-permute-start(bf16[48,2048]{1,0:T(8,128)(2,1)} %get-tuple-element.43), channel_id=1, source_target_pairs={{0,15},{1,0},{2,1},{3,2},{4,3},{5,4},{6,5},{7,6},{8,7},{9,8},{10,9... | collective-permute-start | bytes 589832 | tf_op jit(solution)/shard_map/ppermute | solution.py:291
  123.5 4.8 %collective-permute-start.13 = (bf16[48,2048]{1,0:T(8,128)(2,1)}, bf16[48,2048]{1,0:T(8,128)(2,1)}, u32[]{:S(2)}, u32[]{:S(2)}) collective-permute-start(bf16[48,2048]{1,0:T(8,128)(2,1)} %get-tuple-element.45), channel_id=1, source_target_pairs={{0,14},{1,15},{2,0},{3,1},{4,2},{5,3},{6,4},{7,5},{8,6},{9,7},{10,... | collective-permute-start | bytes 589832 | tf_op jit(solution)/shard_map/ppermute | solution.py:291
  128.4 1.9 collective-permute-start.14
  130.3 6.9 %collective-permute-start.15 = (bf16[32,2048]{1,0:T(8,128)(2,1)}, bf16[32,2048]{1,0:T(8,128)(2,1)}, u32[]{:S(2)}, u32[]{:S(2)}) collective-permute-start(bf16[32,2048]{1,0:T(8,128)(2,1)} %get-tuple-element.47), channel_id=1, source_target_pairs={{0,13},{1,14},{2,15},{3,0},{4,1},{5,2},{6,3},{7,4},{8,5},{9,6},{10... | collective-permute-start | bytes 393224 | tf_op jit(solution)/shard_map/ppermute | solution.py:291
  137.3 2.8 collective-permute-done.14.refs_6_
  140.1 3.3 collective-permute-done.15.refs_7_
  143.4 4.4 %shard_map.207 = (bf16[288,2048]{1,0:T(8,128)(2,1)S(1)}, bf16[256,288]{1,0:T(8,128)(2,1)S(1)}) custom-call(s32[1]{0:T(128)} %bitcast.1.z_ref, s32[288,8]{1,0:T(8,128)S(1)} %copy-done.30, s32[16,288]{1,0:T(8,128)S(1)} %copy-done.35, s32[288,8]{1,0:T(8,128)S(1)} %copy-done.16, bf16[128,2176]{1,0:T(8,128)(2,1)S(1)} %collective-permute-done.8.block_ref.refs_0_, ...), custom_call_target="tpu_custom_call" | custom-call | tf_op jit(solution)/shard_map/pallas_call | solution.py:147
  149.6 4.2 %all-to-all-start.1 = ((bf16[4,72,2048]{2,1,0:T(8,128)(2,1)}), bf16[4,72,2048]{2,1,0:T(8,128)(2,1)S(1)}, u32[]{:S(2)}, u32[]{:S(2)}) async-start(bf16[4,72,2048]{2,1,0:T(8,128)(2,1)} %bitcast.49), calls=%async_computation.1 | async-start | bytes 2359296 | tf_op jit(solution)/shard_map/all_to_all | solution.py:295
  156.7 1.4 copy-done.7
  158.1 5.1 %shard_map.204 = (bf16[384,384]{1,0:T(8,128)(2,1)S(1)}, bf16[384,768]{1,0:T(8,128)(2,1)S(1)}, bf16[384,2048]{1,0:T(8,128)(2,1)S(1)}) custom-call(s32[1]{0:T(128)} %bitcast.y_ref, bf16[384,2048]{1,0:T(8,128)(2,1)S(1)} %bitcast.42, bf16[2048,384]{1,0:T(8,128)(2,1)S(1)} %bitcast.46, bf16[2048,384]{1,0:T(8,128)(2,1)} %bitcast.55, ...), custom_call_target="tpu_custom_call" | custom-call | tf_op jit(solution)/shard_map/pallas_call | solution.py:31
  165.9 1.8 copy-done.8
  168.7 4.2 %shard_map.208 = (bf16[288,384]{1,0:T(8,128)(2,1)S(1)}, bf16[288,768]{1,0:T(8,128)(2,1)S(1)}, bf16[288,2048]{1,0:T(8,128)(2,1)S(1)}) custom-call(s32[1]{0:T(128)} %bitcast.y_ref, bf16[288,2048]{1,0:T(8,128)(2,1)S(1)} %bitcast.44, bf16[2048,384]{1,0:T(8,128)(2,1)S(1)} %bitcast.47, bf16[2048,384]{1,0:T(8,128)(2,1)} %bitcast.56, bf16[288,384]{1,0:T(8,128)(2,1)S(1)} %copy-done.11), custom_call_target="tpu_custom_call" | custom-call | tf_op jit(solution)/shard_map/pallas_call | solution.py:31
  172.9 16.2 %all_to_all.20 = bf16[4,72,2048]{2,1,0:T(8,128)(2,1)S(1)} all-to-all(bf16[4,72,2048]{2,1,0:T(8,128)(2,1)S(1)} %bitcast.50), channel_id=1, replica_groups=mesh['dp'=8,'y'=4,'z'=16] {'y'}, dimensions={0} | all-to-all | bytes 2359296 | tf_op jit(solution)/shard_map/all_to_all | solution.py:295
  189.1 1.6 shard_map.209
  194.8 3.7 %all-to-all-start.3 = ((bf16[4,96,2048]{2,1,0:T(8,128)(2,1)}), bf16[4,96,2048]{2,1,0:T(8,128)(2,1)S(1)}, u32[]{:S(2)}, u32[]{:S(2)}) async-start(bf16[4,96,2048]{2,1,0:T(8,128)(2,1)} %bitcast.48), calls=%async_computation.3 | async-start | bytes 3145728 | tf_op jit(solution)/shard_map/all_to_all | solution.py:295
  198.5 7.4 %collective-permute-start.18 = (bf16[32,2048]{1,0:T(8,128)(2,1)}, bf16[32,2048]{1,0:T(8,128)(2,1)S(1)}, u32[]{:S(2)}, u32[]{:S(2)}) collective-permute-start(bf16[32,2048]{1,0:T(8,128)(2,1)} %copy-done.46), channel_id=1, source_target_pairs={{0,13},{1,14},{2,15},{3,0},{4,1},{5,2},{6,3},{7,4},{8,5},{9,6},{10... | collective-permute-start | bytes 393224 | tf_op jit(solution)/shard_map/ppermute | solution.py:291
  205.9 2.3 collective-permute-start.17
  208.2 3.1 collective-permute-start.16
  211.3 2.7 collective-permute-start.24
  214.1 4.4 %collective-permute-start.25 = (bf16[48,2048]{1,0:T(8,128)(2,1)}, bf16[48,2048]{1,0:T(8,128)(2,1)S(1)}, u32[]{:S(2)}, u32[]{:S(2)}) collective-permute-start(bf16[48,2048]{1,0:T(8,128)(2,1)} %copy-done.41), channel_id=1, source_target_pairs={{0,2},{1,3},{2,4},{3,5},{4,6},{5,7},{6,8},{7,9},{8,10},{9,11},{10,... | collective-permute-start | bytes 589832 | tf_op jit(solution)/shard_map/ppermute | solution.py:291
  218.5 4.4 %collective-permute-start.26 = (bf16[32,2048]{1,0:T(8,128)(2,1)}, bf16[32,2048]{1,0:T(8,128)(2,1)S(1)}, u32[]{:S(2)}, u32[]{:S(2)}) collective-permute-start(bf16[32,2048]{1,0:T(8,128)(2,1)} %copy-done.45), channel_id=1, source_target_pairs={{0,3},{1,4},{2,5},{3,6},{4,7},{5,8},{6,9},{7,10},{8,11},{9,12},{10... | collective-permute-start | bytes 393224 | tf_op jit(solution)/shard_map/ppermute | solution.py:291
  224.3 5.2 %collective-permute-start.19 = (bf16[128,2048]{1,0:T(8,128)(2,1)S(1)}, bf16[128,2048]{1,0:T(8,128)(2,1)S(1)}, u32[]{:S(2)}, u32[]{:S(2)}) collective-permute-start(bf16[128,2048]{1,0:T(8,128)(2,1)S(1)} %shard_map.211), channel_id=1, source_target_pairs={{0,15},{1,0},{2,1},{3,2},{4,3},{5,4},{6,5},{7,6},{8,7},{9,8},{10,9... | collective-permute-start | bytes 1572872 | tf_op jit(solution)/shard_map/ppermute | solution.py:291
  229.5 3.7 %collective-permute-done.26.third_ref = bf16[32,2048]{1,0:T(8,128)(2,1)S(1)} collective-permute-done((bf16[32,2048]{1,0:T(8,128)(2,1)}, bf16[32,2048]{1,0:T(8,128)(2,1)S(1)}, u32[]{:S(2)}, u32[]{:S(2)}) %collective-permute-start.26) | collective-permute-done | bytes 131104 | tf_op jit(solution)/shard_map/ppermute | solution.py:291
  233.4 1.3 copy-done.2
  234.6 1.4 shard_map.216
  236.0 5.0 %collective-permute-start.27 = (bf16[128,2048]{1,0:T(8,128)(2,1)}, bf16[128,2048]{1,0:T(8,128)(2,1)S(1)}, u32[]{:S(2)}, u32[]{:S(2)}) collective-permute-start(bf16[128,2048]{1,0:T(8,128)(2,1)} %shard_map.216), channel_id=1, source_target_pairs={{0,1},{1,2},{2,3},{3,4},{4,5},{5,6},{6,7},{7,8},{8,9},{9,10},{10,1... | collective-permute-start | bytes 1572872 | tf_op jit(solution)/shard_map/ppermute | solution.py:291
  244.1 4.4 %collective-permute-done.27.sum_ref = bf16[128,2048]{1,0:T(8,128)(2,1)S(1)} collective-permute-done((bf16[128,2048]{1,0:T(8,128)(2,1)}, bf16[128,2048]{1,0:T(8,128)(2,1)S(1)}, u32[]{:S(2)}, u32[]{:S(2)}) %collective-permute-start.27) | collective-permute-done | bytes 524320 | tf_op jit(solution)/shard_map/ppermute | solution.py:291
  251.3 1.8 fusion.5
  253.2 3.5 %add_convert_fusion = bf16[2048,768]{1,0:T(8,128)(2,1)} fusion(f32[2048,768]{1,0:T(8,128)S(1)} %fusion.5, bf16[384,2048]{1,0:T(8,128)(2,1)S(1)} %bitcast.43, bf16[384,768]{1,0:T(8,128)(2,1)S(1)} %copy-done.15), kind=kOutput, calls=%fused_computation | convolution fusion | flops 1211105280 | bytes 11599872 | tf_op jit(solution)/shard_map/dot_general | solution.py:53
  256.7 2.0 collective-permute-start.20
  258.7 3.8 %collective-permute-start.28 = (bf16[128,2048]{1,0:T(8,128)(2,1)S(1)}, bf16[128,2048]{1,0:T(8,128)(2,1)S(1)}, u32[]{:S(2)}, u32[]{:S(2)}) collective-permute-start(bf16[128,2048]{1,0:T(8,128)(2,1)S(1)} %shard_map.217), channel_id=1, source_target_pairs={{0,1},{1,2},{2,3},{3,4},{4,5},{5,6},{6,7},{7,8},{8,9},{9,10},{10,1... | collective-permute-start | bytes 1572872 | tf_op jit(solution)/shard_map/ppermute | solution.py:291
  262.6 9.1 %collective-permute-done.20.sum_ref = bf16[128,2048]{1,0:T(8,128)(2,1)S(1)} collective-permute-done((bf16[128,2048]{1,0:T(8,128)(2,1)}, bf16[128,2048]{1,0:T(8,128)(2,1)S(1)}, u32[]{:S(2)}, u32[]{:S(2)}) %collective-permute-start.20) | collective-permute-done | bytes 524320 | tf_op jit(solution)/shard_map/ppermute | solution.py:291
  272.1 1.9 collective-permute-start.21
  274.5 3.9 %collective-permute-start.29 = (bf16[128,2048]{1,0:T(8,128)(2,1)S(1)}, bf16[128,2048]{1,0:T(8,128)(2,1)S(1)}, u32[]{:S(2)}, u32[]{:S(2)}) collective-permute-start(bf16[128,2048]{1,0:T(8,128)(2,1)S(1)} %shard_map.218), channel_id=1, source_target_pairs={{0,1},{1,2},{2,3},{3,4},{4,5},{5,6},{6,7},{7,8},{8,9},{9,10},{10,1... | collective-permute-start | bytes 1572872 | tf_op jit(solution)/shard_map/ppermute | solution.py:291
  278.5 9.1 %collective-permute-done.21.sum_ref = bf16[128,2048]{1,0:T(8,128)(2,1)S(1)} collective-permute-done((bf16[128,2048]{1,0:T(8,128)(2,1)S(1)}, bf16[128,2048]{1,0:T(8,128)(2,1)S(1)}, u32[]{:S(2)}, u32[]{:S(2)}) %collective-permute-start.21) | collective-permute-done | bytes 524320 | tf_op jit(solution)/shard_map/ppermute | solution.py:291
  288.1 3.3 collective-permute-start.22
  291.9 2.9 collective-permute-start.30
  294.7 8.4 %collective-permute-done.22.sum_ref = bf16[128,2048]{1,0:T(8,128)(2,1)S(1)} collective-permute-done((bf16[128,2048]{1,0:T(8,128)(2,1)S(1)}, bf16[128,2048]{1,0:T(8,128)(2,1)S(1)}, u32[]{:S(2)}, u32[]{:S(2)}) %collective-permute-start.22) | collective-permute-done | bytes 524320 | tf_op jit(solution)/shard_map/ppermute | solution.py:291
  303.1 1.2 shard_map.215
  304.4 5.3 %collective-permute-start.23 = (bf16[128,2048]{1,0:T(8,128)(2,1)}, bf16[128,2048]{1,0:T(8,128)(2,1)S(1)}, u32[]{:S(2)}, u32[]{:S(2)}) collective-permute-start(bf16[128,2048]{1,0:T(8,128)(2,1)} %shard_map.215), channel_id=1, source_target_pairs={{0,15},{1,0},{2,1},{3,2},{4,3},{5,4},{6,5},{7,6},{8,7},{9,8},{10,9... | collective-permute-start | bytes 1572872 | tf_op jit(solution)/shard_map/ppermute | solution.py:291
  309.7 1.3 shard_map.220
  310.9 1.9 collective-permute-start.31
  312.9 1.7 shard_map.210
  316.7 6.9 %collective-permute-done.31.down_ref = bf16[128,2048]{1,0:T(8,128)(2,1)} collective-permute-done((bf16[128,2048]{1,0:T(8,128)(2,1)}, bf16[128,2048]{1,0:T(8,128)(2,1)}, u32[]{:S(2)}, u32[]{:S(2)}) %collective-permute-start.31) | collective-permute-done | bytes 524320 | tf_op jit(solution)/shard_map/ppermute | solution.py:291
  323.5 2.5 shard_map.221
  (148 shorter events, 32.7 us)
Async XLA Ops:
  7.2 77.2 %copy-start.29 = (s32[384,8]{1,0:T(8,128)S(1)}, s32[384,8]{1,0:T(8,128)}, u32[]{:S(2)}) copy-start(s32[384,8]{1,0:T(8,128)} %constant.57.clone.row_ref) | copy-start | bytes 36868
  7.2 149.5 %all-gather.5.cloned.1.call-start = ((), (), s32[]{:S(2)}) async-start(), calls=%async_computation.6 | async-start | bytes 1769472 | tf_op jit(solution)/shard_map/all_gather | solution.py:299
  7.9 148.8 %all-gather.7.cloned.1.call-start = ((), (), s32[]{:S(2)}) async-start(), calls=%async_computation.7 | async-start | bytes 1769472 | tf_op jit(solution)/shard_map/all_gather | solution.py:300
  10.7 24.0 %collective-permute-start.1 = (bf16[128,2176]{1,0:T(8,128)(2,1)S(1)}, bf16[128,2176]{1,0:T(8,128)(2,1)S(1)}, u32[]{:S(2)}, u32[]{:S(2)}) collective-permute-start(bf16[128,2176]{1,0:T(8,128)(2,1)S(1)} %shard_map.201.refs_0_), channel_id=1, source_target_pairs={{0,1},{1,2},{2,3},{3,4},{4,5},{5,6},{6,7},{7,8},{8,9},{9,10},{10,1... | collective-permute-start | bytes 1671176 | tf_op jit(solution)/shard_map/ppermute | solution.py:291
  14.5 22.1 %collective-permute-start = (bf16[128,2176]{1,0:T(8,128)(2,1)S(1)}, bf16[128,2176]{1,0:T(8,128)(2,1)S(1)}, u32[]{:S(2)}, u32[]{:S(2)}) collective-permute-start(bf16[128,2176]{1,0:T(8,128)(2,1)S(1)} %shard_map.201.refs_0_), channel_id=1, source_target_pairs={{0,15},{1,0},{2,1},{3,2},{4,3},{5,4},{6,5},{7,6},{8,7},{9,8},{10,9... | collective-permute-start | bytes 1671176 | tf_op jit(solution)/shard_map/ppermute | solution.py:291
  34.7 16.9 %collective-permute-start.3 = (bf16[128,2176]{1,0:T(8,128)(2,1)S(1)}, bf16[128,2176]{1,0:T(8,128)(2,1)S(1)}, u32[]{:S(2)}, u32[]{:S(2)}) collective-permute-start(bf16[128,2176]{1,0:T(8,128)(2,1)S(1)} %collective-permute-done.1.refs_2_), channel_id=1, source_target_pairs={{0,1},{1,2},{2,3},{3,4},{4,5},{5,6},{6,7},{7,8},{8,9},{9,10},{10,1... | collective-permute-start | bytes 1671176 | tf_op jit(solution)/shard_map/ppermute | solution.py:291
  36.7 16.9 %collective-permute-start.2 = (bf16[128,2176]{1,0:T(8,128)(2,1)S(1)}, bf16[128,2176]{1,0:T(8,128)(2,1)S(1)}, u32[]{:S(2)}, u32[]{:S(2)}) collective-permute-start(bf16[128,2176]{1,0:T(8,128)(2,1)S(1)} %collective-permute-done.refs_1_), channel_id=1, source_target_pairs={{0,15},{1,0},{2,1},{3,2},{4,3},{5,4},{6,5},{7,6},{8,7},{9,8},{10,9... | collective-permute-start | bytes 1671176 | tf_op jit(solution)/shard_map/ppermute | solution.py:291
  51.6 16.1 %collective-permute-start.5 = (bf16[128,2176]{1,0:T(8,128)(2,1)S(1)}, bf16[128,2176]{1,0:T(8,128)(2,1)}, u32[]{:S(2)}, u32[]{:S(2)}) collective-permute-start(bf16[128,2176]{1,0:T(8,128)(2,1)S(1)} %collective-permute-done.3.refs_4_), channel_id=1, source_target_pairs={{0,1},{1,2},{2,3},{3,4},{4,5},{5,6},{6,7},{7,8},{8,9},{9,10},{10,1... | collective-permute-start | bytes 1671176 | tf_op jit(solution)/shard_map/ppermute | solution.py:291
  53.6 16.1 %collective-permute-start.4 = (bf16[128,2176]{1,0:T(8,128)(2,1)S(1)}, bf16[128,2176]{1,0:T(8,128)(2,1)}, u32[]{:S(2)}, u32[]{:S(2)}) collective-permute-start(bf16[128,2176]{1,0:T(8,128)(2,1)S(1)} %collective-permute-done.2.refs_3_), channel_id=1, source_target_pairs={{0,15},{1,0},{2,1},{3,2},{4,3},{5,4},{6,5},{7,6},{8,7},{9,8},{10,9... | collective-permute-start | bytes 1671176 | tf_op jit(solution)/shard_map/ppermute | solution.py:291
  67.7 15.4 %collective-permute-start.7 = (bf16[128,2176]{1,0:T(8,128)(2,1)}, bf16[128,2176]{1,0:T(8,128)(2,1)}, u32[]{:S(2)}, u32[]{:S(2)}) collective-permute-start(bf16[128,2176]{1,0:T(8,128)(2,1)} %collective-permute-done.5.refs_6_), channel_id=1, source_target_pairs={{0,1},{1,2},{2,3},{3,4},{4,5},{5,6},{6,7},{7,8},{8,9},{9,10},{10,1... | collective-permute-start | bytes 1671176 | tf_op jit(solution)/shard_map/ppermute | solution.py:291
  69.7 14.6 %collective-permute-start.6 = (bf16[128,2176]{1,0:T(8,128)(2,1)}, bf16[128,2176]{1,0:T(8,128)(2,1)S(1)}, u32[]{:S(2)}, u32[]{:S(2)}) collective-permute-start(bf16[128,2176]{1,0:T(8,128)(2,1)} %collective-permute-done.4.refs_5_), channel_id=1, source_target_pairs={{0,15},{1,0},{2,1},{3,2},{4,3},{5,4},{6,5},{7,6},{8,7},{9,8},{10,9... | collective-permute-start | bytes 1671176 | tf_op jit(solution)/shard_map/ppermute | solution.py:291
  84.3 7.1 %copy-start.17 = (bf16[128,2176]{1,0:T(8,128)(2,1)}, bf16[128,2176]{1,0:T(8,128)(2,1)S(1)}, u32[]{:S(2)}) copy-start(bf16[128,2176]{1,0:T(8,128)(2,1)S(1)} %collective-permute-done.6.refs_7_) | copy-start | bytes 1671172
  91.4 19.5 %copy-start.40 = (s32[8,128]{1,0:T(8,128)S(1)}, s32[8,128]{1,0:T(8,128)}, u32[]{:S(2)}) copy-start(s32[8,128]{1,0:T(8,128)} %constant.60.clone.map_ref) | copy-start | bytes 12292
  91.4 25.1 %copy-start.39 = (s32[8,128]{1,0:T(8,128)S(1)}, s32[8,128]{1,0:T(8,128)}, u32[]{:S(2)}) copy-start(s32[8,128]{1,0:T(8,128)} %constant.61.clone.map_ref) | copy-start | bytes 12292
  91.4 52.0 %copy-start.16 = (s32[288,8]{1,0:T(8,128)S(1)}, s32[288,8]{1,0:T(8,128)}, u32[]{:S(2)}) copy-start(s32[288,8]{1,0:T(8,128)} %constant.64.clone.place_ref) | copy-start | bytes 27652
  91.4 51.9 %copy-start.30 = (s32[288,8]{1,0:T(8,128)S(1)}, s32[288,8]{1,0:T(8,128)}, u32[]{:S(2)}) copy-start(s32[288,8]{1,0:T(8,128)} %constant.62.clone.row_ref) | copy-start | bytes 27652
  91.5 51.9 %copy-start.35 = (s32[16,288]{1,0:T(8,128)S(1)}, s32[16,288]{1,0:T(8,128)}, u32[]{:S(2)}) copy-start(s32[16,288]{1,0:T(8,128)} %constant.63.clone.lane_ref) | copy-start | bytes 55300
  91.5 45.8 %all-to-all-start = ((bf16[4,96,2048]{2,1,0:T(8,128)(2,1)}), bf16[4,96,2048]{2,1,0:T(8,128)(2,1)S(1)}, u32[]{:S(2)}, u32[]{:S(2)}) async-start(bf16[4,96,2048]{2,1,0:T(8,128)(2,1)} %bitcast.57), calls=%async_computation | async-start | bytes 3145728 | tf_op jit(solution)/shard_map/all_to_all | solution.py:295
  96.4 14.6 %collective-permute-start.9 = (bf16[128,2176]{1,0:T(8,128)(2,1)}, bf16[128,2176]{1,0:T(8,128)(2,1)S(1)}, u32[]{:S(2)}, u32[]{:S(2)}) collective-permute-start(bf16[128,2176]{1,0:T(8,128)(2,1)} %collective-permute-done.7.refs_8_), channel_id=1, source_target_pairs={{0,1},{1,2},{2,3},{3,4},{4,5},{5,6},{6,7},{7,8},{8,9},{9,10},{10,1... | collective-permute-start | bytes 1671176 | tf_op jit(solution)/shard_map/ppermute | solution.py:291
  98.3 18.3 %collective-permute-start.8 = (bf16[128,2176]{1,0:T(8,128)(2,1)}, bf16[128,2176]{1,0:T(8,128)(2,1)S(1)}, u32[]{:S(2)}, u32[]{:S(2)}) collective-permute-start(bf16[128,2176]{1,0:T(8,128)(2,1)} %copy-done.17), channel_id=1, source_target_pairs={{0,15},{1,0},{2,1},{3,2},{4,3},{5,4},{6,5},{7,6},{8,7},{9,8},{10,9... | collective-permute-start | bytes 1671176 | tf_op jit(solution)/shard_map/ppermute | solution.py:291
  112.7 17.6 %collective-permute-start.10 = (bf16[48,2048]{1,0:T(8,128)(2,1)S(1)}, bf16[48,2048]{1,0:T(8,128)(2,1)S(1)}, u32[]{:S(2)}, u32[]{:S(2)}) collective-permute-start(bf16[48,2048]{1,0:T(8,128)(2,1)S(1)} %get-tuple-element.40), channel_id=1, source_target_pairs={{0,1},{1,2},{2,3},{3,4},{4,5},{5,6},{6,7},{7,8},{8,9},{9,10},{10,1... | collective-permute-start | bytes 589832 | tf_op jit(solution)/shard_map/ppermute | solution.py:291
  114.6 28.7 %collective-permute-start.12 = (bf16[48,2048]{1,0:T(8,128)(2,1)}, bf16[48,2048]{1,0:T(8,128)(2,1)S(1)}, u32[]{:S(2)}, u32[]{:S(2)}) collective-permute-start(bf16[48,2048]{1,0:T(8,128)(2,1)} %get-tuple-element.44), channel_id=1, source_target_pairs={{0,2},{1,3},{2,4},{3,5},{4,6},{5,7},{6,8},{7,9},{8,10},{9,11},{10,... | collective-permute-start | bytes 589832 | tf_op jit(solution)/shard_map/ppermute | solution.py:291
  118.4 25.0 %collective-permute-start.11 = (bf16[48,2048]{1,0:T(8,128)(2,1)}, bf16[48,2048]{1,0:T(8,128)(2,1)}, u32[]{:S(2)}, u32[]{:S(2)}) collective-permute-start(bf16[48,2048]{1,0:T(8,128)(2,1)} %get-tuple-element.43), channel_id=1, source_target_pairs={{0,15},{1,0},{2,1},{3,2},{4,3},{5,4},{6,5},{7,6},{8,7},{9,8},{10,9... | collective-permute-start | bytes 589832 | tf_op jit(solution)/shard_map/ppermute | solution.py:291
  123.5 19.8 %collective-permute-start.13 = (bf16[48,2048]{1,0:T(8,128)(2,1)}, bf16[48,2048]{1,0:T(8,128)(2,1)}, u32[]{:S(2)}, u32[]{:S(2)}) collective-permute-start(bf16[48,2048]{1,0:T(8,128)(2,1)} %get-tuple-element.45), channel_id=1, source_target_pairs={{0,14},{1,15},{2,0},{3,1},{4,2},{5,3},{6,4},{7,5},{8,6},{9,7},{10,... | collective-permute-start | bytes 589832 | tf_op jit(solution)/shard_map/ppermute | solution.py:291
  128.4 11.7 %collective-permute-start.14 = (bf16[32,2048]{1,0:T(8,128)(2,1)}, bf16[32,2048]{1,0:T(8,128)(2,1)S(1)}, u32[]{:S(2)}, u32[]{:S(2)}) collective-permute-start(bf16[32,2048]{1,0:T(8,128)(2,1)} %get-tuple-element.46), channel_id=1, source_target_pairs={{0,3},{1,4},{2,5},{3,6},{4,7},{5,8},{6,9},{7,10},{8,11},{9,12},{10... | collective-permute-start | bytes 393224 | tf_op jit(solution)/shard_map/ppermute | solution.py:291
  130.3 13.1 %collective-permute-start.15 = (bf16[32,2048]{1,0:T(8,128)(2,1)}, bf16[32,2048]{1,0:T(8,128)(2,1)}, u32[]{:S(2)}, u32[]{:S(2)}) collective-permute-start(bf16[32,2048]{1,0:T(8,128)(2,1)} %get-tuple-element.47), channel_id=1, source_target_pairs={{0,13},{1,14},{2,15},{3,0},{4,1},{5,2},{6,3},{7,4},{8,5},{9,6},{10... | collective-permute-start | bytes 393224 | tf_op jit(solution)/shard_map/ppermute | solution.py:291
  137.3 19.4 %copy-start.3 = (bf16[4,96,2048]{2,1,0:T(8,128)(2,1)}, bf16[4,96,2048]{2,1,0:T(8,128)(2,1)S(1)}, u32[]{:S(2)}) copy-start(bf16[4,96,2048]{2,1,0:T(8,128)(2,1)S(1)} %all-to-all-done) | copy-start | bytes 4718596
  149.6 4.2 %copy-start.47 = (s32[672]{0:T(1024)S(1)}, s32[672]{0:T(1024)}, u32[]{:S(2)}) copy-start(s32[672]{0:T(1024)} %constant.55.clone) | copy-start | bytes 8068
  149.6 4.2 %copy-start.48 = (s32[672]{0:T(1024)S(1)}, s32[672]{0:T(1024)}, u32[]{:S(2)}) copy-start(s32[672]{0:T(1024)} %constant.54.clone) | copy-start | bytes 8068
  149.6 4.2 %copy-start.49 = (s32[672]{0:T(1024)S(1)}, s32[672]{0:T(1024)}, u32[]{:S(2)}) copy-start(s32[672]{0:T(1024)} %constant.53.clone) | copy-start | bytes 8068
  149.6 4.2 %copy-start.50 = (pred[672]{0:T(1024)(128)(4,1)S(1)}, pred[672]{0:T(1024)(128)(4,1)}, u32[]{:S(2)}) copy-start(pred[672]{0:T(1024)(128)(4,1)} %constant.56.clone) | copy-start | bytes 2020
  149.6 16.2 %all-to-all-start.1 = ((bf16[4,72,2048]{2,1,0:T(8,128)(2,1)}), bf16[4,72,2048]{2,1,0:T(8,128)(2,1)S(1)}, u32[]{:S(2)}, u32[]{:S(2)}) async-start(bf16[4,72,2048]{2,1,0:T(8,128)(2,1)} %bitcast.49), calls=%async_computation.1 | async-start | bytes 2359296 | tf_op jit(solution)/shard_map/all_to_all | solution.py:295
  156.7 1.4 copy-start.7
  163.2 1.1 copy-start.9
  165.9 7.0 %copy-start.5 = (bf16[4,72,2048]{2,1,0:T(8,128)(2,1)}, bf16[4,72,2048]{2,1,0:T(8,128)(2,1)S(1)}, u32[]{:S(2)}) copy-start(bf16[4,72,2048]{2,1,0:T(8,128)(2,1)S(1)} %all-to-all-done.1) | copy-start | bytes 3538948
  165.9 1.8 copy-start.8
  172.9 17.8 %copy-start.25 = (bf16[288,768]{1,0:T(8,128)(2,1)}, bf16[288,768]{1,0:T(8,128)(2,1)S(1)}, u32[]{:S(2)}) copy-start(bf16[288,768]{1,0:T(8,128)(2,1)S(1)} %get-tuple-element.68) | copy-start | bytes 1327108
  189.1 33.9 %copy-start.1 = (bf16[4,72,2048]{2,1,0:T(8,128)(2,1)}, bf16[4,72,2048]{2,1,0:T(8,128)(2,1)S(1)}, u32[]{:S(2)}) copy-start(bf16[4,72,2048]{2,1,0:T(8,128)(2,1)S(1)} %all_to_all.20) | copy-start | bytes 3538948
  194.8 28.2 %copy-start.13 = (bf16[256,288]{1,0:T(8,128)(2,1)S(1)}, bf16[256,288]{1,0:T(8,128)(2,1)}, u32[]{:S(2)}) copy-start(bf16[256,288]{1,0:T(8,128)(2,1)} %copy-done.12) | copy-start | bytes 442372
  194.8 47.1 %all-to-all-start.3 = ((bf16[4,96,2048]{2,1,0:T(8,128)(2,1)}), bf16[4,96,2048]{2,1,0:T(8,128)(2,1)S(1)}, u32[]{:S(2)}, u32[]{:S(2)}) async-start(bf16[4,96,2048]{2,1,0:T(8,128)(2,1)} %bitcast.48), calls=%async_computation.3 | async-start | bytes 3145728 | tf_op jit(solution)/shard_map/all_to_all | solution.py:295
  198.5 34.9 %copy-start.32 = (bf16[128,128]{1,0:T(8,128)(2,1)S(1)}, bf16[128,128]{1,0:T(8,128)(2,1)}, u32[]{:S(2)}) copy-start(bf16[128,128]{1,0:T(8,128)(2,1)} %copy-done.31) | copy-start | bytes 98308
  198.5 116.1 %reduce-scatter.2.cloned.1.call-start = ((), (), s32[]{:S(2)}) async-start(), calls=%async_computation.5 | async-start | bytes 3538944 | tf_op jit(solution)/shard_map/reduce_scatter | solution.py:392
  198.5 20.0 %collective-permute-start.18 = (bf16[32,2048]{1,0:T(8,128)(2,1)}, bf16[32,2048]{1,0:T(8,128)(2,1)S(1)}, u32[]{:S(2)}, u32[]{:S(2)}) collective-permute-start(bf16[32,2048]{1,0:T(8,128)(2,1)} %copy-done.46), channel_id=1, source_target_pairs={{0,13},{1,14},{2,15},{3,0},{4,1},{5,2},{6,3},{7,4},{8,5},{9,6},{10... | collective-permute-start | bytes 393224 | tf_op jit(solution)/shard_map/ppermute | solution.py:291
  205.9 17.1 %collective-permute-start.17 = (bf16[48,2048]{1,0:T(8,128)(2,1)}, bf16[48,2048]{1,0:T(8,128)(2,1)S(1)}, u32[]{:S(2)}, u32[]{:S(2)}) collective-permute-start(bf16[48,2048]{1,0:T(8,128)(2,1)} %copy-done.44), channel_id=1, source_target_pairs={{0,14},{1,15},{2,0},{3,1},{4,2},{5,3},{6,4},{7,5},{8,6},{9,7},{10,... | collective-permute-start | bytes 589832 | tf_op jit(solution)/shard_map/ppermute | solution.py:291
  208.2 14.7 %collective-permute-start.16 = (bf16[48,2048]{1,0:T(8,128)(2,1)}, bf16[48,2048]{1,0:T(8,128)(2,1)S(1)}, u32[]{:S(2)}, u32[]{:S(2)}) collective-permute-start(bf16[48,2048]{1,0:T(8,128)(2,1)} %copy-done.43), channel_id=1, source_target_pairs={{0,15},{1,0},{2,1},{3,2},{4,3},{5,4},{6,5},{7,6},{8,7},{9,8},{10,9... | collective-permute-start | bytes 589832 | tf_op jit(solution)/shard_map/ppermute | solution.py:291
  211.3 21.9 %collective-permute-start.24 = (bf16[48,2048]{1,0:T(8,128)(2,1)}, bf16[48,2048]{1,0:T(8,128)(2,1)S(1)}, u32[]{:S(2)}, u32[]{:S(2)}) collective-permute-start(bf16[48,2048]{1,0:T(8,128)(2,1)} %copy-done.42), channel_id=1, source_target_pairs={{0,1},{1,2},{2,3},{3,4},{4,5},{5,6},{6,7},{7,8},{8,9},{9,10},{10,1... | collective-permute-start | bytes 589832 | tf_op jit(solution)/shard_map/ppermute | solution.py:291
  214.1 19.3 %collective-permute-start.25 = (bf16[48,2048]{1,0:T(8,128)(2,1)}, bf16[48,2048]{1,0:T(8,128)(2,1)S(1)}, u32[]{:S(2)}, u32[]{:S(2)}) collective-permute-start(bf16[48,2048]{1,0:T(8,128)(2,1)} %copy-done.41), channel_id=1, source_target_pairs={{0,2},{1,3},{2,4},{3,5},{4,6},{5,7},{6,8},{7,9},{8,10},{9,11},{10,... | collective-permute-start | bytes 589832 | tf_op jit(solution)/shard_map/ppermute | solution.py:291
  218.5 14.7 %collective-permute-start.26 = (bf16[32,2048]{1,0:T(8,128)(2,1)}, bf16[32,2048]{1,0:T(8,128)(2,1)S(1)}, u32[]{:S(2)}, u32[]{:S(2)}) collective-permute-start(bf16[32,2048]{1,0:T(8,128)(2,1)} %copy-done.45), channel_id=1, source_target_pairs={{0,3},{1,4},{2,5},{3,6},{4,7},{5,8},{6,9},{7,10},{8,11},{9,12},{10... | collective-permute-start | bytes 393224 | tf_op jit(solution)/shard_map/ppermute | solution.py:291
  224.3 17.5 %copy-start = (bf16[1152,384]{1,0:T(8,128)(2,1)S(1)}, bf16[1152,384]{1,0:T(8,128)(2,1)}, u32[]{:S(2)}) copy-start(bf16[1152,384]{1,0:T(8,128)(2,1)} %get-tuple-element.61.own_ref) | copy-start | bytes 2654212
  224.3 16.7 %collective-permute-start.19 = (bf16[128,2048]{1,0:T(8,128)(2,1)S(1)}, bf16[128,2048]{1,0:T(8,128)(2,1)S(1)}, u32[]{:S(2)}, u32[]{:S(2)}) collective-permute-start(bf16[128,2048]{1,0:T(8,128)(2,1)S(1)} %shard_map.211), channel_id=1, source_target_pairs={{0,15},{1,0},{2,1},{3,2},{4,3},{5,4},{6,5},{7,6},{8,7},{9,8},{10,9... | collective-permute-start | bytes 1572872 | tf_op jit(solution)/shard_map/ppermute | solution.py:291
  233.4 1.3 copy-start.2
  236.0 12.5 %collective-permute-start.27 = (bf16[128,2048]{1,0:T(8,128)(2,1)}, bf16[128,2048]{1,0:T(8,128)(2,1)S(1)}, u32[]{:S(2)}, u32[]{:S(2)}) collective-permute-start(bf16[128,2048]{1,0:T(8,128)(2,1)} %shard_map.216), channel_id=1, source_target_pairs={{0,1},{1,2},{2,3},{3,4},{4,5},{5,6},{6,7},{7,8},{8,9},{9,10},{10,1... | collective-permute-start | bytes 1572872 | tf_op jit(solution)/shard_map/ppermute | solution.py:291
  244.1 6.7 %copy-start.6 = (bf16[4,72,2048]{2,1,0:T(8,128)(2,1)S(1)}, bf16[4,72,2048]{2,1,0:T(8,128)(2,1)}, u32[]{:S(2)}) copy-start(bf16[4,72,2048]{2,1,0:T(8,128)(2,1)} %copy-done.5) | copy-start | bytes 3538948
  251.3 1.8 copy-start.4
  251.3 1.9 copy-start.15
  256.7 15.0 %collective-permute-start.20 = (bf16[128,2048]{1,0:T(8,128)(2,1)}, bf16[128,2048]{1,0:T(8,128)(2,1)S(1)}, u32[]{:S(2)}, u32[]{:S(2)}) collective-permute-start(bf16[128,2048]{1,0:T(8,128)(2,1)} %copy-done.21), channel_id=1, source_target_pairs={{0,15},{1,0},{2,1},{3,2},{4,3},{5,4},{6,5},{7,6},{8,7},{9,8},{10,9... | collective-permute-start | bytes 1572872 | tf_op jit(solution)/shard_map/ppermute | solution.py:291
  258.7 15.3 %collective-permute-start.28 = (bf16[128,2048]{1,0:T(8,128)(2,1)S(1)}, bf16[128,2048]{1,0:T(8,128)(2,1)S(1)}, u32[]{:S(2)}, u32[]{:S(2)}) collective-permute-start(bf16[128,2048]{1,0:T(8,128)(2,1)S(1)} %shard_map.217), channel_id=1, source_target_pairs={{0,1},{1,2},{2,3},{3,4},{4,5},{5,6},{6,7},{7,8},{8,9},{9,10},{10,1... | collective-permute-start | bytes 1572872 | tf_op jit(solution)/shard_map/ppermute | solution.py:291
  272.1 15.5 %collective-permute-start.21 = (bf16[128,2048]{1,0:T(8,128)(2,1)S(1)}, bf16[128,2048]{1,0:T(8,128)(2,1)S(1)}, u32[]{:S(2)}, u32[]{:S(2)}) collective-permute-start(bf16[128,2048]{1,0:T(8,128)(2,1)S(1)} %shard_map.213), channel_id=1, source_target_pairs={{0,15},{1,0},{2,1},{3,2},{4,3},{5,4},{6,5},{7,6},{8,7},{9,8},{10,9... | collective-permute-start | bytes 1572872 | tf_op jit(solution)/shard_map/ppermute | solution.py:291
  274.5 16.9 %collective-permute-start.29 = (bf16[128,2048]{1,0:T(8,128)(2,1)S(1)}, bf16[128,2048]{1,0:T(8,128)(2,1)S(1)}, u32[]{:S(2)}, u32[]{:S(2)}) collective-permute-start(bf16[128,2048]{1,0:T(8,128)(2,1)S(1)} %shard_map.218), channel_id=1, source_target_pairs={{0,1},{1,2},{2,3},{3,4},{4,5},{5,6},{6,7},{7,8},{8,9},{9,10},{10,1... | collective-permute-start | bytes 1572872 | tf_op jit(solution)/shard_map/ppermute | solution.py:291
  288.1 15.1 %collective-permute-start.22 = (bf16[128,2048]{1,0:T(8,128)(2,1)S(1)}, bf16[128,2048]{1,0:T(8,128)(2,1)S(1)}, u32[]{:S(2)}, u32[]{:S(2)}) collective-permute-start(bf16[128,2048]{1,0:T(8,128)(2,1)S(1)} %shard_map.214), channel_id=1, source_target_pairs={{0,15},{1,0},{2,1},{3,2},{4,3},{5,4},{6,5},{7,6},{8,7},{9,8},{10,9... | collective-permute-start | bytes 1572872 | tf_op jit(solution)/shard_map/ppermute | solution.py:291
  291.9 17.8 %collective-permute-start.30 = (bf16[128,2048]{1,0:T(8,128)(2,1)S(1)}, bf16[128,2048]{1,0:T(8,128)(2,1)S(1)}, u32[]{:S(2)}, u32[]{:S(2)}) collective-permute-start(bf16[128,2048]{1,0:T(8,128)(2,1)S(1)} %shard_map.219), channel_id=1, source_target_pairs={{0,1},{1,2},{2,3},{3,4},{4,5},{5,6},{6,7},{7,8},{8,9},{9,10},{10,1... | collective-permute-start | bytes 1572872 | tf_op jit(solution)/shard_map/ppermute | solution.py:291
  304.4 8.5 %copy-start.28 = (bf16[384,384]{1,0:T(8,128)(2,1)S(1)}, bf16[384,384]{1,0:T(8,128)(2,1)}, u32[]{:S(2)}) copy-start(bf16[384,384]{1,0:T(8,128)(2,1)} %copy-done.27) | copy-start | bytes 884740
  304.4 12.3 %collective-permute-start.23 = (bf16[128,2048]{1,0:T(8,128)(2,1)}, bf16[128,2048]{1,0:T(8,128)(2,1)S(1)}, u32[]{:S(2)}, u32[]{:S(2)}) collective-permute-start(bf16[128,2048]{1,0:T(8,128)(2,1)} %shard_map.215), channel_id=1, source_target_pairs={{0,15},{1,0},{2,1},{3,2},{4,3},{5,4},{6,5},{7,6},{8,7},{9,8},{10,9... | collective-permute-start | bytes 1572872 | tf_op jit(solution)/shard_map/ppermute | solution.py:291
  310.9 12.6 %collective-permute-start.31 = (bf16[128,2048]{1,0:T(8,128)(2,1)}, bf16[128,2048]{1,0:T(8,128)(2,1)}, u32[]{:S(2)}, u32[]{:S(2)}) collective-permute-start(bf16[128,2048]{1,0:T(8,128)(2,1)} %shard_map.220), channel_id=1, source_target_pairs={{0,1},{1,2},{2,3},{3,4},{4,5},{5,6},{6,7},{7,8},{8,9},{9,10},{10,1... | collective-permute-start | bytes 1572872 | tf_op jit(solution)/shard_map/ppermute | solution.py:291
  (25 other events, 20.0 us)
Sparse Core Ops, SparseCore 0:
  10.1 34.9 all-gather.4
  58.9 28.1 all-gather.6
  256.8 39.2 reduce-scatter.1

commit v7 on v4

v7 whole, which is shorter than its diff:
```python
import functools

import jax
import jax.numpy as jnp
from jax import lax
from jax.experimental import pallas as pl
from jax.experimental.pallas import tpu as pltpu
from jax.sharding import Mesh, PartitionSpec as P

N_Y = 4
N_Z = 16
HALVES = 2
STEP = 512
VMEM_BYTES = 48 * 1024 * 1024


def routing_kernel(ids_ref, weights_ref, out_ref):
    rows, tokens = out_ref.shape
    row = lax.broadcasted_iota(jnp.int32, (rows, tokens), 0)
    kind = row % 8
    device = row // 8
    expert = jnp.where(kind < N_Y, kind * N_Z + device % N_Z, device)
    hits = jnp.zeros((rows, tokens), jnp.float32)
    eighths = jnp.zeros((rows, tokens), jnp.float32)
    for choice in range(ids_ref.shape[0]):
        named = ids_ref[choice : choice + 1, :] == expert
        hits = hits + jnp.where(named, 1.0, 0.0)
        eighths = eighths + jnp.where(named, weights_ref[choice : choice + 1, :].astype(jnp.float32), 0.0)
    earlier = lax.broadcasted_iota(jnp.int32, (tokens, tokens), 0)
    later = lax.broadcasted_iota(jnp.int32, (tokens, tokens), 1)
    triangle = jnp.where(earlier < later, 1.0, 0.0).astype(jnp.bfloat16)
    rank = jnp.dot(hits.astype(jnp.bfloat16), triangle, preferred_element_type=jnp.float32)
    rank = jnp.where(hits > 0.0, rank, -1.0)
    out_ref[...] = jnp.where(kind <= N_Y, rank, eighths).astype(jnp.bfloat16)


def array(shape, dtype=jnp.bfloat16):
    return jax.ShapeDtypeStruct(shape, dtype)


def dot(a, b, contract=(1, 0)):
    return lax.dot_general(
        a, b, (((contract[0],), (contract[1],)), ((), ())), preferred_element_type=jnp.float32
    )


def one_hot(condition):
    return jnp.where(condition, 1.0, 0.0).astype(jnp.bfloat16)


PARAMS = pltpu.CompilerParams(vmem_limit_bytes=VMEM_BYTES)
WHOLE = pl.BlockSpec(memory_space=pltpu.VMEM)


def pick_kernel(half, slot_ref, tokens_ref, out_ref, select_ref):
    slots = out_ref.shape[1]
    tokens = tokens_ref.shape[0]

    @pl.when(pl.program_id(0) == 0)
    def _():
        slot = lax.broadcasted_iota(jnp.int32, (slots, tokens), 0) + half * slots
        for y in range(N_Y):
            select_ref[y * slots : (y + 1) * slots, :] = one_hot(slot_ref[y : y + 1, :] == slot)

    picked = dot(select_ref[...], tokens_ref[...]).astype(jnp.bfloat16)
    for y in range(N_Y):
        out_ref[y] = picked[y * slots : (y + 1) * slots]


def pick(half, slot_of, gathered, slots):
    tokens, width = gathered.shape[0] // HALVES, gathered.shape[1]
    return pl.pallas_call(
        functools.partial(pick_kernel, half),
        grid=(width // STEP,),
        out_shape=array((N_Y, slots, width)),
        in_specs=[
            pl.BlockSpec((N_Y, tokens), lambda step: (0, half)),
            pl.BlockSpec((tokens, STEP), lambda step: (half, step)),
        ],
        out_specs=pl.BlockSpec((N_Y, slots, STEP), lambda step: (0, 0, step)),
        scratch_shapes=[pltpu.VMEM((N_Y * slots, tokens), jnp.bfloat16)],
        compiler_params=PARAMS,
    )(slot_of, gathered)


def expert_kernel(
    rows_ref, matrix_ref, weight_ref, cotangent_ref, hidden_ref, grad_ref, row_grads_ref
):
    units = hidden_ref.shape[2]
    slots = hidden_ref.shape[1]
    pre = dot(rows_ref[...], matrix_ref[...])
    weights = jnp.concatenate([weight_ref[y] for y in range(N_Y)], axis=0)
    cotangent = jnp.concatenate([cotangent_ref[y] for y in range(N_Y)], axis=0)
    gate_pre, up_pre = pre[:, :units], pre[:, units:]
    sigmoid_gate = jax.nn.sigmoid(gate_pre)
    activation = gate_pre * sigmoid_gate
    hidden = (activation * up_pre * weights).astype(jnp.bfloat16)
    for y in range(N_Y):
        hidden_ref[y] = hidden[y * slots : (y + 1) * slots]
    act_slope = sigmoid_gate * (1.0 + gate_pre * (1.0 - sigmoid_gate))
    scaled = cotangent.astype(jnp.float32) * weights
    grad_ref[:, :units] = (scaled * up_pre * act_slope).astype(jnp.bfloat16)
    grad_ref[:, units:] = (scaled * activation).astype(jnp.bfloat16)
    row_grads_ref[...] = dot(grad_ref[...], matrix_ref[...], (1, 1)).astype(jnp.bfloat16)


def expert(half, rows, matrix, weight_col, cotangent):
    count, width = rows.shape
    slots, units = count // N_Y, cotangent.shape[2]
    return pl.pallas_call(
        expert_kernel,
        grid=(1,),
        out_shape=(array((N_Y, slots, units)), array((count, 2 * units)), array((count, width))),
        in_specs=[
            WHOLE,
            WHOLE,
            pl.BlockSpec((N_Y, slots, 1), lambda step: (0, half, 0)),
            pl.BlockSpec((N_Y, slots, units), lambda step: (0, half, 0)),
        ],
        out_specs=(
            pl.BlockSpec((N_Y, slots, units), lambda step: (0, 0, 0)),
            pl.BlockSpec((count, 2 * units), lambda step: (0, 0)),
            pl.BlockSpec((count, width), lambda step: (0, 0)),
        ),
        compiler_params=PARAMS,
    )(rows, matrix, weight_col, cotangent)


def add_kernel(half, place_ref, grads_ref, *refs):
    out_ref, select_ref = refs[-2:]
    tokens, rows = select_ref.shape
    slots = rows // N_Y

    @pl.when(pl.program_id(0) == 0)
    def _():
        row = lax.broadcasted_iota(jnp.int32, (tokens, rows), 1)
        mark = place_ref[:, 0:1] - half * slots == row
        mark = mark & (row < slots)
        for y in range(1, N_Y):
            here = place_ref[:, y : y + 1] + (y - half) * slots == row
            mark = mark | (here & (row >= y * slots) & (row < (y + 1) * slots))
        select_ref[...] = one_hot(mark)

    grads = jnp.concatenate([grads_ref[y] for y in range(N_Y)], axis=0)
    out_ref[...] = dot(select_ref[...], grads).astype(jnp.bfloat16)


def add(half, place_of, grads, earlier):
    slots, width = grads.shape[1:]
    count = place_of.shape[0]
    tokens = count // HALVES
    return pl.pallas_call(
        functools.partial(add_kernel, half),
        grid=(width // STEP,),
        out_shape=array((count, width)),
        in_specs=[
            pl.BlockSpec((tokens, N_Y), lambda step: (half, 0)),
            pl.BlockSpec((N_Y, slots, STEP), lambda step: (0, 0, step)),
        ]
        + [pl.BlockSpec(memory_space=pl.ANY)] * len(earlier),
        out_specs=pl.BlockSpec((tokens, STEP), lambda step: (half, step)),
        scratch_shapes=[pltpu.VMEM((tokens, N_Y * slots), jnp.bfloat16)],
        input_output_aliases={2: 0} if earlier else {},
        compiler_params=PARAMS,
    )(place_of, grads, *earlier)


def after(value, *others):
    return lax.optimization_barrier((value,) + others)[0]


def shards(tokens, expert_ids, route_weights, gate_weight, up_weight, cotangent):
    experts = N_Y * N_Z
    groups = lax.axis_size("dp")
    slot_count, units = cotangent.shape[2:]
    capacity = slot_count // experts
    row_slots = N_Z * capacity
    half_slots = row_slots // HALVES
    block, width = tokens.shape[1:]

    def exchange(parts):
        return lax.all_to_all(parts, "y", 0, 0, tiled=True)

    gathered = lax.all_gather(tokens[0], "z", axis=0, tiled=True)

    told = pl.pallas_call(
        routing_kernel,
        out_shape=array((experts * 8, block)),
        in_specs=[WHOLE, WHOLE],
        out_specs=WHOLE,
        compiler_params=PARAMS,
    )(expert_ids[0].T, route_weights[0].T)
    heard = lax.all_to_all(told.reshape(experts, 8, block), ("y", "z"), 0, 0, tiled=True)
    own_row = lax.dynamic_slice_in_dim(heard, lax.axis_index("y") * N_Z, N_Z, axis=0)
    rank = jnp.transpose(own_row[:, :N_Y], (1, 0, 2)).astype(jnp.int32)
    base = capacity * jnp.arange(N_Z, dtype=jnp.int32)[None, :, None]
    slot_of = jnp.where(rank >= 0, rank + base, -1).reshape(N_Y, N_Z * block)
    place_of = slot_of.T
    places = jnp.arange(capacity, dtype=jnp.int32).astype(jnp.bfloat16)
    weight_col = jnp.sum(
        jnp.where(
            heard[:, N_Y, None, :] == places[None, :, None],
            heard[:, N_Y + 1, None, :].astype(jnp.float32),
            0.0,
        ),
        axis=2,
    ).reshape(N_Y, row_slots, 1) / 8.0

    stacked = jnp.concatenate((gate_weight[0], up_weight[0]), axis=1)
    matrix = lax.all_to_all(
        jnp.broadcast_to(stacked[None], (groups,) + stacked.shape), "dp", 0, 0, tiled=True
    ).reshape(width, 2 * units)

    cotangents = cotangent.reshape(N_Y, row_slots, units)
    rows, hidden, grads, back = [], [], [], []
    for half in range(HALVES):
        arrived = exchange(pick(half, slot_of, gathered, half_slots)).reshape(N_Y * half_slots, width)
        results = expert(half, arrived, matrix, weight_col, cotangents)
        for known, result in zip((rows, hidden, grads, back), (arrived,) + tuple(results)):
            known.append(result)
    sums = ()
    for half in range(HALVES):
        own = after(back[half], rows[-1])
        returned = exchange(own.reshape(N_Y, half_slots, width))
        sums = (add(half, place_of, returned, sums),)
    token_grads = lax.psum_scatter(sums[0], "z", scatter_dimension=0, tiled=True).astype(jnp.float32)

    late_grads = [after(value, sums[0]) for value in grads]
    terms = sum(dot(value, grad, (0, 0)) for value, grad in zip(rows, late_grads)).astype(jnp.bfloat16)
    terms = terms.reshape(groups, width // groups, 2 * units)
    weight_grads = jnp.sum(lax.all_to_all(terms, "dp", 0, 0, tiled=True).astype(jnp.float32), axis=0)
    hidden = after(jnp.concatenate([after(value, sums[0]) for value in hidden], axis=1))
    return (
        hidden.reshape(cotangent.shape),
        token_grads[None],
        weight_grads[None, :, :units],
        weight_grads[None, :, units:],
    )


def solution(mesh):
    grid = Mesh(mesh.devices.reshape(mesh.shape["dp"], N_Y, N_Z), ("dp", "y", "z"))
    expert = ("y", "z")
    in_specs = (
        P("dp", expert, None),
        P("dp", expert, None),
        P("dp", expert, None),
        P(expert, "dp", None),
        P(expert, "dp", None),
        P("dp", expert, None, None),
    )
    out_specs = (
        P("dp", expert, None, None),
        P("dp", expert, None),
        P(expert, "dp", None),
        P(expert, "dp", None),
    )
    return jax.shard_map(shards, mesh=grid, in_specs=in_specs, out_specs=out_specs, check_vma=False)
```

time: 329 us -> 333 us (1.012)
  blocking collectives: 26.6 us -> 0 us
  waiting for transfers between devices: 188 us -> 212 us
  Pallas kernels: 21.3 us -> 32.6 us
  local copies, waits for them, and re-layouts: 18 us -> 12.7 us
    all_to_all x4 -> x5, waiting for transfers between devices: 116 us -> 56.1 us  [the longest x4 40.4 us: exchange(): return lax.all_to_all(parts, 'y', 0, 0, tiled=True)]
    all_gather x1, waiting for transfers between devices: 27.8 us -> 69.7 us  [shards(): gathered = lax.all_gather(tokens[0], 'z', axis=0, tiled=True)]
    reduce_scatter x1, waiting for transfers between devices: 9.7 us -> 50 us  [shards(): lax.psum_scatter(sums[0], 'z', scatter_dimension=0, tiled=True)]
    all_to_all x1 -> x0, blocking collectives: 26.6 us -> none  [exchange(): return lax.all_to_all(parts, 'y', 0, 0, tiled=True).reshape(rows.shape)]
    pallas_call x5 -> x7, Pallas kernels: 21.3 us -> 32.6 us  [the longest x2 13.3 us: add(): pl.pallas_call(functools.partial(add_kernel, half), grid=(width // STEP,)...]
    reshape x4 -> x1, local copies, waits for them, and re-layouts: 5.9 us -> 0.33 us  [shards(): slot_of = jnp.where(rank >= 0, rank + base, -1).reshape(N_Y, N_Z * block)]
    unnamed x18 -> x26, local copies, waits for them, and re-layouts: 4.17 us -> 8.9 us
    slice x3 -> x1, local copies, waits for them, and re-layouts: 4.02 us -> 0.06 us  [shards(): heard[:, N_Y, None, :] == places[None, :, None]]
  transfers between devices with their start and end apart: 8 -> 9, of which waited for: 8 -> 8; matrix products, arithmetic and copies ran while one was open for 7% -> 5% of each run, Pallas kernels for 2% -> 8%
where the time goes in v7:
time: 333 us; the launch traced here: 331 us
  waiting for transfers between devices  212 us (64%)
  starting transfers between devices  46.1 us (14%)
  Pallas kernels  32.6 us (10%)
  between operations  14.2 us (4%)
  local copies, waits for them, and re-layouts  12.7 us (4%)
  other arithmetic  6.77 us (2%)
  matrix products  6.65 us (2%)
    all_gather x1, waiting for transfers between devices, shards(): gathered = lax.all_gather(tokens[0], 'z', axis=0, tiled=True)  69.7 us
    reduce_scatter x1, waiting for transfers between devices, shards(): lax.psum_scatter(sums[0], 'z', scatter_dimension=0, tiled=True)  50 us
    all_to_all x4, waiting for transfers between devices, exchange(): return lax.all_to_all(parts, 'y', 0, 0, tiled=True)  40.4 us
    all_to_all x1, waiting for transfers between devices, shards(): lax.all_to_all(terms, 'dp', 0, 0, tiled=True).astype(jnp.float32)  35.6 us
    all_to_all x1, starting transfers between devices, shards(): lax.all_to_all(told.reshape(experts, 8, block), ('y', 'z'), 0, 0, tiled=T...  18.7 us
    all_to_all x4, starting transfers between devices, exchange(): return lax.all_to_all(parts, 'y', 0, 0, tiled=True)  17.3 us
    all_to_all x1, waiting for transfers between devices, shards(): lax.all_to_all(told.reshape(experts, 8, block), ('y', 'z'), 0, 0, tiled=T...  15.7 us
    pallas_call x2, Pallas kernels, add(): pl.pallas_call(functools.partial(add_kernel, half), grid=(width // STEP,)...  13.3 us
  transfers between devices with their start and end apart: 9, of which 8 were waited for; matrix products, arithmetic and copies ran while one was open for 5% of the time, Pallas kernels for 8%

profile of v7, /device:TPU:6, one launch (start us, length us, event | category | flops | bytes accessed | tf_op | source)
XLA Modules:
  0.0 331.2 jit_solution(6708790438427668247)
XLA Ops:
  7.2 0.0 all-gather.3.cloned.1.call-start
  7.2 0.7 all-gather.3.cloned.1.call-update
  7.9 0.0 copy-start.11
  7.9 0.7 copy-done.11
  8.6 0.0 copy-start.12
  8.6 0.7 copy-done.12
  9.3 1.2 shard_map.93
  10.4 18.7 %all-to-all-start = ((bf16[64,8,128]{2,1,0:T(8,128)(2,1)}), bf16[64,8,128]{2,1,0:T(8,128)(2,1)S(1)}, u32[]{:S(2)}, u32[]{:S(2)}) async-start(bf16[64,8,128]{2,1,0:T(8,128)(2,1)} %bitcast.4), calls=%async_computation | async-start | bytes 262144 | tf_op jit(solution)/shard_map/all_to_all | solution.py:193
  29.2 1.1 pad_maximum_fusion.1
  30.2 15.7 %all-to-all-done = bf16[64,8,128]{2,1,0:T(8,128)(2,1)S(1)} async-done(((bf16[64,8,128]{2,1,0:T(8,128)(2,1)}), bf16[64,8,128]{2,1,0:T(8,128)(2,1)S(1)}, u32[]{:S(2)}, u32[]{:S(2)}) %all-to-all-start) | async-done | bytes 131104 | tf_op jit(solution)/shard_map/all_to_all | solution.py:193
  45.9 1.9 broadcast_in_dim.42
  47.8 4.8 %all-to-all-start.2 = ((bf16[8,256,768]{2,1,0:T(8,128)(2,1)}), bf16[8,256,768]{2,1,0:T(8,128)(2,1)}, u32[]{:S(2)}, u32[]{:S(2)}) async-start(bf16[8,256,768]{2,1,0:T(8,128)(2,1)} %broadcast_in_dim.42), calls=%async_computation.2 | async-start | bytes 6291456 | tf_op jit(solution)/shard_map/all_to_all | solution.py:210
  52.6 0.1 fusion.1
  52.7 0.4 copy.27
  53.1 0.3 copy.28.slot_ref
  53.4 69.7 %all-gather.3.cloned.1.call-done = bf16[1,2048,2048]{2,1,0:T(8,128)(2,1)} async-done(((bf16[1,128,2048]{2,1,0:T(8,128)(2,1)}), bf16[1,2048,2048]{2,1,0:T(8,128)(2,1)}) %all-gather.3.cloned.1.call-update) | async-done | bytes 8388624 | tf_op jit(solution)/shard_map/all_gather | solution.py:184
  123.1 4.2 %shard_map.94 = bf16[4,80,2048]{2,1,0:T(8,128)(2,1)S(1)} custom-call(s32[4,2048]{1,0:T(4,128)S(1)} %copy.28.slot_ref, bf16[2048,2048]{1,0:T(8,128)(2,1)} %bitcast.52), custom_call_target="tpu_custom_call" | custom-call | tf_op jit(solution)/shard_map/pallas_call | solution.py:72
  127.3 0.0 copy-start.1
  127.4 1.1 copy-done.1
  128.4 0.0 all-to-all-done.2
  128.4 4.4 %all-to-all-start.1 = ((bf16[4,80,2048]{2,1,0:T(8,128)(2,1)}), bf16[4,80,2048]{2,1,0:T(8,128)(2,1)S(1)}, u32[]{:S(2)}, u32[]{:S(2)}) async-start(bf16[4,80,2048]{2,1,0:T(8,128)(2,1)} %copy-done.1), calls=%async_computation.1 | async-start | bytes 2621440 | tf_op jit(solution)/shard_map/all_to_all | solution.py:182
  132.9 4.2 %shard_map.96 = bf16[4,80,2048]{2,1,0:T(8,128)(2,1)S(1)} custom-call(s32[4,2048]{1,0:T(4,128)S(1)} %copy.28.slot_ref, bf16[2048,2048]{1,0:T(8,128)(2,1)} %bitcast.53), custom_call_target="tpu_custom_call" | custom-call | tf_op jit(solution)/shard_map/pallas_call | solution.py:72
  137.1 0.0 copy-start
  137.1 1.1 copy-done
  138.2 0.0 copy-start.2
  138.2 12.8 %all-to-all-done.1 = bf16[4,80,2048]{2,1,0:T(8,128)(2,1)S(1)} async-done(((bf16[4,80,2048]{2,1,0:T(8,128)(2,1)}), bf16[4,80,2048]{2,1,0:T(8,128)(2,1)S(1)}, u32[]{:S(2)}, u32[]{:S(2)}) %all-to-all-start.1) | async-done | bytes 1310752 | tf_op jit(solution)/shard_map/all_to_all | solution.py:182
  151.0 4.3 %all-to-all-start.3 = ((bf16[4,80,2048]{2,1,0:T(8,128)(2,1)}), bf16[4,80,2048]{2,1,0:T(8,128)(2,1)}, u32[]{:S(2)}, u32[]{:S(2)}) async-start(bf16[4,80,2048]{2,1,0:T(8,128)(2,1)} %copy-done), calls=%async_computation.3 | async-start | bytes 2621440 | tf_op jit(solution)/shard_map/all_to_all | solution.py:182
  155.3 0.1 fusion.3
  155.4 0.2 select_reduce_fusion
  155.6 0.1 copy.31
  155.7 0.1 div.11.weight_ref
  155.9 0.0 copy-done.2
  155.9 4.7 %shard_map.95 = (bf16[4,80,384]{2,1,0:T(8,128)(2,1)S(1)}, bf16[320,768]{1,0:T(8,128)(2,1)S(1)}, bf16[320,2048]{1,0:T(8,128)(2,1)S(1)}) custom-call(bf16[320,2048]{1,0:T(8,128)(2,1)S(1)} %bitcast.44, bf16[2048,768]{1,0:T(8,128)(2,1)} %bitcast.11.matrix_ref, f32[4,160,1]{2,1,0:T(8,128)S(1)} %div.11.weight_ref, bf16[4,160,384]{2,1,0:T(8,128)(2,1)S(1)} %bitcast.46), custom_call_target="tpu_custom_call" | custom-call | tf_op jit(solution)/shard_map/pallas_call | solution.py:110
  160.6 0.0 copy-start.3
  160.6 1.1 copy-done.3
  161.7 0.0 copy-start.7
  161.7 0.8 copy-done.7
  162.4 10.2 %all-to-all-done.3 = bf16[4,80,2048]{2,1,0:T(8,128)(2,1)} async-done(((bf16[4,80,2048]{2,1,0:T(8,128)(2,1)}), bf16[4,80,2048]{2,1,0:T(8,128)(2,1)}, u32[]{:S(2)}, u32[]{:S(2)}) %all-to-all-start.3) | async-done | bytes 1310752 | tf_op jit(solution)/shard_map/all_to_all | solution.py:182
  172.6 4.3 %all-to-all-start.5 = ((bf16[4,80,2048]{2,1,0:T(8,128)(2,1)}), bf16[4,80,2048]{2,1,0:T(8,128)(2,1)}, u32[]{:S(2)}, u32[]{:S(2)}) async-start(bf16[4,80,2048]{2,1,0:T(8,128)(2,1)} %bitcast.48), calls=%async_computation.5 | async-start | bytes 2621440 | tf_op jit(solution)/shard_map/all_to_all | solution.py:182
  176.9 5.1 %shard_map.97 = (bf16[4,80,384]{2,1,0:T(8,128)(2,1)S(1)}, bf16[320,768]{1,0:T(8,128)(2,1)S(1)}, bf16[320,2048]{1,0:T(8,128)(2,1)S(1)}) custom-call(bf16[320,2048]{1,0:T(8,128)(2,1)} %bitcast.16.rows_ref, bf16[2048,768]{1,0:T(8,128)(2,1)} %bitcast.11.matrix_ref, f32[4,160,1]{2,1,0:T(8,128)S(1)} %div.11.weight_ref, bf16[4,160,384]{2,1,0:T(8,128)(2,1)S(1)} %bitcast.47), custom_call_target="tpu_custom_call" | custom-call | tf_op jit(solution)/shard_map/pallas_call | solution.py:110
  182.0 0.0 copy-start.4
  182.0 1.0 copy-done.4
  183.1 0.8 copy-done.5
  183.8 0.0 copy-start.9
  183.9 0.7 copy-done.9
  184.5 8.8 %all-to-all-done.5.grads_ref = bf16[4,80,2048]{2,1,0:T(8,128)(2,1)} async-done(((bf16[4,80,2048]{2,1,0:T(8,128)(2,1)}), bf16[4,80,2048]{2,1,0:T(8,128)(2,1)}, u32[]{:S(2)}, u32[]{:S(2)}) %all-to-all-start.5) | async-done | bytes 1310752 | tf_op jit(solution)/shard_map/all_to_all | solution.py:182
  193.3 4.3 %all-to-all-start.4 = ((bf16[4,80,2048]{2,1,0:T(8,128)(2,1)}), bf16[4,80,2048]{2,1,0:T(8,128)(2,1)}, u32[]{:S(2)}, u32[]{:S(2)}) async-start(bf16[4,80,2048]{2,1,0:T(8,128)(2,1)} %bitcast.49), calls=%async_computation.4 | async-start | bytes 2621440 | tf_op jit(solution)/shard_map/all_to_all | solution.py:182
  197.7 0.2 reduce-scatter.2.cloned.1.call-start
  197.9 6.6 %shard_map.98.refs_0_ = bf16[2048,2048]{1,0:T(8,128)(2,1)} custom-call(s32[2048,4]{1,0:T(8,128)S(1)} %bitcast.42, bf16[4,80,2048]{2,1,0:T(8,128)(2,1)} %all-to-all-done.5.grads_ref), custom_call_target="tpu_custom_call" | custom-call | tf_op jit(solution)/shard_map/pallas_call | solution.py:152
  204.5 8.6 %all-to-all-done.4.grads_ref = bf16[4,80,2048]{2,1,0:T(8,128)(2,1)} async-done(((bf16[4,80,2048]{2,1,0:T(8,128)(2,1)}), bf16[4,80,2048]{2,1,0:T(8,128)(2,1)}, u32[]{:S(2)}, u32[]{:S(2)}) %all-to-all-start.4) | async-done | bytes 1310752 | tf_op jit(solution)/shard_map/all_to_all | solution.py:182
  213.1 6.6 %shard_map.99 = bf16[2048,2048]{1,0:T(8,128)(2,1)} custom-call(s32[2048,4]{1,0:T(8,128)S(1)} %bitcast.43, bf16[4,80,2048]{2,1,0:T(8,128)(2,1)} %all-to-all-done.4.grads_ref, bf16[2048,2048]{1,0:T(8,128)(2,1)} %shard_map.98.refs_0_), custom_call_target="tpu_custom_call", output_to_operand_aliasing={{}: (2, {})} | custom-call | tf_op jit(solution)/shard_map/pallas_call | solution.py:152
  219.8 0.0 reduce-scatter.2.cloned.1.call-update
  219.8 1.0 copy-done.8
  220.8 1.8 fusion.4
  222.6 0.0 copy-done.6
  222.6 4.8 %add_convert_fusion = bf16[2048,768]{1,0:T(8,128)(2,1)} fusion(f32[2048,768]{1,0:T(8,128)S(1)} %fusion.4, bf16[320,2048]{1,0:T(8,128)(2,1)} %bitcast.16.rows_ref, bf16[320,768]{1,0:T(8,128)(2,1)S(1)} %copy-done.6), kind=kOutput, calls=%fused_computation.1 | convolution fusion | flops 1009778688 | bytes 11239424 | tf_op jit(solution)/shard_map/dot_general | solution.py:42
  227.5 4.9 %all-to-all-start.6 = ((bf16[8,256,768]{2,1,0:T(8,128)(2,1)}), bf16[8,256,768]{2,1,0:T(8,128)(2,1)}, u32[]{:S(2)}, u32[]{:S(2)}) async-start(bf16[8,256,768]{2,1,0:T(8,128)(2,1)} %bitcast.54), calls=%async_computation.7 | async-start | bytes 6291456 | tf_op jit(solution)/shard_map/all_to_all | solution.py:231
  232.4 0.0 copy-done.10
  232.4 0.8 pad_maximum_fusion
  233.2 35.6 %all-to-all-done.6 = bf16[8,256,768]{2,1,0:T(8,128)(2,1)} async-done(((bf16[8,256,768]{2,1,0:T(8,128)(2,1)}), bf16[8,256,768]{2,1,0:T(8,128)(2,1)}, u32[]{:S(2)}, u32[]{:S(2)}) %all-to-all-start.6) | async-done | bytes 3145760 | tf_op jit(solution)/shard_map/all_to_all | solution.py:231
  268.9 2.4 convert_reduce_fusion
  271.3 0.9 slice_bitcast_fusion
  272.2 50.0 %reduce-scatter.2.cloned.1.call-done = bf16[128,2048]{1,0:T(8,128)(2,1)} async-done(((bf16[2048,2048]{1,0:T(8,128)(2,1)}), bf16[128,2048]{1,0:T(8,128)(2,1)}) %reduce-scatter.2.cloned.1.call-update) | async-done | bytes 524304 | tf_op jit(solution)/shard_map/reduce_scatter | solution.py:226
  322.2 2.1 bitcast_convert_fusion
  (8 shorter events, 0.0 us)
Async XLA Ops:
  7.2 116.0 %all-gather.3.cloned.1.call-start = ((), (), s32[]{:S(2)}) async-start(), calls=%async_computation.9 | async-start | bytes 8912896 | tf_op jit(solution)/shard_map/all_gather | solution.py:184
  7.9 0.7 copy-start.11
  8.6 0.7 copy-start.12
  10.4 35.5 %all-to-all-start = ((bf16[64,8,128]{2,1,0:T(8,128)(2,1)}), bf16[64,8,128]{2,1,0:T(8,128)(2,1)S(1)}, u32[]{:S(2)}, u32[]{:S(2)}) async-start(bf16[64,8,128]{2,1,0:T(8,128)(2,1)} %bitcast.4), calls=%async_computation | async-start | bytes 262144 | tf_op jit(solution)/shard_map/all_to_all | solution.py:193
  47.8 80.6 %all-to-all-start.2 = ((bf16[8,256,768]{2,1,0:T(8,128)(2,1)}), bf16[8,256,768]{2,1,0:T(8,128)(2,1)}, u32[]{:S(2)}, u32[]{:S(2)}) async-start(bf16[8,256,768]{2,1,0:T(8,128)(2,1)} %broadcast_in_dim.42), calls=%async_computation.2 | async-start | bytes 6291456 | tf_op jit(solution)/shard_map/all_to_all | solution.py:210
  127.3 1.1 copy-start.1
  128.4 22.6 %all-to-all-start.1 = ((bf16[4,80,2048]{2,1,0:T(8,128)(2,1)}), bf16[4,80,2048]{2,1,0:T(8,128)(2,1)S(1)}, u32[]{:S(2)}, u32[]{:S(2)}) async-start(bf16[4,80,2048]{2,1,0:T(8,128)(2,1)} %copy-done.1), calls=%async_computation.1 | async-start | bytes 2621440 | tf_op jit(solution)/shard_map/all_to_all | solution.py:182
  137.1 1.1 copy-start
  138.2 17.7 %copy-start.2 = (bf16[1,1,640,384]{3,2,1,0:T(8,128)(2,1)S(1)}, bf16[1,1,640,384]{3,2,1,0:T(8,128)(2,1)}, u32[]{:S(2)}) copy-start(bf16[1,1,640,384]{3,2,1,0:T(8,128)(2,1)} %param.11) | copy-start | bytes 1474564
  151.0 21.6 %all-to-all-start.3 = ((bf16[4,80,2048]{2,1,0:T(8,128)(2,1)}), bf16[4,80,2048]{2,1,0:T(8,128)(2,1)}, u32[]{:S(2)}, u32[]{:S(2)}) async-start(bf16[4,80,2048]{2,1,0:T(8,128)(2,1)} %copy-done), calls=%async_computation.3 | async-start | bytes 2621440 | tf_op jit(solution)/shard_map/all_to_all | solution.py:182
  160.6 1.1 copy-start.3
  161.7 0.8 copy-start.7
  172.6 20.7 %all-to-all-start.5 = ((bf16[4,80,2048]{2,1,0:T(8,128)(2,1)}), bf16[4,80,2048]{2,1,0:T(8,128)(2,1)}, u32[]{:S(2)}, u32[]{:S(2)}) async-start(bf16[4,80,2048]{2,1,0:T(8,128)(2,1)} %bitcast.48), calls=%async_computation.5 | async-start | bytes 2621440 | tf_op jit(solution)/shard_map/all_to_all | solution.py:182
  182.0 1.1 copy-start.4
  183.1 0.8 copy-start.5
  183.8 0.7 copy-start.9
  193.3 19.8 %all-to-all-start.4 = ((bf16[4,80,2048]{2,1,0:T(8,128)(2,1)}), bf16[4,80,2048]{2,1,0:T(8,128)(2,1)}, u32[]{:S(2)}, u32[]{:S(2)}) async-start(bf16[4,80,2048]{2,1,0:T(8,128)(2,1)} %bitcast.49), calls=%async_computation.4 | async-start | bytes 2621440 | tf_op jit(solution)/shard_map/all_to_all | solution.py:182
  197.7 124.5 %reduce-scatter.2.cloned.1.call-start = ((), (), s32[]{:S(2)}) async-start(), calls=%async_computation.8 | async-start | bytes 8912896 | tf_op jit(solution)/shard_map/reduce_scatter | solution.py:226
  219.8 1.0 copy-start.8
  220.8 1.8 copy-start.6
  227.5 4.9 %copy-start.10 = (bf16[4,80,384]{2,1,0:T(8,128)(2,1)S(1)}, bf16[4,80,384]{2,1,0:T(8,128)(2,1)}, u32[]{:S(2)}) copy-start(bf16[4,80,384]{2,1,0:T(8,128)(2,1)} %copy-done.9) | copy-start | bytes 737284
  227.5 41.4 %all-to-all-start.6 = ((bf16[8,256,768]{2,1,0:T(8,128)(2,1)}), bf16[8,256,768]{2,1,0:T(8,128)(2,1)}, u32[]{:S(2)}, u32[]{:S(2)}) async-start(bf16[8,256,768]{2,1,0:T(8,128)(2,1)} %bitcast.54), calls=%async_computation.7 | async-start | bytes 6291456 | tf_op jit(solution)/shard_map/all_to_all | solution.py:231
Sparse Core Ops, SparseCore 0:
  10.1 112.9 all-gather.2
  219.9 102.2 reduce-scatter.1

commit v8 on v0

v8 whole, which is shorter than its diff:
```python
import functools

import jax
import jax.numpy as jnp
import numpy as np
from jax import lax
from jax.experimental import pallas as pl
from jax.experimental.pallas import tpu as pltpu
from jax.sharding import PartitionSpec as P

LINES = 8
QUARTERS = 4
LANES = 128
VMEM_BYTES = 48 * 1024 * 1024
F32 = jnp.float32
BF16 = jnp.bfloat16


def call(kernel, out_shape, *operands):
    whole = pl.BlockSpec(memory_space=pltpu.VMEM)
    return pl.pallas_call(
        kernel,
        out_shape=out_shape,
        in_specs=[whole] * len(operands),
        out_specs=jax.tree.map(lambda _: whole, out_shape),
        compiler_params=pltpu.CompilerParams(vmem_limit_bytes=VMEM_BYTES),
    )(*operands)


def array(shape, dtype=BF16):
    return jax.ShapeDtypeStruct(shape, dtype)


def iota(shape, dimension):
    return lax.broadcasted_iota(jnp.int32, shape, dimension)


def one_hot(condition):
    return jnp.where(condition, 1.0, 0.0).astype(BF16)


def dot(a, b, contract=(1, 0)):
    return lax.dot_general(a, b, (((contract[0],), (contract[1],)), ((), ())), preferred_element_type=F32)


def of_quarter(select, quarter):
    line = iota(select.shape, 0) & (LINES - 1)
    return jnp.where((line & (QUARTERS - 1)) == quarter, select, jnp.zeros_like(select))


def source_kernel(ids_ref, weights_ref, tokens_ref, out_ref, main_ref, extra_ref):
    tokens, width = tokens_ref.shape
    step = width // QUARTERS
    shape = (out_ref.shape[0], tokens)
    row = iota(shape, 0)
    expert, line = row // LINES, row & (LINES - 1)
    hits = jnp.zeros(shape, F32)
    eighths = jnp.zeros(shape, F32)
    weights = weights_ref[...].astype(F32)
    for choice in range(ids_ref.shape[0]):
        named = ids_ref[choice : choice + 1, :] == expert
        hits = hits + jnp.where(named, 1.0, 0.0)
        eighths = eighths + jnp.where(named, weights[choice : choice + 1, :], 0.0)
    earlier = one_hot(iota((tokens, tokens), 0) < iota((tokens, tokens), 1))
    rank = jnp.where(hits > 0.0, dot(hits.astype(BF16), earlier), -1.0).astype(jnp.int32)
    is_main = rank == line
    is_extra = rank == LINES + line // QUARTERS
    main, extra = one_hot(is_main), one_hot(is_extra)
    main_ref[...] = main
    extra_ref[...] = extra
    out_ref[:, :width] = dot(main, tokens_ref[...]).astype(BF16)
    beside = dot(of_quarter(extra, 0), tokens_ref[:, :step])
    for quarter in range(1, QUARTERS):
        beside = beside + dot(of_quarter(extra, quarter), tokens_ref[:, quarter * step : (quarter + 1) * step])
    out_ref[:, width : width + step] = beside.astype(BF16)
    main_weight = jnp.sum(jnp.where(is_main, eighths, 0.0), axis=1, keepdims=True)
    extra_weight = jnp.sum(jnp.where(is_extra, eighths, 0.0), axis=1, keepdims=True)
    lane = iota((shape[0], LANES), 1)
    both = jnp.where(lane == 0, main_weight, jnp.where(lane == 1, extra_weight, 0.0))
    out_ref[:, width + step :] = both.astype(BF16)


def order_of(sources):
    slots = LINES + 2
    first = [source * slots + slot for source in range(sources) for slot in range(LINES)]
    return np.array(first + [source * slots + slot for slot in (8, 9) for source in range(sources)], np.int32)


def reorder_kernel(row_ref, values_ref, out_ref):
    move = one_hot(iota((row_ref.shape[0], values_ref.shape[0]), 1) == row_ref[...])
    out_ref[...] = dot(move, values_ref[...]).astype(BF16)


def lines_of(rows, lines, quarter):
    row = iota((rows, lines), 0)
    sources = rows // 2
    source, second = row & (sources - 1), row // sources
    return one_hot(iota((rows, lines), 1) == source * LINES + second * QUARTERS + quarter)


def expert_kernel(
    blocks_ref, matrix_ref, cotangent_ref, row_ref, hidden_ref, grad_ref, extra_ref, back_ref
):
    lines, extras = blocks_ref.shape[0], extra_ref.shape[0]
    width = matrix_ref.shape[0]
    step = width // QUARTERS
    units = hidden_ref.shape[1]
    places = [lines_of(extras, lines, quarter) for quarter in range(QUARTERS)]
    beside = blocks_ref[:, width : width + step]
    for quarter in range(QUARTERS):
        extra_ref[:, quarter * step : (quarter + 1) * step] = dot(places[quarter], beside).astype(BF16)
    weights = blocks_ref[:, width + step :]
    main_weight = weights[:, 0:1].astype(F32)
    extra_weight = dot(places[0], weights)[:, 1:2]
    weight = jnp.concatenate((main_weight, extra_weight), axis=0) * 0.125

    pre = jnp.concatenate(
        (dot(blocks_ref[:, :width], matrix_ref[...]), dot(extra_ref[...], matrix_ref[...])), axis=0
    )
    gate_pre, up_pre = pre[:, :units], pre[:, units:]
    sigmoid_gate = jax.nn.sigmoid(gate_pre)
    activation = gate_pre * sigmoid_gate
    hidden = (activation * up_pre * weight).astype(BF16)
    act_slope = sigmoid_gate * (1.0 + gate_pre * (1.0 - sigmoid_gate))
    scaled = cotangent_ref[...].astype(F32) * weight
    grad_ref[:, :units] = (scaled * up_pre * act_slope).astype(BF16)
    grad_ref[:, units:] = (scaled * activation).astype(BF16)
    back_ref[:, :width] = dot(grad_ref[:lines, :], matrix_ref[...], (1, 1)).astype(BF16)
    extra_back = dot(grad_ref[lines:, :], matrix_ref[...], (1, 1)).astype(BF16)
    beside = dot(places[0], extra_back[:, :step], (0, 0))
    for quarter in range(1, QUARTERS):
        beside = beside + dot(places[quarter], extra_back[:, quarter * step : (quarter + 1) * step], (0, 0))
    back_ref[:, width:] = beside.astype(BF16)
    move = one_hot(iota((row_ref.shape[0], hidden.shape[0]), 1) == row_ref[...])
    hidden_ref[...] = dot(move, hidden).astype(BF16)


def token_kernel(main_ref, extra_ref, blocks_ref, out_ref):
    width = out_ref.shape[1]
    step = width // QUARTERS
    extra = extra_ref[...]
    total = dot(main_ref[...], blocks_ref[:, :width], (0, 0))
    for quarter in range(QUARTERS):
        part = slice(quarter * step, (quarter + 1) * step)
        out_ref[:, part] = total[:, part] + dot(of_quarter(extra, quarter), blocks_ref[:, width:], (0, 0))


def shards(tokens, expert_ids, route_weights, gate_weight, up_weight, cotangent):
    experts = lax.axis_size("expert")
    slot_count, units = cotangent.shape[2:]
    block, width = tokens.shape[1:]
    lines, extras = experts * LINES, experts * 2
    step = width // QUARTERS

    def exchange(blocks):
        parts = blocks.reshape(experts, LINES, blocks.shape[1])
        return lax.all_to_all(parts, "expert", 0, 0, tiled=True).reshape(blocks.shape)

    outgoing, main, extra = call(
        source_kernel,
        (array((lines, width + step + LANES)), array((lines, block)), array((lines, block))),
        expert_ids[0].T,
        route_weights[0].T,
        tokens[0],
    )
    arrived = exchange(outgoing)

    stacked = jnp.concatenate((gate_weight[0], up_weight[0]), axis=1)
    matrix = lax.all_gather(stacked, "dp", axis=0, tiled=True)
    order = order_of(experts)
    cotangent_rows = call(
        reorder_kernel, array((slot_count, units)), jnp.asarray(order[:, None]), cotangent[0, 0]
    )
    hidden, grads, extra_rows, back = call(
        expert_kernel,
        (
            array((slot_count, units)),
            array((slot_count, 2 * units)),
            array((extras, width)),
            array((lines, width + step)),
        ),
        arrived,
        matrix,
        cotangent_rows,
        jnp.asarray(np.argsort(order).astype(np.int32)[:, None]),
    )
    token_grads = call(token_kernel, array((block, width), F32), main, extra, exchange(back))

    terms = dot(arrived[:, :width], grads[:lines], (0, 0)) + dot(extra_rows, grads[lines:], (0, 0))
    weight_grads = lax.psum_scatter(terms.astype(BF16), "dp", scatter_dimension=0, tiled=True).astype(F32)
    return (
        hidden[None, None],
        token_grads[None],
        weight_grads[None, :, :units],
        weight_grads[None, :, units:],
    )


def solution(mesh):
    in_specs = (
        P("dp", "expert", None),
        P("dp", "expert", None),
        P("dp", "expert", None),
        P("expert", "dp", None),
        P("expert", "dp", None),
        P("dp", "expert", None, None),
    )
    out_specs = (
        P("dp", "expert", None, None),
        P("dp", "expert", None),
        P("expert", "dp", None),
        P("expert", "dp", None),
    )
    return jax.shard_map(shards, mesh=mesh, in_specs=in_specs, out_specs=out_specs, check_vma=False)
```

time: 469 us -> 308 us (0.66)
  waiting for transfers between devices: 373 us -> 236 us
  local copies, waits for them, and re-layouts: 26.5 us -> 5.86 us
  Pallas kernels: 0 us -> 15.8 us
  matrix products: 17.2 us -> 7.19 us
  starting transfers between devices: 32.4 us -> 26.4 us
    all_to_all x3 -> x2, waiting for transfers between devices: 334 us -> 158 us  [exchange(): lax.all_to_all(parts, 'expert', 0, 0, tiled=True).reshape(blocks.shape)]
    all_gather x1, waiting for transfers between devices: 0.02 us -> 37 us  [shards(): matrix = lax.all_gather(stacked, 'dp', axis=0, tiled=True)]
    pallas_call x0 -> x4, Pallas kernels: none -> 15.8 us  [call(): pl.pallas_call(kernel, out_shape=out_shape, in_specs=[whole] * len(operan...]
    reshape x4 -> x0, local copies, waits for them, and re-layouts: 13.7 us -> none  [the longest x1 4.08 us: shards(): slot_rows = arrived.reshape(slot_count, model_width)]
    dot_general x7 -> x2, matrix products: 17.2 us -> 7.19 us  [dot(): lax.dot_general(a, b, (((contract[0],), (contract[1],)), ((), ())), prefe...]
    gather x4 -> x0, local copies, waits for them, and re-layouts: 7.07 us -> none  [local_slots(): ranked = jnp.take_along_axis(before, chosen, axis=1)]
    all_to_all x3 -> x2, starting transfers between devices: 32.1 us -> 26.2 us  [exchange(): lax.all_to_all(parts, 'expert', 0, 0, tiled=True).reshape(blocks.shape)]
  transfers between devices with their start and end apart: 5 -> 4, of which waited for: 4 -> 4; matrix products, arithmetic and copies ran while one was open for 4% -> 3% of each run, Pallas kernels for 0% -> 0%
where the time goes in v8:
time: 308 us; the launch traced here: 307 us
  waiting for transfers between devices  236 us (77%)
  starting transfers between devices  26.4 us (9%)
  Pallas kernels  15.8 us (5%)
  between operations  14.1 us (5%)
  matrix products  7.19 us (2%)
  local copies, waits for them, and re-layouts  5.86 us (2%)
    all_to_all x2, waiting for transfers between devices, exchange(): lax.all_to_all(parts, 'expert', 0, 0, tiled=True).reshape(blocks.shape)  158 us
    reduce_scatter x1, waiting for transfers between devices, shards(): lax.psum_scatter(terms.astype(BF16), 'dp', scatter_dimension=0, tiled=True)  41.4 us
    all_gather x1, waiting for transfers between devices, shards(): matrix = lax.all_gather(stacked, 'dp', axis=0, tiled=True)  37 us
    all_to_all x2, starting transfers between devices, exchange(): lax.all_to_all(parts, 'expert', 0, 0, tiled=True).reshape(blocks.shape)  26.2 us
    pallas_call x4, Pallas kernels, call(): pl.pallas_call(kernel, out_shape=out_shape, in_specs=[whole] * len(operan...  15.8 us
    dot_general x2, matrix products, dot(): lax.dot_general(a, b, (((contract[0],), (contract[1],)), ((), ())), prefe...  7.19 us
  transfers between devices with their start and end apart: 4, of which 4 were waited for; matrix products, arithmetic and copies ran while one was open for 3% of the time, Pallas kernels for 0%

profile of v8, /device:TPU:6, one launch (start us, length us, event | category | flops | bytes accessed | tf_op | source)
XLA Modules:
  0.0 307.2 jit_solution(14197992754300355277)
XLA Ops:
  7.2 0.0 copy-start.2
  7.2 1.0 copy-done.2
  8.2 0.0 copy-start.6
  8.2 0.7 copy-done.6
  8.9 0.0 copy-start.7
  8.9 0.7 copy-done.7
  9.6 0.0 copy-start.8
  9.6 0.0 copy-start.9
  9.6 3.4 %shard_map.111 = (bf16[512,2688]{1,0:T(8,128)(2,1)}, bf16[512,128]{1,0:T(8,128)(2,1)S(1)}, bf16[512,128]{1,0:T(8,128)(2,1)S(1)}) custom-call(s32[8,128]{1,0:T(8,128)S(1)} %bitcast.25, s32[8,128]{1,0:T(8,128)S(1)} %bitcast.26, bf16[128,2048]{1,0:T(8,128)(2,1)S(1)} %bitcast.23), custom_call_target="tpu_custom_call" | custom-call | tf_op jit(solution)/shard_map/pallas_call | solution.py:21
  13.0 0.0 copy-start.3
  13.0 0.0 copy-start.5
  13.0 0.0 copy-start.4
  13.0 19.1 %all-to-all-start = ((bf16[64,8,2688]{2,1,0:T(8,128)(2,1)}), bf16[64,8,2688]{2,1,0:T(8,128)(2,1)}, u32[]{:S(2)}, u32[]{:S(2)}) async-start(bf16[64,8,2688]{2,1,0:T(8,128)(2,1)} %bitcast.5), calls=%async_computation | async-start | bytes 5505024 | tf_op jit(solution)/shard_map/all_to_all | solution.py:157
  32.1 0.0 all-gather.2.cloned.1.call-start
  32.2 0.0 copy-done.8
  32.2 0.0 copy-done.9
  32.2 0.8 pad_maximum_fusion
  33.0 0.0 all-gather.2.cloned.1.call-update
  33.0 0.0 copy-done.3
  33.0 0.0 copy-done.5
  33.0 0.7 shard_map.112.cotangent_ref
  33.8 37.0 %all-gather.2.cloned.1.call-done.matrix_ref = bf16[2048,768]{1,0:T(8,128)(2,1)} async-done(((bf16[256,768]{1,0:T(8,128)(2,1)}), bf16[2048,768]{1,0:T(8,128)(2,1)}) %all-gather.2.cloned.1.call-update) | async-done | bytes 3145744 | tf_op jit(solution)/shard_map/all_gather | solution.py:169
  70.7 87.9 %all-to-all-done = bf16[64,8,2688]{2,1,0:T(8,128)(2,1)} async-done(((bf16[64,8,2688]{2,1,0:T(8,128)(2,1)}), bf16[64,8,2688]{2,1,0:T(8,128)(2,1)}, u32[]{:S(2)}, u32[]{:S(2)}) %all-to-all-start) | async-done | bytes 2752544 | tf_op jit(solution)/shard_map/all_to_all | solution.py:157
  158.6 0.0 copy-done.4
  158.6 10.0 %shard_map.113 = (bf16[640,384]{1,0:T(8,128)(2,1)}, bf16[640,768]{1,0:T(8,128)(2,1)S(1)}, bf16[128,2048]{1,0:T(8,128)(2,1)S(1)}, bf16[512,2560]{1,0:T(8,128)(2,1)S(1)}) custom-call(bf16[512,2688]{1,0:T(8,128)(2,1)} %bitcast.6.blocks_ref, bf16[2048,768]{1,0:T(8,128)(2,1)} %all-gather.2.cloned.1.call-done.matrix_ref, ...), custom_call_target="tpu_custom_call" | custom-call | tf_op jit(solution)/shard_map/pallas_call | solution.py:21
  168.6 0.0 copy-start
  168.6 1.6 copy-done
  170.2 0.0 copy-start.1
  170.2 0.9 copy-done.1
  171.1 7.1 %all-to-all-start.1 = ((bf16[64,8,2560]{2,1,0:T(8,128)(2,1)}), bf16[64,8,2560]{2,1,0:T(8,128)(2,1)S(1)}, u32[]{:S(2)}, u32[]{:S(2)}) async-start(bf16[64,8,2560]{2,1,0:T(8,128)(2,1)} %bitcast.22), calls=%async_computation.1 | async-start | bytes 5242880 | tf_op jit(solution)/shard_map/all_to_all | solution.py:157
  178.2 0.2 reduce-scatter.2.cloned.1.call-start
  178.4 3.6 %fusion = f32[2048,768]{1,0:T(8,128)S(1)} fusion(bf16[512,2688]{1,0:T(8,128)(2,1)} %bitcast.6.blocks_ref, bf16[640,768]{1,0:T(8,128)(2,1)} %copy-done.1), kind=kOutput, calls=%fused_computation.1 | convolution fusion | flops 1610612736 | bytes 9175040 | tf_op jit(solution)/shard_map/dot_general | solution.py:43
  182.0 3.6 %add_convert_fusion = bf16[2048,768]{1,0:T(8,128)(2,1)} fusion(f32[2048,768]{1,0:T(8,128)S(1)} %fusion, bf16[128,2048]{1,0:T(8,128)(2,1)S(1)} %get-tuple-element.17, bf16[640,768]{1,0:T(8,128)(2,1)} %copy-done.1), kind=kOutput, calls=%fused_computation | convolution fusion | flops 405798912 | bytes 10158080 | tf_op jit(solution)/shard_map/dot_general | solution.py:43
  185.6 0.0 reduce-scatter.2.cloned.1.call-update
  185.6 41.4 %reduce-scatter.2.cloned.1.call-done = bf16[256,768]{1,0:T(8,128)(2,1)} async-done(((bf16[2048,768]{1,0:T(8,128)(2,1)}), bf16[256,768]{1,0:T(8,128)(2,1)}) %reduce-scatter.2.cloned.1.call-update) | async-done | bytes 393232 | tf_op jit(solution)/shard_map/reduce_scatter | solution.py:190
  227.0 1.0 convert_element_type.7
  228.1 0.9 slice_bitcast_fusion
  229.0 69.7 %all-to-all-done.1 = bf16[64,8,2560]{2,1,0:T(8,128)(2,1)S(1)} async-done(((bf16[64,8,2560]{2,1,0:T(8,128)(2,1)}), bf16[64,8,2560]{2,1,0:T(8,128)(2,1)S(1)}, u32[]{:S(2)}, u32[]{:S(2)}) %all-to-all-start.1) | async-done | bytes 2621472 | tf_op jit(solution)/shard_map/all_to_all | solution.py:157
  298.7 1.7 shard_map.114
Async XLA Ops:
  7.2 1.0 copy-start.2
  8.2 0.7 copy-start.6
  8.9 0.7 copy-start.7
  9.6 22.6 %copy-start.8 = (bf16[1,256,384]{2,1,0:T(8,128)(2,1)S(1)}, bf16[1,256,384]{2,1,0:T(8,128)(2,1)}, u32[]{:S(2)}) copy-start(bf16[1,256,384]{2,1,0:T(8,128)(2,1)} %param.12) | copy-start | bytes 589828
  9.6 22.6 %copy-start.9 = (bf16[1,256,384]{2,1,0:T(8,128)(2,1)S(1)}, bf16[1,256,384]{2,1,0:T(8,128)(2,1)}, u32[]{:S(2)}) copy-start(bf16[1,256,384]{2,1,0:T(8,128)(2,1)} %param.11) | copy-start | bytes 589828
  13.0 20.0 %copy-start.3 = (bf16[1,1,640,384]{3,2,1,0:T(8,128)(2,1)S(1)}, bf16[1,1,640,384]{3,2,1,0:T(8,128)(2,1)}, u32[]{:S(2)}) copy-start(bf16[1,1,640,384]{3,2,1,0:T(8,128)(2,1)} %param.13) | copy-start | bytes 1474564
  13.0 20.0 %copy-start.5 = (s32[640,1]{1,0:T(8,128)S(1)}, s32[640,1]{1,0:T(8,128)}, u32[]{:S(2)}) copy-start(s32[640,1]{1,0:T(8,128)} %constant.4.clone.row_ref) | copy-start | bytes 7684
  13.0 145.6 %copy-start.4 = (s32[640,1]{1,0:T(8,128)S(1)}, s32[640,1]{1,0:T(8,128)}, u32[]{:S(2)}) copy-start(s32[640,1]{1,0:T(8,128)} %constant.5.clone.row_ref) | copy-start | bytes 7684
  13.0 145.6 %all-to-all-start = ((bf16[64,8,2688]{2,1,0:T(8,128)(2,1)}), bf16[64,8,2688]{2,1,0:T(8,128)(2,1)}, u32[]{:S(2)}, u32[]{:S(2)}) async-start(bf16[64,8,2688]{2,1,0:T(8,128)(2,1)} %bitcast.5), calls=%async_computation | async-start | bytes 5505024 | tf_op jit(solution)/shard_map/all_to_all | solution.py:157
  32.1 38.6 %all-gather.2.cloned.1.call-start = ((), (), s32[]{:S(2)}) async-start(), calls=%async_computation.3 | async-start | bytes 3538944 | tf_op jit(solution)/shard_map/all_gather | solution.py:169
  168.6 1.6 copy-start
  170.2 0.9 copy-start.1
  171.1 127.6 %all-to-all-start.1 = ((bf16[64,8,2560]{2,1,0:T(8,128)(2,1)}), bf16[64,8,2560]{2,1,0:T(8,128)(2,1)S(1)}, u32[]{:S(2)}, u32[]{:S(2)}) async-start(bf16[64,8,2560]{2,1,0:T(8,128)(2,1)} %bitcast.22), calls=%async_computation.1 | async-start | bytes 5242880 | tf_op jit(solution)/shard_map/all_to_all | solution.py:157
  178.2 48.8 %reduce-scatter.2.cloned.1.call-start = ((), (), s32[]{:S(2)}) async-start(), calls=%async_computation.4 | async-start | bytes 3538944 | tf_op jit(solution)/shard_map/reduce_scatter | solution.py:190
Sparse Core Ops, SparseCore 0:
  35.6 35.0 all-gather.1
  185.7 41.2 reduce-scatter.1

commit v9 on v4

--- a/solution.py
+++ b/solution.py
@@ -11,6 +11,8 @@
 N_Y = 4
 N_Z = 16
 DIRECT = 512
+HALVES = 2
+STEP = 512
 VMEM_BYTES = 48 * 1024 * 1024
 
 
@@ -34,48 +36,22 @@
     out_ref[...] = jnp.where(kind <= N_Y, rank, eighths).astype(jnp.bfloat16)
 
 
-def slot_matrix(slot_ref, part, part_slots, part_tokens):
-    columns = slice(part * part_tokens, (part + 1) * part_tokens)
-    slot = lax.broadcasted_iota(jnp.int32, (part_slots, part_tokens), 0) + part * part_slots
-    return jnp.concatenate(
-        [jnp.where(slot_ref[y : y + 1, columns] == slot, 1.0, 0.0).astype(jnp.bfloat16) for y in range(N_Y)],
-        axis=0,
-    )
-
-
-def pick_kernel(parts, slot_ref, tokens_ref, out_ref):
-    part_slots = out_ref.shape[1] // parts
-    part_tokens = tokens_ref.shape[0] // parts
-    for part in range(parts):
-        select = slot_matrix(slot_ref, part, part_slots, part_tokens)
-        picked = jnp.dot(
-            select,
-            tokens_ref[part * part_tokens : (part + 1) * part_tokens, :],
-            preferred_element_type=jnp.float32,
-        ).astype(jnp.bfloat16)
-        for y in range(N_Y):
-            out_ref[y, part * part_slots : (part + 1) * part_slots, :] = picked[
-                y * part_slots : (y + 1) * part_slots, :
-            ]
-
-
-def add_kernel(parts, slot_ref, grads_ref, out_ref):
-    part_slots = grads_ref.shape[1] // parts
-    part_tokens = out_ref.shape[0] // parts
-    for part in range(parts):
-        select = slot_matrix(slot_ref, part, part_slots, part_tokens)
-        rows = jnp.concatenate(
-            [grads_ref[y, part * part_slots : (part + 1) * part_slots, :] for y in range(N_Y)], axis=0
-        )
-        out_ref[part * part_tokens : (part + 1) * part_tokens, :] = lax.dot_general(
-            select, rows, (((0,), (0,)), ((), ())), preferred_element_type=jnp.float32
-        ).astype(jnp.bfloat16)
+def array(shape, dtype=jnp.bfloat16):
+    return jax.ShapeDtypeStruct(shape, dtype)
 
 
 def dot(a, b, contract=(1, 0)):
     return lax.dot_general(
         a, b, (((contract[0],), (contract[1],)), ((), ())), preferred_element_type=jnp.float32
     )
+
+
+def one_hot(condition):
+    return jnp.where(condition, 1.0, 0.0).astype(jnp.bfloat16)
+
+
+PARAMS = pltpu.CompilerParams(vmem_limit_bytes=VMEM_BYTES)
+WHOLE = pl.BlockSpec(memory_space=pltpu.VMEM)
 
 
 def direct_pick_kernel(rank_ref, expert_ref, place_ref, tokens_ref, out_ref, select_ref):
@@ -87,11 +63,68 @@
     out_ref[...] = dot(select, tokens_ref[...]).astype(jnp.bfloat16)
 
 
-def expert_kernel(
-    direct_ref, rows_ref, matrix_ref, weight_ref, cotangent_ref, hidden_ref, grad_ref, row_grads_ref
-):
+def select_kernel(slot_ref, place_ref, pick_ref, add_ref):
+    halves, rows, tokens = pick_ref.shape
+    slots = rows // N_Y
+    for half in range(halves):
+        part = slice(half * tokens, (half + 1) * tokens)
+        slot = lax.broadcasted_iota(jnp.int32, (slots, tokens), 0) + half * slots
+        for y in range(N_Y):
+            pick_ref[half, y * slots : (y + 1) * slots, :] = one_hot(slot_ref[y : y + 1, part] == slot)
+        row = lax.broadcasted_iota(jnp.int32, (tokens, rows), 1)
+        mark = (place_ref[part, 0:1] - half * slots == row) & (row < slots)
+        for y in range(1, N_Y):
+            here = place_ref[part, y : y + 1] + (y - half) * slots == row
+            mark = mark | (here & (row >= y * slots) & (row < (y + 1) * slots))
+        add_ref[half] = one_hot(mark)
+
+
+def pick_kernel(select_ref, tokens_ref, *out_refs):
+    halves, rows, tokens = select_ref.shape
+    slots = rows // N_Y
+    for half in range(halves):
+        part = tokens_ref[half * tokens : (half + 1) * tokens, :]
+        picked = dot(select_ref[half], part).astype(jnp.bfloat16)
+        for y, out_ref in enumerate(out_refs):
+            out_ref[half * slots : (half + 1) * slots, :] = picked[y * slots : (y + 1) * slots]
+
+
+def add_kernel(select_ref, *refs):
+    grad_refs, out_ref = refs[:-1], refs[-1]
+    halves, tokens, rows = select_ref.shape
+    slots = rows // N_Y
+    for half in range(halves):
+        part = slice(half * slots, (half + 1) * slots)
+        grads = jnp.concatenate([ref[part, :] for ref in grad_refs], axis=0)
+        out_ref[half * tokens : (half + 1) * tokens, :] = dot(select_ref[half], grads).astype(jnp.bfloat16)
+
+
+def by_columns(kernel, out_shapes, select, *values):
+    def part(rows):
+        return pl.BlockSpec((rows, STEP), lambda step: (0, step))
+
+    return pl.pallas_call(
+        kernel,
+        grid=(out_shapes[0].shape[1] // STEP,),
+        out_shape=out_shapes,
+        in_specs=[pl.BlockSpec(select.shape, lambda step: (0, 0, 0))] + [part(value.shape[0]) for value in values],
+        out_specs=tuple(part(shape.shape[0]) for shape in out_shapes),
+        compiler_params=PARAMS,
+    )(select, *values)
+
+
+def expert_kernel(y_ref, direct_ref, matrix_ref, weight_ref, cotangent_ref, *refs):
+    arrived, refs = refs[:N_Y], refs[N_Y:]
+    rows_ref, hidden_ref, grad_ref, direct_back_ref = refs[:4]
+    back_refs = refs[4:]
     units = hidden_ref.shape[1]
     width = direct_ref.shape[1]
+    count = arrived[0].shape[0]
+    parts = [
+        pl.ds(pl.multiple_of(((y_ref[0] + N_Y - k) & (N_Y - 1)) * count, count), count) for k in range(N_Y)
+    ]
+    for part, ref in zip(parts, arrived):
+        rows_ref[part, :] = ref[...]
     pre = dot(direct_ref[...], matrix_ref[:width, :]) + dot(rows_ref[...], matrix_ref[width:, :])
     gate_pre, up_pre = pre[:, :units], pre[:, units:]
     weight = weight_ref[...]
@@ -102,22 +135,19 @@
     scaled = cotangent_ref[...].astype(jnp.float32) * weight
     grad_ref[:, :units] = (scaled * up_pre * act_slope).astype(jnp.bfloat16)
     grad_ref[:, units:] = (scaled * activation).astype(jnp.bfloat16)
-    row_grads_ref[...] = dot(grad_ref[...], matrix_ref[width:, :], (1, 1)).astype(jnp.bfloat16)
-
-
-def call(kernel, out_shape, *operands):
-    whole = pl.BlockSpec(memory_space=pltpu.VMEM)
+    direct_back_ref[...] = dot(grad_ref[...], matrix_ref[:width, :], (1, 1)).astype(jnp.bfloat16)
+    for part, ref in zip(parts, back_refs):
+        ref[...] = dot(grad_ref[part, :], matrix_ref[width:, :], (1, 1)).astype(jnp.bfloat16)
+
+
+def call(kernel, out_shape, *operands, scalars=0):
     return pl.pallas_call(
         kernel,
         out_shape=out_shape,
-        in_specs=[whole] * len(operands),
-        out_specs=jax.tree.map(lambda _: whole, out_shape),
-        compiler_params=pltpu.CompilerParams(vmem_limit_bytes=VMEM_BYTES),
+        in_specs=[pl.BlockSpec(memory_space=pltpu.SMEM)] * scalars + [WHOLE] * (len(operands) - scalars),
+        out_specs=jax.tree.map(lambda _: WHOLE, out_shape),
+        compiler_params=PARAMS,
     )(*operands)
-
-
-def array(shape):
-    return jax.ShapeDtypeStruct(shape, jnp.bfloat16)
 
 
 def after(value, *others):
@@ -133,9 +163,11 @@
     block, model_width = tokens.shape[1:]
     width = model_width - DIRECT
 
-    def exchange(rows):
-        parts = rows.reshape(N_Y, row_slots, rows.shape[1])
-        return lax.all_to_all(parts, "y", 0, 0, tiled=True).reshape(rows.shape)
+    def exchange(parts, sign):
+        moved = [
+            lax.ppermute(parts[k], "y", [(i, (i + sign * k) % N_Y) for i in range(N_Y)]) for k in range(1, N_Y)
+        ]
+        return [parts[0]] + moved
 
     def exchange_direct(rows):
         parts = rows.reshape(experts, 8, capacity * DIRECT // 8)
@@ -150,6 +182,14 @@
     rank = jnp.transpose(own_row[:, :N_Y], (1, 0, 2)).astype(jnp.int32)
     base = capacity * jnp.arange(N_Z, dtype=jnp.int32)[None, :, None]
     slot_of = jnp.where(rank >= 0, rank + base, -1).reshape(N_Y, N_Z * block)
+    slot_of = lax.dynamic_slice_in_dim(jnp.concatenate((slot_of, slot_of)), lax.axis_index("y"), N_Y, axis=0)
+    half_rows, half_tokens = N_Y * row_slots // HALVES, N_Z * block // HALVES
+    pick_select, add_select = call(
+        select_kernel,
+        (array((HALVES, half_rows, half_tokens)), array((HALVES, half_tokens, half_rows))),
+        slot_of,
+        slot_of.T,
+    )
     places = jnp.arange(capacity, dtype=jnp.int32).astype(jnp.bfloat16)
     weight_col = jnp.sum(
         jnp.where(
@@ -159,9 +199,8 @@
         ),
         axis=2,
     ).reshape(slot_count, 1) / 8.0
-
     slots = np.arange(slot_count, dtype=np.int32)[:, None]
-    direct, select = call(
+    direct, direct_select = call(
         direct_pick_kernel,
         (array((slot_count, DIRECT)), array((slot_count, block))),
         told[:, N_Y],
@@ -169,32 +208,43 @@
         jnp.asarray(slots % capacity),
         tokens[0, :, :DIRECT],
     )
-    direct = exchange_direct(direct)
-
     stacked = jnp.concatenate((gate_weight[0], up_weight[0]), axis=1)
     matrix = lax.all_to_all(
         jnp.broadcast_to(stacked[None], (groups,) + stacked.shape), "dp", 0, 0, tiled=True
     ).reshape(model_width, 2 * units)
 
-    picked = call(functools.partial(pick_kernel, 2), array((N_Y, row_slots, width)), slot_of, gathered)
-    rows = exchange(picked.reshape(slot_count, width))
-    hidden, grads, row_grads = call(
+    gathered, direct = lax.optimization_barrier(
+        (gathered, direct.reshape(experts, 8, capacity * DIRECT // 8), weight_col, pick_select, add_select, matrix)
+    )[:2]
+    direct = exchange_direct(direct.reshape(slot_count, DIRECT))
+    part = array((row_slots, width))
+    picked = by_columns(pick_kernel, (part,) * N_Y, pick_select, gathered)
+    results = call(
         expert_kernel,
-        (array((slot_count, units)), array((slot_count, 2 * units)), array((slot_count, width))),
+        (
+            array((slot_count, width)),
+            array((slot_count, units)),
+            array((slot_count, 2 * units)),
+            array((slot_count, DIRECT)),
+        )
+        + (part,) * N_Y,
+        lax.axis_index("y").astype(jnp.int32).reshape(1),
         direct,
-        rows,
         matrix,
         weight_col,
         cotangent[0, 0],
-    )
-
-    returned = exchange(row_grads).reshape(N_Y, row_slots, width)
-    sums = call(functools.partial(add_kernel, 2), array((N_Z * block, width)), slot_of, returned)
+        *exchange(picked, 1),
+        scalars=1,
+    )
+    rows, hidden, grads, direct_back = results[:4]
+
+    direct_back = exchange_direct(direct_back)
+    direct_back, *returned = lax.optimization_barrier((direct_back, *exchange(results[4:], -1)))
+    (sums,) = by_columns(add_kernel, (array((N_Z * block, width)),), add_select, *returned)
     token_grads = lax.psum_scatter(sums, "z", scatter_dimension=0, tiled=True).astype(jnp.float32)
 
+    direct_grads = dot(direct_select, after(direct_back, sums), (0, 0))
     late_grads = after(grads, sums)
-    direct_grads = dot(late_grads, matrix[:DIRECT], (1, 1)).astype(jnp.bfloat16)
-    direct_grads = dot(select, exchange_direct(direct_grads), (0, 0))
     terms = jnp.concatenate(
         (
             dot(direct, late_grads, (0, 0)).astype(jnp.bfloat16),

time: 329 us -> 331 us (level)
  starting transfers between devices: 46.9 us -> 76.1 us
  blocking collectives: 26.6 us -> 0 us
  waiting for transfers between devices: 188 us -> 172 us
  local copies, waits for them, and re-layouts: 18 us -> 27.2 us
  Pallas kernels: 21.3 us -> 25.6 us
    all_to_all x2, waiting for transfers between devices: 80.8 us -> 44.6 us  [exchange_direct(): lax.all_to_all(parts, ('y', 'z'), 0, 0, tiled=True).reshape(rows.shape)]
    all_to_all x1 -> x0, blocking collectives: 26.6 us -> none  [exchange(): return lax.all_to_all(parts, 'y', 0, 0, tiled=True).reshape(rows.shape)]
    all_to_all x1, waiting for transfers between devices: 2.32 us -> 28 us  [shards(): lax.all_to_all(jnp.broadcast_to(stacked[None], (groups,) + stacked.shape)...]
    reduce_scatter x1, waiting for transfers between devices: 9.7 us -> 34 us  [shards(): lax.psum_scatter(sums, 'z', scatter_dimension=0, tiled=True)]
    all_to_all x1 -> x0, waiting for transfers between devices: 23.8 us -> none  [exchange(): return lax.all_to_all(parts, 'y', 0, 0, tiled=True).reshape(rows.shape)]
    ppermute x0 -> x6, starting transfers between devices: none -> 22 us  [exchange(): lax.ppermute(parts[k], 'y', [(i, (i + sign * k) % N_Y) for i in range(N_Y)])]
    all_gather x1, waiting for transfers between devices: 27.8 us -> 14.2 us  [shards(): gathered = lax.all_gather(tokens[0, :, DIRECT:], 'z', axis=0, tiled=True)]
    all_to_all x2, starting transfers between devices: 14.1 us -> 25.6 us  [exchange_direct(): lax.all_to_all(parts, ('y', 'z'), 0, 0, tiled=True).reshape(rows.shape)]
  transfers between devices with their start and end apart: 8 -> 13, of which waited for: 8 -> 9; matrix products, arithmetic and copies ran while one was open for 7% -> 6% of each run, Pallas kernels for 2% -> 3%
where the time goes in v9:
time: 331 us; the launch traced here: 329 us
  waiting for transfers between devices  172 us (52%)
  starting transfers between devices  76.1 us (23%)
  local copies, waits for them, and re-layouts  27.2 us (8%)
  Pallas kernels  25.6 us (8%)
  between operations  14.3 us (4%)
  other arithmetic  6.87 us (2%)
  matrix products  6.54 us (2%)
    all_to_all x2, waiting for transfers between devices, exchange_direct(): lax.all_to_all(parts, ('y', 'z'), 0, 0, tiled=True).reshape(rows.shape)  44.6 us
    all_to_all x1, waiting for transfers between devices, shards(): lax.all_to_all(terms, 'dp', 0, 0, tiled=True).astype(jnp.float32)  34.2 us
    reduce_scatter x1, waiting for transfers between devices, shards(): lax.psum_scatter(sums, 'z', scatter_dimension=0, tiled=True)  34 us
    all_to_all x1, waiting for transfers between devices, shards(): lax.all_to_all(jnp.broadcast_to(stacked[None], (groups,) + stacked.shape)...  28 us
    all_to_all x2, starting transfers between devices, exchange_direct(): lax.all_to_all(parts, ('y', 'z'), 0, 0, tiled=True).reshape(rows.shape)  25.6 us
    ppermute x6, starting transfers between devices, exchange(): lax.ppermute(parts[k], 'y', [(i, (i + sign * k) % N_Y) for i in range(N_Y)])  22 us
    all_to_all x1, starting transfers between devices, shards(): heard = lax.all_to_all(told, ('y', 'z'), 0, 0, tiled=True)  18.7 us
    all_to_all x1, waiting for transfers between devices, shards(): heard = lax.all_to_all(told, ('y', 'z'), 0, 0, tiled=True)  15.9 us
  transfers between devices with their start and end apart: 13, of which 9 were waited for; matrix products, arithmetic and copies ran while one was open for 6% of the time, Pallas kernels for 3%

profile of v9, /device:TPU:6, one launch (start us, length us, event | category | flops | bytes accessed | tf_op | source)
XLA Modules:
  0.0 329.0 jit_solution(1769200761151937514)
XLA Ops:
  7.2 1.8 slice.24
  9.0 0.7 copy-done.11
  9.7 0.7 copy-done.12
  10.4 1.2 shard_map.111
  11.5 18.7 %all-to-all-start = ((bf16[64,8,128]{2,1,0:T(8,128)(2,1)}), bf16[64,8,128]{2,1,0:T(8,128)(2,1)S(1)}, u32[]{:S(2)}, u32[]{:S(2)}) async-start(bf16[64,8,128]{2,1,0:T(8,128)(2,1)} %bitcast.6), calls=%async_computation | async-start | bytes 262144 | tf_op jit(solution)/shard_map/all_to_all | solution.py:180
  30.3 1.1 pad_maximum_fusion.1
  31.3 15.9 %all-to-all-done = bf16[64,8,128]{2,1,0:T(8,128)(2,1)S(1)} async-done(((bf16[64,8,128]{2,1,0:T(8,128)(2,1)}), bf16[64,8,128]{2,1,0:T(8,128)(2,1)S(1)}, u32[]{:S(2)}, u32[]{:S(2)}) %all-to-all-start) | async-done | bytes 131104 | tf_op jit(solution)/shard_map/all_to_all | solution.py:180
  47.3 1.9 broadcast_in_dim.46
  49.2 4.9 %all-to-all-start.1 = ((bf16[8,256,768]{2,1,0:T(8,128)(2,1)}), bf16[8,256,768]{2,1,0:T(8,128)(2,1)}, u32[]{:S(2)}, u32[]{:S(2)}) async-start(bf16[8,256,768]{2,1,0:T(8,128)(2,1)} %broadcast_in_dim.46), calls=%async_computation.1 | async-start | bytes 6291456 | tf_op jit(solution)/shard_map/all_to_all | solution.py:212
  54.1 0.9 slice.32
  55.0 0.9 slice_bitcast_fusion.2.tokens_ref
  56.0 0.5 shard_map.112
  56.5 1.5 reshape.62
  58.0 0.1 fusion.1
  58.1 0.4 copy.33
  58.5 2.4 shard_map.113
  60.9 1.1 copy-done
  62.0 0.2 select_reduce_fusion
  62.3 0.1 copy.27
  62.4 0.1 div.10
  62.5 28.0 %all-to-all-done.1 = bf16[8,256,768]{2,1,0:T(8,128)(2,1)} async-done(((bf16[8,256,768]{2,1,0:T(8,128)(2,1)}), bf16[8,256,768]{2,1,0:T(8,128)(2,1)}, u32[]{:S(2)}, u32[]{:S(2)}) %all-to-all-start.1) | async-done | bytes 3145760 | tf_op jit(solution)/shard_map/all_to_all | solution.py:212
  90.5 14.2 %all-gather.3.cloned.1.call-done = bf16[1,2048,1536]{2,1,0:T(8,128)(2,1)} async-done(((bf16[1,128,1536]{2,1,0:T(8,128)(2,1)}), bf16[1,2048,1536]{2,1,0:T(8,128)(2,1)}) %all-gather.3.cloned.1.call-update) | async-done | bytes 6291472 | tf_op jit(solution)/shard_map/all_gather | solution.py:176
  104.7 11.2 %all-to-all-start.2 = ((bf16[64,8,640]{2,1,0:T(8,128)(2,1)}), bf16[64,8,640]{2,1,0:T(8,128)(2,1)}, u32[]{:S(2)}, u32[]{:S(2)}) async-start(bf16[64,8,640]{2,1,0:T(8,128)(2,1)} %reshape.62), calls=%async_computation.2 | async-start | bytes 1310720 | tf_op jit(solution)/shard_map/all_to_all | solution.py:174
  116.0 1.3 copy-done.1
  117.3 5.9 %shard_map.114 = (bf16[160,1536]{1,0:T(8,128)(2,1)S(1)}, bf16[160,1536]{1,0:T(8,128)(2,1)}, bf16[160,1536]{1,0:T(8,128)(2,1)}, bf16[160,1536]{1,0:T(8,128)(2,1)}) custom-call(bf16[2,320,1024]{2,1,0:T(8,128)(2,1)S(1)} %copy-done.1, bf16[2048,1536]{1,0:T(8,128)(2,1)} %bitcast.46), custom_call_target="tpu_custom_call" | custom-call | tf_op jit(solution)/shard_map/pallas_call | solution.py:106
  123.1 0.8 copy-done.5
  123.9 3.4 %collective-permute-start = (bf16[160,1536]{1,0:T(8,128)(2,1)}, bf16[160,1536]{1,0:T(8,128)(2,1)S(1)}, u32[]{:S(2)}, u32[]{:S(2)}) collective-permute-start(bf16[160,1536]{1,0:T(8,128)(2,1)} %get-tuple-element.35), channel_id=1, source_target_pairs={{0,16},{16,32},{32,48},{48,0},{1,17},{17,33},{33,49},{49,1},{2,18}... | collective-permute-start | bytes 1474568 | tf_op jit(solution)/shard_map/ppermute | solution.py:168
  127.4 4.8 %collective-permute-start.1 = (bf16[160,1536]{1,0:T(8,128)(2,1)}, bf16[160,1536]{1,0:T(8,128)(2,1)}, u32[]{:S(2)}, u32[]{:S(2)}) collective-permute-start(bf16[160,1536]{1,0:T(8,128)(2,1)} %get-tuple-element.36), channel_id=1, source_target_pairs={{0,32},{16,48},{32,0},{48,16},{1,33},{17,49},{33,1},{49,17},{2,34}... | collective-permute-start | bytes 1474568 | tf_op jit(solution)/shard_map/ppermute | solution.py:168
  132.1 3.4 %collective-permute-start.2 = (bf16[160,1536]{1,0:T(8,128)(2,1)}, bf16[160,1536]{1,0:T(8,128)(2,1)}, u32[]{:S(2)}, u32[]{:S(2)}) collective-permute-start(bf16[160,1536]{1,0:T(8,128)(2,1)} %get-tuple-element.37), channel_id=1, source_target_pairs={{0,48},{16,0},{32,16},{48,32},{1,49},{17,1},{33,17},{49,33},{2,50}... | collective-permute-start | bytes 1474568 | tf_op jit(solution)/shard_map/ppermute | solution.py:168
  135.6 0.2 copy.30.weight_ref
  135.8 17.7 %all-to-all-done.2 = bf16[64,8,640]{2,1,0:T(8,128)(2,1)} async-done(((bf16[64,8,640]{2,1,0:T(8,128)(2,1)}), bf16[64,8,640]{2,1,0:T(8,128)(2,1)}, u32[]{:S(2)}, u32[]{:S(2)}) %all-to-all-start.2) | async-done | bytes 655392 | tf_op jit(solution)/shard_map/all_to_all | solution.py:174
  153.5 1.7 reshape.65.direct_ref
  155.2 0.8 copy-done.7
  156.0 0.5 collective-permute-done.1.refs_2_
  156.5 0.9 collective-permute-done.2.refs_3_
  157.4 1.0 copy-done.4
  158.4 1.0 copy-done.6
  159.4 1.0 copy-done.8
  160.5 9.2 %shard_map.115 = (bf16[640,1536]{1,0:T(8,128)(2,1)}, bf16[640,384]{1,0:T(8,128)(2,1)}, bf16[640,768]{1,0:T(8,128)(2,1)}, bf16[640,512]{1,0:T(8,128)(2,1)S(1)}, b...) custom-call(s32[1]{0:T(128)} %bitcast.y_ref, ...), custom_call_target="tpu_custom_call" | custom-call | tf_op jit(solution)/shard_map/pallas_call | solution.py:144
  169.7 0.8 copy-done.2
  170.5 0.8 copy-done.13
  171.3 0.8 copy-done.14
  172.1 0.9 copy-done.15
  172.9 1.5 reshape.66
  174.4 14.4 %all-to-all-start.3 = ((bf16[64,8,640]{2,1,0:T(8,128)(2,1)}), bf16[64,8,640]{2,1,0:T(8,128)(2,1)S(1)}, u32[]{:S(2)}, u32[]{:S(2)}) async-start(bf16[64,8,640]{2,1,0:T(8,128)(2,1)} %reshape.66), calls=%async_computation.3 | async-start | bytes 1310720 | tf_op jit(solution)/shard_map/all_to_all | solution.py:174
  188.9 4.9 %collective-permute-start.3 = (bf16[160,1536]{1,0:T(8,128)(2,1)}, bf16[160,1536]{1,0:T(8,128)(2,1)S(1)}, u32[]{:S(2)}, u32[]{:S(2)}) collective-permute-start(bf16[160,1536]{1,0:T(8,128)(2,1)} %copy-done.15), channel_id=1, source_target_pairs={{0,48},{16,0},{32,16},{48,32},{1,49},{17,1},{33,17},{49,33},{2,50}... | collective-permute-start | bytes 1474568 | tf_op jit(solution)/shard_map/ppermute | solution.py:168
  193.8 2.6 collective-permute-start.4
  196.3 2.9 collective-permute-start.5
  199.2 26.9 %all-to-all-done.3 = bf16[64,8,640]{2,1,0:T(8,128)(2,1)S(1)} async-done(((bf16[64,8,640]{2,1,0:T(8,128)(2,1)}), bf16[64,8,640]{2,1,0:T(8,128)(2,1)S(1)}, u32[]{:S(2)}, u32[]{:S(2)}) %all-to-all-start.3) | async-done | bytes 655392 | tf_op jit(solution)/shard_map/all_to_all | solution.py:174
  226.1 1.5 reshape.67
  227.6 1.0 copy-done.3
  228.6 6.4 %shard_map.116 = bf16[2048,1536]{1,0:T(8,128)(2,1)} custom-call(bf16[2,1024,320]{2,1,0:T(8,128)(2,1)S(1)} %get-tuple-element.31.select_ref, bf16[160,1536]{1,0:T(8,128)(2,1)S(1)} %copy-done.3, bf16[160,1536]{1,0:T(8,128)(2,1)S(1)} %collective-permute-done.3.refs_1_, bf16[160,1536]{1,0:T(8,128)(2,1)} %collective-permute-done.4.refs_2_, ...), custom_call_target="tpu_custom_call" | custom-call | tf_op jit(solution)/shard_map/pallas_call | solution.py:106
  235.0 1.2 copy-done.16
  236.2 0.8 convolution_convert_fusion.1
  237.0 3.6 %convolution_convert_fusion = bf16[1536,768]{1,0:T(8,128)(2,1)S(1)} fusion(bf16[640,1536]{1,0:T(8,128)(2,1)} %get-tuple-element.53, bf16[640,768]{1,0:T(8,128)(2,1)S(1)} %copy-done.16), kind=kOutput, calls=%fused_computation.1 | convolution fusion | flops 1511129088 | bytes 5308416 | tf_op jit(solution)/shard_map/dot_general | solution.py:44
  240.6 1.9 pad_maximum_fusion
  242.5 4.8 %all-to-all-start.4 = ((bf16[8,256,768]{2,1,0:T(8,128)(2,1)}), bf16[8,256,768]{2,1,0:T(8,128)(2,1)S(1)}, u32[]{:S(2)}, u32[]{:S(2)}) async-start(bf16[8,256,768]{2,1,0:T(8,128)(2,1)} %bitcast.19), calls=%async_computation.5 | async-start | bytes 6291456 | tf_op jit(solution)/shard_map/all_to_all | solution.py:255
  247.3 2.1 fusion.4
  249.5 34.2 %all-to-all-done.4 = bf16[8,256,768]{2,1,0:T(8,128)(2,1)S(1)} async-done(((bf16[8,256,768]{2,1,0:T(8,128)(2,1)}), bf16[8,256,768]{2,1,0:T(8,128)(2,1)S(1)}, u32[]{:S(2)}, u32[]{:S(2)}) %all-to-all-start.4) | async-done | bytes 3145760 | tf_op jit(solution)/shard_map/all_to_all | solution.py:255
  283.7 0.4 convert_reduce_fusion
  284.1 0.9 slice_bitcast_fusion
  285.0 34.0 %reduce-scatter.2.cloned.1.call-done = bf16[128,1536]{1,0:T(8,128)(2,1)} async-done(((bf16[2048,1536]{1,0:T(8,128)(2,1)}), bf16[128,1536]{1,0:T(8,128)(2,1)}) %reduce-scatter.2.cloned.1.call-update) | async-done | bytes 393232 | tf_op jit(solution)/shard_map/reduce_scatter | solution.py:244
  319.1 1.1 convert_element_type.26
  320.2 2.0 maximum_bitcast_fusion
  (34 shorter events, 0.3 us)
Async XLA Ops:
  7.2 97.6 %all-gather.3.cloned.1.call-start = ((), (), s32[]{:S(2)}) async-start(), calls=%async_computation.7 | async-start | bytes 6684672 | tf_op jit(solution)/shard_map/all_gather | solution.py:176
  9.0 0.7 copy-start.11
  9.7 0.7 copy-start.12
  11.5 35.7 %all-to-all-start = ((bf16[64,8,128]{2,1,0:T(8,128)(2,1)}), bf16[64,8,128]{2,1,0:T(8,128)(2,1)S(1)}, u32[]{:S(2)}, u32[]{:S(2)}) async-start(bf16[64,8,128]{2,1,0:T(8,128)(2,1)} %bitcast.6), calls=%async_computation | async-start | bytes 262144 | tf_op jit(solution)/shard_map/all_to_all | solution.py:180
  49.2 6.8 %copy-start.9 = (s32[640,1]{1,0:T(8,128)S(1)}, s32[640,1]{1,0:T(8,128)}, u32[]{:S(2)}) copy-start(s32[640,1]{1,0:T(8,128)} %constant.28.clone.expert_ref) | copy-start | bytes 7684
  49.2 6.8 %copy-start.10 = (s32[640,1]{1,0:T(8,128)S(1)}, s32[640,1]{1,0:T(8,128)}, u32[]{:S(2)}) copy-start(s32[640,1]{1,0:T(8,128)} %constant.29.clone.place_ref) | copy-start | bytes 7684
  49.2 41.4 %all-to-all-start.1 = ((bf16[8,256,768]{2,1,0:T(8,128)(2,1)}), bf16[8,256,768]{2,1,0:T(8,128)(2,1)}, u32[]{:S(2)}, u32[]{:S(2)}) async-start(bf16[8,256,768]{2,1,0:T(8,128)(2,1)} %broadcast_in_dim.46), calls=%async_computation.1 | async-start | bytes 6291456 | tf_op jit(solution)/shard_map/all_to_all | solution.py:212
  60.9 1.1 copy-start
  104.7 48.8 %all-to-all-start.2 = ((bf16[64,8,640]{2,1,0:T(8,128)(2,1)}), bf16[64,8,640]{2,1,0:T(8,128)(2,1)}, u32[]{:S(2)}, u32[]{:S(2)}) async-start(bf16[64,8,640]{2,1,0:T(8,128)(2,1)} %reshape.62), calls=%async_computation.2 | async-start | bytes 1310720 | tf_op jit(solution)/shard_map/all_to_all | solution.py:174
  115.9 1.3 copy-start.1
  123.1 0.8 copy-start.5
  123.9 31.3 %collective-permute-start = (bf16[160,1536]{1,0:T(8,128)(2,1)}, bf16[160,1536]{1,0:T(8,128)(2,1)S(1)}, u32[]{:S(2)}, u32[]{:S(2)}) collective-permute-start(bf16[160,1536]{1,0:T(8,128)(2,1)} %get-tuple-element.35), channel_id=1, source_target_pairs={{0,16},{16,32},{32,48},{48,0},{1,17},{17,33},{33,49},{49,1},{2,18}... | collective-permute-start | bytes 1474568 | tf_op jit(solution)/shard_map/ppermute | solution.py:168
  127.4 29.1 %collective-permute-start.1 = (bf16[160,1536]{1,0:T(8,128)(2,1)}, bf16[160,1536]{1,0:T(8,128)(2,1)}, u32[]{:S(2)}, u32[]{:S(2)}) collective-permute-start(bf16[160,1536]{1,0:T(8,128)(2,1)} %get-tuple-element.36), channel_id=1, source_target_pairs={{0,32},{16,48},{32,0},{48,16},{1,33},{17,49},{33,1},{49,17},{2,34}... | collective-permute-start | bytes 1474568 | tf_op jit(solution)/shard_map/ppermute | solution.py:168
  132.1 25.2 %collective-permute-start.2 = (bf16[160,1536]{1,0:T(8,128)(2,1)}, bf16[160,1536]{1,0:T(8,128)(2,1)}, u32[]{:S(2)}, u32[]{:S(2)}) collective-permute-start(bf16[160,1536]{1,0:T(8,128)(2,1)} %get-tuple-element.37), channel_id=1, source_target_pairs={{0,48},{16,0},{32,16},{48,32},{1,49},{17,1},{33,17},{49,33},{2,50}... | collective-permute-start | bytes 1474568 | tf_op jit(solution)/shard_map/ppermute | solution.py:168
  155.2 0.8 copy-start.7
  157.4 1.0 copy-start.4
  158.4 1.0 copy-start.6
  159.4 1.0 copy-start.8
  169.7 0.8 copy-start.2
  170.5 0.8 copy-start.13
  171.3 0.8 copy-start.14
  172.1 0.9 copy-start.15
  174.4 51.7 %all-to-all-start.3 = ((bf16[64,8,640]{2,1,0:T(8,128)(2,1)}), bf16[64,8,640]{2,1,0:T(8,128)(2,1)S(1)}, u32[]{:S(2)}, u32[]{:S(2)}) async-start(bf16[64,8,640]{2,1,0:T(8,128)(2,1)} %reshape.66), calls=%async_computation.3 | async-start | bytes 1310720 | tf_op jit(solution)/shard_map/all_to_all | solution.py:174
  188.8 130.3 %reduce-scatter.2.cloned.1.call-start = ((), (), s32[]{:S(2)}) async-start(), calls=%async_computation.6 | async-start | bytes 6684672 | tf_op jit(solution)/shard_map/reduce_scatter | solution.py:244
  188.9 38.7 %collective-permute-start.3 = (bf16[160,1536]{1,0:T(8,128)(2,1)}, bf16[160,1536]{1,0:T(8,128)(2,1)S(1)}, u32[]{:S(2)}, u32[]{:S(2)}) collective-permute-start(bf16[160,1536]{1,0:T(8,128)(2,1)} %copy-done.15), channel_id=1, source_target_pairs={{0,48},{16,0},{32,16},{48,32},{1,49},{17,1},{33,17},{49,33},{2,50}... | collective-permute-start | bytes 1474568 | tf_op jit(solution)/shard_map/ppermute | solution.py:168
  193.8 33.8 %collective-permute-start.4 = (bf16[160,1536]{1,0:T(8,128)(2,1)}, bf16[160,1536]{1,0:T(8,128)(2,1)}, u32[]{:S(2)}, u32[]{:S(2)}) collective-permute-start(bf16[160,1536]{1,0:T(8,128)(2,1)} %copy-done.14), channel_id=1, source_target_pairs={{0,32},{16,48},{32,0},{48,16},{1,33},{17,49},{33,1},{49,17},{2,34}... | collective-permute-start | bytes 1474568 | tf_op jit(solution)/shard_map/ppermute | solution.py:168
  196.3 31.2 %collective-permute-start.5 = (bf16[160,1536]{1,0:T(8,128)(2,1)}, bf16[160,1536]{1,0:T(8,128)(2,1)}, u32[]{:S(2)}, u32[]{:S(2)}) collective-permute-start(bf16[160,1536]{1,0:T(8,128)(2,1)} %copy-done.13), channel_id=1, source_target_pairs={{0,16},{16,32},{32,48},{48,0},{1,17},{17,33},{33,49},{49,1},{2,18}... | collective-permute-start | bytes 1474568 | tf_op jit(solution)/shard_map/ppermute | solution.py:168
  227.6 1.0 copy-start.3
  235.0 1.2 copy-start.16
  242.5 41.2 %all-to-all-start.4 = ((bf16[8,256,768]{2,1,0:T(8,128)(2,1)}), bf16[8,256,768]{2,1,0:T(8,128)(2,1)S(1)}, u32[]{:S(2)}, u32[]{:S(2)}) async-start(bf16[8,256,768]{2,1,0:T(8,128)(2,1)} %bitcast.19), calls=%async_computation.5 | async-start | bytes 6291456 | tf_op jit(solution)/shard_map/all_to_all | solution.py:255
Sparse Core Ops, SparseCore 0:
  10.7 94.0 all-gather.2
  235.2 83.8 reduce-scatter.1

commit v10 on v8

--- a/solution.py
+++ b/solution.py
@@ -11,7 +11,8 @@
 LINES = 8
 QUARTERS = 4
 LANES = 128
-VMEM_BYTES = 48 * 1024 * 1024
+PARTS = 2
+PARAMS = pltpu.CompilerParams(vmem_limit_bytes=48 * 1024 * 1024)
 F32 = jnp.float32
 BF16 = jnp.bfloat16
 
@@ -23,12 +24,16 @@
         out_shape=out_shape,
         in_specs=[whole] * len(operands),
         out_specs=jax.tree.map(lambda _: whole, out_shape),
-        compiler_params=pltpu.CompilerParams(vmem_limit_bytes=VMEM_BYTES),
+        compiler_params=PARAMS,
     )(*operands)
 
 
 def array(shape, dtype=BF16):
     return jax.ShapeDtypeStruct(shape, dtype)
+
+
+def hbm(shape):
+    return pltpu.HBM(shape, BF16)
 
 
 def iota(shape, dimension):
@@ -48,7 +53,15 @@
     return jnp.where((line & (QUARTERS - 1)) == quarter, select, jnp.zeros_like(select))
 
 
-def source_kernel(ids_ref, weights_ref, tokens_ref, out_ref, main_ref, extra_ref):
+def source_kernel(
+    ids_in, weights_in, tokens_in, out_ref, main_ref, extra_ref, ids_ref, weights_ref, tokens_ref, fetched
+):
+    pairs = ((ids_in, ids_ref), (weights_in, weights_ref), (tokens_in, tokens_ref))
+    copies = [pltpu.make_async_copy(here, there, fetched.at[i]) for i, (here, there) in enumerate(pairs)]
+    for copy in copies:
+        copy.start()
+    for copy in copies[:2]:
+        copy.wait()
     tokens, width = tokens_ref.shape
     step = width // QUARTERS
     shape = (out_ref.shape[0], tokens)
@@ -68,6 +81,7 @@
     main, extra = one_hot(is_main), one_hot(is_extra)
     main_ref[...] = main
     extra_ref[...] = extra
+    copies[2].wait()
     out_ref[:, :width] = dot(main, tokens_ref[...]).astype(BF16)
     beside = dot(of_quarter(extra, 0), tokens_ref[:, :step])
     for quarter in range(1, QUARTERS):
@@ -99,7 +113,7 @@
 
 
 def expert_kernel(
-    blocks_ref, matrix_ref, cotangent_ref, row_ref, hidden_ref, grad_ref, extra_ref, back_ref
+    blocks_ref, matrix_ref, cotangent_ref, row_ref, hidden_ref, main_grad_ref, extra_grad_ref, extra_ref, back_ref
 ):
     lines, extras = blocks_ref.shape[0], extra_ref.shape[0]
     width = matrix_ref.shape[0]
@@ -114,19 +128,21 @@
     extra_weight = dot(places[0], weights)[:, 1:2]
     weight = jnp.concatenate((main_weight, extra_weight), axis=0) * 0.125
 
-    pre = jnp.concatenate(
-        (dot(blocks_ref[:, :width], matrix_ref[...]), dot(extra_ref[...], matrix_ref[...])), axis=0
-    )
+    pre = dot(jnp.concatenate((blocks_ref[:, :width], extra_ref[...]), axis=0), matrix_ref[...])
     gate_pre, up_pre = pre[:, :units], pre[:, units:]
     sigmoid_gate = jax.nn.sigmoid(gate_pre)
     activation = gate_pre * sigmoid_gate
     hidden = (activation * up_pre * weight).astype(BF16)
     act_slope = sigmoid_gate * (1.0 + gate_pre * (1.0 - sigmoid_gate))
     scaled = cotangent_ref[...].astype(F32) * weight
-    grad_ref[:, :units] = (scaled * up_pre * act_slope).astype(BF16)
-    grad_ref[:, units:] = (scaled * activation).astype(BF16)
-    back_ref[:, :width] = dot(grad_ref[:lines, :], matrix_ref[...], (1, 1)).astype(BF16)
-    extra_back = dot(grad_ref[lines:, :], matrix_ref[...], (1, 1)).astype(BF16)
+    grad_gate = (scaled * up_pre * act_slope).astype(BF16)
+    grad_up = (scaled * activation).astype(BF16)
+    grads = jnp.concatenate((grad_gate, grad_up), axis=1)
+    main_grad_ref[...] = grads[:lines]
+    extra_grad_ref[...] = grads[lines:]
+    back = dot(grads, matrix_ref[...], (1, 1)).astype(BF16)
+    back_ref[:, :width] = back[:lines]
+    extra_back = back[lines:]
     beside = dot(places[0], extra_back[:, :step], (0, 0))
     for quarter in range(1, QUARTERS):
         beside = beside + dot(places[quarter], extra_back[:, quarter * step : (quarter + 1) * step], (0, 0))
@@ -156,37 +172,61 @@
         parts = blocks.reshape(experts, LINES, blocks.shape[1])
         return lax.all_to_all(parts, "expert", 0, 0, tiled=True).reshape(blocks.shape)
 
-    outgoing, main, extra = call(
+    sources = (expert_ids[0].T, route_weights[0].T, tokens[0])
+    vmem = pl.BlockSpec(memory_space=pltpu.VMEM)
+    out_blocks = ((lines, width + step + LANES), (lines, block), (lines, block))
+    outgoing, main, extra = pl.pallas_call(
         source_kernel,
-        (array((lines, width + step + LANES)), array((lines, block)), array((lines, block))),
-        expert_ids[0].T,
-        route_weights[0].T,
-        tokens[0],
-    )
+        grid=(1,),
+        out_shape=(hbm((lines, width + step + LANES)), hbm((lines, block)), hbm((lines, block))),
+        in_specs=[pl.BlockSpec(memory_space=pltpu.HBM)] * 3,
+        out_specs=tuple(pl.BlockSpec(shape, lambda step: (0, 0)) for shape in out_blocks),
+        scratch_shapes=[pltpu.VMEM(value.shape, value.dtype) for value in sources]
+        + [pltpu.SemaphoreType.DMA((3,))],
+        compiler_params=PARAMS,
+    )(*[pltpu.with_memory_space_constraint(value, pltpu.HBM) for value in sources])
     arrived = exchange(outgoing)
 
     stacked = jnp.concatenate((gate_weight[0], up_weight[0]), axis=1)
     matrix = lax.all_gather(stacked, "dp", axis=0, tiled=True)
-    order = order_of(experts)
+    part_slots, part_lines, part_extras = slot_count // PARTS, lines // PARTS, extras // PARTS
+    order = order_of(experts // PARTS)
+    rows_of = np.concatenate([order + part * part_slots for part in range(PARTS)])
     cotangent_rows = call(
-        reorder_kernel, array((slot_count, units)), jnp.asarray(order[:, None]), cotangent[0, 0]
-    )
-    hidden, grads, extra_rows, back = call(
+        reorder_kernel, array((slot_count, units)), jnp.asarray(rows_of[:, None]), cotangent[0, 0]
+    )
+
+    def part_of(rows, columns):
+        return pl.BlockSpec((rows, columns), lambda part: (part, 0))
+
+    hidden, main_grads, extra_grads, extra_rows, back = pl.pallas_call(
         expert_kernel,
-        (
+        grid=(PARTS,),
+        out_shape=(
             array((slot_count, units)),
-            array((slot_count, 2 * units)),
-            array((extras, width)),
-            array((lines, width + step)),
+            hbm((lines, 2 * units)),
+            hbm((extras, 2 * units)),
+            hbm((extras, width)),
+            hbm((lines, width + step)),
         ),
-        arrived,
-        matrix,
-        cotangent_rows,
-        jnp.asarray(np.argsort(order).astype(np.int32)[:, None]),
-    )
+        in_specs=[
+            part_of(part_lines, width + step + LANES),
+            vmem,
+            part_of(part_slots, units),
+            vmem,
+        ],
+        out_specs=(
+            part_of(part_slots, units),
+            part_of(part_lines, 2 * units),
+            part_of(part_extras, 2 * units),
+            part_of(part_extras, width),
+            part_of(part_lines, width + step),
+        ),
+        compiler_params=PARAMS,
+    )(arrived, matrix, cotangent_rows, jnp.asarray(np.argsort(order).astype(np.int32)[:, None]))
     token_grads = call(token_kernel, array((block, width), F32), main, extra, exchange(back))
 
-    terms = dot(arrived[:, :width], grads[:lines], (0, 0)) + dot(extra_rows, grads[lines:], (0, 0))
+    terms = dot(arrived[:, :width], main_grads, (0, 0)) + dot(extra_rows, extra_grads, (0, 0))
     weight_grads = lax.psum_scatter(terms.astype(BF16), "dp", scatter_dimension=0, tiled=True).astype(F32)
     return (
         hidden[None, None],

time: 308 us -> 306 us (level)
    pallas_call x0 -> x2, Pallas kernels: none -> 14.5 us  [the longest x1 10.4 us: shards(): pl.pallas_call(expert_kernel, grid=(PARTS,), out_shape=(array((slot_count...]
    pallas_call x4 -> x2, Pallas kernels: 15.8 us -> 4.19 us  [call(): pl.pallas_call(kernel, out_shape=out_shape, in_specs=[whole] * len(operan...]
  transfers between devices with their start and end apart: 4 -> 4, of which waited for: 4 -> 4; matrix products, arithmetic and copies ran while one was open for 3% -> 2% of each run, Pallas kernels for 0% -> 0%
where the time goes in v10:
time: 306 us; the launch traced here: 305 us
  waiting for transfers between devices  237 us (77%)
  starting transfers between devices  26.4 us (9%)
  Pallas kernels  18.7 us (6%)
  between operations  14.2 us (5%)
  matrix products  4.5 us (1%)
    all_to_all x2, waiting for transfers between devices, exchange(): lax.all_to_all(parts, 'expert', 0, 0, tiled=True).reshape(blocks.shape)  160 us
    reduce_scatter x1, waiting for transfers between devices, shards(): lax.psum_scatter(terms.astype(BF16), 'dp', scatter_dimension=0, tiled=True)  41.9 us
    all_gather x1, waiting for transfers between devices, shards(): matrix = lax.all_gather(stacked, 'dp', axis=0, tiled=True)  35.1 us
    all_to_all x2, starting transfers between devices, exchange(): lax.all_to_all(parts, 'expert', 0, 0, tiled=True).reshape(blocks.shape)  26.3 us
    pallas_call x1, Pallas kernels, shards(): pl.pallas_call(expert_kernel, grid=(PARTS,), out_shape=(array((slot_count...  10.4 us
  transfers between devices with their start and end apart: 4, of which 4 were waited for; matrix products, arithmetic and copies ran while one was open for 2% of the time, Pallas kernels for 0%

profile of v10, /device:TPU:6, one launch (start us, length us, event | category | flops | bytes accessed | tf_op | source)
XLA Modules:
  0.0 305.3 jit_solution(9876152431711620796)
XLA Ops:
  7.2 0.0 copy-start.7
  7.2 0.0 copy-start.8
  7.2 4.1 %shard_map.111 = (bf16[512,2688]{1,0:T(8,128)(2,1)}, bf16[512,128]{1,0:T(8,128)(2,1)}, bf16[512,128]{1,0:T(8,128)(2,1)}) custom-call(s32[8,128]{1,0:T(8,128)} %bitcast.32, s32[8,128]{1,0:T(8,128)} %bitcast.33, bf16[128,2048]{1,0:T(8,128)(2,1)} %bitcast.29), custom_call_target="tpu_custom_call" | custom-call | tf_op jit(solution)/shard_map/pallas_call | solution.py:178
  11.3 0.0 copy-start.2
  11.3 18.9 %all-to-all-start = ((bf16[64,8,2688]{2,1,0:T(8,128)(2,1)}), bf16[64,8,2688]{2,1,0:T(8,128)(2,1)S(1)}, u32[]{:S(2)}, u32[]{:S(2)}) async-start(bf16[64,8,2688]{2,1,0:T(8,128)(2,1)} %bitcast.26), calls=%async_computation | async-start | bytes 5505024 | tf_op jit(solution)/shard_map/all_to_all | solution.py:173
  30.2 0.0 all-gather.2.cloned.1.call-start
  30.3 0.0 copy-done.7
  30.3 0.0 copy-done.8
  30.3 0.8 pad_maximum_fusion
  31.1 0.0 all-gather.2.cloned.1.call-update
  31.1 0.0 copy-start
  31.1 1.0 copy-done
  32.1 0.0 copy-start.1
  32.1 1.0 copy-done.1
  33.1 0.7 shard_map.112.cotangent_ref
  33.8 35.1 %all-gather.2.cloned.1.call-done.matrix_ref = bf16[2048,768]{1,0:T(8,128)(2,1)} async-done(((bf16[256,768]{1,0:T(8,128)(2,1)}), bf16[2048,768]{1,0:T(8,128)(2,1)}) %all-gather.2.cloned.1.call-update) | async-done | bytes 3145744 | tf_op jit(solution)/shard_map/all_gather | solution.py:191
  68.9 87.9 %all-to-all-done = bf16[64,8,2688]{2,1,0:T(8,128)(2,1)S(1)} async-done(((bf16[64,8,2688]{2,1,0:T(8,128)(2,1)}), bf16[64,8,2688]{2,1,0:T(8,128)(2,1)S(1)}, u32[]{:S(2)}, u32[]{:S(2)}) %all-to-all-start) | async-done | bytes 2752544 | tf_op jit(solution)/shard_map/all_to_all | solution.py:173
  156.8 0.0 copy-done.2
  156.8 10.4 %shard_map.113 = (bf16[640,384]{1,0:T(8,128)(2,1)}, bf16[512,768]{1,0:T(8,128)(2,1)}, bf16[128,768]{1,0:T(8,128)(2,1)}, bf16[128,2048]{1,0:T(8,128)(2,1)}, bf16[512,2560]{1,0:T(8,128)(2,1)}) custom-call(bf16[512,2688]{1,0:T(8,128)(2,1)S(1)} %bitcast.23, bf16[2048,768]{1,0:T(8,128)(2,1)} %all-gather.2.cloned.1.call-done.matrix_ref, ...), custom_call_target="tpu_custom_call" | custom-call | tf_op jit(solution)/shard_map/pallas_call | solution.py:202
  167.2 0.0 copy-start.5
  167.2 7.4 %all-to-all-start.1 = ((bf16[64,8,2560]{2,1,0:T(8,128)(2,1)}), bf16[64,8,2560]{2,1,0:T(8,128)(2,1)}, u32[]{:S(2)}, u32[]{:S(2)}) async-start(bf16[64,8,2560]{2,1,0:T(8,128)(2,1)} %bitcast.27), calls=%async_computation.1 | async-start | bytes 5242880 | tf_op jit(solution)/shard_map/all_to_all | solution.py:173
  174.6 0.0 reduce-scatter.2.cloned.1.call-start
  174.7 0.0 copy-done.5
  174.7 0.0 copy-start.6
  174.7 0.0 copy-start.9
  174.7 1.8 fusion
  176.6 0.0 copy-done.6
  176.6 0.0 copy-done.9
  176.6 2.7 add_convert_fusion
  179.3 0.0 copy-start.3
  179.3 0.0 copy-start.4
  179.3 0.0 reduce-scatter.2.cloned.1.call-update
  179.3 41.9 %reduce-scatter.2.cloned.1.call-done = bf16[256,768]{1,0:T(8,128)(2,1)} async-done(((bf16[2048,768]{1,0:T(8,128)(2,1)}), bf16[256,768]{1,0:T(8,128)(2,1)}) %reduce-scatter.2.cloned.1.call-update) | async-done | bytes 393232 | tf_op jit(solution)/shard_map/reduce_scatter | solution.py:230
  221.2 1.0 convert_element_type.7
  222.2 0.9 slice_bitcast_fusion
  223.1 71.9 %all-to-all-done.1 = bf16[64,8,2560]{2,1,0:T(8,128)(2,1)} async-done(((bf16[64,8,2560]{2,1,0:T(8,128)(2,1)}), bf16[64,8,2560]{2,1,0:T(8,128)(2,1)}, u32[]{:S(2)}, u32[]{:S(2)}) %all-to-all-start.1) | async-done | bytes 2621472 | tf_op jit(solution)/shard_map/all_to_all | solution.py:173
  295.0 0.0 copy-done.3
  295.0 0.0 copy-done.4
  295.0 3.4 %shard_map.114 = f32[128,2048]{1,0:T(8,128)} custom-call(bf16[512,128]{1,0:T(8,128)(2,1)S(1)} %copy-done.3, bf16[512,128]{1,0:T(8,128)(2,1)S(1)} %copy-done.4, bf16[512,2560]{1,0:T(8,128)(2,1)} %bitcast.12.blocks_ref), custom_call_target="tpu_custom_call" | custom-call | tf_op jit(solution)/shard_map/pallas_call | solution.py:22
Async XLA Ops:
  7.2 23.1 %copy-start.7 = (bf16[1,256,384]{2,1,0:T(8,128)(2,1)S(1)}, bf16[1,256,384]{2,1,0:T(8,128)(2,1)}, u32[]{:S(2)}) copy-start(bf16[1,256,384]{2,1,0:T(8,128)(2,1)} %param.12) | copy-start | bytes 589828
  7.2 23.1 %copy-start.8 = (bf16[1,256,384]{2,1,0:T(8,128)(2,1)S(1)}, bf16[1,256,384]{2,1,0:T(8,128)(2,1)}, u32[]{:S(2)}) copy-start(bf16[1,256,384]{2,1,0:T(8,128)(2,1)} %param.11) | copy-start | bytes 589828
  11.3 145.5 %copy-start.2 = (s32[320,1]{1,0:T(8,128)S(1)}, s32[320,1]{1,0:T(8,128)}, u32[]{:S(2)}) copy-start(s32[320,1]{1,0:T(8,128)} %constant.5.clone.row_ref) | copy-start | bytes 3844
  11.3 145.5 %all-to-all-start = ((bf16[64,8,2688]{2,1,0:T(8,128)(2,1)}), bf16[64,8,2688]{2,1,0:T(8,128)(2,1)S(1)}, u32[]{:S(2)}, u32[]{:S(2)}) async-start(bf16[64,8,2688]{2,1,0:T(8,128)(2,1)} %bitcast.26), calls=%async_computation | async-start | bytes 5505024 | tf_op jit(solution)/shard_map/all_to_all | solution.py:173
  30.2 38.7 %all-gather.2.cloned.1.call-start = ((), (), s32[]{:S(2)}) async-start(), calls=%async_computation.3 | async-start | bytes 3538944 | tf_op jit(solution)/shard_map/all_gather | solution.py:191
  31.1 1.0 copy-start
  32.1 1.0 copy-start.1
  167.2 7.5 %copy-start.5 = (bf16[512,768]{1,0:T(8,128)(2,1)S(1)}, bf16[512,768]{1,0:T(8,128)(2,1)}, u32[]{:S(2)}) copy-start(bf16[512,768]{1,0:T(8,128)(2,1)} %get-tuple-element.17) | copy-start | bytes 2359300
  167.2 127.8 %all-to-all-start.1 = ((bf16[64,8,2560]{2,1,0:T(8,128)(2,1)}), bf16[64,8,2560]{2,1,0:T(8,128)(2,1)}, u32[]{:S(2)}, u32[]{:S(2)}) async-start(bf16[64,8,2560]{2,1,0:T(8,128)(2,1)} %bitcast.27), calls=%async_computation.1 | async-start | bytes 5242880 | tf_op jit(solution)/shard_map/all_to_all | solution.py:173
  174.6 46.5 %reduce-scatter.2.cloned.1.call-start = ((), (), s32[]{:S(2)}) async-start(), calls=%async_computation.4 | async-start | bytes 3538944 | tf_op jit(solution)/shard_map/reduce_scatter | solution.py:230
  174.7 1.9 copy-start.6
  174.7 1.9 copy-start.9
  179.3 115.8 %copy-start.3 = (bf16[512,128]{1,0:T(8,128)(2,1)S(1)}, bf16[512,128]{1,0:T(8,128)(2,1)}, u32[]{:S(2)}) copy-start(bf16[512,128]{1,0:T(8,128)(2,1)} %get-tuple-element.14.main_ref) | copy-start | bytes 393220
  179.3 115.8 %copy-start.4 = (bf16[512,128]{1,0:T(8,128)(2,1)S(1)}, bf16[512,128]{1,0:T(8,128)(2,1)}, u32[]{:S(2)}) copy-start(bf16[512,128]{1,0:T(8,128)(2,1)} %get-tuple-element.15.extra_ref) | copy-start | bytes 393220
Sparse Core Ops, SparseCore 0:
  33.8 35.1 all-gather.1
  179.4 41.6 reduce-scatter.1

commit v11 on v10

--- a/solution.py
+++ b/solution.py
@@ -6,9 +6,11 @@
 from jax import lax
 from jax.experimental import pallas as pl
 from jax.experimental.pallas import tpu as pltpu
-from jax.sharding import PartitionSpec as P
+from jax.sharding import Mesh, PartitionSpec as P
 
 LINES = 8
+N_Y = 4
+N_Z = 16
 QUARTERS = 4
 LANES = 128
 PARTS = 2
@@ -54,7 +56,7 @@
 
 
 def source_kernel(
-    ids_in, weights_in, tokens_in, out_ref, main_ref, extra_ref, ids_ref, weights_ref, tokens_ref, fetched
+    ids_in, weights_in, tokens_in, out_ref, main_ref, extra_ref, table_ref, ids_ref, weights_ref, tokens_ref, fetched
 ):
     pairs = ((ids_in, ids_ref), (weights_in, weights_ref), (tokens_in, tokens_ref))
     copies = [pltpu.make_async_copy(here, there, fetched.at[i]) for i, (here, there) in enumerate(pairs)]
@@ -79,8 +81,8 @@
     is_main = rank == line
     is_extra = rank == LINES + line // QUARTERS
     main, extra = one_hot(is_main), one_hot(is_extra)
-    main_ref[...] = main
-    extra_ref[...] = extra
+    main_ref[...] = jnp.where(is_main, eighths * 0.125, 0.0).astype(BF16)
+    extra_ref[...] = jnp.where(is_extra, eighths * 0.125, 0.0).astype(BF16)
     copies[2].wait()
     out_ref[:, :width] = dot(main, tokens_ref[...]).astype(BF16)
     beside = dot(of_quarter(extra, 0), tokens_ref[:, :step])
@@ -89,9 +91,12 @@
     out_ref[:, width : width + step] = beside.astype(BF16)
     main_weight = jnp.sum(jnp.where(is_main, eighths, 0.0), axis=1, keepdims=True)
     extra_weight = jnp.sum(jnp.where(is_extra, eighths, 0.0), axis=1, keepdims=True)
-    lane = iota((shape[0], LANES), 1)
-    both = jnp.where(lane == 0, main_weight, jnp.where(lane == 1, extra_weight, 0.0))
-    out_ref[:, width + step :] = both.astype(BF16)
+    lane, line = iota((shape[0], LANES), 1), iota((shape[0], LANES), 0) & (LINES - 1)
+    is_second = (lane == LINES + line // QUARTERS) & ((line & (QUARTERS - 1)) == 0)
+    both = jnp.where(lane == line, main_weight, jnp.where(is_second, extra_weight, 0.0))
+    experts = table_ref.shape[0]
+    gather = one_hot(iota((experts, shape[0]), 1) // LINES == iota((experts, shape[0]), 0))
+    table_ref[...] = dot(gather, both.astype(BF16)).astype(BF16)
 
 
 def order_of(sources):
@@ -112,23 +117,45 @@
     return one_hot(iota((rows, lines), 1) == source * LINES + second * QUARTERS + quarter)
 
 
-def expert_kernel(
-    blocks_ref, matrix_ref, cotangent_ref, row_ref, hidden_ref, main_grad_ref, extra_grad_ref, extra_ref, back_ref
+def rows_of_blocks(blocks_ref, places, width):
+    step = width // QUARTERS
+    beside = blocks_ref[:, width:]
+    extra = jnp.concatenate([dot(place, beside).astype(BF16) for place in places], axis=1)
+    return jnp.concatenate((blocks_ref[:, :width], extra), axis=0)
+
+
+def places_of(lines):
+    return [lines_of(lines // QUARTERS, lines, quarter) for quarter in range(QUARTERS)]
+
+
+def back_kernel(blocks_ref, matrix_ref, cotangent_ref, back_ref):
+    lines, width = blocks_ref.shape[0], matrix_ref.shape[0]
+    step, units = width // QUARTERS, cotangent_ref.shape[1]
+    places = places_of(lines)
+    pre = dot(rows_of_blocks(blocks_ref, places, width), matrix_ref[...])
+    gate_pre, up_pre = pre[:, :units], pre[:, units:]
+    sigmoid_gate = jax.nn.sigmoid(gate_pre)
+    act_slope = sigmoid_gate * (1.0 + gate_pre * (1.0 - sigmoid_gate))
+    cotangent = cotangent_ref[...].astype(F32)
+    grad_gate = (cotangent * up_pre * act_slope).astype(BF16)
+    grad_up = (cotangent * (gate_pre * sigmoid_gate)).astype(BF16)
+    back = dot(jnp.concatenate((grad_gate, grad_up), axis=1), matrix_ref[...], (1, 1)).astype(BF16)
+    back_ref[:, :width] = back[:lines]
+    beside = dot(places[0], back[lines:, :step], (0, 0))
+    for quarter in range(1, QUARTERS):
+        beside = beside + dot(places[quarter], back[lines:, quarter * step : (quarter + 1) * step], (0, 0))
+    back_ref[:, width:] = beside.astype(BF16)
+
+
+def hidden_kernel(
+    blocks_ref, matrix_ref, cotangent_ref, weight_ref, row_ref, hidden_ref, main_grad_ref, extra_grad_ref, extra_ref
 ):
-    lines, extras = blocks_ref.shape[0], extra_ref.shape[0]
-    width = matrix_ref.shape[0]
-    step = width // QUARTERS
-    units = hidden_ref.shape[1]
-    places = [lines_of(extras, lines, quarter) for quarter in range(QUARTERS)]
-    beside = blocks_ref[:, width : width + step]
-    for quarter in range(QUARTERS):
-        extra_ref[:, quarter * step : (quarter + 1) * step] = dot(places[quarter], beside).astype(BF16)
-    weights = blocks_ref[:, width + step :]
-    main_weight = weights[:, 0:1].astype(F32)
-    extra_weight = dot(places[0], weights)[:, 1:2]
-    weight = jnp.concatenate((main_weight, extra_weight), axis=0) * 0.125
-
-    pre = dot(jnp.concatenate((blocks_ref[:, :width], extra_ref[...]), axis=0), matrix_ref[...])
+    lines, width = blocks_ref.shape[0], matrix_ref.shape[0]
+    units = cotangent_ref.shape[1]
+    rows = rows_of_blocks(blocks_ref, places_of(lines), width)
+    extra_ref[...] = rows[lines:]
+    pre = dot(rows, matrix_ref[...])
+    weight = weight_ref[...] * 0.125
     gate_pre, up_pre = pre[:, :units], pre[:, units:]
     sigmoid_gate = jax.nn.sigmoid(gate_pre)
     activation = gate_pre * sigmoid_gate
@@ -140,13 +167,6 @@
     grads = jnp.concatenate((grad_gate, grad_up), axis=1)
     main_grad_ref[...] = grads[:lines]
     extra_grad_ref[...] = grads[lines:]
-    back = dot(grads, matrix_ref[...], (1, 1)).astype(BF16)
-    back_ref[:, :width] = back[:lines]
-    extra_back = back[lines:]
-    beside = dot(places[0], extra_back[:, :step], (0, 0))
-    for quarter in range(1, QUARTERS):
-        beside = beside + dot(places[quarter], extra_back[:, quarter * step : (quarter + 1) * step], (0, 0))
-    back_ref[:, width:] = beside.astype(BF16)
     move = one_hot(iota((row_ref.shape[0], hidden.shape[0]), 1) == row_ref[...])
     hidden_ref[...] = dot(move, hidden).astype(BF16)
 
@@ -162,7 +182,7 @@
 
 
 def shards(tokens, expert_ids, route_weights, gate_weight, up_weight, cotangent):
-    experts = lax.axis_size("expert")
+    experts = N_Y * N_Z
     slot_count, units = cotangent.shape[2:]
     block, width = tokens.shape[1:]
     lines, extras = experts * LINES, experts * 2
@@ -170,15 +190,15 @@
 
     def exchange(blocks):
         parts = blocks.reshape(experts, LINES, blocks.shape[1])
-        return lax.all_to_all(parts, "expert", 0, 0, tiled=True).reshape(blocks.shape)
+        return lax.all_to_all(parts, ("y", "z"), 0, 0, tiled=True).reshape(blocks.shape)
 
     sources = (expert_ids[0].T, route_weights[0].T, tokens[0])
     vmem = pl.BlockSpec(memory_space=pltpu.VMEM)
-    out_blocks = ((lines, width + step + LANES), (lines, block), (lines, block))
-    outgoing, main, extra = pl.pallas_call(
+    out_blocks = ((lines, width + step), (lines, block), (lines, block), (experts, LANES))
+    outgoing, main, extra, table = pl.pallas_call(
         source_kernel,
         grid=(1,),
-        out_shape=(hbm((lines, width + step + LANES)), hbm((lines, block)), hbm((lines, block))),
+        out_shape=tuple(hbm(shape) for shape in out_blocks),
         in_specs=[pl.BlockSpec(memory_space=pltpu.HBM)] * 3,
         out_specs=tuple(pl.BlockSpec(shape, lambda step: (0, 0)) for shape in out_blocks),
         scratch_shapes=[pltpu.VMEM(value.shape, value.dtype) for value in sources]
@@ -199,20 +219,38 @@
     def part_of(rows, columns):
         return pl.BlockSpec((rows, columns), lambda part: (part, 0))
 
-    hidden, main_grads, extra_grads, extra_rows, back = pl.pallas_call(
-        expert_kernel,
+    tables = lax.all_gather(table, "z", axis=0).reshape(N_Z, N_Y, N_Z, LANES)
+    tables = lax.dynamic_index_in_dim(tables, lax.axis_index("z"), 2, keepdims=False)
+    tables = lax.all_gather(tables.reshape(N_Z * N_Y, LANES), "y", axis=0).reshape(experts, N_Y, LANES)
+    tables = lax.dynamic_index_in_dim(tables, lax.axis_index("y"), 1, keepdims=False).astype(F32)
+    first = tables[:, :LINES].reshape(PARTS, part_lines)
+    second = tables[:, LINES : LINES + 2].reshape(PARTS, experts // PARTS, 2).transpose(0, 2, 1)
+    weight_col = jnp.concatenate((first, second.reshape(PARTS, part_extras)), axis=1).reshape(slot_count, 1)
+    arrived, weight_col = lax.optimization_barrier((arrived, weight_col))
+    back = pl.pallas_call(
+        back_kernel,
+        grid=(PARTS,),
+        out_shape=hbm((lines, width + step)),
+        in_specs=[part_of(part_lines, width + step), vmem, part_of(part_slots, units)],
+        out_specs=part_of(part_lines, width + step),
+        compiler_params=PARAMS,
+    )(arrived, matrix, cotangent_rows)
+
+    arrived, _ = lax.optimization_barrier((arrived, back))
+    hidden, main_grads, extra_grads, extra_rows = pl.pallas_call(
+        hidden_kernel,
         grid=(PARTS,),
         out_shape=(
             array((slot_count, units)),
             hbm((lines, 2 * units)),
             hbm((extras, 2 * units)),
             hbm((extras, width)),
-            hbm((lines, width + step)),
         ),
         in_specs=[
-            part_of(part_lines, width + step + LANES),
+            part_of(part_lines, width + step),
             vmem,
             part_of(part_slots, units),
+            part_of(part_slots, 1),
             vmem,
         ],
         out_specs=(
@@ -220,10 +258,9 @@
             part_of(part_lines, 2 * units),
             part_of(part_extras, 2 * units),
             part_of(part_extras, width),
-            part_of(part_lines, width + step),
         ),
         compiler_params=PARAMS,
-    )(arrived, matrix, cotangent_rows, jnp.asarray(np.argsort(order).astype(np.int32)[:, None]))
+    )(arrived, matrix, cotangent_rows, weight_col, jnp.asarray(np.argsort(order).astype(np.int32)[:, None]))
     token_grads = call(token_kernel, array((block, width), F32), main, extra, exchange(back))
 
     terms = dot(arrived[:, :width], main_grads, (0, 0)) + dot(extra_rows, extra_grads, (0, 0))
@@ -237,18 +274,20 @@
 
 
 def solution(mesh):
+    grid = Mesh(mesh.devices.reshape(mesh.shape["dp"], N_Y, N_Z), ("dp", "y", "z"))
+    expert = ("y", "z")
     in_specs = (
-        P("dp", "expert", None),
-        P("dp", "expert", None),
-        P("dp", "expert", None),
-        P("expert", "dp", None),
-        P("expert", "dp", None),
-        P("dp", "expert", None, None),
+        P("dp", expert, None),
+        P("dp", expert, None),
+        P("dp", expert, None),
+        P(expert, "dp", None),
+        P(expert, "dp", None),
+        P("dp", expert, None, None),
     )
     out_specs = (
-        P("dp", "expert", None, None),
-        P("dp", "expert", None),
-        P("expert", "dp", None),
-        P("expert", "dp", None),
-    )
-    return jax.shard_map(shards, mesh=mesh, in_specs=in_specs, out_specs=out_specs, check_vma=False)
+        P("dp", expert, None, None),
+        P("dp", expert, None),
+        P(expert, "dp", None),
+        P(expert, "dp", None),
+    )
+    return jax.shard_map(shards, mesh=grid, in_specs=in_specs, out_specs=out_specs, check_vma=False)

time: 306 us -> 329 us (1.075)
  blocking collectives: 0 us -> 150 us
  waiting for transfers between devices: 237 us -> 92.3 us
  Pallas kernels: 18.7 us -> 25.6 us
  starting transfers between devices: 26.4 us -> 32.5 us
    all_gather x0 -> x2, blocking collectives: none -> 150 us  [the longest x1 138 us: shards(): tables = lax.all_gather(table, 'z', axis=0).reshape(N_Z, N_Y, N_Z, LANES)]
    all_to_all x2, waiting for transfers between devices: 160 us -> 50.4 us  [exchange(): lax.all_to_all(parts, ('y', 'z'), 0, 0, tiled=True).reshape(blocks.shape)]
    all_gather x1, waiting for transfers between devices: 35.1 us -> 0.02 us  [shards(): matrix = lax.all_gather(stacked, 'dp', axis=0, tiled=True)]
    pallas_call x2 -> x3, Pallas kernels: 14.5 us -> 21.4 us  [the longest x1 10.6 us: shards(): pl.pallas_call(back_kernel, grid=(PARTS,), out_shape=hbm((lines, width +...]
    all_to_all x2, starting transfers between devices: 26.3 us -> 32.2 us  [exchange(): lax.all_to_all(parts, ('y', 'z'), 0, 0, tiled=True).reshape(blocks.shape)]
  transfers between devices with their start and end apart: 4 -> 4, of which waited for: 4 -> 2; matrix products, arithmetic and copies ran while one was open for 2% -> 3% of each run, Pallas kernels for 0% -> 2%
where the time goes in v11:
time: 329 us; the launch traced here: 326 us
  blocking collectives  150 us (46%)
  waiting for transfers between devices  92.3 us (28%)
  starting transfers between devices  32.5 us (10%)
  Pallas kernels  25.6 us (8%)
  between operations  14.2 us (4%)
  matrix products  5.7 us (2%)
  local copies, waits for them, and re-layouts  3.56 us (1%)
    all_gather x1, blocking collectives, shards(): tables = lax.all_gather(table, 'z', axis=0).reshape(N_Z, N_Y, N_Z, LANES)  138 us
    all_to_all x2, waiting for transfers between devices, exchange(): lax.all_to_all(parts, ('y', 'z'), 0, 0, tiled=True).reshape(blocks.shape)  50.4 us
    reduce_scatter x1, waiting for transfers between devices, shards(): lax.psum_scatter(terms.astype(BF16), 'dp', scatter_dimension=0, tiled=True)  41.8 us
    all_to_all x2, starting transfers between devices, exchange(): lax.all_to_all(parts, ('y', 'z'), 0, 0, tiled=True).reshape(blocks.shape)  32.2 us
    all_gather x1, blocking collectives, shards(): lax.all_gather(tables.reshape(N_Z * N_Y, LANES), 'y', axis=0)  12.4 us
    pallas_call x1, Pallas kernels, shards(): pl.pallas_call(back_kernel, grid=(PARTS,), out_shape=hbm((lines, width +...  10.6 us
  transfers between devices with their start and end apart: 4, of which 2 were waited for; matrix products, arithmetic and copies ran while one was open for 3% of the time, Pallas kernels for 2%

profile of v11, /device:TPU:6, one launch (start us, length us, event | category | flops | bytes accessed | tf_op | source)
XLA Modules:
  0.0 326.1 jit_solution(11844322068759287601)
XLA Ops:
  7.2 0.0 copy-start.6
  7.2 0.0 copy-start.7
  7.2 4.3 %shard_map.111 = (bf16[512,2560]{1,0:T(8,128)(2,1)}, bf16[512,128]{1,0:T(8,128)(2,1)}, bf16[512,128]{1,0:T(8,128)(2,1)}, bf16[64,128]{1,0:T(8,128)(2,1)}) custom-call(s32[8,128]{1,0:T(8,128)} %bitcast.48, s32[8,128]{1,0:T(8,128)} %bitcast.49, bf16[128,2048]{1,0:T(8,128)(2,1)} %bitcast.38), custom_call_target="tpu_custom_call" | custom-call | tf_op jit(solution)/shard_map/pallas_call | solution.py:198
  11.5 0.0 copy-start.9
  11.5 0.0 copy-start.1
  11.5 18.9 %all-to-all-start = ((bf16[64,8,2560]{2,1,0:T(8,128)(2,1)}), bf16[64,8,2560]{2,1,0:T(8,128)(2,1)S(1)}, u32[]{:S(2)}, u32[]{:S(2)}) async-start(bf16[64,8,2560]{2,1,0:T(8,128)(2,1)} %bitcast.36), calls=%async_computation | async-start | bytes 5242880 | tf_op jit(solution)/shard_map/all_to_all | solution.py:193
  30.4 0.0 all-gather.3.cloned.1.call-start
  30.5 0.0 copy-done.6
  30.5 0.0 copy-done.7
  30.5 0.8 pad_maximum_fusion
  31.3 0.0 all-gather.3.cloned.1.call-update
  31.3 0.0 copy-done.9
  31.3 138.0 %all-gather = bf16[1024,128]{1,0:T(8,128)(2,1)S(1)} all-gather(bf16[64,128]{1,0:T(8,128)(2,1)S(1)} %copy-done.9), channel_id=2, replica_groups=mesh['dp'=8,'y'=4,'z'=16] {'z'}, dimensions={0}, use_global_device_ids=true | all-gather | bytes 278528 | tf_op jit(solution)/shard_map/all_gather | solution.py:222
  169.4 12.4 %all_gather.14 = bf16[4,64,128]{2,1,0:T(8,128)(2,1)S(1)} all-gather(bf16[1,64,128]{2,1,0:T(8,128)(2,1)S(1)} %bitcast.46), channel_id=1, replica_groups=mesh['dp'=8,'y'=4,'z'=16] {'y'}, dimensions={0}, use_global_device_ids=true | all-gather | bytes 81920 | tf_op jit(solution)/shard_map/all_gather | solution.py:224
  181.8 0.1 slice.21
  181.9 0.1 reshape.45
  182.0 0.1 copy.22
  182.0 0.1 reshape.47
  182.1 0.1 reshape.48
  182.2 0.0 copy-done.1
  182.2 0.0 copy-start
  182.2 1.0 copy-done
  183.3 0.7 shard_map.112.cotangent_ref
  184.0 0.0 all-to-all-done
  184.0 0.0 all-gather.3.cloned.1.call-done.matrix_ref
  184.0 10.6 %shard_map.113 = bf16[512,2560]{1,0:T(8,128)(2,1)} custom-call(bf16[512,2560]{1,0:T(8,128)(2,1)S(1)} %bitcast.31, bf16[2048,768]{1,0:T(8,128)(2,1)} %all-gather.3.cloned.1.call-done.matrix_ref, bf16[640,384]{1,0:T(8,128)(2,1)S(1)} %shard_map.112.cotangent_ref), custom_call_target="tpu_custom_call" | custom-call | tf_op jit(solution)/shard_map/pallas_call | solution.py:230
  194.6 13.4 %all-to-all-start.1 = ((bf16[64,8,2560]{2,1,0:T(8,128)(2,1)}), bf16[64,8,2560]{2,1,0:T(8,128)(2,1)}, u32[]{:S(2)}, u32[]{:S(2)}) async-start(bf16[64,8,2560]{2,1,0:T(8,128)(2,1)} %bitcast.35), calls=%async_computation.1 | async-start | bytes 5242880 | tf_op jit(solution)/shard_map/all_to_all | solution.py:193
  208.0 0.2 reduce-scatter.2.cloned.1.call-start
  208.2 0.2 copy.20.weight_ref
  208.4 0.0 copy-start.2
  208.4 0.9 copy-done.2
  209.3 6.5 %shard_map.114 = (bf16[640,384]{1,0:T(8,128)(2,1)}, bf16[512,768]{1,0:T(8,128)(2,1)}, bf16[128,768]{1,0:T(8,128)(2,1)}, bf16[128,2048]{1,0:T(8,128)(2,1)}) custom-call(bf16[512,2560]{1,0:T(8,128)(2,1)S(1)} %bitcast.32, bf16[2048,768]{1,0:T(8,128)(2,1)} %all-gather.3.cloned.1.call-done.matrix_ref, bf16[640,384]{1,0:T(8,128)(2,1)S(1)} %shard_map.112.cotangent_ref, ...), custom_call_target="tpu_custom_call" | custom-call | tf_op jit(solution)/shard_map/pallas_call | solution.py:240
  215.9 0.0 copy-start.5
  215.9 0.0 copy-start.8
  215.9 3.0 fusion
  218.9 0.0 copy-done.5
  218.9 0.0 copy-done.8
  218.9 2.7 add_convert_fusion
  221.6 0.0 copy-start.3
  221.6 0.0 copy-start.4
  221.6 0.0 reduce-scatter.2.cloned.1.call-update
  221.6 41.8 %reduce-scatter.2.cloned.1.call-done = bf16[256,768]{1,0:T(8,128)(2,1)} async-done(((bf16[2048,768]{1,0:T(8,128)(2,1)}), bf16[256,768]{1,0:T(8,128)(2,1)}) %reduce-scatter.2.cloned.1.call-update) | async-done | bytes 393232 | tf_op jit(solution)/shard_map/reduce_scatter | solution.py:267
  263.4 1.0 convert_element_type.15
  264.5 0.9 slice_bitcast_fusion
  265.4 50.4 %all-to-all-done.1 = bf16[64,8,2560]{2,1,0:T(8,128)(2,1)} async-done(((bf16[64,8,2560]{2,1,0:T(8,128)(2,1)}), bf16[64,8,2560]{2,1,0:T(8,128)(2,1)}, u32[]{:S(2)}, u32[]{:S(2)}) %all-to-all-start.1) | async-done | bytes 2621472 | tf_op jit(solution)/shard_map/all_to_all | solution.py:193
  315.8 0.0 copy-done.3
  315.8 0.0 copy-done.4
  315.8 3.4 %shard_map.115 = f32[128,2048]{1,0:T(8,128)} custom-call(bf16[512,128]{1,0:T(8,128)(2,1)S(1)} %copy-done.3, bf16[512,128]{1,0:T(8,128)(2,1)S(1)} %copy-done.4, bf16[512,2560]{1,0:T(8,128)(2,1)} %bitcast.19.blocks_ref), custom_call_target="tpu_custom_call" | custom-call | tf_op jit(solution)/shard_map/pallas_call | solution.py:24
  (4 shorter events, 0.1 us)
Async XLA Ops:
  7.2 23.3 %copy-start.6 = (bf16[1,256,384]{2,1,0:T(8,128)(2,1)S(1)}, bf16[1,256,384]{2,1,0:T(8,128)(2,1)}, u32[]{:S(2)}) copy-start(bf16[1,256,384]{2,1,0:T(8,128)(2,1)} %param.12) | copy-start | bytes 589828
  7.2 23.3 %copy-start.7 = (bf16[1,256,384]{2,1,0:T(8,128)(2,1)S(1)}, bf16[1,256,384]{2,1,0:T(8,128)(2,1)}, u32[]{:S(2)}) copy-start(bf16[1,256,384]{2,1,0:T(8,128)(2,1)} %param.11) | copy-start | bytes 589828
  11.5 19.8 %copy-start.9 = (bf16[64,128]{1,0:T(8,128)(2,1)S(1)}, bf16[64,128]{1,0:T(8,128)(2,1)}, u32[]{:S(2)}) copy-start(bf16[64,128]{1,0:T(8,128)(2,1)} %get-tuple-element.16) | copy-start | bytes 49156
  11.5 170.7 %copy-start.1 = (s32[640,1]{1,0:T(8,128)S(1)}, s32[640,1]{1,0:T(8,128)}, u32[]{:S(2)}) copy-start(s32[640,1]{1,0:T(8,128)} %constant.24.clone.row_ref) | copy-start | bytes 7684
  11.5 172.5 %all-to-all-start = ((bf16[64,8,2560]{2,1,0:T(8,128)(2,1)}), bf16[64,8,2560]{2,1,0:T(8,128)(2,1)S(1)}, u32[]{:S(2)}, u32[]{:S(2)}) async-start(bf16[64,8,2560]{2,1,0:T(8,128)(2,1)} %bitcast.36), calls=%async_computation | async-start | bytes 5242880 | tf_op jit(solution)/shard_map/all_to_all | solution.py:193
  30.4 153.6 %all-gather.3.cloned.1.call-start = ((), (), s32[]{:S(2)}) async-start(), calls=%async_computation.3 | async-start | bytes 3538944 | tf_op jit(solution)/shard_map/all_gather | solution.py:211
  182.2 1.0 copy-start
  194.6 121.2 %all-to-all-start.1 = ((bf16[64,8,2560]{2,1,0:T(8,128)(2,1)}), bf16[64,8,2560]{2,1,0:T(8,128)(2,1)}, u32[]{:S(2)}, u32[]{:S(2)}) async-start(bf16[64,8,2560]{2,1,0:T(8,128)(2,1)} %bitcast.35), calls=%async_computation.1 | async-start | bytes 5242880 | tf_op jit(solution)/shard_map/all_to_all | solution.py:193
  208.0 55.4 %reduce-scatter.2.cloned.1.call-start = ((), (), s32[]{:S(2)}) async-start(), calls=%async_computation.4 | async-start | bytes 3538944 | tf_op jit(solution)/shard_map/reduce_scatter | solution.py:267
  208.4 0.9 copy-start.2
  215.9 3.1 copy-start.5
  215.9 3.1 copy-start.8
  221.6 94.2 %copy-start.3 = (bf16[512,128]{1,0:T(8,128)(2,1)S(1)}, bf16[512,128]{1,0:T(8,128)(2,1)}, u32[]{:S(2)}) copy-start(bf16[512,128]{1,0:T(8,128)(2,1)} %get-tuple-element.21.main_ref) | copy-start | bytes 393220
  221.6 94.2 %copy-start.4 = (bf16[512,128]{1,0:T(8,128)(2,1)S(1)}, bf16[512,128]{1,0:T(8,128)(2,1)}, u32[]{:S(2)}) copy-start(bf16[512,128]{1,0:T(8,128)(2,1)} %get-tuple-element.22.extra_ref) | copy-start | bytes 393220
Sparse Core Ops, SparseCore 0:
  33.9 35.1 all-gather.2
  221.8 41.6 reduce-scatter.1

commit v12 on v10

--- a/solution.py
+++ b/solution.py
@@ -58,14 +58,17 @@
 ):
     pairs = ((ids_in, ids_ref), (weights_in, weights_ref), (tokens_in, tokens_ref))
     copies = [pltpu.make_async_copy(here, there, fetched.at[i]) for i, (here, there) in enumerate(pairs)]
-    for copy in copies:
-        copy.start()
-    for copy in copies[:2]:
-        copy.wait()
+    @pl.when(pl.program_id(0) == 0)
+    def _():
+        for copy in copies:
+            copy.start()
+        for copy in copies:
+            copy.wait()
+
     tokens, width = tokens_ref.shape
     step = width // QUARTERS
     shape = (out_ref.shape[0], tokens)
-    row = iota(shape, 0)
+    row = iota(shape, 0) + pl.program_id(0) * shape[0]
     expert, line = row // LINES, row & (LINES - 1)
     hits = jnp.zeros(shape, F32)
     eighths = jnp.zeros(shape, F32)
@@ -81,7 +84,6 @@
     main, extra = one_hot(is_main), one_hot(is_extra)
     main_ref[...] = main
     extra_ref[...] = extra
-    copies[2].wait()
     out_ref[:, :width] = dot(main, tokens_ref[...]).astype(BF16)
     beside = dot(of_quarter(extra, 0), tokens_ref[:, :step])
     for quarter in range(1, QUARTERS):
@@ -151,14 +153,11 @@
     hidden_ref[...] = dot(move, hidden).astype(BF16)
 
 
-def token_kernel(main_ref, extra_ref, blocks_ref, out_ref):
-    width = out_ref.shape[1]
-    step = width // QUARTERS
+def token_kernel(main_ref, extra_ref, blocks_ref, beside_ref, out_ref):
     extra = extra_ref[...]
-    total = dot(main_ref[...], blocks_ref[:, :width], (0, 0))
-    for quarter in range(QUARTERS):
-        part = slice(quarter * step, (quarter + 1) * step)
-        out_ref[:, part] = total[:, part] + dot(of_quarter(extra, quarter), blocks_ref[:, width:], (0, 0))
+    line = iota(extra.shape, 0) & (QUARTERS - 1)
+    own = jnp.where(line == pl.program_id(0), extra, jnp.zeros_like(extra))
+    out_ref[...] = dot(main_ref[...], blocks_ref[...], (0, 0)) + dot(own, beside_ref[...], (0, 0))
 
 
 def shards(tokens, expert_ids, route_weights, gate_weight, up_weight, cotangent):
@@ -177,10 +176,12 @@
     out_blocks = ((lines, width + step + LANES), (lines, block), (lines, block))
     outgoing, main, extra = pl.pallas_call(
         source_kernel,
-        grid=(1,),
+        grid=(QUARTERS,),
         out_shape=(hbm((lines, width + step + LANES)), hbm((lines, block)), hbm((lines, block))),
         in_specs=[pl.BlockSpec(memory_space=pltpu.HBM)] * 3,
-        out_specs=tuple(pl.BlockSpec(shape, lambda step: (0, 0)) for shape in out_blocks),
+        out_specs=tuple(
+            pl.BlockSpec((rows // QUARTERS, columns), lambda part: (part, 0)) for rows, columns in out_blocks
+        ),
         scratch_shapes=[pltpu.VMEM(value.shape, value.dtype) for value in sources]
         + [pltpu.SemaphoreType.DMA((3,))],
         compiler_params=PARAMS,
@@ -224,7 +225,20 @@
         ),
         compiler_params=PARAMS,
     )(arrived, matrix, cotangent_rows, jnp.asarray(np.argsort(order).astype(np.int32)[:, None]))
-    token_grads = call(token_kernel, array((block, width), F32), main, extra, exchange(back))
+    returned = exchange(back)
+    token_grads = pl.pallas_call(
+        token_kernel,
+        grid=(QUARTERS,),
+        out_shape=array((block, width), F32),
+        in_specs=[
+            pl.BlockSpec((lines, block), lambda part: (0, 0)),
+            pl.BlockSpec((lines, block), lambda part: (0, 0)),
+            pl.BlockSpec((lines, step), lambda part: (0, part)),
+            pl.BlockSpec((lines, step), lambda part: (0, QUARTERS)),
+        ],
+        out_specs=pl.BlockSpec((block, step), lambda part: (0, part)),
+        compiler_params=PARAMS,
+    )(main, extra, returned, returned)
 
     terms = dot(arrived[:, :width], main_grads, (0, 0)) + dot(extra_rows, extra_grads, (0, 0))
     weight_grads = lax.psum_scatter(terms.astype(BF16), "dp", scatter_dimension=0, tiled=True).astype(F32)

time: 306 us -> 308 us (level)
    pallas_call x1 -> x2, Pallas kernels: 4.13 us -> 9.4 us  [the longest x1 5.02 us: shards(): pl.pallas_call(source_kernel, grid=(QUARTERS,), out_shape=(hbm((lines, wi...]
    pallas_call x2 -> x1, Pallas kernels: 4.19 us -> 0.74 us  [call(): pl.pallas_call(kernel, out_shape=out_shape, in_specs=[whole] * len(operan...]
where the time goes in v12:
time: 308 us; the launch traced here: 307 us
  waiting for transfers between devices  237 us (77%)
  starting transfers between devices  26.4 us (9%)
  Pallas kernels  20.5 us (7%)
  between operations  14.2 us (5%)
  matrix products  4.5 us (1%)
    all_to_all x2, waiting for transfers between devices, exchange(): lax.all_to_all(parts, 'expert', 0, 0, tiled=True).reshape(blocks.shape)  160 us
    reduce_scatter x1, waiting for transfers between devices, shards(): lax.psum_scatter(terms.astype(BF16), 'dp', scatter_dimension=0, tiled=True)  41.8 us
    all_gather x1, waiting for transfers between devices, shards(): matrix = lax.all_gather(stacked, 'dp', axis=0, tiled=True)  35 us
    all_to_all x2, starting transfers between devices, exchange(): lax.all_to_all(parts, 'expert', 0, 0, tiled=True).reshape(blocks.shape)  26.3 us
    pallas_call x1, Pallas kernels, shards(): pl.pallas_call(expert_kernel, grid=(PARTS,), out_shape=(array((slot_count...  10.4 us
  transfers between devices with their start and end apart: 4, of which 4 were waited for; matrix products, arithmetic and copies ran while one was open for 2% of the time, Pallas kernels for 0%

profile of v12, /device:TPU:6, one launch (start us, length us, event | category | flops | bytes accessed | tf_op | source)
XLA Modules:
  0.0 307.1 jit_solution(13846734662830242096)
XLA Ops:
  7.2 0.0 copy-start.7
  7.2 0.0 copy-start.8
  7.2 5.0 %shard_map.111 = (bf16[512,2688]{1,0:T(8,128)(2,1)}, bf16[512,128]{1,0:T(8,128)(2,1)}, bf16[512,128]{1,0:T(8,128)(2,1)}) custom-call(s32[8,128]{1,0:T(8,128)} %bitcast.32, s32[8,128]{1,0:T(8,128)} %bitcast.33, bf16[128,2048]{1,0:T(8,128)(2,1)} %bitcast.29), custom_call_target="tpu_custom_call" | custom-call | tf_op jit(solution)/shard_map/pallas_call | solution.py:177
  12.2 0.0 copy-start.2
  12.2 18.9 %all-to-all-start = ((bf16[64,8,2688]{2,1,0:T(8,128)(2,1)}), bf16[64,8,2688]{2,1,0:T(8,128)(2,1)S(1)}, u32[]{:S(2)}, u32[]{:S(2)}) async-start(bf16[64,8,2688]{2,1,0:T(8,128)(2,1)} %bitcast.26), calls=%async_computation | async-start | bytes 5505024 | tf_op jit(solution)/shard_map/all_to_all | solution.py:172
  31.1 0.0 all-gather.2.cloned.1.call-start
  31.2 0.0 copy-done.7
  31.2 0.0 copy-done.8
  31.2 0.8 pad_maximum_fusion
  32.0 0.0 all-gather.2.cloned.1.call-update
  32.0 0.0 copy-start
  32.0 1.0 copy-done
  33.0 0.0 copy-start.1
  33.0 1.0 copy-done.1
  34.0 0.7 shard_map.112.cotangent_ref
  34.7 35.0 %all-gather.2.cloned.1.call-done.matrix_ref = bf16[2048,768]{1,0:T(8,128)(2,1)} async-done(((bf16[256,768]{1,0:T(8,128)(2,1)}), bf16[2048,768]{1,0:T(8,128)(2,1)}) %all-gather.2.cloned.1.call-update) | async-done | bytes 3145744 | tf_op jit(solution)/shard_map/all_gather | solution.py:192
  69.8 87.9 %all-to-all-done = bf16[64,8,2688]{2,1,0:T(8,128)(2,1)S(1)} async-done(((bf16[64,8,2688]{2,1,0:T(8,128)(2,1)}), bf16[64,8,2688]{2,1,0:T(8,128)(2,1)S(1)}, u32[]{:S(2)}, u32[]{:S(2)}) %all-to-all-start) | async-done | bytes 2752544 | tf_op jit(solution)/shard_map/all_to_all | solution.py:172
  157.7 0.0 copy-done.2
  157.7 10.4 %shard_map.113 = (bf16[640,384]{1,0:T(8,128)(2,1)}, bf16[512,768]{1,0:T(8,128)(2,1)}, bf16[128,768]{1,0:T(8,128)(2,1)}, bf16[128,2048]{1,0:T(8,128)(2,1)}, bf16[512,2560]{1,0:T(8,128)(2,1)}) custom-call(bf16[512,2688]{1,0:T(8,128)(2,1)S(1)} %bitcast.23, bf16[2048,768]{1,0:T(8,128)(2,1)} %all-gather.2.cloned.1.call-done.matrix_ref, ...), custom_call_target="tpu_custom_call" | custom-call | tf_op jit(solution)/shard_map/pallas_call | solution.py:203
  168.1 0.0 copy-start.5
  168.1 7.4 %all-to-all-start.1 = ((bf16[64,8,2560]{2,1,0:T(8,128)(2,1)}), bf16[64,8,2560]{2,1,0:T(8,128)(2,1)}, u32[]{:S(2)}, u32[]{:S(2)}) async-start(bf16[64,8,2560]{2,1,0:T(8,128)(2,1)} %bitcast.27), calls=%async_computation.1 | async-start | bytes 5242880 | tf_op jit(solution)/shard_map/all_to_all | solution.py:172
  175.6 0.0 reduce-scatter.2.cloned.1.call-start
  175.6 0.0 copy-done.5
  175.6 0.0 copy-start.6
  175.6 0.0 copy-start.9
  175.6 1.8 fusion
  177.5 0.0 copy-done.6
  177.5 0.0 copy-done.9
  177.5 2.7 add_convert_fusion
  180.2 0.0 copy-start.3
  180.2 0.0 copy-start.4
  180.2 0.0 reduce-scatter.2.cloned.1.call-update
  180.2 41.8 %reduce-scatter.2.cloned.1.call-done = bf16[256,768]{1,0:T(8,128)(2,1)} async-done(((bf16[2048,768]{1,0:T(8,128)(2,1)}), bf16[256,768]{1,0:T(8,128)(2,1)}) %reduce-scatter.2.cloned.1.call-update) | async-done | bytes 393232 | tf_op jit(solution)/shard_map/reduce_scatter | solution.py:244
  222.0 1.0 convert_element_type.7
  223.1 0.9 slice_bitcast_fusion
  224.0 71.9 %all-to-all-done.1 = bf16[64,8,2560]{2,1,0:T(8,128)(2,1)} async-done(((bf16[64,8,2560]{2,1,0:T(8,128)(2,1)}), bf16[64,8,2560]{2,1,0:T(8,128)(2,1)}, u32[]{:S(2)}, u32[]{:S(2)}) %all-to-all-start.1) | async-done | bytes 2621472 | tf_op jit(solution)/shard_map/all_to_all | solution.py:172
  295.9 0.0 copy-done.3
  295.9 0.0 copy-done.4
  295.9 4.4 %shard_map.114 = f32[128,2048]{1,0:T(8,128)} custom-call(bf16[512,128]{1,0:T(8,128)(2,1)S(1)} %copy-done.3, bf16[512,128]{1,0:T(8,128)(2,1)S(1)} %copy-done.4, bf16[512,2560]{1,0:T(8,128)(2,1)} %bitcast.12.blocks_ref.beside_ref, bf16[512,2560]{1,0:T(8,128)(2,1)} %bitcast.12.blocks_ref.beside_ref), custom_call_target="tpu_custom_call" | custom-call | tf_op jit(solution)/shard_map/pallas_call | solution.py:229
Async XLA Ops:
  7.2 24.0 %copy-start.7 = (bf16[1,256,384]{2,1,0:T(8,128)(2,1)S(1)}, bf16[1,256,384]{2,1,0:T(8,128)(2,1)}, u32[]{:S(2)}) copy-start(bf16[1,256,384]{2,1,0:T(8,128)(2,1)} %param.12) | copy-start | bytes 589828
  7.2 24.0 %copy-start.8 = (bf16[1,256,384]{2,1,0:T(8,128)(2,1)S(1)}, bf16[1,256,384]{2,1,0:T(8,128)(2,1)}, u32[]{:S(2)}) copy-start(bf16[1,256,384]{2,1,0:T(8,128)(2,1)} %param.11) | copy-start | bytes 589828
  12.2 145.5 %copy-start.2 = (s32[320,1]{1,0:T(8,128)S(1)}, s32[320,1]{1,0:T(8,128)}, u32[]{:S(2)}) copy-start(s32[320,1]{1,0:T(8,128)} %constant.5.clone.row_ref) | copy-start | bytes 3844
  12.2 145.5 %all-to-all-start = ((bf16[64,8,2688]{2,1,0:T(8,128)(2,1)}), bf16[64,8,2688]{2,1,0:T(8,128)(2,1)S(1)}, u32[]{:S(2)}, u32[]{:S(2)}) async-start(bf16[64,8,2688]{2,1,0:T(8,128)(2,1)} %bitcast.26), calls=%async_computation | async-start | bytes 5505024 | tf_op jit(solution)/shard_map/all_to_all | solution.py:172
  31.1 38.7 %all-gather.2.cloned.1.call-start = ((), (), s32[]{:S(2)}) async-start(), calls=%async_computation.3 | async-start | bytes 3538944 | tf_op jit(solution)/shard_map/all_gather | solution.py:192
  32.0 1.0 copy-start
  33.0 1.0 copy-start.1
  168.1 7.5 %copy-start.5 = (bf16[512,768]{1,0:T(8,128)(2,1)S(1)}, bf16[512,768]{1,0:T(8,128)(2,1)}, u32[]{:S(2)}) copy-start(bf16[512,768]{1,0:T(8,128)(2,1)} %get-tuple-element.17) | copy-start | bytes 2359300
  168.1 127.8 %all-to-all-start.1 = ((bf16[64,8,2560]{2,1,0:T(8,128)(2,1)}), bf16[64,8,2560]{2,1,0:T(8,128)(2,1)}, u32[]{:S(2)}, u32[]{:S(2)}) async-start(bf16[64,8,2560]{2,1,0:T(8,128)(2,1)} %bitcast.27), calls=%async_computation.1 | async-start | bytes 5242880 | tf_op jit(solution)/shard_map/all_to_all | solution.py:172
  175.6 46.5 %reduce-scatter.2.cloned.1.call-start = ((), (), s32[]{:S(2)}) async-start(), calls=%async_computation.4 | async-start | bytes 3538944 | tf_op jit(solution)/shard_map/reduce_scatter | solution.py:244
  175.6 1.9 copy-start.6
  175.6 1.9 copy-start.9
  180.2 115.7 %copy-start.3 = (bf16[512,128]{1,0:T(8,128)(2,1)S(1)}, bf16[512,128]{1,0:T(8,128)(2,1)}, u32[]{:S(2)}) copy-start(bf16[512,128]{1,0:T(8,128)(2,1)} %get-tuple-element.14.main_ref) | copy-start | bytes 393220
  180.2 115.7 %copy-start.4 = (bf16[512,128]{1,0:T(8,128)(2,1)S(1)}, bf16[512,128]{1,0:T(8,128)(2,1)}, u32[]{:S(2)}) copy-start(bf16[512,128]{1,0:T(8,128)(2,1)} %get-tuple-element.15.extra_ref) | copy-start | bytes 393220
Sparse Core Ops, SparseCore 0:
  34.6 35.0 all-gather.1
  180.3 41.6 reduce-scatter.1
